TPU v7x, 256 devices: a whole 4x4x8 slice. The times are simulated.
256 devices in a mesh: alpha: 16 (over z_hi, x), beta: 4 (over z_lo, core), chol: 4 (over y).
Axes of the slice: x: 4, y: 4, z: 8 (z_hi: 4, z_lo: 2; z = z_hi * 2 + z_lo), core: 2. Of those that a mesh axis runs over, the one named last changes fastest.
Arguments:
- ci_vector: bfloat16 [2048, 4096], P('alpha', 'beta'), may hold values from -6 to 6
- a_tiles: bfloat16 [64, 16, 6, 128, 128], P('chol', 'alpha'), may hold values from -0.21875 to 0.21875
- a_source: int32 [16, 6], P('alpha'), may hold values from 0 to 15
- a_sign: int32 [16, 6], P('alpha'), may hold values from -1 to 1, as said below
- b_tiles: bfloat16 [64, 32, 3, 128, 128], P('chol', 'beta'), may hold values from -0.0390625 to 0.0390625
- b_source: int32 [32, 3], P('beta'), may hold values from 0 to 31
- b_sign: int32 [32, 3], P('beta'), may hold values from -1 to 1, as said below
Outputs:
- sigma_out: bfloat16 [2048, 4096], P('alpha', ('beta', 'chol'))
Inputs may be any that keep to these rules, and one draw needn't show every extreme that they name: `a_sign`: in each row the first c slots are live with sign +1 or -1 and the rest are 0, c between 1 and 6; some row has all 6 slots live. `b_sign`: in each row the first c slots are live with sign +1 or -1 and the rest are 0, c between 1 and 3; some row has all 3 slots live.
All inputs are finite; a program needn't handle non-finite values.
Results may differ from a plain program's by a relative error of at most 0.0049.
Values may be sent and summed in bfloat16 or wider, within the bound.
No kernel may reach another device: no remote copies, remote signals or barrier semaphores. Data moves between devices by JAX's collectives and lax.ppermute only.
A program may use at most 128 MiB of HBM per device.

v0:
```python
import jax
import jax.numpy as jnp
from jax import lax
from jax.sharding import PartitionSpec as P


def build_panel(source_rows, a_tiles, a_source, a_sign):
    block_size = a_tiles.shape[-1]
    stacked = source_rows.reshape(-1, block_size, source_rows.shape[1])
    picked = jnp.take(stacked, a_source[0], axis=0)
    weighted = a_tiles[:, 0] * a_sign[0].astype(jnp.bfloat16)[None, :, None, None]
    product = jnp.einsum("qkij,kjn->qin", weighted, picked, preferred_element_type=jnp.float32)
    return product.astype(jnp.bfloat16)


def per_device(ci_vector, a_tiles, a_source, a_sign, b_tiles, b_source, b_sign):
    beta_rows = lax.all_gather(ci_vector, "beta", axis=1, tiled=True)
    all_rows = lax.all_gather(beta_rows, "alpha", axis=0, tiled=True)
    panel = build_panel(all_rows, a_tiles, a_source, a_sign)
    block_size = a_tiles.shape[-1]
    vectors = panel.shape[0]
    column_blocks = panel.reshape(vectors, block_size, -1, block_size)
    chosen = jnp.take(column_blocks, b_source, axis=2)
    weighted_b = b_tiles * b_sign.astype(jnp.bfloat16)[None, :, :, None, None]
    partial_sum = jnp.einsum(
        "qiulm,qulrm->iur", chosen, weighted_b, preferred_element_type=jnp.float32
    )
    partial_sum = partial_sum.reshape(block_size, -1)
    return lax.psum_scatter(partial_sum, "chol", scatter_dimension=1, tiled=True).astype(
        jnp.bfloat16
    )


def solution(mesh):
    placed = (
        P("alpha", "beta"),
        P("chol", "alpha", None, None, None),
        P("alpha", None),
        P("alpha", None),
        P("chol", "beta", None, None, None),
        P("beta", None),
        P("beta", None),
    )
    return jax.shard_map(
        per_device,
        mesh=mesh,
        in_specs=placed,
        out_specs=P("alpha", ("beta", "chol")),
        check_vma=False,
    )
```

profile of v0, /device:TPU:6, one launch (start us, length us, event | category | flops | bytes accessed | tf_op | source)
XLA Modules:
  0.0 329.0 jit_solution(12011580073282993414)
XLA Ops:
  6.5 0.0 all-gather.3.cloned.1.call-start
  6.5 0.7 all-gather.3.cloned.1.call-update
  7.3 0.0 all-gather.5.cloned.1.call-start
  7.3 28.1 %all-gather.3.cloned.1.call-done = bf16[128,4096]{1,0:T(8,128)(2,1)} async-done(((bf16[128,1024]{1,0:T(8,128)(2,1)}), bf16[128,4096]{1,0:T(8,128)(2,1)}) %all-gather.3.cloned.1.call-update) | async-done | bytes 1048592 | tf_op jit(solution)/shard_map/all_gather | solution.py:17
  35.4 0.0 all-gather.5.cloned.1.call-update
  35.4 0.0 reduce-scatter.2.cloned.1.call-start
  35.5 0.7 compare_select_fusion
  36.2 0.1 copy.16
  36.2 0.1 reshape.68
  36.3 0.7 convert_element_type.19
  37.0 0.1 copy.14
  37.1 0.7 compare_and_fusion.1
  37.8 0.1 copy.15
  37.9 0.7 fusion.10
  38.6 0.7 compare_and_fusion
  39.2 0.7 convert_bitcast_fusion
  39.9 189.1 %all-gather.5.cloned.1.call-done = bf16[2048,4096]{1,0:T(8,128)(2,1)} async-done(((bf16[128,4096]{1,0:T(8,128)(2,1)}), bf16[2048,4096]{1,0:T(8,128)(2,1)}) %all-gather.5.cloned.1.call-update) | async-done | bytes 16777232 | tf_op jit(solution)/shard_map/all_gather | solution.py:18
  229.0 9.8 %gather_fusion = bf16[6,128,4096]{2,1,0:T(8,128)(2,1)} fusion(bf16[16,128,4096]{2,1,0:T(8,128)(2,1)} %bitcast.39, s32[1024]{0:T(1024)S(1)} %pad_clamp_fusion.1), kind=kCustom, calls=%fused_computation | custom fusion | bytes 12582936 | tf_op jit(solution)/shard_map/jit(_take)/gather | solution.py:10
  238.8 16.5 %fusion = bf16[16,16,32,8,128]{4,3,2,1,0:T(8,128)(2,1)S(1)} fusion(bf16[6,128,4096]{2,1,0:T(8,128)(2,1)} %gather_fusion, pred[6]{0:T(512)(128)(4,1)S(1)} %compare_and_fusion, bf16[16,1,6,128,128]{4,3,2,1,0:T(8,128)(2,1)} %param.8, bf16[6]{0:T(256)(128)(2,1)S(1)} %convert_bitcast_fusion), kind=kOutput, calls=%fused_computation.3 | convolution fusion | flops 12898009088 | bytes 26214418 | tf_op jit(solution)/shard_map/qkij,kjn->qin/dot_general | solution.py:12
  255.3 8.3 %copy.28 = bf16[16,16,32,8,128]{4,3,1,2,0:T(8,128)(2,1)} copy(bf16[16,16,32,8,128]{4,3,2,1,0:T(8,128)(2,1)S(1)} %fusion) | data formatting | bytes 33554432 | tf_op jit(solution)/shard_map/reshape | solution.py:22
  263.6 11.8 %gather_fusion.1 = bf16[24,16,128,128]{3,2,1,0:T(8,128)(2,1)} fusion(bf16[16,128,32,128]{3,1,2,0:T(8,128)(2,1)} %bitcast.37, s32[1024]{0:T(1024)S(1)} %pad_clamp_fusion), kind=kCustom, calls=%fused_computation.1 | custom fusion | bytes 25165920 | tf_op jit(solution)/shard_map/jit(_take)/gather | solution.py:23
  275.5 10.1 %fusion.1 = f32[8,128,128,1,1]{2,1,3,0,4:T(8,128)S(1)} fusion(bf16[16,8,3,128,128]{4,3,2,1,0:T(8,128)(2,1)} %param.11, bf16[8,3]{1,0:T(8,128)(2,1)S(1)} %copy.14, bf16[8,3,16,128,128]{4,3,2,1,0:T(8,128)(2,1)} %bitcast.38, pred[8,3]{1,0:T(8,128)(4,1)S(1)} %copy.15), kind=kOutput, calls=%fused_computation.5 | convolution fusion | flops 1623195648 | bytes 25690184 | tf_op jit(solution)/shard_map/qiulm,qulrm->iur/dot_general | solution.py:25
  285.6 1.0 copy.19
  286.6 0.0 reduce-scatter.2.cloned.1.call-update
  286.6 34.3 %reduce-scatter.2.cloned.1.call-done = f32[128,256]{1,0:T(8,128)} async-done(((f32[128,1024]{1,0:T(8,128)}), f32[128,256]{1,0:T(8,128)}) %reduce-scatter.2.cloned.1.call-update) | async-done | bytes 131088 | tf_op jit(solution)/shard_map/reduce_scatter | solution.py:29
  321.0 1.5 convert_element_type.23
  (2 shorter events, 0.0 us)
Async XLA Ops:
  6.5 28.9 %all-gather.3.cloned.1.call-start = ((), (), s32[]{:S(2)}) async-start(), calls=%async_computation.1 | async-start | bytes 1310720 | tf_op jit(solution)/shard_map/all_gather | solution.py:17
  7.3 221.7 %all-gather.5.cloned.1.call-start = ((), (), s32[]{:S(2)}) async-start(), calls=%async_computation.2 | async-start | bytes 17825792 | tf_op jit(solution)/shard_map/all_gather | solution.py:18
  35.4 285.5 %reduce-scatter.2.cloned.1.call-start = ((), (), s32[]{:S(2)}) async-start(), calls=%async_computation.3 | async-start | bytes 655360 | tf_op jit(solution)/shard_map/reduce_scatter | solution.py:29
Sparse Core Ops, SparseCore 0:
  9.2 26.1 all-gather.2
  37.8 191.1 all-gather.4
  286.8 34.1 reduce-scatter.1
where the time goes:
time: 329 us
  waiting for transfers between devices  252 us (77%)
  local copies, waits for them, and re-layouts  31.3 us (10%)
  matrix products  26.6 us (8%)
  between operations  13.1 us (4%)
  other arithmetic  5.59 us (2%)
    all_gather x1, waiting for transfers between devices, per_device(): all_rows = lax.all_gather(beta_rows, 'alpha', axis=0, tiled=True)  189 us
    reduce_scatter x1, waiting for transfers between devices, per_device(): lax.psum_scatter(partial_sum, 'chol', scatter_dimension=1, tiled=True)  34.3 us
    all_gather x1, waiting for transfers between devices, per_device(): beta_rows = lax.all_gather(ci_vector, 'beta', axis=1, tiled=True)  28.1 us
    dot_general x1, matrix products, build_panel(): jnp.einsum('qkij,kjn->qin', weighted, picked, preferred_element_type=jnp....  16.5 us
    gather x1, local copies, waits for them, and re-layouts, per_device(): chosen = jnp.take(column_blocks, b_source, axis=2)  11.8 us
    dot_general x1, matrix products, per_device(): jnp.einsum('qiulm,qulrm->iur', chosen, weighted_b, preferred_element_type...  10.1 us
    gather x1, local copies, waits for them, and re-layouts, build_panel(): picked = jnp.take(stacked, a_source[0], axis=0)  9.81 us
    reshape x1, local copies, waits for them, and re-layouts, per_device(): column_blocks = panel.reshape(vectors, block_size, -1, block_size)  8.32 us
  transfers between devices with their start and end apart: 3, of which 3 were waited for; matrix products, arithmetic and copies ran while one was open for 1% of the time, Pallas kernels for 0%

commit v1 on v0

v1 whole, which is shorter than its diff:
```python
import jax
import jax.numpy as jnp
from jax import lax
from jax.experimental import pallas as pl
from jax.experimental.pallas import tpu as pltpu
from jax.sharding import PartitionSpec as P

BLK = 128
VECTORS_PER_DOT = 2
VECTORS_PER_GROUP = 4
X_SIZE = 4
SMEM = pl.BlockSpec(memory_space=pltpu.SMEM)
VMEM = pl.BlockSpec(memory_space=pltpu.VMEM)
HBM = pl.BlockSpec(memory_space=pltpu.HBM)


def shifted(value, axis, size, moves_to):
    return lax.ppermute(value, axis, [(i, moves_to(i)) for i in range(size)])


def pick_kernel(place_ref, source_ref, sign_ref, own_ref, next_ref, prev_ref, far_low_ref, far_high_ref, out_ref):
    slots = source_ref.shape[1]
    alpha = place_ref[0]
    for k in range(slots):
        source = source_ref[0, k]
        sign = sign_ref[0, k].astype(jnp.float32).astype(out_ref.dtype)
        dz = lax.rem(source // X_SIZE - alpha // X_SIZE + 4, 4)
        dx = lax.rem(source % X_SIZE - alpha % X_SIZE + X_SIZE, X_SIZE)

        def put(ref, at, k=k, sign=sign):
            for half in range(2):
                out_ref[half, k * BLK : (k + 1) * BLK, :] = (
                    ref[at, :, half * BLK : (half + 1) * BLK] * sign
                )

        for distance, ref in ((0, own_ref), (1, next_ref), (3, prev_ref)):

            @pl.when(dx == distance)
            def _(ref=ref):
                put(ref, dz)

        @pl.when(jnp.logical_and(dx == 2, dz < 2))
        def _():
            put(far_low_ref, jnp.minimum(dz, 1))

        @pl.when(jnp.logical_and(dx == 2, dz >= 2))
        def _():
            put(far_high_ref, jnp.maximum(dz - 2, 0))


def choose(index, low, high, act):
    if high - low == 1:
        act(low)
        return
    middle = (low + high) // 2

    @pl.when(index < middle)
    def _():
        choose(index, low, middle, act)

    @pl.when(index >= middle)
    def _():
        choose(index, middle, high, act)


def contract_kernel(place_ref, source_ref, sign_ref, a_hbm, b_ref, *rest):
    units = rest[:16]
    own_ref, *piece_refs = rest[16:20]
    acc, tasks, a_ref, c_buf, b_buf, a_sem, c_sem, b_sem = rest[20:]
    pairs = sign_ref.shape[0] * sign_ref.shape[1]
    slots = sign_ref.shape[1]
    vectors, a_slots = a_ref.shape[:2]
    beta, chol = place_ref[1], place_ref[2]
    a_copy = pltpu.make_async_copy(a_hbm, a_ref, a_sem)
    a_copy.start()
    acc[...] = jnp.zeros_like(acc)

    count = jnp.int32(0)
    for pair in range(pairs):
        tasks[count] = pair
        count = count + jnp.where(sign_ref[pair // slots, pair % slots] != 0, 1, 0)
    steps = (count + 1) // 2

    def task_of(step, half):
        at = jnp.minimum(2 * step + half, count - 1)
        pair = tasks[at]
        u = pair // slots
        l = pair - u * slots
        return u, l

    def c_copy(unit, m, slot, half):
        return pltpu.make_async_copy(
            unit.at[m & 1], c_buf.at[slot, :, pl.ds(half * BLK, BLK)], c_sem.at[slot, half]
        )

    def b_copy(u, l, slot, half):
        return pltpu.make_async_copy(b_ref.at[:, u, l], b_buf.at[slot, half], b_sem.at[slot, half])

    def start(step, slot):
        for half in range(2):
            u, l = task_of(step, half)
            b_copy(u, l, slot, half).start()
            m = source_ref[u, l]
            distance = ((m >> 3) ^ beta) * 4 + (((m >> 1) - chol) & 3)
            choose(distance, 0, len(units), lambda i: c_copy(units[i], m, slot, half).start())

    @pl.when(steps > 0)
    def _():
        start(0, 0)

    a_copy.wait()

    def body(step, carry):
        slot = step & 1

        @pl.when(step + 1 < steps)
        def _():
            start(step + 1, 1 - slot)

        for half in range(2):
            c_copy(units[0], 0, slot, half).wait()
            b_copy(0, 0, slot, half).wait()
        sums = [jnp.zeros((BLK, BLK), jnp.float32) for _ in range(2)]
        for group in range(0, vectors, VECTORS_PER_GROUP):
            panels = []
            for first in range(group, group + VECTORS_PER_GROUP, VECTORS_PER_DOT):
                rows = [
                    jnp.concatenate([a_ref[q, k] for k in range(a_slots)], axis=1)
                    for q in range(first, first + VECTORS_PER_DOT)
                ]
                panel = jnp.dot(
                    jnp.concatenate(rows, axis=0), c_buf[slot], preferred_element_type=jnp.float32
                ).astype(jnp.bfloat16)
                panels += [panel[r * BLK : (r + 1) * BLK] for r in range(VECTORS_PER_DOT)]
            for half in range(2):
                left = [panel[:, half * BLK : (half + 1) * BLK] for panel in panels]
                right = [b_buf[slot, half, group + r] for r in range(VECTORS_PER_GROUP)]
                sums[half] += lax.dot_general(
                    jnp.concatenate(left, axis=1),
                    jnp.concatenate(right, axis=1),
                    (((1,), (1,)), ((), ())),
                    preferred_element_type=jnp.float32,
                )
        for half in range(2):
            u, l = task_of(step, half)
            live = 2 * step + half < count
            factor = jnp.where(live, sign_ref[u, l], 0).astype(jnp.float32)
            lanes = pl.ds(pl.multiple_of((u & 1) * BLK, BLK), BLK)
            acc[u >> 1, :, lanes] += factor * sums[half]
        return carry

    lax.fori_loop(0, steps, body, 0)
    own_ref[...] = acc[chol]
    for shift, piece_ref in enumerate(piece_refs, 1):
        piece_ref[...] = acc[(chol + shift) & 3].astype(piece_ref.dtype)


def contract(place, b_source, b_sign, a_tiles, b_tiles, units):
    vectors, blocks, slots = b_tiles.shape[:3]
    flops = 2 * a_tiles.size * blocks * slots * BLK + 2 * b_tiles.size * BLK
    moved = 2 * (b_tiles.size + a_tiles.size + units[0].size * len(units))
    share = (BLK, blocks * BLK // 4)
    return pl.pallas_call(
        contract_kernel,
        out_shape=[jax.ShapeDtypeStruct(share, jnp.float32)] + [jax.ShapeDtypeStruct(share, jnp.bfloat16)] * 3,
        in_specs=[SMEM, SMEM, SMEM, HBM, HBM] + [HBM] * len(units),
        out_specs=[VMEM] * 4,
        scratch_shapes=[
            pltpu.VMEM((4,) + share, jnp.float32),
            pltpu.SMEM((blocks * slots + 1,), jnp.int32),
            pltpu.VMEM(a_tiles.shape, a_tiles.dtype),
            pltpu.VMEM((2, a_tiles.shape[1] * BLK, 2 * BLK), jnp.bfloat16),
            pltpu.VMEM((2, 2, vectors, BLK, BLK), jnp.bfloat16),
            pltpu.SemaphoreType.DMA,
            pltpu.SemaphoreType.DMA((2, 2)),
            pltpu.SemaphoreType.DMA((2, 2)),
        ],
        compiler_params=pltpu.CompilerParams(vmem_limit_bytes=47 * 1024 * 1024),
        cost_estimate=pl.CostEstimate(flops=flops, bytes_accessed=moved, transcendentals=0),
    )(place, b_source, b_sign, a_tiles, b_tiles, *units)


def gather_sources(place, quarter, a_source, a_sign, alphas):
    zs = alphas // X_SIZE

    def z_from(value, distance):
        return shifted(value, "alpha", alphas, lambda i: (i // X_SIZE - distance) % zs * X_SIZE + i % X_SIZE)

    def x_from(value, distance):
        return shifted(value, "alpha", alphas, lambda i: i // X_SIZE * X_SIZE + (i % X_SIZE - distance) % X_SIZE)

    own = jnp.stack([quarter] + [z_from(quarter, distance) for distance in (1, 2, 3)])
    nxt, prev = x_from(own, 1), x_from(own, 3)
    far_low, far_high = x_from(prev[:2], 3), x_from(nxt[2:], 1)
    slots = a_source.shape[1]
    return pl.pallas_call(
        pick_kernel,
        out_shape=jax.ShapeDtypeStruct((2, slots * BLK, BLK), quarter.dtype),
        in_specs=[SMEM, SMEM, SMEM] + [VMEM] * 5,
        out_specs=VMEM,
        compiler_params=pltpu.CompilerParams(vmem_limit_bytes=8 * 1024 * 1024),
    )(place, a_source, a_sign, own, nxt, prev, far_low, far_high)


def gather_group(unit, betas, chols):
    def y_from(value, distance):
        return shifted(value, "chol", chols, lambda i: (i - distance) % chols)

    def z_other(value):
        return shifted(value, "beta", betas, lambda i: i ^ 2)

    def core_other(value):
        return shifted(value, "beta", betas, lambda i: i ^ 1)

    def onward(i):
        beta, chol = i // chols, i % chols
        return beta * chols + (chol + (1 if beta % 2 == 0 else -1)) % chols

    after, before, across = y_from(unit, 1), y_from(unit, 3), z_other(unit)
    first_core = lax.axis_index("beta") % 2 == 0
    middle = shifted(jnp.where(first_core, before, after), ("beta", "chol"), betas * chols, onward)
    near = [unit, after, middle, before]
    far = [across, y_from(across, 1), z_other(middle), y_from(across, 3)]
    return near + [core_other(v) for v in near] + far + [core_other(v) for v in far]


def per_device(sizes, ci_vector, a_tiles, a_source, a_sign, b_tiles, b_source, b_sign):
    chols = sizes["chol"]
    chol = lax.axis_index("chol")
    place = jnp.stack([lax.axis_index("alpha"), lax.axis_index("beta"), chol]).astype(jnp.int32)
    width = ci_vector.shape[1] // chols
    quarter = lax.dynamic_slice_in_dim(ci_vector, chol * width, width, axis=1)
    unit = gather_sources(place, quarter, a_source, a_sign, sizes["alpha"])
    units = gather_group(unit, sizes["beta"], chols)
    own, *pieces = contract(place, b_source, b_sign, a_tiles[:, 0], b_tiles, units)
    for shift, piece in enumerate(pieces, 1):
        own = own + shifted(piece, "chol", chols, lambda i: (i + shift) % chols).astype(jnp.float32)
    return own.astype(jnp.bfloat16)


def solution(mesh):
    placed = (
        P("alpha", "beta"),
        P("chol", "alpha", None, None, None),
        P("alpha", None),
        P("alpha", None),
        P("chol", "beta", None, None, None),
        P("beta", None),
        P("beta", None),
    )
    sizes = dict(mesh.shape)

    def body(*args):
        return per_device(sizes, *args)

    return jax.shard_map(
        body,
        mesh=mesh,
        in_specs=placed,
        out_specs=P("alpha", ("beta", "chol")),
        check_vma=False,
    )
```

time: 329 us -> 95.7 us (0.29)
  waiting for transfers between devices: 252 us -> 39.5 us
  starting transfers between devices: 0.08 us -> 29.6 us
  matrix products: 26.6 us -> 0 us
  local copies, waits for them, and re-layouts: 31.3 us -> 5.56 us
  Pallas kernels: 0 us -> 19.1 us
  between operations: 13.1 us -> 0.1 us
  other arithmetic: 5.59 us -> 0.82 us
    all_gather x2 -> x0, waiting for transfers between devices: 217 us -> none  [the longest x1 189 us: per_device(): all_rows = lax.all_gather(beta_rows, 'alpha', axis=0, tiled=True)]
    ppermute x0 -> x25, waiting for transfers between devices: none -> 39.5 us  [shifted(): return lax.ppermute(value, axis, [(i, moves_to(i)) for i in range(size)])]
    reduce_scatter x1 -> x0, waiting for transfers between devices: 34.3 us -> none  [per_device(): lax.psum_scatter(partial_sum, 'chol', scatter_dimension=1, tiled=True)]
    ppermute x0 -> x25, starting transfers between devices: none -> 29.6 us  [shifted(): return lax.ppermute(value, axis, [(i, moves_to(i)) for i in range(size)])]
    dot_general x2 -> x0, matrix products: 26.6 us -> none  [the longest x1 16.5 us: build_panel(): jnp.einsum('qkij,kjn->qin', weighted, picked, preferred_element_type=jnp....]
    gather x2 -> x0, local copies, waits for them, and re-layouts: 21.7 us -> none  [the longest x1 11.8 us: per_device(): chosen = jnp.take(column_blocks, b_source, axis=2)]
    pallas_call x0 -> x2, Pallas kernels: none -> 19.1 us  [the longest x1 18.2 us: contract(): pl.pallas_call(contract_kernel, out_shape=[jax.ShapeDtypeStruct(share, jn...]
    reshape x2 -> x0, local copies, waits for them, and re-layouts: 9.32 us -> none  [the longest x1 8.32 us: per_device(): column_blocks = panel.reshape(vectors, block_size, -1, block_size)]
  transfers between devices with their start and end apart: 3 -> 25, of which waited for: 3 -> 12; matrix products, arithmetic and copies ran while one was open for 1% -> 2% of each run, Pallas kernels for 0% -> 0%
where the time goes in v1:
time: 95.7 us; the launch traced here: 94.7 us
  waiting for transfers between devices  39.5 us (41%)
  starting transfers between devices  29.6 us (31%)
  Pallas kernels  19.1 us (20%)
  local copies, waits for them, and re-layouts  5.56 us (6%)
    ppermute x25, waiting for transfers between devices, shifted(): return lax.ppermute(value, axis, [(i, moves_to(i)) for i in range(size)])  39.5 us
    ppermute x25, starting transfers between devices, shifted(): return lax.ppermute(value, axis, [(i, moves_to(i)) for i in range(size)])  29.6 us
    pallas_call x1, Pallas kernels, contract(): pl.pallas_call(contract_kernel, out_shape=[jax.ShapeDtypeStruct(share, jn...  18.2 us
    unnamed x12, local copies, waits for them, and re-layouts  5.52 us
  transfers between devices with their start and end apart: 25, of which 12 were waited for; matrix products, arithmetic and copies ran while one was open for 2% of the time, Pallas kernels for 0%

profile of v1, /device:TPU:6, one launch (start us, length us, event | category | flops | bytes accessed | tf_op | source)
XLA Modules:
  0.0 94.7 jit_solution(10179238198666381932)
XLA Ops:
  0.0 0.9 %copy-done = bf16[128,1024]{1,0:T(8,128)(2,1)S(1)} copy-done((bf16[128,1024]{1,0:T(8,128)(2,1)S(1)}, bf16[128,1024]{1,0:T(8,128)(2,1)}, u32[]{:S(2)}) %copy-start) | copy-done | bytes 262168
  1.0 7.3 %collective-permute-start.1 = (bf16[128,256]{1,0:T(8,128)(2,1)S(1)}, bf16[128,256]{1,0:T(8,128)(2,1)S(1)}, u32[]{:S(2)}, u32[]{:S(2)}) collective-permute-start(bf16[128,256]{1,0:T(8,128)(2,1)S(1)} %constant_dynamic-slice_fusion), channel_id=1, source_target_pairs={{0,128},{16,144},{32,160},{48,176},{64,192},{80,208},{96,224},{112... | collective-permute-start | bytes 196616 | tf_op jit(solution)/shard_map/ppermute | solution.py:18
  8.2 2.9 %collective-permute-start.2 = (bf16[128,256]{1,0:T(8,128)(2,1)S(1)}, bf16[128,256]{1,0:T(8,128)(2,1)S(1)}, u32[]{:S(2)}, u32[]{:S(2)}) collective-permute-start(bf16[128,256]{1,0:T(8,128)(2,1)S(1)} %constant_dynamic-slice_fusion), channel_id=1, source_target_pairs={{0,64},{16,80},{32,96},{48,112},{64,128},{80,144},{96,160},{112,17... | collective-permute-start | bytes 196616 | tf_op jit(solution)/shard_map/ppermute | solution.py:18
  11.2 4.0 %collective-permute-done = bf16[128,256]{1,0:T(8,128)(2,1)S(1)} collective-permute-done((bf16[128,256]{1,0:T(8,128)(2,1)S(1)}, bf16[128,256]{1,0:T(8,128)(2,1)S(1)}, u32[]{:S(2)}, u32[]{:S(2)}) %collective-permute-start) | collective-permute-done | bytes 65568 | tf_op jit(solution)/shard_map/ppermute | solution.py:18
  15.8 1.5 %collective-permute-start.3 = (bf16[4,128,256]{2,1,0:T(8,128)(2,1)S(1)}, bf16[4,128,256]{2,1,0:T(8,128)(2,1)S(1)}, u32[]{:S(2)}, u32[]{:S(2)}) collective-permute-start(bf16[4,128,256]{2,1,0:T(8,128)(2,1)S(1)} %pad_maximum_fusion.own_ref), channel_id=1, source_target_pairs={{0,48},{16,0},{32,16},{48,32},{64,112},{80,64},{96,80},{112,96},{1... | collective-permute-start | bytes 786440 | tf_op jit(solution)/shard_map/ppermute | solution.py:18
  17.3 6.2 %collective-permute-done.4.prev_ref = bf16[4,128,256]{2,1,0:T(8,128)(2,1)S(1)} collective-permute-done((bf16[4,128,256]{2,1,0:T(8,128)(2,1)S(1)}, bf16[4,128,256]{2,1,0:T(8,128)(2,1)S(1)}, u32[]{:S(2)}, u32[]{:S(2)}) %collective-permute-start.4) | collective-permute-done | bytes 262176 | tf_op jit(solution)/shard_map/ppermute | solution.py:18
  23.5 1.8 %collective-permute-start.5 = (bf16[2,128,256]{2,1,0:T(8,128)(2,1)S(1)}, bf16[2,128,256]{2,1,0:T(8,128)(2,1)S(1)}, u32[]{:S(2)}, u32[]{:S(2)}) collective-permute-start(bf16[2,128,256]{2,1,0:T(8,128)(2,1)S(1)} %slice.8), channel_id=1, source_target_pairs={{0,16},{16,32},{32,48},{48,0},{64,80},{80,96},{96,112},{112,64},{1... | collective-permute-start | bytes 393224 | tf_op jit(solution)/shard_map/ppermute | solution.py:18
  25.8 2.8 %collective-permute-done.5.far_low_ref = bf16[2,128,256]{2,1,0:T(8,128)(2,1)S(1)} collective-permute-done((bf16[2,128,256]{2,1,0:T(8,128)(2,1)S(1)}, bf16[2,128,256]{2,1,0:T(8,128)(2,1)S(1)}, u32[]{:S(2)}, u32[]{:S(2)}) %collective-permute-start.5) | collective-permute-done | bytes 131104 | tf_op jit(solution)/shard_map/ppermute | solution.py:18
  28.6 3.0 %collective-permute-done.6.far_high_ref = bf16[2,128,256]{2,1,0:T(8,128)(2,1)S(1)} collective-permute-done((bf16[2,128,256]{2,1,0:T(8,128)(2,1)S(1)}, bf16[2,128,256]{2,1,0:T(8,128)(2,1)S(1)}, u32[]{:S(2)}, u32[]{:S(2)}) %collective-permute-start.6) | collective-permute-done | bytes 131104 | tf_op jit(solution)/shard_map/ppermute | solution.py:18
  31.6 0.7 copy-done.1
  32.2 0.7 copy-done.2
  32.9 0.9 shard_map.73.rest_0_
  33.7 1.7 %collective-permute-start.8 = (bf16[2,768,128]{2,1,0:T(8,128)(2,1)S(1)}, bf16[2,768,128]{2,1,0:T(8,128)(2,1)S(1)}, u32[]{:S(2)}, u32[]{:S(2)}) collective-permute-start(bf16[2,768,128]{2,1,0:T(8,128)(2,1)S(1)} %shard_map.73.rest_0_), channel_id=1, source_target_pairs={{0,1},{1,2},{2,3},{3,0},{4,5},{5,6},{6,7},{7,4},{8,9},{9,10},{10,1... | collective-permute-start | bytes 1179656 | tf_op jit(solution)/shard_map/ppermute | solution.py:18
  35.4 1.7 %collective-permute-start.7 = (bf16[2,768,128]{2,1,0:T(8,128)(2,1)S(1)}, bf16[2,768,128]{2,1,0:T(8,128)(2,1)S(1)}, u32[]{:S(2)}, u32[]{:S(2)}) collective-permute-start(bf16[2,768,128]{2,1,0:T(8,128)(2,1)S(1)} %shard_map.73.rest_0_), channel_id=1, source_target_pairs={{0,3},{1,0},{2,1},{3,2},{4,7},{5,4},{6,5},{7,6},{8,11},{9,8},{10,9... | collective-permute-start | bytes 1179656 | tf_op jit(solution)/shard_map/ppermute | solution.py:18
  37.0 6.8 %collective-permute-done.8.rest_3_ = bf16[2,768,128]{2,1,0:T(8,128)(2,1)S(1)} collective-permute-done((bf16[2,768,128]{2,1,0:T(8,128)(2,1)S(1)}, bf16[2,768,128]{2,1,0:T(8,128)(2,1)S(1)}, u32[]{:S(2)}, u32[]{:S(2)}) %collective-permute-start.8) | collective-permute-done | bytes 393248 | tf_op jit(solution)/shard_map/ppermute | solution.py:18
  44.3 2.0 %collective-permute-start.9 = (bf16[2,768,128]{2,1,0:T(8,128)(2,1)S(1)}, bf16[2,768,128]{2,1,0:T(8,128)(2,1)S(1)}, u32[]{:S(2)}, u32[]{:S(2)}) collective-permute-start(bf16[2,768,128]{2,1,0:T(8,128)(2,1)S(1)} %broadcast_select_fusion), channel_id=1, source_target_pairs={{0,1},{1,2},{2,3},{3,0},{4,7},{5,4},{6,5},{7,6},{8,9},{9,10},{10,1... | collective-permute-start | bytes 1179656 | tf_op jit(solution)/shard_map/ppermute | solution.py:18
  46.2 1.3 %collective-permute-start.17 = (bf16[2,768,128]{2,1,0:T(8,128)(2,1)S(1)}, bf16[2,768,128]{2,1,0:T(8,128)(2,1)}, u32[]{:S(2)}, u32[]{:S(2)}) collective-permute-start(bf16[2,768,128]{2,1,0:T(8,128)(2,1)S(1)} %collective-permute-done.14.rest_8_), channel_id=1, source_target_pairs={{0,1},{1,2},{2,3},{3,0},{4,5},{5,6},{6,7},{7,4},{8,9},{9,10},{10,1... | collective-permute-start | bytes 1179656 | tf_op jit(solution)/shard_map/ppermute | solution.py:18
  47.5 2.0 %collective-permute-start.15 = (bf16[2,768,128]{2,1,0:T(8,128)(2,1)S(1)}, bf16[2,768,128]{2,1,0:T(8,128)(2,1)}, u32[]{:S(2)}, u32[]{:S(2)}) collective-permute-start(bf16[2,768,128]{2,1,0:T(8,128)(2,1)S(1)} %collective-permute-done.14.rest_8_), channel_id=1, source_target_pairs={{0,3},{1,0},{2,1},{3,2},{4,7},{5,4},{6,5},{7,6},{8,11},{9,8},{10,9... | collective-permute-start | bytes 1179656 | tf_op jit(solution)/shard_map/ppermute | solution.py:18
  49.5 6.5 %collective-permute-done.9.rest_2_ = bf16[2,768,128]{2,1,0:T(8,128)(2,1)S(1)} collective-permute-done((bf16[2,768,128]{2,1,0:T(8,128)(2,1)S(1)}, bf16[2,768,128]{2,1,0:T(8,128)(2,1)S(1)}, u32[]{:S(2)}, u32[]{:S(2)}) %collective-permute-start.9) | collective-permute-done | bytes 393248 | tf_op jit(solution)/shard_map/ppermute | solution.py:18
  56.0 5.8 %collective-permute-done.17.rest_11_ = bf16[2,768,128]{2,1,0:T(8,128)(2,1)} collective-permute-done((bf16[2,768,128]{2,1,0:T(8,128)(2,1)S(1)}, bf16[2,768,128]{2,1,0:T(8,128)(2,1)}, u32[]{:S(2)}, u32[]{:S(2)}) %collective-permute-start.17) | collective-permute-done | bytes 393248 | tf_op jit(solution)/shard_map/ppermute | solution.py:18
  62.4 0.8 copy-done.3
  63.1 0.8 collective-permute-done.16.rest_10_
  63.9 0.8 copy.8.source_ref
  64.7 0.8 copy.9.sign_ref
  66.0 1.0 %copy-done.4 = bf16[2,768,128]{2,1,0:T(8,128)(2,1)S(1)} copy-done((bf16[2,768,128]{2,1,0:T(8,128)(2,1)S(1)}, bf16[2,768,128]{2,1,0:T(8,128)(2,1)}, u32[]{:S(2)}) %copy-start.4) | copy-done | bytes 393240
  67.0 18.2 %shard_map.74 = (f32[128,256]{1,0:T(8,128)S(1)}, bf16[128,256]{1,0:T(8,128)(2,1)S(1)}, bf16[128,256]{1,0:T(8,128)(2,1)S(1)}, bf16[128,256]{1,0:T(8,128)(2,1)S(1)}) custom-call(s32[3]{0:T(128)S(1)} %pad_add_fusion.place_ref, s32[8,3]{1,0:T(8,128)S(1)} %copy.8.source_ref, s32[8,3]{1,0:T(8,128)S(1)} %copy.9.sign_ref, bf16[16,6,128,128]{3,2,1,0:T(8,128)(2,1)} %bitcast.12, ...), custom_call_target="tpu_custom_call" | custom-call | flops 11274289152 | bytes 22020096 | tf_op jit(solution)/shard_map/pallas_call | solution.py:163
  85.2 1.4 %collective-permute-start.22 = (bf16[128,256]{1,0:T(8,128)(2,1)S(1)}, bf16[128,256]{1,0:T(8,128)(2,1)S(1)}, u32[]{:S(2)}, u32[]{:S(2)}) collective-permute-start(bf16[128,256]{1,0:T(8,128)(2,1)S(1)} %get-tuple-element.10), channel_id=1, source_target_pairs={{0,1},{1,2},{2,3},{3,0},{4,5},{5,6},{6,7},{7,4},{8,9},{9,10},{10,1... | collective-permute-start | bytes 196616 | tf_op jit(solution)/shard_map/ppermute | solution.py:18
  86.6 3.1 %collective-permute-start.23 = (bf16[128,256]{1,0:T(8,128)(2,1)S(1)}, bf16[128,256]{1,0:T(8,128)(2,1)S(1)}, u32[]{:S(2)}, u32[]{:S(2)}) collective-permute-start(bf16[128,256]{1,0:T(8,128)(2,1)S(1)} %get-tuple-element.11), channel_id=1, source_target_pairs={{0,2},{1,3},{2,0},{3,1},{4,6},{5,7},{6,4},{7,5},{8,10},{9,11},{10,... | collective-permute-start | bytes 196616 | tf_op jit(solution)/shard_map/ppermute | solution.py:18
  89.7 1.5 %collective-permute-start.24 = (bf16[128,256]{1,0:T(8,128)(2,1)S(1)}, bf16[128,256]{1,0:T(8,128)(2,1)S(1)}, u32[]{:S(2)}, u32[]{:S(2)}) collective-permute-start(bf16[128,256]{1,0:T(8,128)(2,1)S(1)} %get-tuple-element.12), channel_id=1, source_target_pairs={{0,3},{1,0},{2,1},{3,2},{4,7},{5,4},{6,5},{7,6},{8,11},{9,8},{10,9... | collective-permute-start | bytes 196616 | tf_op jit(solution)/shard_map/ppermute | solution.py:18
  91.2 1.4 %collective-permute-done.23 = bf16[128,256]{1,0:T(8,128)(2,1)S(1)} collective-permute-done((bf16[128,256]{1,0:T(8,128)(2,1)S(1)}, bf16[128,256]{1,0:T(8,128)(2,1)S(1)}, u32[]{:S(2)}, u32[]{:S(2)}) %collective-permute-start.23) | collective-permute-done | bytes 65568 | tf_op jit(solution)/shard_map/ppermute | solution.py:18
  92.7 1.3 %collective-permute-done.24 = bf16[128,256]{1,0:T(8,128)(2,1)S(1)} collective-permute-done((bf16[128,256]{1,0:T(8,128)(2,1)S(1)}, bf16[128,256]{1,0:T(8,128)(2,1)S(1)}, u32[]{:S(2)}, u32[]{:S(2)}) %collective-permute-start.24) | collective-permute-done | bytes 65568 | tf_op jit(solution)/shard_map/ppermute | solution.py:18
  94.0 0.7 add_convert_fusion
  (40 shorter events, 2.6 us)
Async XLA Ops:
  0.0 1.0 %copy-start = (bf16[128,1024]{1,0:T(8,128)(2,1)S(1)}, bf16[128,1024]{1,0:T(8,128)(2,1)}, u32[]{:S(2)}) copy-start(bf16[128,1024]{1,0:T(8,128)(2,1)} %param.7) | copy-start | bytes 786436
  1.0 10.2 %collective-permute-start.1 = (bf16[128,256]{1,0:T(8,128)(2,1)S(1)}, bf16[128,256]{1,0:T(8,128)(2,1)S(1)}, u32[]{:S(2)}, u32[]{:S(2)}) collective-permute-start(bf16[128,256]{1,0:T(8,128)(2,1)S(1)} %constant_dynamic-slice_fusion), channel_id=1, source_target_pairs={{0,128},{16,144},{32,160},{48,176},{64,192},{80,208},{96,224},{112... | collective-permute-start | bytes 196616 | tf_op jit(solution)/shard_map/ppermute | solution.py:18
  8.2 6.9 %collective-permute-start = (bf16[128,256]{1,0:T(8,128)(2,1)S(1)}, bf16[128,256]{1,0:T(8,128)(2,1)S(1)}, u32[]{:S(2)}, u32[]{:S(2)}) collective-permute-start(bf16[128,256]{1,0:T(8,128)(2,1)S(1)} %constant_dynamic-slice_fusion), channel_id=1, source_target_pairs={{0,192},{16,208},{32,224},{48,240},{64,0},{80,16},{96,32},{112,48}... | collective-permute-start | bytes 196616 | tf_op jit(solution)/shard_map/ppermute | solution.py:18
  8.2 6.9 %collective-permute-start.2 = (bf16[128,256]{1,0:T(8,128)(2,1)S(1)}, bf16[128,256]{1,0:T(8,128)(2,1)S(1)}, u32[]{:S(2)}, u32[]{:S(2)}) collective-permute-start(bf16[128,256]{1,0:T(8,128)(2,1)S(1)} %constant_dynamic-slice_fusion), channel_id=1, source_target_pairs={{0,64},{16,80},{32,96},{48,112},{64,128},{80,144},{96,160},{112,17... | collective-permute-start | bytes 196616 | tf_op jit(solution)/shard_map/ppermute | solution.py:18
  15.2 8.3 %collective-permute-start.4 = (bf16[4,128,256]{2,1,0:T(8,128)(2,1)S(1)}, bf16[4,128,256]{2,1,0:T(8,128)(2,1)S(1)}, u32[]{:S(2)}, u32[]{:S(2)}) collective-permute-start(bf16[4,128,256]{2,1,0:T(8,128)(2,1)S(1)} %pad_maximum_fusion.own_ref), channel_id=1, source_target_pairs={{0,16},{16,32},{32,48},{48,0},{64,80},{80,96},{96,112},{112,64},{1... | collective-permute-start | bytes 786440 | tf_op jit(solution)/shard_map/ppermute | solution.py:18
  15.8 9.5 %collective-permute-start.3 = (bf16[4,128,256]{2,1,0:T(8,128)(2,1)S(1)}, bf16[4,128,256]{2,1,0:T(8,128)(2,1)S(1)}, u32[]{:S(2)}, u32[]{:S(2)}) collective-permute-start(bf16[4,128,256]{2,1,0:T(8,128)(2,1)S(1)} %pad_maximum_fusion.own_ref), channel_id=1, source_target_pairs={{0,48},{16,0},{32,16},{48,32},{64,112},{80,64},{96,80},{112,96},{1... | collective-permute-start | bytes 786440 | tf_op jit(solution)/shard_map/ppermute | solution.py:18
  23.5 5.0 %collective-permute-start.5 = (bf16[2,128,256]{2,1,0:T(8,128)(2,1)S(1)}, bf16[2,128,256]{2,1,0:T(8,128)(2,1)S(1)}, u32[]{:S(2)}, u32[]{:S(2)}) collective-permute-start(bf16[2,128,256]{2,1,0:T(8,128)(2,1)S(1)} %slice.8), channel_id=1, source_target_pairs={{0,16},{16,32},{32,48},{48,0},{64,80},{80,96},{96,112},{112,64},{1... | collective-permute-start | bytes 393224 | tf_op jit(solution)/shard_map/ppermute | solution.py:18
  25.3 6.3 %collective-permute-start.6 = (bf16[2,128,256]{2,1,0:T(8,128)(2,1)S(1)}, bf16[2,128,256]{2,1,0:T(8,128)(2,1)S(1)}, u32[]{:S(2)}, u32[]{:S(2)}) collective-permute-start(bf16[2,128,256]{2,1,0:T(8,128)(2,1)S(1)} %slice.9), channel_id=1, source_target_pairs={{0,48},{16,0},{32,16},{48,32},{64,112},{80,64},{96,80},{112,96},{1... | collective-permute-start | bytes 393224 | tf_op jit(solution)/shard_map/ppermute | solution.py:18
  31.6 0.7 copy-start.1
  32.2 0.7 copy-start.2
  33.7 10.1 %collective-permute-start.8 = (bf16[2,768,128]{2,1,0:T(8,128)(2,1)S(1)}, bf16[2,768,128]{2,1,0:T(8,128)(2,1)S(1)}, u32[]{:S(2)}, u32[]{:S(2)}) collective-permute-start(bf16[2,768,128]{2,1,0:T(8,128)(2,1)S(1)} %shard_map.73.rest_0_), channel_id=1, source_target_pairs={{0,1},{1,2},{2,3},{3,0},{4,5},{5,6},{6,7},{7,4},{8,9},{9,10},{10,1... | collective-permute-start | bytes 1179656 | tf_op jit(solution)/shard_map/ppermute | solution.py:18
  35.4 8.8 %collective-permute-start.7 = (bf16[2,768,128]{2,1,0:T(8,128)(2,1)S(1)}, bf16[2,768,128]{2,1,0:T(8,128)(2,1)S(1)}, u32[]{:S(2)}, u32[]{:S(2)}) collective-permute-start(bf16[2,768,128]{2,1,0:T(8,128)(2,1)S(1)} %shard_map.73.rest_0_), channel_id=1, source_target_pairs={{0,3},{1,0},{2,1},{3,2},{4,7},{5,4},{6,5},{7,6},{8,11},{9,8},{10,9... | collective-permute-start | bytes 1179656 | tf_op jit(solution)/shard_map/ppermute | solution.py:18
  37.0 9.2 %collective-permute-start.14 = (bf16[2,768,128]{2,1,0:T(8,128)(2,1)S(1)}, bf16[2,768,128]{2,1,0:T(8,128)(2,1)S(1)}, u32[]{:S(2)}, u32[]{:S(2)}) collective-permute-start(bf16[2,768,128]{2,1,0:T(8,128)(2,1)S(1)} %shard_map.73.rest_0_), channel_id=1, source_target_pairs={{0,8},{4,12},{8,0},{12,4},{1,9},{5,13},{9,1},{13,5},{2,10},{6,14},... | collective-permute-start | bytes 1179656 | tf_op jit(solution)/shard_map/ppermute | solution.py:18
  37.0 12.4 %collective-permute-start.10 = (bf16[2,768,128]{2,1,0:T(8,128)(2,1)S(1)}, bf16[2,768,128]{2,1,0:T(8,128)(2,1)S(1)}, u32[]{:S(2)}, u32[]{:S(2)}) collective-permute-start(bf16[2,768,128]{2,1,0:T(8,128)(2,1)S(1)} %shard_map.73.rest_0_), channel_id=1, source_target_pairs={{0,4},{4,0},{8,12},{12,8},{1,5},{5,1},{9,13},{13,9},{2,6},{6,2},{1... | collective-permute-start | bytes 1179656 | tf_op jit(solution)/shard_map/ppermute | solution.py:18
  44.3 11.8 %collective-permute-start.9 = (bf16[2,768,128]{2,1,0:T(8,128)(2,1)S(1)}, bf16[2,768,128]{2,1,0:T(8,128)(2,1)S(1)}, u32[]{:S(2)}, u32[]{:S(2)}) collective-permute-start(bf16[2,768,128]{2,1,0:T(8,128)(2,1)S(1)} %broadcast_select_fusion), channel_id=1, source_target_pairs={{0,1},{1,2},{2,3},{3,0},{4,7},{5,4},{6,5},{7,6},{8,9},{9,10},{10,1... | collective-permute-start | bytes 1179656 | tf_op jit(solution)/shard_map/ppermute | solution.py:18
  46.2 9.8 %collective-permute-start.18 = (bf16[2,768,128]{2,1,0:T(8,128)(2,1)S(1)}, bf16[2,768,128]{2,1,0:T(8,128)(2,1)S(1)}, u32[]{:S(2)}, u32[]{:S(2)}) collective-permute-start(bf16[2,768,128]{2,1,0:T(8,128)(2,1)S(1)} %collective-permute-done.14.rest_8_), channel_id=1, source_target_pairs={{0,4},{4,0},{8,12},{12,8},{1,5},{5,1},{9,13},{13,9},{2,6},{6,2},{1... | collective-permute-start | bytes 1179656 | tf_op jit(solution)/shard_map/ppermute | solution.py:18
  46.2 15.6 %collective-permute-start.17 = (bf16[2,768,128]{2,1,0:T(8,128)(2,1)S(1)}, bf16[2,768,128]{2,1,0:T(8,128)(2,1)}, u32[]{:S(2)}, u32[]{:S(2)}) collective-permute-start(bf16[2,768,128]{2,1,0:T(8,128)(2,1)S(1)} %collective-permute-done.14.rest_8_), channel_id=1, source_target_pairs={{0,1},{1,2},{2,3},{3,0},{4,5},{5,6},{6,7},{7,4},{8,9},{9,10},{10,1... | collective-permute-start | bytes 1179656 | tf_op jit(solution)/shard_map/ppermute | solution.py:18
  47.5 14.3 %collective-permute-start.15 = (bf16[2,768,128]{2,1,0:T(8,128)(2,1)S(1)}, bf16[2,768,128]{2,1,0:T(8,128)(2,1)}, u32[]{:S(2)}, u32[]{:S(2)}) collective-permute-start(bf16[2,768,128]{2,1,0:T(8,128)(2,1)S(1)} %collective-permute-done.14.rest_8_), channel_id=1, source_target_pairs={{0,3},{1,0},{2,1},{3,2},{4,7},{5,4},{6,5},{7,6},{8,11},{9,8},{10,9... | collective-permute-start | bytes 1179656 | tf_op jit(solution)/shard_map/ppermute | solution.py:18
  49.5 12.9 %collective-permute-start.13 = (bf16[2,768,128]{2,1,0:T(8,128)(2,1)S(1)}, bf16[2,768,128]{2,1,0:T(8,128)(2,1)S(1)}, u32[]{:S(2)}, u32[]{:S(2)}) collective-permute-start(bf16[2,768,128]{2,1,0:T(8,128)(2,1)S(1)} %collective-permute-done.8.rest_3_), channel_id=1, source_target_pairs={{0,4},{4,0},{8,12},{12,8},{1,5},{5,1},{9,13},{13,9},{2,6},{6,2},{1... | collective-permute-start | bytes 1179656 | tf_op jit(solution)/shard_map/ppermute | solution.py:18
  56.0 7.9 %collective-permute-start.16 = (bf16[2,768,128]{2,1,0:T(8,128)(2,1)S(1)}, bf16[2,768,128]{2,1,0:T(8,128)(2,1)}, u32[]{:S(2)}, u32[]{:S(2)}) collective-permute-start(bf16[2,768,128]{2,1,0:T(8,128)(2,1)S(1)} %collective-permute-done.9.rest_2_), channel_id=1, source_target_pairs={{0,8},{4,12},{8,0},{12,4},{1,9},{5,13},{9,1},{13,5},{2,10},{6,14},... | collective-permute-start | bytes 1179656 | tf_op jit(solution)/shard_map/ppermute | solution.py:18
  56.0 9.4 %collective-permute-start.11 = (bf16[2,768,128]{2,1,0:T(8,128)(2,1)S(1)}, bf16[2,768,128]{2,1,0:T(8,128)(2,1)}, u32[]{:S(2)}, u32[]{:S(2)}) collective-permute-start(bf16[2,768,128]{2,1,0:T(8,128)(2,1)S(1)} %collective-permute-done.7.rest_1_), channel_id=1, source_target_pairs={{0,4},{4,0},{8,12},{12,8},{1,5},{5,1},{9,13},{13,9},{2,6},{6,2},{1... | collective-permute-start | bytes 1179656 | tf_op jit(solution)/shard_map/ppermute | solution.py:18
  61.9 3.6 %collective-permute-start.12 = (bf16[2,768,128]{2,1,0:T(8,128)(2,1)S(1)}, bf16[2,768,128]{2,1,0:T(8,128)(2,1)}, u32[]{:S(2)}, u32[]{:S(2)}) collective-permute-start(bf16[2,768,128]{2,1,0:T(8,128)(2,1)S(1)} %collective-permute-done.9.rest_2_), channel_id=1, source_target_pairs={{0,4},{4,0},{8,12},{12,8},{1,5},{5,1},{9,13},{13,9},{2,6},{6,2},{1... | collective-permute-start | bytes 1179656 | tf_op jit(solution)/shard_map/ppermute | solution.py:18
  61.9 3.6 %collective-permute-start.21 = (bf16[2,768,128]{2,1,0:T(8,128)(2,1)}, bf16[2,768,128]{2,1,0:T(8,128)(2,1)}, u32[]{:S(2)}, u32[]{:S(2)}) collective-permute-start(bf16[2,768,128]{2,1,0:T(8,128)(2,1)} %collective-permute-done.17.rest_11_), channel_id=1, source_target_pairs={{0,4},{4,0},{8,12},{12,8},{1,5},{5,1},{9,13},{13,9},{2,6},{6,2},{1... | collective-permute-start | bytes 1179656 | tf_op jit(solution)/shard_map/ppermute | solution.py:18
  62.4 0.8 copy-start.3
  63.1 2.3 %collective-permute-start.19 = (bf16[2,768,128]{2,1,0:T(8,128)(2,1)}, bf16[2,768,128]{2,1,0:T(8,128)(2,1)}, u32[]{:S(2)}, u32[]{:S(2)}) collective-permute-start(bf16[2,768,128]{2,1,0:T(8,128)(2,1)} %collective-permute-done.15.rest_9_), channel_id=1, source_target_pairs={{0,4},{4,0},{8,12},{12,8},{1,5},{5,1},{9,13},{13,9},{2,6},{6,2},{1... | collective-permute-start | bytes 1179656 | tf_op jit(solution)/shard_map/ppermute | solution.py:18
  63.9 2.1 %collective-permute-start.20 = (bf16[2,768,128]{2,1,0:T(8,128)(2,1)}, bf16[2,768,128]{2,1,0:T(8,128)(2,1)}, u32[]{:S(2)}, u32[]{:S(2)}) collective-permute-start(bf16[2,768,128]{2,1,0:T(8,128)(2,1)} %collective-permute-done.16.rest_10_), channel_id=1, source_target_pairs={{0,4},{4,0},{8,12},{12,8},{1,5},{5,1},{9,13},{13,9},{2,6},{6,2},{1... | collective-permute-start | bytes 1179656 | tf_op jit(solution)/shard_map/ppermute | solution.py:18
  66.0 1.0 %copy-start.4 = (bf16[2,768,128]{2,1,0:T(8,128)(2,1)S(1)}, bf16[2,768,128]{2,1,0:T(8,128)(2,1)}, u32[]{:S(2)}) copy-start(bf16[2,768,128]{2,1,0:T(8,128)(2,1)} %copy-done.3) | copy-start | bytes 1179652
  85.2 6.0 %collective-permute-start.22 = (bf16[128,256]{1,0:T(8,128)(2,1)S(1)}, bf16[128,256]{1,0:T(8,128)(2,1)S(1)}, u32[]{:S(2)}, u32[]{:S(2)}) collective-permute-start(bf16[128,256]{1,0:T(8,128)(2,1)S(1)} %get-tuple-element.10), channel_id=1, source_target_pairs={{0,1},{1,2},{2,3},{3,0},{4,5},{5,6},{6,7},{7,4},{8,9},{9,10},{10,1... | collective-permute-start | bytes 196616 | tf_op jit(solution)/shard_map/ppermute | solution.py:18
  86.6 6.1 %collective-permute-start.23 = (bf16[128,256]{1,0:T(8,128)(2,1)S(1)}, bf16[128,256]{1,0:T(8,128)(2,1)S(1)}, u32[]{:S(2)}, u32[]{:S(2)}) collective-permute-start(bf16[128,256]{1,0:T(8,128)(2,1)S(1)} %get-tuple-element.11), channel_id=1, source_target_pairs={{0,2},{1,3},{2,0},{3,1},{4,6},{5,7},{6,4},{7,5},{8,10},{9,11},{10,... | collective-permute-start | bytes 196616 | tf_op jit(solution)/shard_map/ppermute | solution.py:18
  89.7 4.3 %collective-permute-start.24 = (bf16[128,256]{1,0:T(8,128)(2,1)S(1)}, bf16[128,256]{1,0:T(8,128)(2,1)S(1)}, u32[]{:S(2)}, u32[]{:S(2)}) collective-permute-start(bf16[128,256]{1,0:T(8,128)(2,1)S(1)} %get-tuple-element.12), channel_id=1, source_target_pairs={{0,3},{1,0},{2,1},{3,2},{4,7},{5,4},{6,5},{7,6},{8,11},{9,8},{10,9... | collective-permute-start | bytes 196616 | tf_op jit(solution)/shard_map/ppermute | solution.py:18

commit v2 on v1

v2 whole, which is shorter than its diff:
```python
import functools

import jax
import jax.numpy as jnp
from jax import lax
from jax.experimental import pallas as pl
from jax.experimental.pallas import tpu as pltpu
from jax.sharding import PartitionSpec as P

BLK = 128
VECTORS_PER_DOT = 2
VECTORS_PER_GROUP = 4
X_SIZE = 4
A_SLOTS, B_SLOTS, B_BLOCKS = 6, 3, 8
ALPHA, BETA, CHOL, A_SOURCE = 0, 1, 2, 3
A_SIGN = A_SOURCE + A_SLOTS
B_SOURCE = A_SIGN + A_SLOTS
B_SIGN = B_SOURCE + B_SLOTS * B_BLOCKS
ARRIVAL = 0x67532410
SMEM = pl.BlockSpec(memory_space=pltpu.SMEM)
VMEM = pl.BlockSpec(memory_space=pltpu.VMEM)
HBM = pl.BlockSpec(memory_space=pltpu.HBM)


def shifted(value, axis, size, moves_to):
    return lax.ppermute(value, axis, [(i, moves_to(i)) for i in range(size)])


def choose(index, low, high, act):
    if high - low == 1:
        act(low)
        return
    middle = (low + high) // 2

    @pl.when(index < middle)
    def _():
        choose(index, low, middle, act)

    @pl.when(index >= middle)
    def _():
        choose(index, middle, high, act)


def pick_kernel(meta_ref, *refs):
    stacks, out_ref = refs[:X_SIZE], refs[X_SIZE]
    alpha = meta_ref[ALPHA]
    for k in range(A_SLOTS):
        source = meta_ref[A_SOURCE + k]
        sign = meta_ref[A_SIGN + k].astype(jnp.float32).astype(out_ref.dtype)
        dz = ((source >> 2) - (alpha >> 2)) & 3
        dx = (source - alpha) & 3

        def put(i, k=k, sign=sign, dz=dz):
            for half in range(2):
                block = stacks[i][dz, :, half * BLK : (half + 1) * BLK]
                out_ref[half, k * BLK : (k + 1) * BLK, :] = block * sign

        choose(dx, 0, X_SIZE, put)


def contract_kernel(first_unit, count_units, has_sum, last, meta_ref, a_ref, b_ref, *rest):
    units, rest = rest[:count_units], rest[count_units:]
    if has_sum:
        sum_ref, rest = rest[0], rest[1:]
    if last:
        own_ref, *piece_refs = rest[:4]
        acc, rest = rest[4], rest[5:]
    else:
        acc, rest = rest[0], rest[1:]
    tasks, places, c_buf, b_buf, c_sem, b_sem = rest
    pairs = B_BLOCKS * B_SLOTS
    vectors = a_ref.shape[0]
    beta, chol = meta_ref[BETA], meta_ref[CHOL]
    acc[...] = sum_ref[...] if has_sum else jnp.zeros_like(acc)

    count = jnp.int32(0)
    for pair in range(pairs):
        m = meta_ref[B_SOURCE + pair]
        owner = m >> 3
        crossed = owner ^ beta
        dy = ((m >> 1) - chol) & 3
        dy = jnp.where((crossed & 2) * (owner & 1) != 0, (4 - dy) & 3, dy)
        code = (crossed & 2) * 2 + dy
        place = ((jnp.int32(ARRIVAL) >> (4 * code)) & 7) * 2 + (crossed & 1) - first_unit
        tasks[count] = pair
        places[count] = place
        here = (meta_ref[B_SIGN + pair] != 0) & (place >= 0) & (place < count_units)
        count = count + jnp.where(here, 1, 0)
    steps = (count + 1) >> 1

    def index_of(step, half):
        return jnp.minimum(2 * step + half, count - 1)

    def c_copy(unit, m, slot, half):
        return pltpu.make_async_copy(
            unit.at[m & 1], c_buf.at[slot, :, pl.ds(half * BLK, BLK)], c_sem.at[slot, half]
        )

    def b_copy(u, l, slot, half):
        return pltpu.make_async_copy(b_ref.at[:, u, l], b_buf.at[slot, half], b_sem.at[slot, half])

    def start(step, slot):
        for half in range(2):
            at = index_of(step, half)
            pair = tasks[at]
            m = meta_ref[B_SOURCE + pair]
            choose(places[at], 0, count_units, lambda i: c_copy(units[i], m, slot, half).start())
            u = pair // B_SLOTS
            b_copy(u, pair - u * B_SLOTS, slot, half).start()

    @pl.when(steps > 0)
    def _():
        start(0, 0)

    def body(step, carry):
        slot = step & 1

        @pl.when(step + 1 < steps)
        def _():
            start(step + 1, 1 - slot)

        for half in range(2):
            c_copy(units[0], 0, slot, half).wait()
            b_copy(0, 0, slot, half).wait()
        sums = [jnp.zeros((BLK, BLK), jnp.float32) for _ in range(2)]
        for group in range(0, vectors, VECTORS_PER_GROUP):
            panels = []
            for first in range(group, group + VECTORS_PER_GROUP, VECTORS_PER_DOT):
                rows = [
                    jnp.concatenate([a_ref[q, k] for k in range(A_SLOTS)], axis=1)
                    for q in range(first, first + VECTORS_PER_DOT)
                ]
                panel = jnp.dot(
                    jnp.concatenate(rows, axis=0), c_buf[slot], preferred_element_type=jnp.float32
                ).astype(jnp.bfloat16)
                panels += [panel[r * BLK : (r + 1) * BLK] for r in range(VECTORS_PER_DOT)]
            for half in range(2):
                left = [panel[:, half * BLK : (half + 1) * BLK] for panel in panels]
                right = [b_buf[slot, half, group + r] for r in range(VECTORS_PER_GROUP)]
                sums[half] += lax.dot_general(
                    jnp.concatenate(left, axis=1),
                    jnp.concatenate(right, axis=1),
                    (((1,), (1,)), ((), ())),
                    preferred_element_type=jnp.float32,
                )
        for half in range(2):
            pair = tasks[index_of(step, half)]
            live = 2 * step + half < count
            factor = jnp.where(live, meta_ref[B_SIGN + pair], 0).astype(jnp.float32)
            u = pair // B_SLOTS
            lanes = pl.ds(pl.multiple_of((u & 1) * BLK, BLK), BLK)
            acc[u >> 1, :, lanes] += factor * sums[half]
        return carry

    lax.fori_loop(0, steps, body, 0)
    if last:
        own_ref[...] = acc[chol]
        for shift, piece_ref in enumerate(piece_refs, 1):
            piece_ref[...] = acc[(chol + shift) & 3].astype(piece_ref.dtype)


def contract(meta, a_tiles, b_tiles, units, first_unit, running=None, last=False):
    vectors, blocks = b_tiles.shape[:2]
    part = len(units) / 16
    flops = int(part * 2 * (a_tiles.size * blocks * B_SLOTS * BLK + b_tiles.size * BLK))
    moved = int(part * 2 * b_tiles.size) + 2 * a_tiles.size
    share = (BLK, blocks * BLK // 4)
    whole = jax.ShapeDtypeStruct((4,) + share, jnp.float32)
    shares = [jax.ShapeDtypeStruct(share, jnp.float32)] + [jax.ShapeDtypeStruct(share, jnp.bfloat16)] * 3
    sums = [] if running is None else [running]
    return pl.pallas_call(
        functools.partial(contract_kernel, first_unit, len(units), bool(sums), last),
        out_shape=shares if last else whole,
        in_specs=[SMEM, VMEM, HBM] + [HBM] * len(units) + [VMEM] * len(sums),
        out_specs=[VMEM] * 4 if last else VMEM,
        scratch_shapes=[pltpu.VMEM(whole.shape, jnp.float32)] * last
        + [
            pltpu.SMEM((blocks * B_SLOTS + 1,), jnp.int32),
            pltpu.SMEM((blocks * B_SLOTS + 1,), jnp.int32),
            pltpu.VMEM((2, A_SLOTS * BLK, 2 * BLK), jnp.bfloat16),
            pltpu.VMEM((2, 2, vectors, BLK, BLK), jnp.bfloat16),
            pltpu.SemaphoreType.DMA((2, 2)),
            pltpu.SemaphoreType.DMA((2, 2)),
        ],
        compiler_params=pltpu.CompilerParams(vmem_limit_bytes=47 * 1024 * 1024),
        cost_estimate=pl.CostEstimate(flops=flops, bytes_accessed=moved, transcendentals=0),
    )(meta, a_tiles, b_tiles, *units, *sums)


def gather_sources(meta, quarter, sizes):
    alphas, betas = sizes["alpha"], sizes["beta"]
    zs = alphas // X_SIZE

    def x_moved(i, distance):
        return i // X_SIZE * X_SIZE + (i + distance) % X_SIZE

    def z_from(value, distance):
        return shifted(value, "alpha", alphas, lambda i: (i // X_SIZE - distance) % zs * X_SIZE + i % X_SIZE)

    def x_from(value, distance):
        return shifted(value, "alpha", alphas, lambda i: x_moved(i, -distance))

    def onward(i):
        alpha, beta = i // betas, i % betas
        return x_moved(alpha, 1 if beta % 2 == 0 else -1) * betas + beta

    own = jnp.stack([quarter] + [z_from(quarter, distance) for distance in (1, 2, 3)])
    own, meta = lax.optimization_barrier((own, meta))
    after, before = x_from(own, 1), x_from(own, 3)
    first_core = lax.axis_index("beta") % 2 == 0
    far = shifted(jnp.where(first_core, before, after), ("alpha", "beta"), alphas * betas, onward)
    unit = pl.pallas_call(
        pick_kernel,
        out_shape=jax.ShapeDtypeStruct((2, A_SLOTS * BLK, BLK), quarter.dtype),
        in_specs=[SMEM] + [VMEM] * X_SIZE,
        out_specs=VMEM,
        compiler_params=pltpu.CompilerParams(vmem_limit_bytes=8 * 1024 * 1024),
    )(meta, own, after, far, before)
    return meta, unit


def gather_and_contract(meta, unit, a_tiles, b_tiles, sizes):
    betas, chols = sizes["beta"], sizes["chol"]

    def y_from(value, distance):
        return shifted(value, "chol", chols, lambda i: (i - distance) % chols)

    def z_other(value):
        return shifted(value, "beta", betas, lambda i: i ^ 2)

    def both(values):
        return [v for value in values for v in (value, shifted(value, "beta", betas, lambda i: i ^ 1))]

    def by_core(value, sense):
        def moved(i):
            beta, chol = i // chols, i % chols
            return beta * chols + (chol + (sense if beta % 2 == 0 else -sense)) % chols

        return shifted(value, ("beta", "chol"), betas * chols, moved)

    after, before, across = y_from(unit, 1), y_from(unit, 3), z_other(unit)
    onward = jnp.where(lax.axis_index("beta") % 2 == 0, before, after)
    middle, far_onward, far_back = by_core(onward, 1), z_other(onward), by_core(across, -1)
    first = both([unit, after, before, across])
    running = contract(meta, a_tiles, b_tiles, first, 0)
    running, middle, far_back, far_onward = lax.optimization_barrier((running, middle, far_back, far_onward))
    far_middle = by_core(far_onward, 1)
    second = both([middle, far_back, far_onward])
    running = contract(meta, a_tiles, b_tiles, second, 8, running)
    running, far_middle = lax.optimization_barrier((running, far_middle))
    return contract(meta, a_tiles, b_tiles, both([far_middle]), 14, running, last=True)


def per_device(sizes, ci_vector, a_tiles, a_source, a_sign, b_tiles, b_source, b_sign):
    chols = sizes["chol"]
    chol = lax.axis_index("chol")
    place = jnp.stack([lax.axis_index("alpha"), lax.axis_index("beta"), chol]).astype(jnp.int32)
    meta = jnp.concatenate([place] + [v.reshape(-1) for v in (a_source, a_sign, b_source, b_sign)])
    width = ci_vector.shape[1] // chols
    quarter = lax.dynamic_slice_in_dim(ci_vector, chol * width, width, axis=1)
    meta, unit = gather_sources(meta, quarter, sizes)
    own, *pieces = gather_and_contract(meta, unit, a_tiles[:, 0], b_tiles, sizes)
    for shift, piece in enumerate(pieces, 1):
        own = own + shifted(piece, "chol", chols, lambda i: (i + shift) % chols).astype(jnp.float32)
    return own.astype(jnp.bfloat16)


def solution(mesh):
    placed = (
        P("alpha", "beta"),
        P("chol", "alpha", None, None, None),
        P("alpha", None),
        P("alpha", None),
        P("chol", "beta", None, None, None),
        P("beta", None),
        P("beta", None),
    )
    sizes = dict(mesh.shape)

    def body(*args):
        return per_device(sizes, *args)

    return jax.shard_map(
        body,
        mesh=mesh,
        in_specs=placed,
        out_specs=P("alpha", ("beta", "chol")),
        check_vma=False,
    )
```

time: 95.7 us -> 97.1 us (1.015)
  the two profiles are of different devices: /device:TPU:6 before, /device:TPU:32 now
where the time goes in v2:
time: 97.1 us; the launch traced here: 97.5 us
  waiting for transfers between devices  33.4 us (34%)
  starting transfers between devices  32.9 us (34%)
  Pallas kernels  22.4 us (23%)
  local copies, waits for them, and re-layouts  5.28 us (5%)
  other arithmetic  3.29 us (3%)
    ppermute x24, waiting for transfers between devices, shifted(): return lax.ppermute(value, axis, [(i, moves_to(i)) for i in range(size)])  33.4 us
    ppermute x24, starting transfers between devices, shifted(): return lax.ppermute(value, axis, [(i, moves_to(i)) for i in range(size)])  32.9 us
    pallas_call x3, Pallas kernels, contract(): pl.pallas_call(functools.partial(contract_kernel, first_unit, len(units),...  21.2 us
    unnamed x8, local copies, waits for them, and re-layouts  4.35 us
  transfers between devices with their start and end apart: 24, of which 14 were waited for; matrix products, arithmetic and copies ran while one was open for 3% of the time, Pallas kernels for 16%

profile of v2, /device:TPU:32, one launch (start us, length us, event | category | flops | bytes accessed | tf_op | source)
XLA Modules:
  0.0 97.5 jit_solution(17634212704126626262)
XLA Ops:
  0.0 0.9 copy-done
  1.0 3.3 %collective-permute-start.2 = (bf16[128,256]{1,0:T(8,128)(2,1)S(1)}, bf16[128,256]{1,0:T(8,128)(2,1)S(1)}, u32[]{:S(2)}, u32[]{:S(2)}) collective-permute-start(bf16[128,256]{1,0:T(8,128)(2,1)S(1)} %constant_dynamic-slice_fusion), channel_id=1, source_target_pairs={{0,64},{16,80},{32,96},{48,112},{64,128},{80,144},{96,160},{112,17... | collective-permute-start | bytes 196616 | tf_op jit(solution)/shard_map/ppermute | solution.py:26
  4.3 4.5 %collective-permute-start.1 = (bf16[128,256]{1,0:T(8,128)(2,1)S(1)}, bf16[128,256]{1,0:T(8,128)(2,1)}, u32[]{:S(2)}, u32[]{:S(2)}) collective-permute-start(bf16[128,256]{1,0:T(8,128)(2,1)S(1)} %constant_dynamic-slice_fusion), channel_id=1, source_target_pairs={{0,128},{16,144},{32,160},{48,176},{64,192},{80,208},{96,224},{112... | collective-permute-start | bytes 196616 | tf_op jit(solution)/shard_map/ppermute | solution.py:26
  8.8 2.7 %collective-permute-start = (bf16[128,256]{1,0:T(8,128)(2,1)S(1)}, bf16[128,256]{1,0:T(8,128)(2,1)}, u32[]{:S(2)}, u32[]{:S(2)}) collective-permute-start(bf16[128,256]{1,0:T(8,128)(2,1)S(1)} %constant_dynamic-slice_fusion), channel_id=1, source_target_pairs={{0,192},{16,208},{32,224},{48,240},{64,0},{80,16},{96,32},{112,48}... | collective-permute-start | bytes 196616 | tf_op jit(solution)/shard_map/ppermute | solution.py:26
  11.5 0.8 copy.10
  12.3 0.8 copy.11
  13.1 0.7 concatenate.3.meta_ref
  13.9 0.7 collective-permute-done
  14.7 1.6 %pad_maximum_fusion.refs_0_ = bf16[4,128,256]{2,1,0:T(8,128)(2,1)} fusion(bf16[1,128,256]{2,1,0:T(8,128)(2,1)S(1)} %bitcast.14, bf16[1,128,256]{2,1,0:T(8,128)(2,1)} %bitcast.2, bf16[1,128,256]{2,1,0:T(8,128)(2,1)} %bitcast.1, bf16[1,128,256]{2,1,0:T(8,128)(2,1)S(1)} %fusion), kind=kLoop, calls=%fused_computation.1 | loop fusion | flops 393216 | bytes 524288 | tf_op jit(solution)/shard_map/stack | solution.py:207
  16.3 2.8 %collective-permute-start.3 = (bf16[4,128,256]{2,1,0:T(8,128)(2,1)}, bf16[4,128,256]{2,1,0:T(8,128)(2,1)}, u32[]{:S(2)}, u32[]{:S(2)}) collective-permute-start(bf16[4,128,256]{2,1,0:T(8,128)(2,1)} %pad_maximum_fusion.refs_0_), channel_id=1, source_target_pairs={{0,48},{16,0},{32,16},{48,32},{64,112},{80,64},{96,80},{112,96},{1... | collective-permute-start | bytes 786440 | tf_op jit(solution)/shard_map/ppermute | solution.py:26
  19.0 5.6 %collective-permute-done.3.refs_1_ = bf16[4,128,256]{2,1,0:T(8,128)(2,1)} collective-permute-done((bf16[4,128,256]{2,1,0:T(8,128)(2,1)}, bf16[4,128,256]{2,1,0:T(8,128)(2,1)}, u32[]{:S(2)}, u32[]{:S(2)}) %collective-permute-start.3) | collective-permute-done | bytes 262176 | tf_op jit(solution)/shard_map/ppermute | solution.py:26
  24.7 3.4 %collective-permute-done.4.refs_3_ = bf16[4,128,256]{2,1,0:T(8,128)(2,1)} collective-permute-done((bf16[4,128,256]{2,1,0:T(8,128)(2,1)}, bf16[4,128,256]{2,1,0:T(8,128)(2,1)}, u32[]{:S(2)}, u32[]{:S(2)}) %collective-permute-start.4) | collective-permute-done | bytes 262176 | tf_op jit(solution)/shard_map/ppermute | solution.py:26
  28.1 1.0 %broadcast_select_fusion.1 = bf16[4,128,256]{2,1,0:T(8,128)(2,1)S(1)} fusion(bf16[4,128,256]{2,1,0:T(8,128)(2,1)} %collective-permute-done.4.refs_3_, bf16[4,128,256]{2,1,0:T(8,128)(2,1)} %collective-permute-done.3.refs_1_, pred[]{:T(512)S(6)} %eq.7), kind=kLoop, calls=%fused_computation.2 | loop fusion | flops 131072 | bytes 786433 | tf_op jit(solution)/shard_map/jit(_where)/select_n | solution.py:211
  29.1 7.6 %collective-permute-done.5.refs_2_ = bf16[4,128,256]{2,1,0:T(8,128)(2,1)S(1)} collective-permute-done((bf16[4,128,256]{2,1,0:T(8,128)(2,1)S(1)}, bf16[4,128,256]{2,1,0:T(8,128)(2,1)S(1)}, u32[]{:S(2)}, u32[]{:S(2)}) %collective-permute-start.5) | collective-permute-done | bytes 262176 | tf_op jit(solution)/shard_map/ppermute | solution.py:26
  36.7 1.3 %shard_map.73.rest_0_ = bf16[2,768,128]{2,1,0:T(8,128)(2,1)S(1)} custom-call(s32[63]{0:T(128)S(1)} %concatenate.3.meta_ref, bf16[4,128,256]{2,1,0:T(8,128)(2,1)} %pad_maximum_fusion.refs_0_, bf16[4,128,256]{2,1,0:T(8,128)(2,1)} %collective-permute-done.3.refs_1_, bf16[4,128,256]{2,1,0:T(8,128)(2,1)S(1)} %collective-permute-done.5.refs_2_, ...), custom_call_target="tpu_custom_call" | custom-call | tf_op jit(solution)/shard_map/pallas_call | solution.py:212
  38.0 3.1 %collective-permute-start.7 = (bf16[2,768,128]{2,1,0:T(8,128)(2,1)S(1)}, bf16[2,768,128]{2,1,0:T(8,128)(2,1)S(1)}, u32[]{:S(2)}, u32[]{:S(2)}) collective-permute-start(bf16[2,768,128]{2,1,0:T(8,128)(2,1)S(1)} %shard_map.73.rest_0_), channel_id=1, source_target_pairs={{0,3},{1,0},{2,1},{3,2},{4,7},{5,4},{6,5},{7,6},{8,11},{9,8},{10,9... | collective-permute-start | bytes 1179656 | tf_op jit(solution)/shard_map/ppermute | solution.py:26
  41.1 2.6 %collective-permute-start.11 = (bf16[2,768,128]{2,1,0:T(8,128)(2,1)S(1)}, bf16[2,768,128]{2,1,0:T(8,128)(2,1)S(1)}, u32[]{:S(2)}, u32[]{:S(2)}) collective-permute-start(bf16[2,768,128]{2,1,0:T(8,128)(2,1)S(1)} %shard_map.73.rest_0_), channel_id=1, source_target_pairs={{0,8},{4,12},{8,0},{12,4},{1,9},{5,13},{9,1},{13,5},{2,10},{6,14},... | collective-permute-start | bytes 1179656 | tf_op jit(solution)/shard_map/ppermute | solution.py:26
  43.7 2.7 %collective-permute-done.7.rest_2_ = bf16[2,768,128]{2,1,0:T(8,128)(2,1)S(1)} collective-permute-done((bf16[2,768,128]{2,1,0:T(8,128)(2,1)S(1)}, bf16[2,768,128]{2,1,0:T(8,128)(2,1)S(1)}, u32[]{:S(2)}, u32[]{:S(2)}) %collective-permute-start.7) | collective-permute-done | bytes 393248 | tf_op jit(solution)/shard_map/ppermute | solution.py:26
  46.4 3.7 %collective-permute-done.9.rest_4_ = bf16[2,768,128]{2,1,0:T(8,128)(2,1)S(1)} collective-permute-done((bf16[2,768,128]{2,1,0:T(8,128)(2,1)S(1)}, bf16[2,768,128]{2,1,0:T(8,128)(2,1)S(1)}, u32[]{:S(2)}, u32[]{:S(2)}) %collective-permute-start.9) | collective-permute-done | bytes 393248 | tf_op jit(solution)/shard_map/ppermute | solution.py:26
  50.8 2.7 %collective-permute-start.15 = (bf16[2,768,128]{2,1,0:T(8,128)(2,1)S(1)}, bf16[2,768,128]{2,1,0:T(8,128)(2,1)S(1)}, u32[]{:S(2)}, u32[]{:S(2)}) collective-permute-start(bf16[2,768,128]{2,1,0:T(8,128)(2,1)S(1)} %broadcast_select_fusion), channel_id=1, source_target_pairs={{0,8},{4,12},{8,0},{12,4},{1,9},{5,13},{9,1},{13,5},{2,10},{6,14},... | collective-permute-start | bytes 1179656 | tf_op jit(solution)/shard_map/ppermute | solution.py:26
  53.5 3.1 %collective-permute-start.14 = (bf16[2,768,128]{2,1,0:T(8,128)(2,1)S(1)}, bf16[2,768,128]{2,1,0:T(8,128)(2,1)S(1)}, u32[]{:S(2)}, u32[]{:S(2)}) collective-permute-start(bf16[2,768,128]{2,1,0:T(8,128)(2,1)S(1)} %collective-permute-done.11.rest_6_), channel_id=1, source_target_pairs={{0,3},{1,0},{2,1},{3,2},{4,5},{5,6},{6,7},{7,4},{8,11},{9,8},{10,9... | collective-permute-start | bytes 1179656 | tf_op jit(solution)/shard_map/ppermute | solution.py:26
  56.6 1.9 %copy-done.1 = bf16[16,1,6,128,128]{4,3,2,1,0:T(8,128)(2,1)S(1)} copy-done((bf16[16,1,6,128,128]{4,3,2,1,0:T(8,128)(2,1)S(1)}, bf16[16,1,6,128,128]{4,3,2,1,0:T(8,128)(2,1)}, u32[]{:S(2)}) %copy-start.1) | copy-done | bytes 3145752
  58.5 8.8 %shard_map.74.rest_6_ = f32[4,128,256]{2,1,0:T(8,128)S(1)} custom-call(s32[63]{0:T(128)S(1)} %concatenate.3.meta_ref, bf16[16,6,128,128]{3,2,1,0:T(8,128)(2,1)S(1)} %bitcast.11, bf16[16,8,3,128,128]{4,3,2,1,0:T(8,128)(2,1)} %b_ref.5, bf16[2,768,128]{2,1,0:T(8,128)(2,1)S(1)} %shard_map.73.rest_0_, bf16[2,768,128]{2,1,0:T(8,128)(2,1)S(1)} %collective-permute-done.6.rest_1_, ...), custom_call_target="tpu_custom_call" | custom-call | flops 5637144576 | bytes 9437184 | tf_op jit(solution)/shard_map/pallas_call | solution.py:171
  68.0 1.1 %collective-permute-done.16.rest_1_ = bf16[2,768,128]{2,1,0:T(8,128)(2,1)S(1)} collective-permute-done((bf16[2,768,128]{2,1,0:T(8,128)(2,1)S(1)}, bf16[2,768,128]{2,1,0:T(8,128)(2,1)S(1)}, u32[]{:S(2)}, u32[]{:S(2)}) %collective-permute-start.16) | collective-permute-done | bytes 393248 | tf_op jit(solution)/shard_map/ppermute | solution.py:26
  70.3 7.0 %shard_map.75.rest_2_ = f32[4,128,256]{2,1,0:T(8,128)S(1)} custom-call(s32[63]{0:T(128)S(1)} %concatenate.3.meta_ref, bf16[16,6,128,128]{3,2,1,0:T(8,128)(2,1)S(1)} %bitcast.12, bf16[16,8,3,128,128]{4,3,2,1,0:T(8,128)(2,1)} %b_ref.5, bf16[2,768,128]{2,1,0:T(8,128)(2,1)S(1)} %collective-permute-done.13.rest_0_, ...), custom_call_target="tpu_custom_call" | custom-call | flops 4227858432 | bytes 7864320 | tf_op jit(solution)/shard_map/pallas_call | solution.py:171
  77.6 1.7 %collective-permute-done.20.rest_1_ = bf16[2,768,128]{2,1,0:T(8,128)(2,1)S(1)} collective-permute-done((bf16[2,768,128]{2,1,0:T(8,128)(2,1)S(1)}, bf16[2,768,128]{2,1,0:T(8,128)(2,1)S(1)}, u32[]{:S(2)}, u32[]{:S(2)}) %collective-permute-start.20) | collective-permute-done | bytes 393248 | tf_op jit(solution)/shard_map/ppermute | solution.py:26
  79.3 5.3 %shard_map.76 = (f32[128,256]{1,0:T(8,128)S(1)}, bf16[128,256]{1,0:T(8,128)(2,1)S(1)}, bf16[128,256]{1,0:T(8,128)(2,1)S(1)}, bf16[128,256]{1,0:T(8,128)(2,1)S(1)}) custom-call(s32[63]{0:T(128)S(1)} %concatenate.3.meta_ref, bf16[16,6,128,128]{3,2,1,0:T(8,128)(2,1)S(1)} %bitcast.13, bf16[16,8,3,128,128]{4,3,2,1,0:T(8,128)(2,1)} %b_ref.5, ...), custom_call_target="tpu_custom_call" | custom-call | flops 1409286144 | bytes 4718592 | tf_op jit(solution)/shard_map/pallas_call | solution.py:171
  84.6 5.3 %collective-permute-start.23 = (bf16[128,256]{1,0:T(8,128)(2,1)S(1)}, bf16[128,256]{1,0:T(8,128)(2,1)S(1)}, u32[]{:S(2)}, u32[]{:S(2)}) collective-permute-start(bf16[128,256]{1,0:T(8,128)(2,1)S(1)} %get-tuple-element.28), channel_id=1, source_target_pairs={{0,3},{1,0},{2,1},{3,2},{4,7},{5,4},{6,5},{7,6},{8,11},{9,8},{10,9... | collective-permute-start | bytes 196616 | tf_op jit(solution)/shard_map/ppermute | solution.py:26
  89.9 1.4 %collective-permute-start.22 = (bf16[128,256]{1,0:T(8,128)(2,1)S(1)}, bf16[128,256]{1,0:T(8,128)(2,1)S(1)}, u32[]{:S(2)}, u32[]{:S(2)}) collective-permute-start(bf16[128,256]{1,0:T(8,128)(2,1)S(1)} %get-tuple-element.27), channel_id=1, source_target_pairs={{0,2},{1,3},{2,0},{3,1},{4,6},{5,7},{6,4},{7,5},{8,10},{9,11},{10,... | collective-permute-start | bytes 196616 | tf_op jit(solution)/shard_map/ppermute | solution.py:26
  91.3 1.8 %collective-permute-done.23 = bf16[128,256]{1,0:T(8,128)(2,1)S(1)} collective-permute-done((bf16[128,256]{1,0:T(8,128)(2,1)S(1)}, bf16[128,256]{1,0:T(8,128)(2,1)S(1)}, u32[]{:S(2)}, u32[]{:S(2)}) %collective-permute-start.23) | collective-permute-done | bytes 65568 | tf_op jit(solution)/shard_map/ppermute | solution.py:26
  93.2 2.6 %collective-permute-done.22 = bf16[128,256]{1,0:T(8,128)(2,1)S(1)} collective-permute-done((bf16[128,256]{1,0:T(8,128)(2,1)S(1)}, bf16[128,256]{1,0:T(8,128)(2,1)S(1)}, u32[]{:S(2)}, u32[]{:S(2)}) %collective-permute-start.22) | collective-permute-done | bytes 65568 | tf_op jit(solution)/shard_map/ppermute | solution.py:26
  95.8 1.0 %collective-permute-done.21 = bf16[128,256]{1,0:T(8,128)(2,1)S(1)} collective-permute-done((bf16[128,256]{1,0:T(8,128)(2,1)S(1)}, bf16[128,256]{1,0:T(8,128)(2,1)S(1)}, u32[]{:S(2)}, u32[]{:S(2)}) %collective-permute-start.21) | collective-permute-done | bytes 65568 | tf_op jit(solution)/shard_map/ppermute | solution.py:26
  (37 shorter events, 3.7 us)
Async XLA Ops:
  0.0 1.0 copy-start
  0.0 70.3 %copy-start.2 = (bf16[16,1,6,128,128]{4,3,2,1,0:T(8,128)(2,1)S(1)}, bf16[16,1,6,128,128]{4,3,2,1,0:T(8,128)(2,1)}, u32[]{:S(2)}) copy-start(bf16[16,1,6,128,128]{4,3,2,1,0:T(8,128)(2,1)} %param.8) | copy-start | bytes 9437188
  1.0 13.0 %collective-permute-start.2 = (bf16[128,256]{1,0:T(8,128)(2,1)S(1)}, bf16[128,256]{1,0:T(8,128)(2,1)S(1)}, u32[]{:S(2)}, u32[]{:S(2)}) collective-permute-start(bf16[128,256]{1,0:T(8,128)(2,1)S(1)} %constant_dynamic-slice_fusion), channel_id=1, source_target_pairs={{0,64},{16,80},{32,96},{48,112},{64,128},{80,144},{96,160},{112,17... | collective-permute-start | bytes 196616 | tf_op jit(solution)/shard_map/ppermute | solution.py:26
  4.3 9.6 %collective-permute-start.1 = (bf16[128,256]{1,0:T(8,128)(2,1)S(1)}, bf16[128,256]{1,0:T(8,128)(2,1)}, u32[]{:S(2)}, u32[]{:S(2)}) collective-permute-start(bf16[128,256]{1,0:T(8,128)(2,1)S(1)} %constant_dynamic-slice_fusion), channel_id=1, source_target_pairs={{0,128},{16,144},{32,160},{48,176},{64,192},{80,208},{96,224},{112... | collective-permute-start | bytes 196616 | tf_op jit(solution)/shard_map/ppermute | solution.py:26
  8.8 5.8 %collective-permute-start = (bf16[128,256]{1,0:T(8,128)(2,1)S(1)}, bf16[128,256]{1,0:T(8,128)(2,1)}, u32[]{:S(2)}, u32[]{:S(2)}) collective-permute-start(bf16[128,256]{1,0:T(8,128)(2,1)S(1)} %constant_dynamic-slice_fusion), channel_id=1, source_target_pairs={{0,192},{16,208},{32,224},{48,240},{64,0},{80,16},{96,32},{112,48}... | collective-permute-start | bytes 196616 | tf_op jit(solution)/shard_map/ppermute | solution.py:26
  16.3 8.4 %collective-permute-start.3 = (bf16[4,128,256]{2,1,0:T(8,128)(2,1)}, bf16[4,128,256]{2,1,0:T(8,128)(2,1)}, u32[]{:S(2)}, u32[]{:S(2)}) collective-permute-start(bf16[4,128,256]{2,1,0:T(8,128)(2,1)} %pad_maximum_fusion.refs_0_), channel_id=1, source_target_pairs={{0,48},{16,0},{32,16},{48,32},{64,112},{80,64},{96,80},{112,96},{1... | collective-permute-start | bytes 786440 | tf_op jit(solution)/shard_map/ppermute | solution.py:26
  19.0 9.1 %collective-permute-start.4 = (bf16[4,128,256]{2,1,0:T(8,128)(2,1)}, bf16[4,128,256]{2,1,0:T(8,128)(2,1)}, u32[]{:S(2)}, u32[]{:S(2)}) collective-permute-start(bf16[4,128,256]{2,1,0:T(8,128)(2,1)} %pad_maximum_fusion.refs_0_), channel_id=1, source_target_pairs={{0,16},{16,32},{32,48},{48,0},{64,80},{80,96},{96,112},{112,64},{1... | collective-permute-start | bytes 786440 | tf_op jit(solution)/shard_map/ppermute | solution.py:26
  29.1 7.7 %collective-permute-start.5 = (bf16[4,128,256]{2,1,0:T(8,128)(2,1)S(1)}, bf16[4,128,256]{2,1,0:T(8,128)(2,1)S(1)}, u32[]{:S(2)}, u32[]{:S(2)}) collective-permute-start(bf16[4,128,256]{2,1,0:T(8,128)(2,1)S(1)} %broadcast_select_fusion.1), channel_id=1, source_target_pairs={{0,16},{4,52},{8,24},{12,60},{16,32},{20,4},{24,40},{28,12},{32,48... | collective-permute-start | bytes 786440 | tf_op jit(solution)/shard_map/ppermute | solution.py:26
  38.0 8.4 %collective-permute-start.7 = (bf16[2,768,128]{2,1,0:T(8,128)(2,1)S(1)}, bf16[2,768,128]{2,1,0:T(8,128)(2,1)S(1)}, u32[]{:S(2)}, u32[]{:S(2)}) collective-permute-start(bf16[2,768,128]{2,1,0:T(8,128)(2,1)S(1)} %shard_map.73.rest_0_), channel_id=1, source_target_pairs={{0,3},{1,0},{2,1},{3,2},{4,7},{5,4},{6,5},{7,6},{8,11},{9,8},{10,9... | collective-permute-start | bytes 1179656 | tf_op jit(solution)/shard_map/ppermute | solution.py:26
  41.1 9.0 %collective-permute-start.9 = (bf16[2,768,128]{2,1,0:T(8,128)(2,1)S(1)}, bf16[2,768,128]{2,1,0:T(8,128)(2,1)S(1)}, u32[]{:S(2)}, u32[]{:S(2)}) collective-permute-start(bf16[2,768,128]{2,1,0:T(8,128)(2,1)S(1)} %shard_map.73.rest_0_), channel_id=1, source_target_pairs={{0,1},{1,2},{2,3},{3,0},{4,5},{5,6},{6,7},{7,4},{8,9},{9,10},{10,1... | collective-permute-start | bytes 1179656 | tf_op jit(solution)/shard_map/ppermute | solution.py:26
  41.1 9.0 %collective-permute-start.11 = (bf16[2,768,128]{2,1,0:T(8,128)(2,1)S(1)}, bf16[2,768,128]{2,1,0:T(8,128)(2,1)S(1)}, u32[]{:S(2)}, u32[]{:S(2)}) collective-permute-start(bf16[2,768,128]{2,1,0:T(8,128)(2,1)S(1)} %shard_map.73.rest_0_), channel_id=1, source_target_pairs={{0,8},{4,12},{8,0},{12,4},{1,9},{5,13},{9,1},{13,5},{2,10},{6,14},... | collective-permute-start | bytes 1179656 | tf_op jit(solution)/shard_map/ppermute | solution.py:26
  43.7 7.0 %collective-permute-start.6 = (bf16[2,768,128]{2,1,0:T(8,128)(2,1)S(1)}, bf16[2,768,128]{2,1,0:T(8,128)(2,1)S(1)}, u32[]{:S(2)}, u32[]{:S(2)}) collective-permute-start(bf16[2,768,128]{2,1,0:T(8,128)(2,1)S(1)} %shard_map.73.rest_0_), channel_id=1, source_target_pairs={{0,4},{4,0},{8,12},{12,8},{1,5},{5,1},{9,13},{13,9},{2,6},{6,2},{1... | collective-permute-start | bytes 1179656 | tf_op jit(solution)/shard_map/ppermute | solution.py:26
  46.4 7.0 %collective-permute-start.8 = (bf16[2,768,128]{2,1,0:T(8,128)(2,1)S(1)}, bf16[2,768,128]{2,1,0:T(8,128)(2,1)S(1)}, u32[]{:S(2)}, u32[]{:S(2)}) collective-permute-start(bf16[2,768,128]{2,1,0:T(8,128)(2,1)S(1)} %collective-permute-done.7.rest_2_), channel_id=1, source_target_pairs={{0,4},{4,0},{8,12},{12,8},{1,5},{5,1},{9,13},{13,9},{2,6},{6,2},{1... | collective-permute-start | bytes 1179656 | tf_op jit(solution)/shard_map/ppermute | solution.py:26
  50.1 6.5 %collective-permute-start.10 = (bf16[2,768,128]{2,1,0:T(8,128)(2,1)S(1)}, bf16[2,768,128]{2,1,0:T(8,128)(2,1)S(1)}, u32[]{:S(2)}, u32[]{:S(2)}) collective-permute-start(bf16[2,768,128]{2,1,0:T(8,128)(2,1)S(1)} %collective-permute-done.9.rest_4_), channel_id=1, source_target_pairs={{0,4},{4,0},{8,12},{12,8},{1,5},{5,1},{9,13},{13,9},{2,6},{6,2},{1... | collective-permute-start | bytes 1179656 | tf_op jit(solution)/shard_map/ppermute | solution.py:26
  50.1 6.5 %collective-permute-start.12 = (bf16[2,768,128]{2,1,0:T(8,128)(2,1)S(1)}, bf16[2,768,128]{2,1,0:T(8,128)(2,1)S(1)}, u32[]{:S(2)}, u32[]{:S(2)}) collective-permute-start(bf16[2,768,128]{2,1,0:T(8,128)(2,1)S(1)} %collective-permute-done.11.rest_6_), channel_id=1, source_target_pairs={{0,4},{4,0},{8,12},{12,8},{1,5},{5,1},{9,13},{13,9},{2,6},{6,2},{1... | collective-permute-start | bytes 1179656 | tf_op jit(solution)/shard_map/ppermute | solution.py:26
  50.7 16.7 %collective-permute-start.13 = (bf16[2,768,128]{2,1,0:T(8,128)(2,1)S(1)}, bf16[2,768,128]{2,1,0:T(8,128)(2,1)S(1)}, u32[]{:S(2)}, u32[]{:S(2)}) collective-permute-start(bf16[2,768,128]{2,1,0:T(8,128)(2,1)S(1)} %broadcast_select_fusion), channel_id=1, source_target_pairs={{0,1},{1,2},{2,3},{3,0},{4,7},{5,4},{6,5},{7,6},{8,9},{9,10},{10,1... | collective-permute-start | bytes 1179656 | tf_op jit(solution)/shard_map/ppermute | solution.py:26
  50.8 16.6 %collective-permute-start.15 = (bf16[2,768,128]{2,1,0:T(8,128)(2,1)S(1)}, bf16[2,768,128]{2,1,0:T(8,128)(2,1)S(1)}, u32[]{:S(2)}, u32[]{:S(2)}) collective-permute-start(bf16[2,768,128]{2,1,0:T(8,128)(2,1)S(1)} %broadcast_select_fusion), channel_id=1, source_target_pairs={{0,8},{4,12},{8,0},{12,4},{1,9},{5,13},{9,1},{13,5},{2,10},{6,14},... | collective-permute-start | bytes 1179656 | tf_op jit(solution)/shard_map/ppermute | solution.py:26
  53.5 13.9 %collective-permute-start.14 = (bf16[2,768,128]{2,1,0:T(8,128)(2,1)S(1)}, bf16[2,768,128]{2,1,0:T(8,128)(2,1)S(1)}, u32[]{:S(2)}, u32[]{:S(2)}) collective-permute-start(bf16[2,768,128]{2,1,0:T(8,128)(2,1)S(1)} %collective-permute-done.11.rest_6_), channel_id=1, source_target_pairs={{0,3},{1,0},{2,1},{3,2},{4,5},{5,6},{6,7},{7,4},{8,11},{9,8},{10,9... | collective-permute-start | bytes 1179656 | tf_op jit(solution)/shard_map/ppermute | solution.py:26
  56.6 1.9 %copy-start.1 = (bf16[16,1,6,128,128]{4,3,2,1,0:T(8,128)(2,1)S(1)}, bf16[16,1,6,128,128]{4,3,2,1,0:T(8,128)(2,1)}, u32[]{:S(2)}) copy-start(bf16[16,1,6,128,128]{4,3,2,1,0:T(8,128)(2,1)} %param.8) | copy-start | bytes 9437188
  67.3 1.8 %collective-permute-start.16 = (bf16[2,768,128]{2,1,0:T(8,128)(2,1)S(1)}, bf16[2,768,128]{2,1,0:T(8,128)(2,1)S(1)}, u32[]{:S(2)}, u32[]{:S(2)}) collective-permute-start(bf16[2,768,128]{2,1,0:T(8,128)(2,1)S(1)} %collective-permute-done.13.rest_0_), channel_id=1, source_target_pairs={{0,4},{4,0},{8,12},{12,8},{1,5},{5,1},{9,13},{13,9},{2,6},{6,2},{1... | collective-permute-start | bytes 1179656 | tf_op jit(solution)/shard_map/ppermute | solution.py:26
  67.4 2.3 %collective-permute-start.17 = (bf16[2,768,128]{2,1,0:T(8,128)(2,1)S(1)}, bf16[2,768,128]{2,1,0:T(8,128)(2,1)S(1)}, u32[]{:S(2)}, u32[]{:S(2)}) collective-permute-start(bf16[2,768,128]{2,1,0:T(8,128)(2,1)S(1)} %collective-permute-done.14.rest_2_), channel_id=1, source_target_pairs={{0,4},{4,0},{8,12},{12,8},{1,5},{5,1},{9,13},{13,9},{2,6},{6,2},{1... | collective-permute-start | bytes 1179656 | tf_op jit(solution)/shard_map/ppermute | solution.py:26
  67.9 2.3 %collective-permute-start.18 = (bf16[2,768,128]{2,1,0:T(8,128)(2,1)S(1)}, bf16[2,768,128]{2,1,0:T(8,128)(2,1)S(1)}, u32[]{:S(2)}, u32[]{:S(2)}) collective-permute-start(bf16[2,768,128]{2,1,0:T(8,128)(2,1)S(1)} %collective-permute-done.15.rest_4_), channel_id=1, source_target_pairs={{0,4},{4,0},{8,12},{12,8},{1,5},{5,1},{9,13},{13,9},{2,6},{6,2},{1... | collective-permute-start | bytes 1179656 | tf_op jit(solution)/shard_map/ppermute | solution.py:26
  68.0 9.5 %collective-permute-start.19 = (bf16[2,768,128]{2,1,0:T(8,128)(2,1)S(1)}, bf16[2,768,128]{2,1,0:T(8,128)(2,1)S(1)}, u32[]{:S(2)}, u32[]{:S(2)}) collective-permute-start(bf16[2,768,128]{2,1,0:T(8,128)(2,1)S(1)} %collective-permute-done.15.rest_4_), channel_id=1, source_target_pairs={{0,1},{1,2},{2,3},{3,0},{4,7},{5,4},{6,5},{7,6},{8,9},{9,10},{10,1... | collective-permute-start | bytes 1179656 | tf_op jit(solution)/shard_map/ppermute | solution.py:26
  77.6 1.7 %collective-permute-start.20 = (bf16[2,768,128]{2,1,0:T(8,128)(2,1)S(1)}, bf16[2,768,128]{2,1,0:T(8,128)(2,1)S(1)}, u32[]{:S(2)}, u32[]{:S(2)}) collective-permute-start(bf16[2,768,128]{2,1,0:T(8,128)(2,1)S(1)} %collective-permute-done.19.rest_0_), channel_id=1, source_target_pairs={{0,4},{4,0},{8,12},{12,8},{1,5},{5,1},{9,13},{13,9},{2,6},{6,2},{1... | collective-permute-start | bytes 1179656 | tf_op jit(solution)/shard_map/ppermute | solution.py:26
  84.6 8.5 %collective-permute-start.23 = (bf16[128,256]{1,0:T(8,128)(2,1)S(1)}, bf16[128,256]{1,0:T(8,128)(2,1)S(1)}, u32[]{:S(2)}, u32[]{:S(2)}) collective-permute-start(bf16[128,256]{1,0:T(8,128)(2,1)S(1)} %get-tuple-element.28), channel_id=1, source_target_pairs={{0,3},{1,0},{2,1},{3,2},{4,7},{5,4},{6,5},{7,6},{8,11},{9,8},{10,9... | collective-permute-start | bytes 196616 | tf_op jit(solution)/shard_map/ppermute | solution.py:26
  89.9 5.9 %collective-permute-start.22 = (bf16[128,256]{1,0:T(8,128)(2,1)S(1)}, bf16[128,256]{1,0:T(8,128)(2,1)S(1)}, u32[]{:S(2)}, u32[]{:S(2)}) collective-permute-start(bf16[128,256]{1,0:T(8,128)(2,1)S(1)} %get-tuple-element.27), channel_id=1, source_target_pairs={{0,2},{1,3},{2,0},{3,1},{4,6},{5,7},{6,4},{7,5},{8,10},{9,11},{10,... | collective-permute-start | bytes 196616 | tf_op jit(solution)/shard_map/ppermute | solution.py:26
  91.3 5.5 %collective-permute-start.21 = (bf16[128,256]{1,0:T(8,128)(2,1)S(1)}, bf16[128,256]{1,0:T(8,128)(2,1)S(1)}, u32[]{:S(2)}, u32[]{:S(2)}) collective-permute-start(bf16[128,256]{1,0:T(8,128)(2,1)S(1)} %get-tuple-element.26), channel_id=1, source_target_pairs={{0,1},{1,2},{2,3},{3,0},{4,5},{5,6},{6,7},{7,4},{8,9},{9,10},{10,1... | collective-permute-start | bytes 196616 | tf_op jit(solution)/shard_map/ppermute | solution.py:26

commit v3 on v2

v3 whole, which is shorter than its diff:
```python
import functools

import jax
import jax.numpy as jnp
from jax import lax
from jax.experimental import pallas as pl
from jax.experimental.pallas import tpu as pltpu
from jax.sharding import PartitionSpec as P

BLK = 128
VECTORS_PER_GROUP = 4
WIDE, NARROW = 4, 2
X_SIZE = 4
A_SLOTS, B_SLOTS, B_BLOCKS = 6, 3, 8
ALPHA, BETA, CHOL, A_SOURCE = 0, 1, 2, 3
A_SIGN = A_SOURCE + A_SLOTS
B_SOURCE = A_SIGN + A_SLOTS
B_SIGN = B_SOURCE + B_SLOTS * B_BLOCKS
ARRIVAL = 0x67532410
SMEM = pl.BlockSpec(memory_space=pltpu.SMEM)
VMEM = pl.BlockSpec(memory_space=pltpu.VMEM)
HBM = pl.BlockSpec(memory_space=pltpu.HBM)


def shifted(value, axis, size, moves_to):
    return lax.ppermute(value, axis, [(i, moves_to(i)) for i in range(size)])


def choose(index, low, high, act):
    if high - low == 1:
        act(low)
        return
    middle = (low + high) // 2

    @pl.when(index < middle)
    def _():
        choose(index, low, middle, act)

    @pl.when(index >= middle)
    def _():
        choose(index, middle, high, act)


def flip_kernel(a_ref, out_ref):
    for q in range(a_ref.shape[0]):
        for k in range(A_SLOTS):
            out_ref[k * BLK : (k + 1) * BLK, q * BLK : (q + 1) * BLK] = a_ref[q, 0, k].T


def pick_kernel(meta_ref, own_ref, after_ref, before_ref, far_low_ref, far_high_ref, out_ref):
    alpha = meta_ref[ALPHA]
    for k in range(A_SLOTS):
        source = meta_ref[A_SOURCE + k]
        sign = meta_ref[A_SIGN + k].astype(jnp.float32).astype(out_ref.dtype)
        dz = ((source >> 2) - (alpha >> 2)) & 3
        dx = (source - alpha) & 3

        def put(ref, at, k=k, sign=sign):
            for half in range(2):
                block = ref[at, :, half * BLK : (half + 1) * BLK]
                out_ref[half, :, k * BLK : (k + 1) * BLK] = block.T * sign

        for distance, ref in ((0, own_ref), (1, after_ref), (3, before_ref)):

            @pl.when(dx == distance)
            def _(ref=ref, put=put, dz=dz):
                put(ref, dz)

        @pl.when((dx == 2) & (dz < 2))
        def _(put=put, dz=dz):
            put(far_low_ref, jnp.minimum(dz, 1))

        @pl.when((dx == 2) & (dz >= 2))
        def _(put=put, dz=dz):
            put(far_high_ref, jnp.maximum(dz - 2, 0))


def contract_kernel(first_unit, count_units, has_sum, last, meta_ref, a_ref, b_ref, *rest):
    units, rest = rest[:count_units], rest[count_units:]
    if has_sum:
        sum_ref, rest = rest[0], rest[1:]
    if last:
        own_ref, *piece_refs = rest[:4]
        acc, rest = rest[4], rest[5:]
    else:
        acc, rest = rest[0], rest[1:]
    tasks, places, c_buf, b_buf, c_sem, b_sem = rest
    pairs = B_BLOCKS * B_SLOTS
    vectors = b_ref.shape[0]
    beta, chol = meta_ref[BETA], meta_ref[CHOL]
    acc[...] = sum_ref[...] if has_sum else jnp.zeros_like(acc)

    count = jnp.int32(0)
    for pair in range(pairs):
        m = meta_ref[B_SOURCE + pair]
        owner = m >> 3
        crossed = owner ^ beta
        dy = ((m >> 1) - chol) & 3
        dy = jnp.where((crossed & 2) * (owner & 1) != 0, (4 - dy) & 3, dy)
        code = (crossed & 2) * 2 + dy
        place = ((jnp.int32(ARRIVAL) >> (4 * code)) & 7) * 2 + (crossed & 1) - first_unit
        tasks[count] = pair
        places[count] = place
        here = (meta_ref[B_SIGN + pair] != 0) & (place >= 0) & (place < count_units)
        count = count + jnp.where(here, 1, 0)
    wide_steps = count >> 2
    narrow_steps = (count - WIDE * wide_steps + 1) >> 1
    steps = wide_steps + narrow_steps

    def first_of(step):
        return jnp.where(step < wide_steps, WIDE * step, NARROW * step + (WIDE - NARROW) * wide_steps)

    def c_copy(unit, m, slot, lane):
        return pltpu.make_async_copy(
            unit.at[m & 1], c_buf.at[slot, pl.ds(lane * BLK, BLK)], c_sem.at[slot, lane]
        )

    def b_copy(u, l, slot, lane):
        return pltpu.make_async_copy(b_ref.at[:, u, l], b_buf.at[slot, lane], b_sem.at[slot, lane])

    def start(step, slot, lanes):
        for lane in lanes:
            at = jnp.minimum(first_of(step) + lane, count - 1)
            pair = tasks[at]
            m = meta_ref[B_SOURCE + pair]
            choose(places[at], 0, count_units, lambda i: c_copy(units[i], m, slot, lane).start())
            u = pair // B_SLOTS
            b_copy(u, pair - u * B_SLOTS, slot, lane).start()

    def start_step(step, slot):
        @pl.when(step < steps)
        def _():
            start(step, slot, range(NARROW))

        @pl.when(step < wide_steps)
        def _():
            start(step, slot, range(NARROW, WIDE))

    start_step(0, 0)

    def body(width, step, carry):
        slot = step & 1
        start_step(step + 1, 1 - slot)
        for lane in range(width):
            c_copy(units[0], 0, slot, lane).wait()
            b_copy(0, 0, slot, lane).wait()
        sums = [jnp.zeros((BLK, BLK), jnp.float32) for _ in range(width)]
        for group in range(0, vectors, VECTORS_PER_GROUP):
            columns = slice(group * BLK, (group + VECTORS_PER_GROUP) * BLK)
            panel = jnp.dot(
                c_buf[slot, : width * BLK], a_ref[:, columns], preferred_element_type=jnp.float32
            ).astype(jnp.bfloat16)
            for lane in range(width):
                tiles = [b_buf[slot, lane, group + r] for r in range(VECTORS_PER_GROUP)]
                blocks = [
                    panel[lane * BLK : (lane + 1) * BLK, r * BLK : (r + 1) * BLK]
                    for r in range(VECTORS_PER_GROUP)
                ]
                sums[lane] += jnp.dot(
                    jnp.concatenate(tiles, axis=1),
                    jnp.concatenate(blocks, axis=0),
                    preferred_element_type=jnp.float32,
                )
        for lane in range(width):
            at = first_of(step) + lane
            pair = tasks[jnp.minimum(at, count - 1)]
            factor = jnp.where(at < count, meta_ref[B_SIGN + pair], 0).astype(jnp.float32)
            acc[pair // B_SLOTS] += factor * sums[lane]
        return carry

    lax.fori_loop(0, wide_steps, functools.partial(body, WIDE), 0)
    lax.fori_loop(wide_steps, steps, functools.partial(body, NARROW), 0)
    if last:
        for shift, out_ref in enumerate([own_ref] + piece_refs):
            for half in range(2):
                block = acc[((chol + shift) & 3) * 2 + half].T
                out_ref[:, half * BLK : (half + 1) * BLK] = block.astype(out_ref.dtype)


def contract(meta, a_flipped, b_tiles, units, first_unit, running=None, last=False):
    vectors, blocks = b_tiles.shape[:2]
    part = len(units) / 16
    flops = int(part * 2 * (a_flipped.size * blocks * B_SLOTS * BLK + b_tiles.size * BLK))
    moved = int(part * 2 * b_tiles.size) + 2 * a_flipped.size
    share = (BLK, blocks * BLK // 4)
    whole = jax.ShapeDtypeStruct((blocks, BLK, BLK), jnp.float32)
    shares = [jax.ShapeDtypeStruct(share, jnp.float32)] + [jax.ShapeDtypeStruct(share, jnp.bfloat16)] * 3
    sums = [] if running is None else [running]
    return pl.pallas_call(
        functools.partial(contract_kernel, first_unit, len(units), bool(sums), last),
        out_shape=shares if last else whole,
        in_specs=[SMEM, VMEM, HBM] + [HBM] * len(units) + [VMEM] * len(sums),
        out_specs=[VMEM] * 4 if last else VMEM,
        scratch_shapes=[pltpu.VMEM(whole.shape, jnp.float32)] * last
        + [
            pltpu.SMEM((blocks * B_SLOTS + 1,), jnp.int32),
            pltpu.SMEM((blocks * B_SLOTS + 1,), jnp.int32),
            pltpu.VMEM((2, WIDE * BLK, A_SLOTS * BLK), jnp.bfloat16),
            pltpu.VMEM((2, WIDE, vectors, BLK, BLK), jnp.bfloat16),
            pltpu.SemaphoreType.DMA((2, WIDE)),
            pltpu.SemaphoreType.DMA((2, WIDE)),
        ],
        compiler_params=pltpu.CompilerParams(vmem_limit_bytes=47 * 1024 * 1024),
        cost_estimate=pl.CostEstimate(flops=flops, bytes_accessed=moved, transcendentals=0),
    )(meta, a_flipped, b_tiles, *units, *sums)


def flip(a_tiles):
    vectors = a_tiles.shape[0]
    return pl.pallas_call(
        flip_kernel,
        out_shape=jax.ShapeDtypeStruct((A_SLOTS * BLK, vectors * BLK), a_tiles.dtype),
        in_specs=[VMEM],
        out_specs=VMEM,
        compiler_params=pltpu.CompilerParams(vmem_limit_bytes=16 * 1024 * 1024),
        cost_estimate=pl.CostEstimate(flops=0, bytes_accessed=4 * a_tiles.size, transcendentals=0),
    )(a_tiles)


def gather_sources(meta, quarter, a_tiles, alphas):
    zs = alphas // X_SIZE

    def z_from(value, distance):
        return shifted(value, "alpha", alphas, lambda i: (i // X_SIZE - distance) % zs * X_SIZE + i % X_SIZE)

    def x_from(value, distance):
        return shifted(value, "alpha", alphas, lambda i: i // X_SIZE * X_SIZE + (i % X_SIZE - distance) % X_SIZE)

    own = jnp.stack([quarter] + [z_from(quarter, distance) for distance in (1, 2, 3)])
    after, before = x_from(own, 1), x_from(own, 3)
    after, meta, a_flipped = lax.optimization_barrier((after, meta, flip(a_tiles)))
    far_low, far_high = x_from(before[:2], 3), x_from(after[2:], 1)
    unit = pl.pallas_call(
        pick_kernel,
        out_shape=jax.ShapeDtypeStruct((2, BLK, A_SLOTS * BLK), quarter.dtype),
        in_specs=[SMEM] + [VMEM] * 5,
        out_specs=VMEM,
        compiler_params=pltpu.CompilerParams(vmem_limit_bytes=8 * 1024 * 1024),
    )(meta, own, after, before, far_low, far_high)
    return meta, unit, a_flipped


def gather_and_contract(meta, unit, a_flipped, b_tiles, sizes):
    betas, chols = sizes["beta"], sizes["chol"]

    def y_from(value, distance):
        return shifted(value, "chol", chols, lambda i: (i - distance) % chols)

    def z_other(value):
        return shifted(value, "beta", betas, lambda i: i ^ 2)

    def both(values):
        return [v for value in values for v in (value, shifted(value, "beta", betas, lambda i: i ^ 1))]

    def by_core(value, sense):
        def moved(i):
            beta, chol = i // chols, i % chols
            return beta * chols + (chol + (sense if beta % 2 == 0 else -sense)) % chols

        return shifted(value, ("beta", "chol"), betas * chols, moved)

    after, before, across = y_from(unit, 1), y_from(unit, 3), z_other(unit)
    onward = jnp.where(lax.axis_index("beta") % 2 == 0, before, after)
    middle, far_onward, far_back = by_core(onward, 1), z_other(onward), by_core(across, -1)
    first = both([unit, after, before, across])
    running = contract(meta, a_flipped, b_tiles, first, 0)
    running, middle, far_back, far_onward = lax.optimization_barrier((running, middle, far_back, far_onward))
    far_middle = by_core(far_onward, 1)
    second = both([middle, far_back, far_onward])
    running = contract(meta, a_flipped, b_tiles, second, 8, running)
    running, far_middle = lax.optimization_barrier((running, far_middle))
    return contract(meta, a_flipped, b_tiles, both([far_middle]), 14, running, last=True)


def per_device(sizes, ci_vector, a_tiles, a_source, a_sign, b_tiles, b_source, b_sign):
    chols = sizes["chol"]
    chol = lax.axis_index("chol")
    place = jnp.stack([lax.axis_index("alpha"), lax.axis_index("beta"), chol]).astype(jnp.int32)
    meta = jnp.concatenate([place] + [v.reshape(-1) for v in (a_source, a_sign, b_source, b_sign)])
    width = ci_vector.shape[1] // chols
    quarter = lax.dynamic_slice_in_dim(ci_vector, chol * width, width, axis=1)
    meta, unit, a_flipped = gather_sources(meta, quarter, a_tiles, sizes["alpha"])
    own, *pieces = gather_and_contract(meta, unit, a_flipped, b_tiles, sizes)
    for shift, piece in enumerate(pieces, 1):
        own = own + shifted(piece, "chol", chols, lambda i: (i + shift) % chols).astype(jnp.float32)
    return own.astype(jnp.bfloat16)


def solution(mesh):
    placed = (
        P("alpha", "beta"),
        P("chol", "alpha", None, None, None),
        P("alpha", None),
        P("alpha", None),
        P("chol", "beta", None, None, None),
        P("beta", None),
        P("beta", None),
    )
    sizes = dict(mesh.shape)

    def body(*args):
        return per_device(sizes, *args)

    return jax.shard_map(
        body,
        mesh=mesh,
        in_specs=placed,
        out_specs=P("alpha", ("beta", "chol")),
        check_vma=False,
    )
```

time: 97.1 us -> 96.5 us (level)
  the two profiles are of different devices: /device:TPU:32 before, /device:TPU:6 now
where the time goes in v3:
time: 96.5 us
  waiting for transfers between devices  31.4 us (33%)
  starting transfers between devices  30 us (31%)
  Pallas kernels  26 us (27%)
  local copies, waits for them, and re-layouts  6.45 us (7%)
  other arithmetic  2.44 us (3%)
    ppermute x25, waiting for transfers between devices, shifted(): return lax.ppermute(value, axis, [(i, moves_to(i)) for i in range(size)])  31.4 us
    ppermute x25, starting transfers between devices, shifted(): return lax.ppermute(value, axis, [(i, moves_to(i)) for i in range(size)])  30 us
    pallas_call x3, Pallas kernels, contract(): pl.pallas_call(functools.partial(contract_kernel, first_unit, len(units),...  22.5 us
    unnamed x10, local copies, waits for them, and re-layouts  4.36 us
    pallas_call x1, Pallas kernels, gather_sources(): pl.pallas_call(pick_kernel, out_shape=jax.ShapeDtypeStruct((2, BLK, A_SLO...  2.45 us
  transfers between devices with their start and end apart: 25, of which 14 were waited for; matrix products, arithmetic and copies ran while one was open for 4% of the time, Pallas kernels for 20%

profile of v3, /device:TPU:6, one launch (start us, length us, event | category | flops | bytes accessed | tf_op | source)
XLA Modules:
  0.0 96.5 jit_solution(16378425791976214623)
XLA Ops:
  0.0 0.9 copy-done
  1.0 3.3 %collective-permute-start.2 = (bf16[128,256]{1,0:T(8,128)(2,1)S(1)}, bf16[128,256]{1,0:T(8,128)(2,1)S(1)}, u32[]{:S(2)}, u32[]{:S(2)}) collective-permute-start(bf16[128,256]{1,0:T(8,128)(2,1)S(1)} %constant_dynamic-slice_fusion), channel_id=1, source_target_pairs={{0,64},{16,80},{32,96},{48,112},{64,128},{80,144},{96,160},{112,17... | collective-permute-start | bytes 196616 | tf_op jit(solution)/shard_map/ppermute | solution.py:26
  4.3 5.4 %collective-permute-start.1 = (bf16[128,256]{1,0:T(8,128)(2,1)S(1)}, bf16[128,256]{1,0:T(8,128)(2,1)S(1)}, u32[]{:S(2)}, u32[]{:S(2)}) collective-permute-start(bf16[128,256]{1,0:T(8,128)(2,1)S(1)} %constant_dynamic-slice_fusion), channel_id=1, source_target_pairs={{0,128},{16,144},{32,160},{48,176},{64,192},{80,208},{96,224},{112... | collective-permute-start | bytes 196616 | tf_op jit(solution)/shard_map/ppermute | solution.py:26
  9.7 2.7 %collective-permute-start = (bf16[128,256]{1,0:T(8,128)(2,1)S(1)}, bf16[128,256]{1,0:T(8,128)(2,1)S(1)}, u32[]{:S(2)}, u32[]{:S(2)}) collective-permute-start(bf16[128,256]{1,0:T(8,128)(2,1)S(1)} %constant_dynamic-slice_fusion), channel_id=1, source_target_pairs={{0,192},{16,208},{32,224},{48,240},{64,0},{80,16},{96,32},{112,48}... | collective-permute-start | bytes 196616 | tf_op jit(solution)/shard_map/ppermute | solution.py:26
  12.4 1.4 %collective-permute-done.1 = bf16[128,256]{1,0:T(8,128)(2,1)S(1)} collective-permute-done((bf16[128,256]{1,0:T(8,128)(2,1)S(1)}, bf16[128,256]{1,0:T(8,128)(2,1)S(1)}, u32[]{:S(2)}, u32[]{:S(2)}) %collective-permute-start.1) | collective-permute-done | bytes 65568 | tf_op jit(solution)/shard_map/ppermute | solution.py:26
  13.8 2.8 %collective-permute-done = bf16[128,256]{1,0:T(8,128)(2,1)S(1)} collective-permute-done((bf16[128,256]{1,0:T(8,128)(2,1)S(1)}, bf16[128,256]{1,0:T(8,128)(2,1)S(1)}, u32[]{:S(2)}, u32[]{:S(2)}) %collective-permute-start) | collective-permute-done | bytes 65568 | tf_op jit(solution)/shard_map/ppermute | solution.py:26
  17.4 0.8 collective-permute-start.3
  18.2 2.4 %collective-permute-start.4 = (bf16[4,128,256]{2,1,0:T(8,128)(2,1)}, bf16[4,128,256]{2,1,0:T(8,128)(2,1)}, u32[]{:S(2)}, u32[]{:S(2)}) collective-permute-start(bf16[4,128,256]{2,1,0:T(8,128)(2,1)} %pad_maximum_fusion.own_ref), channel_id=1, source_target_pairs={{0,16},{16,32},{32,48},{48,0},{64,80},{80,96},{96,112},{112,64},{1... | collective-permute-start | bytes 786440 | tf_op jit(solution)/shard_map/ppermute | solution.py:26
  20.6 0.8 copy.10
  21.4 0.8 copy.11
  22.3 1.9 %copy-done.1 = bf16[16,1,6,128,128]{4,3,2,1,0:T(8,128)(2,1)S(1)} copy-done((bf16[16,1,6,128,128]{4,3,2,1,0:T(8,128)(2,1)S(1)}, bf16[16,1,6,128,128]{4,3,2,1,0:T(8,128)(2,1)}, u32[]{:S(2)}) %copy-start.1) | copy-done | bytes 3145752
  24.2 1.0 %shard_map.73.a_ref = bf16[768,2048]{1,0:T(8,128)(2,1)S(1)} custom-call(bf16[16,1,6,128,128]{4,3,2,1,0:T(8,128)(2,1)S(1)} %copy-done.1), custom_call_target="tpu_custom_call" | custom-call | bytes 6291456 | tf_op jit(solution)/shard_map/pallas_call | solution.py:210
  25.3 1.8 %collective-permute-done.3.after_ref = bf16[4,128,256]{2,1,0:T(8,128)(2,1)} collective-permute-done((bf16[4,128,256]{2,1,0:T(8,128)(2,1)}, bf16[4,128,256]{2,1,0:T(8,128)(2,1)}, u32[]{:S(2)}, u32[]{:S(2)}) %collective-permute-start.3) | collective-permute-done | bytes 262176 | tf_op jit(solution)/shard_map/ppermute | solution.py:26
  27.1 0.9 slice.8
  28.0 3.0 %collective-permute-start.5 = (bf16[2,128,256]{2,1,0:T(8,128)(2,1)S(1)}, bf16[2,128,256]{2,1,0:T(8,128)(2,1)S(1)}, u32[]{:S(2)}, u32[]{:S(2)}) collective-permute-start(bf16[2,128,256]{2,1,0:T(8,128)(2,1)S(1)} %slice.8), channel_id=1, source_target_pairs={{0,16},{16,32},{32,48},{48,0},{64,80},{80,96},{96,112},{112,64},{1... | collective-permute-start | bytes 393224 | tf_op jit(solution)/shard_map/ppermute | solution.py:26
  31.1 0.9 slice.7
  32.1 1.5 %collective-permute-done.5.far_low_ref = bf16[2,128,256]{2,1,0:T(8,128)(2,1)S(1)} collective-permute-done((bf16[2,128,256]{2,1,0:T(8,128)(2,1)S(1)}, bf16[2,128,256]{2,1,0:T(8,128)(2,1)S(1)}, u32[]{:S(2)}, u32[]{:S(2)}) %collective-permute-start.5) | collective-permute-done | bytes 131104 | tf_op jit(solution)/shard_map/ppermute | solution.py:26
  33.6 4.6 %collective-permute-done.6.far_high_ref = bf16[2,128,256]{2,1,0:T(8,128)(2,1)S(1)} collective-permute-done((bf16[2,128,256]{2,1,0:T(8,128)(2,1)S(1)}, bf16[2,128,256]{2,1,0:T(8,128)(2,1)S(1)}, u32[]{:S(2)}, u32[]{:S(2)}) %collective-permute-start.6) | collective-permute-done | bytes 131104 | tf_op jit(solution)/shard_map/ppermute | solution.py:26
  38.2 2.5 %shard_map.74.rest_0_ = bf16[2,128,768]{2,1,0:T(8,128)(2,1)} custom-call(s32[63]{0:T(128)S(1)} %concatenate.3.meta_ref, bf16[4,128,256]{2,1,0:T(8,128)(2,1)} %pad_maximum_fusion.own_ref, bf16[4,128,256]{2,1,0:T(8,128)(2,1)} %collective-permute-done.3.after_ref, bf16[4,128,256]{2,1,0:T(8,128)(2,1)} %collective-permute-done.4.before_ref, ...), custom_call_target="tpu_custom_call" | custom-call | tf_op jit(solution)/shard_map/pallas_call | solution.py:233
  40.7 3.0 %collective-permute-start.8 = (bf16[2,128,768]{2,1,0:T(8,128)(2,1)}, bf16[2,128,768]{2,1,0:T(8,128)(2,1)}, u32[]{:S(2)}, u32[]{:S(2)}) collective-permute-start(bf16[2,128,768]{2,1,0:T(8,128)(2,1)} %shard_map.74.rest_0_), channel_id=1, source_target_pairs={{0,3},{1,0},{2,1},{3,2},{4,7},{5,4},{6,5},{7,6},{8,11},{9,8},{10,9... | collective-permute-start | bytes 1179656 | tf_op jit(solution)/shard_map/ppermute | solution.py:26
  43.7 6.2 %collective-permute-done.8.rest_2_ = bf16[2,128,768]{2,1,0:T(8,128)(2,1)} collective-permute-done((bf16[2,128,768]{2,1,0:T(8,128)(2,1)}, bf16[2,128,768]{2,1,0:T(8,128)(2,1)}, u32[]{:S(2)}, u32[]{:S(2)}) %collective-permute-start.8) | collective-permute-done | bytes 393248 | tf_op jit(solution)/shard_map/ppermute | solution.py:26
  50.0 3.4 %collective-permute-done.10.rest_4_ = bf16[2,128,768]{2,1,0:T(8,128)(2,1)} collective-permute-done((bf16[2,128,768]{2,1,0:T(8,128)(2,1)}, bf16[2,128,768]{2,1,0:T(8,128)(2,1)}, u32[]{:S(2)}, u32[]{:S(2)}) %collective-permute-start.10) | collective-permute-done | bytes 393248 | tf_op jit(solution)/shard_map/ppermute | solution.py:26
  53.9 1.0 %broadcast_select_fusion = bf16[2,128,768]{2,1,0:T(8,128)(2,1)S(1)} fusion(bf16[2,128,768]{2,1,0:T(8,128)(2,1)} %collective-permute-done.10.rest_4_, bf16[2,128,768]{2,1,0:T(8,128)(2,1)} %collective-permute-done.8.rest_2_, pred[]{:T(512)S(6)} %eq.5), kind=kLoop, calls=%fused_computation | loop fusion | flops 196608 | bytes 1179649 | tf_op jit(solution)/shard_map/jit(_where)/select_n | solution.py:263
  55.3 3.2 %collective-permute-start.15 = (bf16[2,128,768]{2,1,0:T(8,128)(2,1)}, bf16[2,128,768]{2,1,0:T(8,128)(2,1)S(1)}, u32[]{:S(2)}, u32[]{:S(2)}) collective-permute-start(bf16[2,128,768]{2,1,0:T(8,128)(2,1)} %collective-permute-done.12.rest_6_), channel_id=1, source_target_pairs={{0,3},{1,0},{2,1},{3,2},{4,5},{5,6},{6,7},{7,4},{8,11},{9,8},{10,9... | collective-permute-start | bytes 1179656 | tf_op jit(solution)/shard_map/ppermute | solution.py:26
  58.5 11.0 %shard_map.75.rest_6_ = f32[8,128,128]{2,1,0:T(8,128)S(1)} custom-call(s32[63]{0:T(128)S(1)} %concatenate.3.meta_ref, bf16[768,2048]{1,0:T(8,128)(2,1)S(1)} %shard_map.73.a_ref, bf16[16,8,3,128,128]{4,3,2,1,0:T(8,128)(2,1)} %b_ref.5, bf16[2,128,768]{2,1,0:T(8,128)(2,1)} %shard_map.74.rest_0_, bf16[2,128,768]{2,1,0:T(8,128)(2,1)} %collective-permute-done.7.rest_1_, ...), custom_call_target="tpu_custom_call" | custom-call | flops 5637144576 | bytes 9437184 | tf_op jit(solution)/shard_map/pallas_call | solution.py:189
  70.3 1.1 %collective-permute-done.17.rest_1_ = bf16[2,128,768]{2,1,0:T(8,128)(2,1)S(1)} collective-permute-done((bf16[2,128,768]{2,1,0:T(8,128)(2,1)S(1)}, bf16[2,128,768]{2,1,0:T(8,128)(2,1)S(1)}, u32[]{:S(2)}, u32[]{:S(2)}) %collective-permute-start.17) | collective-permute-done | bytes 393248 | tf_op jit(solution)/shard_map/ppermute | solution.py:26
  72.5 7.3 %shard_map.76.rest_2_ = f32[8,128,128]{2,1,0:T(8,128)S(1)} custom-call(s32[63]{0:T(128)S(1)} %concatenate.3.meta_ref, bf16[768,2048]{1,0:T(8,128)(2,1)S(1)} %shard_map.73.a_ref, bf16[16,8,3,128,128]{4,3,2,1,0:T(8,128)(2,1)} %b_ref.5, bf16[2,128,768]{2,1,0:T(8,128)(2,1)S(1)} %collective-permute-done.14.rest_0_, ...), custom_call_target="tpu_custom_call" | custom-call | flops 4227858432 | bytes 7864320 | tf_op jit(solution)/shard_map/pallas_call | solution.py:189
  80.0 1.6 %collective-permute-done.21.rest_1_ = bf16[2,128,768]{2,1,0:T(8,128)(2,1)S(1)} collective-permute-done((bf16[2,128,768]{2,1,0:T(8,128)(2,1)S(1)}, bf16[2,128,768]{2,1,0:T(8,128)(2,1)S(1)}, u32[]{:S(2)}, u32[]{:S(2)}) %collective-permute-start.21) | collective-permute-done | bytes 393248 | tf_op jit(solution)/shard_map/ppermute | solution.py:26
  81.6 4.3 %shard_map.77 = (f32[128,256]{1,0:T(8,128)S(1)}, bf16[128,256]{1,0:T(8,128)(2,1)S(1)}, bf16[128,256]{1,0:T(8,128)(2,1)S(1)}, bf16[128,256]{1,0:T(8,128)(2,1)S(1)}) custom-call(s32[63]{0:T(128)S(1)} %concatenate.3.meta_ref, bf16[768,2048]{1,0:T(8,128)(2,1)S(1)} %shard_map.73.a_ref, bf16[16,8,3,128,128]{4,3,2,1,0:T(8,128)(2,1)} %b_ref.5, ...), custom_call_target="tpu_custom_call" | custom-call | flops 1409286144 | bytes 4718592 | tf_op jit(solution)/shard_map/pallas_call | solution.py:189
  85.9 3.3 %collective-permute-start.24 = (bf16[128,256]{1,0:T(8,128)(2,1)S(1)}, bf16[128,256]{1,0:T(8,128)(2,1)S(1)}, u32[]{:S(2)}, u32[]{:S(2)}) collective-permute-start(bf16[128,256]{1,0:T(8,128)(2,1)S(1)} %get-tuple-element.30), channel_id=1, source_target_pairs={{0,3},{1,0},{2,1},{3,2},{4,7},{5,4},{6,5},{7,6},{8,11},{9,8},{10,9... | collective-permute-start | bytes 196616 | tf_op jit(solution)/shard_map/ppermute | solution.py:26
  90.1 2.1 %collective-permute-done.24 = bf16[128,256]{1,0:T(8,128)(2,1)S(1)} collective-permute-done((bf16[128,256]{1,0:T(8,128)(2,1)S(1)}, bf16[128,256]{1,0:T(8,128)(2,1)S(1)}, u32[]{:S(2)}, u32[]{:S(2)}) %collective-permute-start.24) | collective-permute-done | bytes 65568 | tf_op jit(solution)/shard_map/ppermute | solution.py:26
  92.3 3.0 %collective-permute-done.23 = bf16[128,256]{1,0:T(8,128)(2,1)S(1)} collective-permute-done((bf16[128,256]{1,0:T(8,128)(2,1)S(1)}, bf16[128,256]{1,0:T(8,128)(2,1)S(1)}, u32[]{:S(2)}, u32[]{:S(2)}) %collective-permute-start.23) | collective-permute-done | bytes 65568 | tf_op jit(solution)/shard_map/ppermute | solution.py:26
  (43 shorter events, 6.2 us)
Async XLA Ops:
  0.0 1.0 copy-start
  1.0 11.4 %collective-permute-start.2 = (bf16[128,256]{1,0:T(8,128)(2,1)S(1)}, bf16[128,256]{1,0:T(8,128)(2,1)S(1)}, u32[]{:S(2)}, u32[]{:S(2)}) collective-permute-start(bf16[128,256]{1,0:T(8,128)(2,1)S(1)} %constant_dynamic-slice_fusion), channel_id=1, source_target_pairs={{0,64},{16,80},{32,96},{48,112},{64,128},{80,144},{96,160},{112,17... | collective-permute-start | bytes 196616 | tf_op jit(solution)/shard_map/ppermute | solution.py:26
  4.3 9.5 %collective-permute-start.1 = (bf16[128,256]{1,0:T(8,128)(2,1)S(1)}, bf16[128,256]{1,0:T(8,128)(2,1)S(1)}, u32[]{:S(2)}, u32[]{:S(2)}) collective-permute-start(bf16[128,256]{1,0:T(8,128)(2,1)S(1)} %constant_dynamic-slice_fusion), channel_id=1, source_target_pairs={{0,128},{16,144},{32,160},{48,176},{64,192},{80,208},{96,224},{112... | collective-permute-start | bytes 196616 | tf_op jit(solution)/shard_map/ppermute | solution.py:26
  9.7 6.9 %collective-permute-start = (bf16[128,256]{1,0:T(8,128)(2,1)S(1)}, bf16[128,256]{1,0:T(8,128)(2,1)S(1)}, u32[]{:S(2)}, u32[]{:S(2)}) collective-permute-start(bf16[128,256]{1,0:T(8,128)(2,1)S(1)} %constant_dynamic-slice_fusion), channel_id=1, source_target_pairs={{0,192},{16,208},{32,224},{48,240},{64,0},{80,16},{96,32},{112,48}... | collective-permute-start | bytes 196616 | tf_op jit(solution)/shard_map/ppermute | solution.py:26
  17.4 9.7 %collective-permute-start.3 = (bf16[4,128,256]{2,1,0:T(8,128)(2,1)}, bf16[4,128,256]{2,1,0:T(8,128)(2,1)}, u32[]{:S(2)}, u32[]{:S(2)}) collective-permute-start(bf16[4,128,256]{2,1,0:T(8,128)(2,1)} %pad_maximum_fusion.own_ref), channel_id=1, source_target_pairs={{0,48},{16,0},{32,16},{48,32},{64,112},{80,64},{96,80},{112,96},{1... | collective-permute-start | bytes 786440 | tf_op jit(solution)/shard_map/ppermute | solution.py:26
  18.2 8.9 %collective-permute-start.4 = (bf16[4,128,256]{2,1,0:T(8,128)(2,1)}, bf16[4,128,256]{2,1,0:T(8,128)(2,1)}, u32[]{:S(2)}, u32[]{:S(2)}) collective-permute-start(bf16[4,128,256]{2,1,0:T(8,128)(2,1)} %pad_maximum_fusion.own_ref), channel_id=1, source_target_pairs={{0,16},{16,32},{32,48},{48,0},{64,80},{80,96},{96,112},{112,64},{1... | collective-permute-start | bytes 786440 | tf_op jit(solution)/shard_map/ppermute | solution.py:26
  22.3 1.9 %copy-start.1 = (bf16[16,1,6,128,128]{4,3,2,1,0:T(8,128)(2,1)S(1)}, bf16[16,1,6,128,128]{4,3,2,1,0:T(8,128)(2,1)}, u32[]{:S(2)}) copy-start(bf16[16,1,6,128,128]{4,3,2,1,0:T(8,128)(2,1)} %a_ref.1) | copy-start | bytes 9437188
  24.2 1.0 %copy-start.2 = (s32[1,6]{1,0:T(1,128)S(1)}, s32[1,6]{1,0:T(1,128)}, u32[]{:S(2)}) copy-start(s32[1,6]{1,0:T(1,128)} %param.9) | copy-start | bytes 76
  24.2 1.0 %copy-start.3 = (s32[1,6]{1,0:T(1,128)S(1)}, s32[1,6]{1,0:T(1,128)}, u32[]{:S(2)}) copy-start(s32[1,6]{1,0:T(1,128)} %param.10) | copy-start | bytes 76
  28.0 5.6 %collective-permute-start.5 = (bf16[2,128,256]{2,1,0:T(8,128)(2,1)S(1)}, bf16[2,128,256]{2,1,0:T(8,128)(2,1)S(1)}, u32[]{:S(2)}, u32[]{:S(2)}) collective-permute-start(bf16[2,128,256]{2,1,0:T(8,128)(2,1)S(1)} %slice.8), channel_id=1, source_target_pairs={{0,16},{16,32},{32,48},{48,0},{64,80},{80,96},{96,112},{112,64},{1... | collective-permute-start | bytes 393224 | tf_op jit(solution)/shard_map/ppermute | solution.py:26
  32.0 6.3 %collective-permute-start.6 = (bf16[2,128,256]{2,1,0:T(8,128)(2,1)S(1)}, bf16[2,128,256]{2,1,0:T(8,128)(2,1)S(1)}, u32[]{:S(2)}, u32[]{:S(2)}) collective-permute-start(bf16[2,128,256]{2,1,0:T(8,128)(2,1)S(1)} %slice.7), channel_id=1, source_target_pairs={{0,48},{16,0},{32,16},{48,32},{64,112},{80,64},{96,80},{112,96},{1... | collective-permute-start | bytes 393224 | tf_op jit(solution)/shard_map/ppermute | solution.py:26
  40.7 9.3 %collective-permute-start.8 = (bf16[2,128,768]{2,1,0:T(8,128)(2,1)}, bf16[2,128,768]{2,1,0:T(8,128)(2,1)}, u32[]{:S(2)}, u32[]{:S(2)}) collective-permute-start(bf16[2,128,768]{2,1,0:T(8,128)(2,1)} %shard_map.74.rest_0_), channel_id=1, source_target_pairs={{0,3},{1,0},{2,1},{3,2},{4,7},{5,4},{6,5},{7,6},{8,11},{9,8},{10,9... | collective-permute-start | bytes 1179656 | tf_op jit(solution)/shard_map/ppermute | solution.py:26
  43.7 9.7 %collective-permute-start.10 = (bf16[2,128,768]{2,1,0:T(8,128)(2,1)}, bf16[2,128,768]{2,1,0:T(8,128)(2,1)}, u32[]{:S(2)}, u32[]{:S(2)}) collective-permute-start(bf16[2,128,768]{2,1,0:T(8,128)(2,1)} %shard_map.74.rest_0_), channel_id=1, source_target_pairs={{0,1},{1,2},{2,3},{3,0},{4,5},{5,6},{6,7},{7,4},{8,9},{9,10},{10,1... | collective-permute-start | bytes 1179656 | tf_op jit(solution)/shard_map/ppermute | solution.py:26
  43.7 9.7 %collective-permute-start.12 = (bf16[2,128,768]{2,1,0:T(8,128)(2,1)}, bf16[2,128,768]{2,1,0:T(8,128)(2,1)}, u32[]{:S(2)}, u32[]{:S(2)}) collective-permute-start(bf16[2,128,768]{2,1,0:T(8,128)(2,1)} %shard_map.74.rest_0_), channel_id=1, source_target_pairs={{0,8},{4,12},{8,0},{12,4},{1,9},{5,13},{9,1},{13,5},{2,10},{6,14},... | collective-permute-start | bytes 1179656 | tf_op jit(solution)/shard_map/ppermute | solution.py:26
  43.7 11.5 %collective-permute-start.7 = (bf16[2,128,768]{2,1,0:T(8,128)(2,1)}, bf16[2,128,768]{2,1,0:T(8,128)(2,1)}, u32[]{:S(2)}, u32[]{:S(2)}) collective-permute-start(bf16[2,128,768]{2,1,0:T(8,128)(2,1)} %shard_map.74.rest_0_), channel_id=1, source_target_pairs={{0,4},{4,0},{8,12},{12,8},{1,5},{5,1},{9,13},{13,9},{2,6},{6,2},{1... | collective-permute-start | bytes 1179656 | tf_op jit(solution)/shard_map/ppermute | solution.py:26
  50.0 5.4 %collective-permute-start.9 = (bf16[2,128,768]{2,1,0:T(8,128)(2,1)}, bf16[2,128,768]{2,1,0:T(8,128)(2,1)}, u32[]{:S(2)}, u32[]{:S(2)}) collective-permute-start(bf16[2,128,768]{2,1,0:T(8,128)(2,1)} %collective-permute-done.8.rest_2_), channel_id=1, source_target_pairs={{0,4},{4,0},{8,12},{12,8},{1,5},{5,1},{9,13},{13,9},{2,6},{6,2},{1... | collective-permute-start | bytes 1179656 | tf_op jit(solution)/shard_map/ppermute | solution.py:26
  53.4 5.1 %collective-permute-start.11 = (bf16[2,128,768]{2,1,0:T(8,128)(2,1)}, bf16[2,128,768]{2,1,0:T(8,128)(2,1)}, u32[]{:S(2)}, u32[]{:S(2)}) collective-permute-start(bf16[2,128,768]{2,1,0:T(8,128)(2,1)} %collective-permute-done.10.rest_4_), channel_id=1, source_target_pairs={{0,4},{4,0},{8,12},{12,8},{1,5},{5,1},{9,13},{13,9},{2,6},{6,2},{1... | collective-permute-start | bytes 1179656 | tf_op jit(solution)/shard_map/ppermute | solution.py:26
  53.4 5.1 %collective-permute-start.13 = (bf16[2,128,768]{2,1,0:T(8,128)(2,1)}, bf16[2,128,768]{2,1,0:T(8,128)(2,1)}, u32[]{:S(2)}, u32[]{:S(2)}) collective-permute-start(bf16[2,128,768]{2,1,0:T(8,128)(2,1)} %collective-permute-done.12.rest_6_), channel_id=1, source_target_pairs={{0,4},{4,0},{8,12},{12,8},{1,5},{5,1},{9,13},{13,9},{2,6},{6,2},{1... | collective-permute-start | bytes 1179656 | tf_op jit(solution)/shard_map/ppermute | solution.py:26
  54.9 14.6 %collective-permute-start.14 = (bf16[2,128,768]{2,1,0:T(8,128)(2,1)S(1)}, bf16[2,128,768]{2,1,0:T(8,128)(2,1)S(1)}, u32[]{:S(2)}, u32[]{:S(2)}) collective-permute-start(bf16[2,128,768]{2,1,0:T(8,128)(2,1)S(1)} %broadcast_select_fusion), channel_id=1, source_target_pairs={{0,1},{1,2},{2,3},{3,0},{4,7},{5,4},{6,5},{7,6},{8,9},{9,10},{10,1... | collective-permute-start | bytes 1179656 | tf_op jit(solution)/shard_map/ppermute | solution.py:26
  55.2 14.3 %collective-permute-start.16 = (bf16[2,128,768]{2,1,0:T(8,128)(2,1)S(1)}, bf16[2,128,768]{2,1,0:T(8,128)(2,1)S(1)}, u32[]{:S(2)}, u32[]{:S(2)}) collective-permute-start(bf16[2,128,768]{2,1,0:T(8,128)(2,1)S(1)} %broadcast_select_fusion), channel_id=1, source_target_pairs={{0,8},{4,12},{8,0},{12,4},{1,9},{5,13},{9,1},{13,5},{2,10},{6,14},... | collective-permute-start | bytes 1179656 | tf_op jit(solution)/shard_map/ppermute | solution.py:26
  55.3 14.2 %collective-permute-start.15 = (bf16[2,128,768]{2,1,0:T(8,128)(2,1)}, bf16[2,128,768]{2,1,0:T(8,128)(2,1)S(1)}, u32[]{:S(2)}, u32[]{:S(2)}) collective-permute-start(bf16[2,128,768]{2,1,0:T(8,128)(2,1)} %collective-permute-done.12.rest_6_), channel_id=1, source_target_pairs={{0,3},{1,0},{2,1},{3,2},{4,5},{5,6},{6,7},{7,4},{8,11},{9,8},{10,9... | collective-permute-start | bytes 1179656 | tf_op jit(solution)/shard_map/ppermute | solution.py:26
  69.6 1.8 %collective-permute-start.17 = (bf16[2,128,768]{2,1,0:T(8,128)(2,1)S(1)}, bf16[2,128,768]{2,1,0:T(8,128)(2,1)S(1)}, u32[]{:S(2)}, u32[]{:S(2)}) collective-permute-start(bf16[2,128,768]{2,1,0:T(8,128)(2,1)S(1)} %collective-permute-done.14.rest_0_), channel_id=1, source_target_pairs={{0,4},{4,0},{8,12},{12,8},{1,5},{5,1},{9,13},{13,9},{2,6},{6,2},{1... | collective-permute-start | bytes 1179656 | tf_op jit(solution)/shard_map/ppermute | solution.py:26
  69.7 2.3 %collective-permute-start.18 = (bf16[2,128,768]{2,1,0:T(8,128)(2,1)S(1)}, bf16[2,128,768]{2,1,0:T(8,128)(2,1)S(1)}, u32[]{:S(2)}, u32[]{:S(2)}) collective-permute-start(bf16[2,128,768]{2,1,0:T(8,128)(2,1)S(1)} %collective-permute-done.15.rest_2_), channel_id=1, source_target_pairs={{0,4},{4,0},{8,12},{12,8},{1,5},{5,1},{9,13},{13,9},{2,6},{6,2},{1... | collective-permute-start | bytes 1179656 | tf_op jit(solution)/shard_map/ppermute | solution.py:26
  70.2 2.3 %collective-permute-start.19 = (bf16[2,128,768]{2,1,0:T(8,128)(2,1)S(1)}, bf16[2,128,768]{2,1,0:T(8,128)(2,1)S(1)}, u32[]{:S(2)}, u32[]{:S(2)}) collective-permute-start(bf16[2,128,768]{2,1,0:T(8,128)(2,1)S(1)} %collective-permute-done.16.rest_4_), channel_id=1, source_target_pairs={{0,4},{4,0},{8,12},{12,8},{1,5},{5,1},{9,13},{13,9},{2,6},{6,2},{1... | collective-permute-start | bytes 1179656 | tf_op jit(solution)/shard_map/ppermute | solution.py:26
  70.3 9.5 %collective-permute-start.20 = (bf16[2,128,768]{2,1,0:T(8,128)(2,1)S(1)}, bf16[2,128,768]{2,1,0:T(8,128)(2,1)S(1)}, u32[]{:S(2)}, u32[]{:S(2)}) collective-permute-start(bf16[2,128,768]{2,1,0:T(8,128)(2,1)S(1)} %collective-permute-done.16.rest_4_), channel_id=1, source_target_pairs={{0,1},{1,2},{2,3},{3,0},{4,7},{5,4},{6,5},{7,6},{8,9},{9,10},{10,1... | collective-permute-start | bytes 1179656 | tf_op jit(solution)/shard_map/ppermute | solution.py:26
  79.8 1.8 %collective-permute-start.21 = (bf16[2,128,768]{2,1,0:T(8,128)(2,1)S(1)}, bf16[2,128,768]{2,1,0:T(8,128)(2,1)S(1)}, u32[]{:S(2)}, u32[]{:S(2)}) collective-permute-start(bf16[2,128,768]{2,1,0:T(8,128)(2,1)S(1)} %collective-permute-done.20.rest_0_), channel_id=1, source_target_pairs={{0,4},{4,0},{8,12},{12,8},{1,5},{5,1},{9,13},{13,9},{2,6},{6,2},{1... | collective-permute-start | bytes 1179656 | tf_op jit(solution)/shard_map/ppermute | solution.py:26
  85.9 6.4 %collective-permute-start.24 = (bf16[128,256]{1,0:T(8,128)(2,1)S(1)}, bf16[128,256]{1,0:T(8,128)(2,1)S(1)}, u32[]{:S(2)}, u32[]{:S(2)}) collective-permute-start(bf16[128,256]{1,0:T(8,128)(2,1)S(1)} %get-tuple-element.30), channel_id=1, source_target_pairs={{0,3},{1,0},{2,1},{3,2},{4,7},{5,4},{6,5},{7,6},{8,11},{9,8},{10,9... | collective-permute-start | bytes 196616 | tf_op jit(solution)/shard_map/ppermute | solution.py:26
  89.2 6.1 %collective-permute-start.23 = (bf16[128,256]{1,0:T(8,128)(2,1)S(1)}, bf16[128,256]{1,0:T(8,128)(2,1)S(1)}, u32[]{:S(2)}, u32[]{:S(2)}) collective-permute-start(bf16[128,256]{1,0:T(8,128)(2,1)S(1)} %get-tuple-element.29), channel_id=1, source_target_pairs={{0,2},{1,3},{2,0},{3,1},{4,6},{5,7},{6,4},{7,5},{8,10},{9,11},{10,... | collective-permute-start | bytes 196616 | tf_op jit(solution)/shard_map/ppermute | solution.py:26
  89.8 6.0 %collective-permute-start.22 = (bf16[128,256]{1,0:T(8,128)(2,1)S(1)}, bf16[128,256]{1,0:T(8,128)(2,1)S(1)}, u32[]{:S(2)}, u32[]{:S(2)}) collective-permute-start(bf16[128,256]{1,0:T(8,128)(2,1)S(1)} %get-tuple-element.28), channel_id=1, source_target_pairs={{0,1},{1,2},{2,3},{3,0},{4,5},{5,6},{6,7},{7,4},{8,9},{9,10},{10,1... | collective-permute-start | bytes 196616 | tf_op jit(solution)/shard_map/ppermute | solution.py:26

commit v4 on v3

v4 whole, which is shorter than its diff:
```python
import functools

import jax
import jax.numpy as jnp
from jax import lax
from jax.experimental import pallas as pl
from jax.experimental.pallas import tpu as pltpu
from jax.sharding import PartitionSpec as P

BLK = 128
VECTORS_PER_GROUP = 4
WIDE, NARROW = 4, 2
X_SIZE = 4
A_SLOTS, B_SLOTS, B_BLOCKS = 6, 3, 8
PAIRS = B_SLOTS * B_BLOCKS
ALPHA, BETA, CHOL, A_SOURCE = 0, 1, 2, 3
A_SIGN = A_SOURCE + A_SLOTS
B_SOURCE = A_SIGN + A_SLOTS
B_SIGN = B_SOURCE + PAIRS
OTHER = 2 * PAIRS
ARRIVAL = 0x67521430
FIRST_UNITS = (0, 1, 4, 7, 8)
KERNELS = len(FIRST_UNITS) - 1
PLAN = 64
SMEM = pl.BlockSpec(memory_space=pltpu.SMEM)
VMEM = pl.BlockSpec(memory_space=pltpu.VMEM)
HBM = pl.BlockSpec(memory_space=pltpu.HBM)


def shifted(value, axis, size, moves_to):
    return lax.ppermute(value, axis, [(i, moves_to(i)) for i in range(size)])


def choose(index, low, high, act):
    if high - low == 1:
        act(low)
        return
    middle = (low + high) // 2

    @pl.when(index < middle)
    def _():
        choose(index, low, middle, act)

    @pl.when(index >= middle)
    def _():
        choose(index, middle, high, act)


def flip_kernel(a_hbm, out_ref, a_buf, sems):
    parts = sems.shape[0]
    size = a_buf.shape[0] // parts
    copies = [
        pltpu.make_async_copy(a_hbm.at[pl.ds(p * size, size)], a_buf.at[pl.ds(p * size, size)], sems.at[p])
        for p in range(parts)
    ]
    for copy in copies:
        copy.start()
    for p, copy in enumerate(copies):
        copy.wait()
        for q in range(p * size, (p + 1) * size):
            for k in range(A_SLOTS):
                out_ref[k * BLK : (k + 1) * BLK, q * BLK : (q + 1) * BLK] = a_buf[q, 0, k].T


def plan_kernel(meta_ref, plan_ref):
    beta, chol = meta_ref[BETA], meta_ref[CHOL]
    core = beta & 1
    counts = [jnp.int32(0)] * KERNELS
    for pair in range(2 * PAIRS):
        base = OTHER if pair >= PAIRS else 0
        m = meta_ref[B_SOURCE + base + pair % PAIRS]
        sign = meta_ref[B_SIGN + base + pair % PAIRS]
        owner = m >> 3
        dy = ((m >> 1) - chol) & 3
        dy = jnp.where(core != 0, (4 - dy) & 3, dy)
        unit = (jnp.int32(ARRIVAL) >> (4 * (((owner ^ beta) & 2) * 2 + dy))) & 7
        live = (sign != 0) & ((owner & 1) == core)
        for index in range(KERNELS):
            low, high = FIRST_UNITS[index], FIRST_UNITS[index + 1]
            entry = pair + ((unit - low) << 6) + ((m & 1) << 9) + ((sign + 1) << 10)
            plan_ref[index * PLAN + 1 + counts[index]] = entry
            counts[index] = counts[index] + jnp.where(live & (unit >= low) & (unit < high), 1, 0)
    for index in range(KERNELS):
        plan_ref[index * PLAN] = counts[index]


def pick_kernel(meta_ref, own_ref, back_ref, far_ref, ahead_ref, out_ref):
    alpha = meta_ref[ALPHA]
    core = meta_ref[BETA] & 1
    for k in range(A_SLOTS):
        source = meta_ref[A_SOURCE + k]
        sign = meta_ref[A_SIGN + k].astype(jnp.float32).astype(out_ref.dtype)
        dz = ((source >> 2) - (alpha >> 2)) & 3
        dx = (source - alpha) & 3
        dx = jnp.where(core != 0, (4 - dx) & 3, dx)

        def put(i, k=k, sign=sign, dz=dz):
            for half in range(2):
                block = (own_ref, back_ref, far_ref, ahead_ref)[i][dz, :, half * BLK : (half + 1) * BLK]
                out_ref[half, :, k * BLK : (k + 1) * BLK] = block.T * sign

        choose(dx, 0, X_SIZE, put)


def contract_kernel(index, last, plan_ref, a_ref, b_own, b_other, *rest):
    count_units = FIRST_UNITS[index + 1] - FIRST_UNITS[index]
    units, rest = rest[:count_units], rest[count_units:]
    if index:
        sum_ref, rest = rest[0], rest[1:]
    if last:
        chol_ref, mine_ref, other_ref, acc, c_buf, b_buf, c_sem, b_sem = rest
    else:
        acc, c_buf, b_buf, c_sem, b_sem = rest
    vectors = b_own.shape[0]
    count = plan_ref[index * PLAN]
    wide_steps = count >> 2
    narrow_steps = (count - WIDE * wide_steps + 1) >> 1
    steps = wide_steps + narrow_steps

    def first_of(step):
        return jnp.where(step < wide_steps, WIDE * step, NARROW * step + (WIDE - NARROW) * wide_steps)

    def entry_of(at):
        return plan_ref[index * PLAN + 1 + jnp.minimum(at, count - 1)]

    def c_copy(unit, half, slot, lane):
        return pltpu.make_async_copy(
            unit.at[half], c_buf.at[slot, pl.ds(lane * BLK, BLK)], c_sem.at[slot, lane]
        )

    def b_copy(ref, u, l, slot, lane, part):
        vectors_of = (pl.ds(0, VECTORS_PER_GROUP), pl.ds(VECTORS_PER_GROUP, vectors - VECTORS_PER_GROUP))[part]
        return pltpu.make_async_copy(
            ref.at[vectors_of, u, l], b_buf.at[slot, lane, vectors_of], b_sem.at[slot, lane, part]
        )

    def start_c(step, slot, lanes):
        for lane in lanes:
            entry = entry_of(first_of(step) + lane)
            half = (entry >> 9) & 1
            choose((entry >> 6) & 7, 0, count_units, lambda i: c_copy(units[i], half, slot, lane).start())

    def start_b(step, slot, lanes, part):
        for lane in lanes:
            entry = entry_of(first_of(step) + lane)
            pair = entry & 63
            foreign = pair >= PAIRS
            pair = jnp.where(foreign, pair - PAIRS, pair)
            u = pair // B_SLOTS
            l = pair - u * B_SLOTS

            @pl.when(foreign)
            def _(u=u, l=l, lane=lane):
                b_copy(b_other, u, l, slot, lane, part).start()

            @pl.when(jnp.logical_not(foreign))
            def _(u=u, l=l, lane=lane):
                b_copy(b_own, u, l, slot, lane, part).start()

    def start_step(step, slot):
        def start(lanes):
            start_c(step, slot, lanes)
            for part in range(2):
                start_b(step, slot, lanes, part)

        @pl.when(step < wide_steps)
        def _():
            start(range(WIDE))

        @pl.when((step >= wide_steps) & (step < steps))
        def _():
            start(range(NARROW))

    start_step(0, 0)
    acc[...] = sum_ref[...] if index else jnp.zeros_like(acc)

    def body(width, step, carry):
        slot = step & 1
        start_step(step + 1, 1 - slot)
        for lane in range(width):
            c_copy(units[0], 0, slot, lane).wait()
        sums = [jnp.zeros((BLK, BLK), jnp.float32) for _ in range(width)]
        for group in range(0, vectors, VECTORS_PER_GROUP):
            columns = slice(group * BLK, (group + VECTORS_PER_GROUP) * BLK)
            panel = jnp.dot(
                c_buf[slot, : width * BLK], a_ref[:, columns], preferred_element_type=jnp.float32
            ).astype(jnp.bfloat16)
            if group <= VECTORS_PER_GROUP:
                for lane in range(width):
                    b_copy(b_own, 0, 0, slot, lane, group // VECTORS_PER_GROUP).wait()
            for lane in range(width):
                tiles = [b_buf[slot, lane, group + r] for r in range(VECTORS_PER_GROUP)]
                blocks = [
                    panel[lane * BLK : (lane + 1) * BLK, r * BLK : (r + 1) * BLK]
                    for r in range(VECTORS_PER_GROUP)
                ]
                sums[lane] += jnp.dot(
                    jnp.concatenate(tiles, axis=1),
                    jnp.concatenate(blocks, axis=0),
                    preferred_element_type=jnp.float32,
                )
        for lane in range(width):
            at = first_of(step) + lane
            entry = entry_of(at)
            factor = jnp.where(at < count, (entry >> 10) - 1, 0).astype(jnp.float32)
            acc[(entry & 63) // B_SLOTS] += factor * sums[lane]
        return carry

    lax.fori_loop(0, wide_steps, functools.partial(body, WIDE), 0)
    lax.fori_loop(wide_steps, steps, functools.partial(body, NARROW), 0)
    if last:
        for shift in range(4):
            for half in range(2):
                u = ((chol_ref[0] + shift) & 3) * 2 + half
                lanes = slice(half * BLK, (half + 1) * BLK)
                mine_ref[shift, :, lanes] = acc[u].T
                other_ref[shift, :, lanes] = acc[B_BLOCKS + u].T


def contract(index, plan, a_flipped, b_own, b_other, units, running=None, chol=None):
    vectors, blocks = b_own.shape[:2]
    last = chol is not None
    part = len(units) / 8
    flops = int(part * 2 * (a_flipped.size * blocks * B_SLOTS * BLK + b_own.size * BLK))
    moved = int(part * 2 * b_own.size) + 2 * a_flipped.size
    whole = jax.ShapeDtypeStruct((2 * blocks, BLK, BLK), jnp.float32)
    shares = jax.ShapeDtypeStruct((4, BLK, blocks * BLK // 4), jnp.float32)
    sums = [] if running is None else [running]
    chols = [chol] if last else []
    return pl.pallas_call(
        functools.partial(contract_kernel, index, last),
        out_shape=[shares, shares] if last else whole,
        in_specs=[SMEM, VMEM, HBM, HBM] + [HBM] * len(units) + [VMEM] * len(sums) + [SMEM] * len(chols),
        out_specs=[VMEM, VMEM] if last else VMEM,
        scratch_shapes=[pltpu.VMEM(whole.shape, jnp.float32)] * last
        + [
            pltpu.VMEM((2, WIDE * BLK, A_SLOTS * BLK), jnp.bfloat16),
            pltpu.VMEM((2, WIDE, vectors, BLK, BLK), jnp.bfloat16),
            pltpu.SemaphoreType.DMA((2, WIDE)),
            pltpu.SemaphoreType.DMA((2, WIDE, 2)),
        ],
        compiler_params=pltpu.CompilerParams(vmem_limit_bytes=47 * 1024 * 1024),
        cost_estimate=pl.CostEstimate(flops=flops, bytes_accessed=moved, transcendentals=0),
    )(plan, a_flipped, b_own, b_other, *units, *sums, *chols)


def merge_kernel(mine_ref, arrived_ref, own_ref, *piece_refs):
    own_ref[...] = mine_ref[0] + arrived_ref[0]
    for shift, piece_ref in enumerate(piece_refs, 1):
        piece_ref[...] = (mine_ref[shift] + arrived_ref[shift]).astype(piece_ref.dtype)


def merge(mine, arrived):
    shape = mine.shape[1:]
    return pl.pallas_call(
        merge_kernel,
        out_shape=[jax.ShapeDtypeStruct(shape, jnp.float32)] + [jax.ShapeDtypeStruct(shape, jnp.bfloat16)] * 3,
        in_specs=[VMEM, VMEM],
        out_specs=[VMEM] * 4,
        compiler_params=pltpu.CompilerParams(vmem_limit_bytes=8 * 1024 * 1024),
    )(mine, arrived)


def flip(a_tiles):
    vectors = a_tiles.shape[0]
    return pl.pallas_call(
        flip_kernel,
        out_shape=jax.ShapeDtypeStruct((A_SLOTS * BLK, vectors * BLK), a_tiles.dtype),
        in_specs=[HBM],
        out_specs=VMEM,
        scratch_shapes=[pltpu.VMEM(a_tiles.shape, a_tiles.dtype), pltpu.SemaphoreType.DMA((4,))],
        compiler_params=pltpu.CompilerParams(vmem_limit_bytes=48 * 1024 * 1024),
        cost_estimate=pl.CostEstimate(flops=0, bytes_accessed=4 * a_tiles.size, transcendentals=0),
    )(a_tiles)


def make_plan(meta):
    return pl.pallas_call(
        plan_kernel,
        out_shape=jax.ShapeDtypeStruct((KERNELS * PLAN,), jnp.int32),
        in_specs=[SMEM],
        out_specs=SMEM,
    )(meta)


def gather_sources(meta, quarter, sizes):
    alphas, betas = sizes["alpha"], sizes["beta"]
    zs = alphas // X_SIZE

    def z_from(value, distance):
        return shifted(value, "alpha", alphas, lambda i: (i // X_SIZE - distance) % zs * X_SIZE + i % X_SIZE)

    def by_core(value, sense):
        def moved(i):
            alpha, beta = i // betas, i % betas
            x = (alpha + (sense if beta % 2 == 0 else -sense)) % X_SIZE
            return (alpha // X_SIZE * X_SIZE + x) * betas + beta

        return shifted(value, ("alpha", "beta"), alphas * betas, moved)

    others = [z_from(quarter, distance) for distance in (1, 2, 3)]
    others[1], meta = lax.optimization_barrier((others[1], meta))
    own = jnp.stack([quarter] + others)
    ahead, back = by_core(own, 1), by_core(own, -1)
    ahead, plan = lax.optimization_barrier((ahead, make_plan(meta)))
    far = by_core(ahead, 1)
    unit = pl.pallas_call(
        pick_kernel,
        out_shape=jax.ShapeDtypeStruct((2, BLK, A_SLOTS * BLK), quarter.dtype),
        in_specs=[SMEM] + [VMEM] * 4,
        out_specs=VMEM,
        compiler_params=pltpu.CompilerParams(vmem_limit_bytes=8 * 1024 * 1024),
    )(meta, own, back, far, ahead)
    return plan, unit


def gather_and_contract(plan, chol, unit, a_tiles, b_own, b_other, sizes):
    betas, chols = sizes["beta"], sizes["chol"]

    def z_other(value):
        return shifted(value, "beta", betas, lambda i: i ^ 2)

    def by_core(value, sense):
        def moved(i):
            beta, chol = i // chols, i % chols
            return beta * chols + (chol + (sense if beta % 2 == 0 else -sense)) % chols

        return shifted(value, ("beta", "chol"), betas * chols, moved)

    ahead, across, back = by_core(unit, 1), z_other(unit), by_core(unit, -1)
    tiles = (plan, flip(a_tiles), b_own, b_other)
    running = contract(0, *tiles, [unit])
    running, ahead, across, back = lax.optimization_barrier((running, ahead, across, back))
    middle, far_ahead, far_back = by_core(ahead, 1), z_other(ahead), by_core(across, -1)
    running = contract(1, *tiles, [ahead, across, back], running)
    running, middle, far_back, far_ahead = lax.optimization_barrier((running, middle, far_back, far_ahead))
    far_middle = by_core(far_ahead, 1)
    running = contract(2, *tiles, [middle, far_back, far_ahead], running)
    running, far_middle = lax.optimization_barrier((running, far_middle))
    return contract(3, *tiles, [far_middle], running, chol=chol)


def per_device(sizes, ci_vector, a_tiles, a_source, a_sign, b_tiles, b_source, b_sign):
    betas, chols = sizes["beta"], sizes["chol"]

    def core_other(value):
        return shifted(value, "beta", betas, lambda i: i ^ 1)

    chol = lax.axis_index("chol").astype(jnp.int32)
    width = ci_vector.shape[1] // chols
    quarter = lax.dynamic_slice_in_dim(ci_vector, chol * width, width, axis=1)
    place = jnp.stack([lax.axis_index("alpha"), lax.axis_index("beta"), chol]).astype(jnp.int32)
    pairs = jnp.concatenate([b_source.reshape(-1), b_sign.reshape(-1)])
    meta = jnp.concatenate([place, a_source.reshape(-1), a_sign.reshape(-1), pairs, core_other(pairs)])
    plan, unit = gather_sources(meta, quarter, sizes)
    mine, other = gather_and_contract(plan, chol[None], unit, a_tiles, b_tiles, core_other(b_tiles), sizes)
    own, *pieces = merge(mine, core_other(other))
    for shift, piece in enumerate(pieces, 1):
        own = own + shifted(piece, "chol", chols, lambda i: (i + shift) % chols).astype(jnp.float32)
    return own.astype(jnp.bfloat16)


def solution(mesh):
    placed = (
        P("alpha", "beta"),
        P("chol", "alpha", None, None, None),
        P("alpha", None),
        P("alpha", None),
        P("chol", "beta", None, None, None),
        P("beta", None),
        P("beta", None),
    )
    sizes = dict(mesh.shape)

    def body(*args):
        return per_device(sizes, *args)

    return jax.shard_map(
        body,
        mesh=mesh,
        in_specs=placed,
        out_specs=P("alpha", ("beta", "chol")),
        check_vma=False,
    )
```

time: 96.5 us -> 92.7 us (0.961); the launches traced: 96.5 us -> 94.6 us
  waiting for transfers between devices: 31.4 us -> 23.6 us
  starting transfers between devices: 30 us -> 36.6 us
  Pallas kernels: 26 us -> 28.2 us
  other arithmetic: 2.44 us -> 0.78 us
  local copies, waits for them, and re-layouts: 6.45 us -> 5.18 us
    ppermute x25 -> x19, waiting for transfers between devices: 31.4 us -> 23.6 us  [shifted(): return lax.ppermute(value, axis, [(i, moves_to(i)) for i in range(size)])]
    ppermute x25 -> x19, starting transfers between devices: 30 us -> 36.6 us  [shifted(): return lax.ppermute(value, axis, [(i, moves_to(i)) for i in range(size)])]
    pallas_call x3 -> x6, Pallas kernels: 22.5 us -> 24.8 us  [the longest x4 22.5 us: contract(): pl.pallas_call(functools.partial(contract_kernel, index, last), out_shape...]
    slice x2 -> x0, local copies, waits for them, and re-layouts: 1.83 us -> none  [gather_sources(): far_low, far_high = (x_from(before[:2], 3), x_from(after[2:], 1))]
    pallas_call x1, Pallas kernels: 2.45 us -> 1.07 us  [gather_sources(): pl.pallas_call(pick_kernel, out_shape=jax.ShapeDtypeStruct((2, BLK, A_SLO...]
    pallas_call x1, Pallas kernels: 1 us -> 2.33 us  [flip(): pl.pallas_call(flip_kernel, out_shape=jax.ShapeDtypeStruct((A_SLOTS * BLK...]
    concatenate x1, local copies, waits for them, and re-layouts: 0.08 us -> 1.26 us  [per_device(): jnp.concatenate([place, a_source.reshape(-1), a_sign.reshape(-1), pairs,...]
    select_n x1 -> x0, other arithmetic: 1.04 us -> none  [gather_and_contract(): onward = jnp.where(lax.axis_index('beta') % 2 == 0, before, after)]
  transfers between devices with their start and end apart: 25 -> 19, of which waited for: 14 -> 9; matrix products, arithmetic and copies ran while one was open for 4% -> 3% of each run, Pallas kernels for 20% -> 25%
where the time goes in v4:
time: 92.7 us; the launch traced here: 94.6 us
  starting transfers between devices  36.6 us (39%)
  Pallas kernels  28.2 us (30%)
  waiting for transfers between devices  23.6 us (25%)
  local copies, waits for them, and re-layouts  5.18 us (6%)
    ppermute x19, starting transfers between devices, shifted(): return lax.ppermute(value, axis, [(i, moves_to(i)) for i in range(size)])  36.6 us
    ppermute x19, waiting for transfers between devices, shifted(): return lax.ppermute(value, axis, [(i, moves_to(i)) for i in range(size)])  23.6 us
    pallas_call x4, Pallas kernels, contract(): pl.pallas_call(functools.partial(contract_kernel, index, last), out_shape...  22.5 us
    unnamed x8, local copies, waits for them, and re-layouts  3.72 us
    pallas_call x1, Pallas kernels, flip(): pl.pallas_call(flip_kernel, out_shape=jax.ShapeDtypeStruct((A_SLOTS * BLK...  2.33 us
    pallas_call x1, Pallas kernels, make_plan(): pl.pallas_call(plan_kernel, out_shape=jax.ShapeDtypeStruct((KERNELS * PLA...  2.27 us
  transfers between devices with their start and end apart: 19, of which 9 were waited for; matrix products, arithmetic and copies ran while one was open for 3% of the time, Pallas kernels for 25%

profile of v4, /device:TPU:6, one launch (start us, length us, event | category | flops | bytes accessed | tf_op | source)
XLA Modules:
  0.0 94.6 jit_solution(10529075031649769392)
XLA Ops:
  0.0 0.9 copy-done
  1.0 7.3 %collective-permute-start.1 = (bf16[128,256]{1,0:T(8,128)(2,1)S(1)}, bf16[128,256]{1,0:T(8,128)(2,1)S(1)}, u32[]{:S(2)}, u32[]{:S(2)}) collective-permute-start(bf16[128,256]{1,0:T(8,128)(2,1)S(1)} %constant_dynamic-slice_fusion), channel_id=1, source_target_pairs={{0,128},{16,144},{32,160},{48,176},{64,192},{80,208},{96,224},{112... | collective-permute-start | bytes 196616 | tf_op jit(solution)/shard_map/ppermute | solution.py:31
  8.2 2.9 %collective-permute-start.3 = (bf16[128,256]{1,0:T(8,128)(2,1)S(1)}, bf16[128,256]{1,0:T(8,128)(2,1)S(1)}, u32[]{:S(2)}, u32[]{:S(2)}) collective-permute-start(bf16[128,256]{1,0:T(8,128)(2,1)S(1)} %constant_dynamic-slice_fusion), channel_id=1, source_target_pairs={{0,64},{16,80},{32,96},{48,112},{64,128},{80,144},{96,160},{112,17... | collective-permute-start | bytes 196616 | tf_op jit(solution)/shard_map/ppermute | solution.py:31
  11.2 0.8 copy.10
  12.0 0.8 copy.11
  13.0 6.1 %collective-permute-done.2 = s32[48]{0:T(128)S(1)} collective-permute-done((s32[48]{0:T(128)S(1)}, s32[48]{0:T(128)S(1)}, u32[]{:S(2)}, u32[]{:S(2)}) %collective-permute-start.2) | collective-permute-done | bytes 224 | tf_op jit(solution)/shard_map/ppermute | solution.py:31
  19.1 1.3 %concatenate.8.meta_ref = s32[111]{0:T(128)} concatenate(s32[1]{0:T(128)} %bitcast.2, s32[1]{0:T(128)} %bitcast.3, s32[1]{0:T(128)} %bitcast.4.rest_2_, s32[6]{0:T(128)} %bitcast.13, s32[6]{0:T(128)} %bitcast.14, s32[24]{0:T(128)S(1)} %reshape.14, s32[24]{0:T(128)S(1)} %reshape.15, s32[48]{0:T(128)S(1)} %collective-permute-done.2), dimensions={0} | concatenate | bytes 888 | tf_op jit(solution)/shard_map/concatenate | solution.py:354
  20.4 2.3 %collective-permute-start.4 = (bf16[4,128,256]{2,1,0:T(8,128)(2,1)S(1)}, bf16[4,128,256]{2,1,0:T(8,128)(2,1)S(1)}, u32[]{:S(2)}, u32[]{:S(2)}) collective-permute-start(bf16[4,128,256]{2,1,0:T(8,128)(2,1)S(1)} %pad_maximum_fusion.own_ref), channel_id=1, source_target_pairs={{0,16},{4,52},{8,24},{12,60},{16,32},{20,4},{24,40},{28,12},{32,48... | collective-permute-start | bytes 786440 | tf_op jit(solution)/shard_map/ppermute | solution.py:31
  22.7 2.3 %shard_map.73.plan_ref = s32[256]{0:T(256)} custom-call(s32[111]{0:T(128)} %concatenate.8.meta_ref), custom_call_target="tpu_custom_call" | custom-call | tf_op jit(solution)/shard_map/pallas_call | solution.py:278
  25.0 4.4 %collective-permute-done.4.ahead_ref = bf16[4,128,256]{2,1,0:T(8,128)(2,1)S(1)} collective-permute-done((bf16[4,128,256]{2,1,0:T(8,128)(2,1)S(1)}, bf16[4,128,256]{2,1,0:T(8,128)(2,1)S(1)}, u32[]{:S(2)}, u32[]{:S(2)}) %collective-permute-start.4) | collective-permute-done | bytes 262176 | tf_op jit(solution)/shard_map/ppermute | solution.py:31
  29.5 3.6 %collective-permute-start.7 = (bf16[4,128,256]{2,1,0:T(8,128)(2,1)S(1)}, bf16[4,128,256]{2,1,0:T(8,128)(2,1)S(1)}, u32[]{:S(2)}, u32[]{:S(2)}) collective-permute-start(bf16[4,128,256]{2,1,0:T(8,128)(2,1)S(1)} %collective-permute-done.4.ahead_ref), channel_id=1, source_target_pairs={{0,16},{4,52},{8,24},{12,60},{16,32},{20,4},{24,40},{28,12},{32,48... | collective-permute-start | bytes 786440 | tf_op jit(solution)/shard_map/ppermute | solution.py:31
  33.1 3.9 %collective-permute-done.7.far_ref = bf16[4,128,256]{2,1,0:T(8,128)(2,1)S(1)} collective-permute-done((bf16[4,128,256]{2,1,0:T(8,128)(2,1)S(1)}, bf16[4,128,256]{2,1,0:T(8,128)(2,1)S(1)}, u32[]{:S(2)}, u32[]{:S(2)}) %collective-permute-start.7) | collective-permute-done | bytes 262176 | tf_op jit(solution)/shard_map/ppermute | solution.py:31
  37.6 1.1 %shard_map.75.rest_0_ = bf16[2,128,768]{2,1,0:T(8,128)(2,1)S(1)} custom-call(s32[111]{0:T(128)S(1)} %copy-done.2, bf16[4,128,256]{2,1,0:T(8,128)(2,1)S(1)} %pad_maximum_fusion.own_ref, bf16[4,128,256]{2,1,0:T(8,128)(2,1)S(1)} %collective-permute-done.6.back_ref, bf16[4,128,256]{2,1,0:T(8,128)(2,1)S(1)} %collective-permute-done.7.far_ref, ...), custom_call_target="tpu_custom_call" | custom-call | tf_op jit(solution)/shard_map/pallas_call | solution.py:307
  38.6 2.0 %collective-permute-start.10 = (bf16[2,128,768]{2,1,0:T(8,128)(2,1)S(1)}, bf16[2,128,768]{2,1,0:T(8,128)(2,1)S(1)}, u32[]{:S(2)}, u32[]{:S(2)}) collective-permute-start(bf16[2,128,768]{2,1,0:T(8,128)(2,1)S(1)} %shard_map.75.rest_0_), channel_id=1, source_target_pairs={{0,3},{1,0},{2,1},{3,2},{4,5},{5,6},{6,7},{7,4},{8,11},{9,8},{10,9... | collective-permute-start | bytes 1179656 | tf_op jit(solution)/shard_map/ppermute | solution.py:31
  40.6 1.9 %collective-permute-start.9 = (bf16[2,128,768]{2,1,0:T(8,128)(2,1)S(1)}, bf16[2,128,768]{2,1,0:T(8,128)(2,1)S(1)}, u32[]{:S(2)}, u32[]{:S(2)}) collective-permute-start(bf16[2,128,768]{2,1,0:T(8,128)(2,1)S(1)} %shard_map.75.rest_0_), channel_id=1, source_target_pairs={{0,8},{4,12},{8,0},{12,4},{1,9},{5,13},{9,1},{13,5},{2,10},{6,14},... | collective-permute-start | bytes 1179656 | tf_op jit(solution)/shard_map/ppermute | solution.py:31
  42.5 2.3 %shard_map.74.a_ref = bf16[768,2048]{1,0:T(8,128)(2,1)S(1)} custom-call(bf16[16,1,6,128,128]{4,3,2,1,0:T(8,128)(2,1)} %a_hbm.1), custom_call_target="tpu_custom_call" | custom-call | bytes 6291456 | tf_op jit(solution)/shard_map/pallas_call | solution.py:266
  44.9 0.7 copy-done.1
  45.6 5.1 %shard_map.76.rest_3_ = f32[16,128,128]{2,1,0:T(8,128)S(1)} custom-call(s32[256]{0:T(256)S(1)} %copy-done.1, bf16[768,2048]{1,0:T(8,128)(2,1)S(1)} %shard_map.74.a_ref, bf16[16,8,3,128,128]{4,3,2,1,0:T(8,128)(2,1)} %b_own.7, bf16[16,8,3,128,128]{4,3,2,1,0:T(8,128)(2,1)} %collective-permute-done.5.b_other, bf16[2,128,768]{2,1,0:T(8,128)(2,1)S(1)} %shard_map.75.rest_0_), custom_call_target="tpu_custom_call" | custom-call | flops 1409286144 | bytes 4718592 | tf_op jit(solution)/shard_map/pallas_call | solution.py:230
  50.7 0.8 collective-permute-done.8.rest_0_
  51.6 1.3 %collective-permute-start.11 = (bf16[2,128,768]{2,1,0:T(8,128)(2,1)S(1)}, bf16[2,128,768]{2,1,0:T(8,128)(2,1)S(1)}, u32[]{:S(2)}, u32[]{:S(2)}) collective-permute-start(bf16[2,128,768]{2,1,0:T(8,128)(2,1)S(1)} %collective-permute-done.8.rest_0_), channel_id=1, source_target_pairs={{0,1},{1,2},{2,3},{3,0},{4,7},{5,4},{6,5},{7,6},{8,9},{9,10},{10,1... | collective-permute-start | bytes 1179656 | tf_op jit(solution)/shard_map/ppermute | solution.py:31
  52.9 2.0 %collective-permute-start.12 = (bf16[2,128,768]{2,1,0:T(8,128)(2,1)S(1)}, bf16[2,128,768]{2,1,0:T(8,128)(2,1)S(1)}, u32[]{:S(2)}, u32[]{:S(2)}) collective-permute-start(bf16[2,128,768]{2,1,0:T(8,128)(2,1)S(1)} %collective-permute-done.9.rest_1_), channel_id=1, source_target_pairs={{0,3},{1,0},{2,1},{3,2},{4,5},{5,6},{6,7},{7,4},{8,11},{9,8},{10,9... | collective-permute-start | bytes 1179656 | tf_op jit(solution)/shard_map/ppermute | solution.py:31
  55.0 7.3 %shard_map.77.rest_3_ = f32[16,128,128]{2,1,0:T(8,128)S(1)} custom-call(s32[256]{0:T(256)S(1)} %copy-done.1, bf16[768,2048]{1,0:T(8,128)(2,1)S(1)} %shard_map.74.a_ref, bf16[16,8,3,128,128]{4,3,2,1,0:T(8,128)(2,1)} %b_own.7, bf16[16,8,3,128,128]{4,3,2,1,0:T(8,128)(2,1)} %collective-permute-done.5.b_other, ...), custom_call_target="tpu_custom_call" | custom-call | flops 4227858432 | bytes 7864320 | tf_op jit(solution)/shard_map/pallas_call | solution.py:230
  62.4 1.5 %collective-permute-done.11.rest_0_ = bf16[2,128,768]{2,1,0:T(8,128)(2,1)S(1)} collective-permute-done((bf16[2,128,768]{2,1,0:T(8,128)(2,1)S(1)}, bf16[2,128,768]{2,1,0:T(8,128)(2,1)S(1)}, u32[]{:S(2)}, u32[]{:S(2)}) %collective-permute-start.11) | collective-permute-done | bytes 393248 | tf_op jit(solution)/shard_map/ppermute | solution.py:31
  63.9 1.0 %collective-permute-start.14 = (bf16[2,128,768]{2,1,0:T(8,128)(2,1)S(1)}, bf16[2,128,768]{2,1,0:T(8,128)(2,1)S(1)}, u32[]{:S(2)}, u32[]{:S(2)}) collective-permute-start(bf16[2,128,768]{2,1,0:T(8,128)(2,1)S(1)} %collective-permute-done.13.rest_2_), channel_id=1, source_target_pairs={{0,1},{1,2},{2,3},{3,0},{4,7},{5,4},{6,5},{7,6},{8,9},{9,10},{10,1... | collective-permute-start | bytes 1179656 | tf_op jit(solution)/shard_map/ppermute | solution.py:31
  64.9 6.0 %shard_map.78.rest_1_ = f32[16,128,128]{2,1,0:T(8,128)S(1)} custom-call(s32[256]{0:T(256)S(1)} %copy-done.1, bf16[768,2048]{1,0:T(8,128)(2,1)S(1)} %shard_map.74.a_ref, bf16[16,8,3,128,128]{4,3,2,1,0:T(8,128)(2,1)} %b_own.7, bf16[16,8,3,128,128]{4,3,2,1,0:T(8,128)(2,1)} %collective-permute-done.5.b_other, ...), custom_call_target="tpu_custom_call" | custom-call | flops 4227858432 | bytes 7864320 | tf_op jit(solution)/shard_map/pallas_call | solution.py:230
  70.9 2.0 %collective-permute-done.14.rest_0_ = bf16[2,128,768]{2,1,0:T(8,128)(2,1)S(1)} collective-permute-done((bf16[2,128,768]{2,1,0:T(8,128)(2,1)S(1)}, bf16[2,128,768]{2,1,0:T(8,128)(2,1)S(1)}, u32[]{:S(2)}, u32[]{:S(2)}) %collective-permute-start.14) | collective-permute-done | bytes 393248 | tf_op jit(solution)/shard_map/ppermute | solution.py:31
  72.9 4.1 %shard_map.79 = (f32[4,128,256]{2,1,0:T(8,128)S(1)}, f32[4,128,256]{2,1,0:T(8,128)S(1)}) custom-call(s32[256]{0:T(256)S(1)} %copy-done.1, bf16[768,2048]{1,0:T(8,128)(2,1)S(1)} %shard_map.74.a_ref, bf16[16,8,3,128,128]{4,3,2,1,0:T(8,128)(2,1)} %b_own.7, bf16[16,8,3,128,128]{4,3,2,1,0:T(8,128)(2,1)} %collective-permute-done.5.b_other, ...), custom_call_target="tpu_custom_call" | custom-call | flops 1409286144 | bytes 4718592 | tf_op jit(solution)/shard_map/pallas_call | solution.py:230
  77.3 1.7 %collective-permute-done.15.arrived_ref = f32[4,128,256]{2,1,0:T(8,128)S(1)} collective-permute-done((f32[4,128,256]{2,1,0:T(8,128)S(1)}, f32[4,128,256]{2,1,0:T(8,128)S(1)}, u32[]{:S(2)}, u32[]{:S(2)}) %collective-permute-start.15) | collective-permute-done | bytes 524320 | tf_op jit(solution)/shard_map/ppermute | solution.py:31
  79.1 9.0 %collective-permute-start.16 = (bf16[128,256]{1,0:T(8,128)(2,1)S(1)}, bf16[128,256]{1,0:T(8,128)(2,1)S(1)}, u32[]{:S(2)}, u32[]{:S(2)}) collective-permute-start(bf16[128,256]{1,0:T(8,128)(2,1)S(1)} %get-tuple-element.42), channel_id=1, source_target_pairs={{0,1},{1,2},{2,3},{3,0},{4,5},{5,6},{6,7},{7,4},{8,9},{9,10},{10,1... | collective-permute-start | bytes 196616 | tf_op jit(solution)/shard_map/ppermute | solution.py:31
  88.1 2.8 %collective-permute-start.18 = (bf16[128,256]{1,0:T(8,128)(2,1)S(1)}, bf16[128,256]{1,0:T(8,128)(2,1)S(1)}, u32[]{:S(2)}, u32[]{:S(2)}) collective-permute-start(bf16[128,256]{1,0:T(8,128)(2,1)S(1)} %get-tuple-element.44), channel_id=1, source_target_pairs={{0,3},{1,0},{2,1},{3,2},{4,7},{5,4},{6,5},{7,6},{8,11},{9,8},{10,9... | collective-permute-start | bytes 196616 | tf_op jit(solution)/shard_map/ppermute | solution.py:31
  90.9 3.0 %collective-permute-done.17 = bf16[128,256]{1,0:T(8,128)(2,1)S(1)} collective-permute-done((bf16[128,256]{1,0:T(8,128)(2,1)S(1)}, bf16[128,256]{1,0:T(8,128)(2,1)S(1)}, u32[]{:S(2)}, u32[]{:S(2)}) %collective-permute-start.17) | collective-permute-done | bytes 65568 | tf_op jit(solution)/shard_map/ppermute | solution.py:31
  93.9 0.7 add_convert_fusion
  (30 shorter events, 1.7 us)
Async XLA Ops:
  0.0 1.0 %copy-start = (bf16[128,1024]{1,0:T(8,128)(2,1)S(1)}, bf16[128,1024]{1,0:T(8,128)(2,1)}, u32[]{:S(2)}) copy-start(bf16[128,1024]{1,0:T(8,128)(2,1)} %param.7) | copy-start | bytes 786436
  0.0 44.9 %collective-permute-start.5 = (bf16[16,8,3,128,128]{4,3,2,1,0:T(8,128)(2,1)}, bf16[16,8,3,128,128]{4,3,2,1,0:T(8,128)(2,1)}, u32[]{:S(2)}, u32[]{:S(2)}) collective-permute-start(bf16[16,8,3,128,128]{4,3,2,1,0:T(8,128)(2,1)} %b_own.7), channel_id=1, source_target_pairs={{0,4},{4,0},{8,12},{12,8},{1,5},{5,1},{9,13},{13,9},{2,6},{6,2},{1... | collective-permute-start | bytes 37748744 | tf_op jit(solution)/shard_map/ppermute | solution.py:31
  1.0 19.4 %collective-permute-start.1 = (bf16[128,256]{1,0:T(8,128)(2,1)S(1)}, bf16[128,256]{1,0:T(8,128)(2,1)S(1)}, u32[]{:S(2)}, u32[]{:S(2)}) collective-permute-start(bf16[128,256]{1,0:T(8,128)(2,1)S(1)} %constant_dynamic-slice_fusion), channel_id=1, source_target_pairs={{0,128},{16,144},{32,160},{48,176},{64,192},{80,208},{96,224},{112... | collective-permute-start | bytes 196616 | tf_op jit(solution)/shard_map/ppermute | solution.py:31
  8.2 12.2 %collective-permute-start = (bf16[128,256]{1,0:T(8,128)(2,1)S(1)}, bf16[128,256]{1,0:T(8,128)(2,1)S(1)}, u32[]{:S(2)}, u32[]{:S(2)}) collective-permute-start(bf16[128,256]{1,0:T(8,128)(2,1)S(1)} %constant_dynamic-slice_fusion), channel_id=1, source_target_pairs={{0,192},{16,208},{32,224},{48,240},{64,0},{80,16},{96,32},{112,48}... | collective-permute-start | bytes 196616 | tf_op jit(solution)/shard_map/ppermute | solution.py:31
  8.2 12.2 %collective-permute-start.3 = (bf16[128,256]{1,0:T(8,128)(2,1)S(1)}, bf16[128,256]{1,0:T(8,128)(2,1)S(1)}, u32[]{:S(2)}, u32[]{:S(2)}) collective-permute-start(bf16[128,256]{1,0:T(8,128)(2,1)S(1)} %constant_dynamic-slice_fusion), channel_id=1, source_target_pairs={{0,64},{16,80},{32,96},{48,112},{64,128},{80,144},{96,160},{112,17... | collective-permute-start | bytes 196616 | tf_op jit(solution)/shard_map/ppermute | solution.py:31
  12.9 6.2 %collective-permute-start.2 = (s32[48]{0:T(128)S(1)}, s32[48]{0:T(128)S(1)}, u32[]{:S(2)}, u32[]{:S(2)}) collective-permute-start(s32[48]{0:T(128)S(1)} %pad_add_fusion), channel_id=1, source_target_pairs={{0,4},{4,0},{8,12},{12,8},{1,5},{5,1},{9,13},{13,9},{2,6},{6,2},{1... | collective-permute-start | bytes 584 | tf_op jit(solution)/shard_map/ppermute | solution.py:31
  20.4 9.0 %collective-permute-start.4 = (bf16[4,128,256]{2,1,0:T(8,128)(2,1)S(1)}, bf16[4,128,256]{2,1,0:T(8,128)(2,1)S(1)}, u32[]{:S(2)}, u32[]{:S(2)}) collective-permute-start(bf16[4,128,256]{2,1,0:T(8,128)(2,1)S(1)} %pad_maximum_fusion.own_ref), channel_id=1, source_target_pairs={{0,16},{4,52},{8,24},{12,60},{16,32},{20,4},{24,40},{28,12},{32,48... | collective-permute-start | bytes 786440 | tf_op jit(solution)/shard_map/ppermute | solution.py:31
  22.7 10.3 %collective-permute-start.6 = (bf16[4,128,256]{2,1,0:T(8,128)(2,1)S(1)}, bf16[4,128,256]{2,1,0:T(8,128)(2,1)S(1)}, u32[]{:S(2)}, u32[]{:S(2)}) collective-permute-start(bf16[4,128,256]{2,1,0:T(8,128)(2,1)S(1)} %pad_maximum_fusion.own_ref), channel_id=1, source_target_pairs={{0,48},{4,20},{8,56},{12,28},{16,0},{20,36},{24,8},{28,44},{32,16}... | collective-permute-start | bytes 786440 | tf_op jit(solution)/shard_map/ppermute | solution.py:31
  29.5 7.5 %collective-permute-start.7 = (bf16[4,128,256]{2,1,0:T(8,128)(2,1)S(1)}, bf16[4,128,256]{2,1,0:T(8,128)(2,1)S(1)}, u32[]{:S(2)}, u32[]{:S(2)}) collective-permute-start(bf16[4,128,256]{2,1,0:T(8,128)(2,1)S(1)} %collective-permute-done.4.ahead_ref), channel_id=1, source_target_pairs={{0,16},{4,52},{8,24},{12,60},{16,32},{20,4},{24,40},{28,12},{32,48... | collective-permute-start | bytes 786440 | tf_op jit(solution)/shard_map/ppermute | solution.py:31
  37.0 0.6 copy-start.2
  38.6 12.0 %collective-permute-start.10 = (bf16[2,128,768]{2,1,0:T(8,128)(2,1)S(1)}, bf16[2,128,768]{2,1,0:T(8,128)(2,1)S(1)}, u32[]{:S(2)}, u32[]{:S(2)}) collective-permute-start(bf16[2,128,768]{2,1,0:T(8,128)(2,1)S(1)} %shard_map.75.rest_0_), channel_id=1, source_target_pairs={{0,3},{1,0},{2,1},{3,2},{4,5},{5,6},{6,7},{7,4},{8,11},{9,8},{10,9... | collective-permute-start | bytes 1179656 | tf_op jit(solution)/shard_map/ppermute | solution.py:31
  40.6 10.1 %collective-permute-start.9 = (bf16[2,128,768]{2,1,0:T(8,128)(2,1)S(1)}, bf16[2,128,768]{2,1,0:T(8,128)(2,1)S(1)}, u32[]{:S(2)}, u32[]{:S(2)}) collective-permute-start(bf16[2,128,768]{2,1,0:T(8,128)(2,1)S(1)} %shard_map.75.rest_0_), channel_id=1, source_target_pairs={{0,8},{4,12},{8,0},{12,4},{1,9},{5,13},{9,1},{13,5},{2,10},{6,14},... | collective-permute-start | bytes 1179656 | tf_op jit(solution)/shard_map/ppermute | solution.py:31
  42.5 9.0 %collective-permute-start.8 = (bf16[2,128,768]{2,1,0:T(8,128)(2,1)S(1)}, bf16[2,128,768]{2,1,0:T(8,128)(2,1)S(1)}, u32[]{:S(2)}, u32[]{:S(2)}) collective-permute-start(bf16[2,128,768]{2,1,0:T(8,128)(2,1)S(1)} %shard_map.75.rest_0_), channel_id=1, source_target_pairs={{0,1},{1,2},{2,3},{3,0},{4,7},{5,4},{6,5},{7,6},{8,9},{9,10},{10,1... | collective-permute-start | bytes 1179656 | tf_op jit(solution)/shard_map/ppermute | solution.py:31
  44.9 0.7 copy-start.1
  51.5 10.9 %collective-permute-start.13 = (bf16[2,128,768]{2,1,0:T(8,128)(2,1)S(1)}, bf16[2,128,768]{2,1,0:T(8,128)(2,1)S(1)}, u32[]{:S(2)}, u32[]{:S(2)}) collective-permute-start(bf16[2,128,768]{2,1,0:T(8,128)(2,1)S(1)} %collective-permute-done.8.rest_0_), channel_id=1, source_target_pairs={{0,8},{4,12},{8,0},{12,4},{1,9},{5,13},{9,1},{13,5},{2,10},{6,14},... | collective-permute-start | bytes 1179656 | tf_op jit(solution)/shard_map/ppermute | solution.py:31
  51.6 12.3 %collective-permute-start.11 = (bf16[2,128,768]{2,1,0:T(8,128)(2,1)S(1)}, bf16[2,128,768]{2,1,0:T(8,128)(2,1)S(1)}, u32[]{:S(2)}, u32[]{:S(2)}) collective-permute-start(bf16[2,128,768]{2,1,0:T(8,128)(2,1)S(1)} %collective-permute-done.8.rest_0_), channel_id=1, source_target_pairs={{0,1},{1,2},{2,3},{3,0},{4,7},{5,4},{6,5},{7,6},{8,9},{9,10},{10,1... | collective-permute-start | bytes 1179656 | tf_op jit(solution)/shard_map/ppermute | solution.py:31
  52.9 9.5 %collective-permute-start.12 = (bf16[2,128,768]{2,1,0:T(8,128)(2,1)S(1)}, bf16[2,128,768]{2,1,0:T(8,128)(2,1)S(1)}, u32[]{:S(2)}, u32[]{:S(2)}) collective-permute-start(bf16[2,128,768]{2,1,0:T(8,128)(2,1)S(1)} %collective-permute-done.9.rest_1_), channel_id=1, source_target_pairs={{0,3},{1,0},{2,1},{3,2},{4,5},{5,6},{6,7},{7,4},{8,11},{9,8},{10,9... | collective-permute-start | bytes 1179656 | tf_op jit(solution)/shard_map/ppermute | solution.py:31
  63.9 9.0 %collective-permute-start.14 = (bf16[2,128,768]{2,1,0:T(8,128)(2,1)S(1)}, bf16[2,128,768]{2,1,0:T(8,128)(2,1)S(1)}, u32[]{:S(2)}, u32[]{:S(2)}) collective-permute-start(bf16[2,128,768]{2,1,0:T(8,128)(2,1)S(1)} %collective-permute-done.13.rest_2_), channel_id=1, source_target_pairs={{0,1},{1,2},{2,3},{3,0},{4,7},{5,4},{6,5},{7,6},{8,9},{9,10},{10,1... | collective-permute-start | bytes 1179656 | tf_op jit(solution)/shard_map/ppermute | solution.py:31
  77.0 2.0 %collective-permute-start.15 = (f32[4,128,256]{2,1,0:T(8,128)S(1)}, f32[4,128,256]{2,1,0:T(8,128)S(1)}, u32[]{:S(2)}, u32[]{:S(2)}) collective-permute-start(f32[4,128,256]{2,1,0:T(8,128)S(1)} %get-tuple-element.40), channel_id=1, source_target_pairs={{0,4},{4,0},{8,12},{12,8},{1,5},{5,1},{9,13},{13,9},{2,6},{6,2},{1... | collective-permute-start | bytes 1572872 | tf_op jit(solution)/shard_map/ppermute | solution.py:31
  79.1 11.8 %collective-permute-start.16 = (bf16[128,256]{1,0:T(8,128)(2,1)S(1)}, bf16[128,256]{1,0:T(8,128)(2,1)S(1)}, u32[]{:S(2)}, u32[]{:S(2)}) collective-permute-start(bf16[128,256]{1,0:T(8,128)(2,1)S(1)} %get-tuple-element.42), channel_id=1, source_target_pairs={{0,1},{1,2},{2,3},{3,0},{4,5},{5,6},{6,7},{7,4},{8,9},{9,10},{10,1... | collective-permute-start | bytes 196616 | tf_op jit(solution)/shard_map/ppermute | solution.py:31
  88.1 5.8 %collective-permute-start.17 = (bf16[128,256]{1,0:T(8,128)(2,1)S(1)}, bf16[128,256]{1,0:T(8,128)(2,1)S(1)}, u32[]{:S(2)}, u32[]{:S(2)}) collective-permute-start(bf16[128,256]{1,0:T(8,128)(2,1)S(1)} %get-tuple-element.43), channel_id=1, source_target_pairs={{0,2},{1,3},{2,0},{3,1},{4,6},{5,7},{6,4},{7,5},{8,10},{9,11},{10,... | collective-permute-start | bytes 196616 | tf_op jit(solution)/shard_map/ppermute | solution.py:31
  88.1 5.8 %collective-permute-start.18 = (bf16[128,256]{1,0:T(8,128)(2,1)S(1)}, bf16[128,256]{1,0:T(8,128)(2,1)S(1)}, u32[]{:S(2)}, u32[]{:S(2)}) collective-permute-start(bf16[128,256]{1,0:T(8,128)(2,1)S(1)} %get-tuple-element.44), channel_id=1, source_target_pairs={{0,3},{1,0},{2,1},{3,2},{4,7},{5,4},{6,5},{7,6},{8,11},{9,8},{10,9... | collective-permute-start | bytes 196616 | tf_op jit(solution)/shard_map/ppermute | solution.py:31

commit v5 on v4

--- a/solution.py
+++ b/solution.py
@@ -180,11 +180,16 @@
         for lane in range(width):
             c_copy(units[0], 0, slot, lane).wait()
         sums = [jnp.zeros((BLK, BLK), jnp.float32) for _ in range(width)]
-        for group in range(0, vectors, VECTORS_PER_GROUP):
+
+        def panel_of(group):
             columns = slice(group * BLK, (group + VECTORS_PER_GROUP) * BLK)
-            panel = jnp.dot(
+            return jnp.dot(
                 c_buf[slot, : width * BLK], a_ref[:, columns], preferred_element_type=jnp.float32
             ).astype(jnp.bfloat16)
+
+        panel = panel_of(0)
+        for group in range(0, vectors, VECTORS_PER_GROUP):
+            following = panel_of(group + VECTORS_PER_GROUP) if group + VECTORS_PER_GROUP < vectors else None
             if group <= VECTORS_PER_GROUP:
                 for lane in range(width):
                     b_copy(b_own, 0, 0, slot, lane, group // VECTORS_PER_GROUP).wait()
@@ -199,6 +204,7 @@
                     jnp.concatenate(blocks, axis=0),
                     preferred_element_type=jnp.float32,
                 )
+            panel = following
         for lane in range(width):
             at = first_of(step) + lane
             entry = entry_of(at)
@@ -283,7 +289,7 @@
     )(meta)
 
 
-def gather_sources(meta, quarter, sizes):
+def gather_sources(meta, quarter, b_tiles, sizes):
     alphas, betas = sizes["alpha"], sizes["beta"]
     zs = alphas // X_SIZE
 
@@ -299,7 +305,7 @@
         return shifted(value, ("alpha", "beta"), alphas * betas, moved)
 
     others = [z_from(quarter, distance) for distance in (1, 2, 3)]
-    others[1], meta = lax.optimization_barrier((others[1], meta))
+    others, meta, b_held = lax.optimization_barrier((others, meta, b_tiles))
     own = jnp.stack([quarter] + others)
     ahead, back = by_core(own, 1), by_core(own, -1)
     ahead, plan = lax.optimization_barrier((ahead, make_plan(meta)))
@@ -311,7 +317,7 @@
         out_specs=VMEM,
         compiler_params=pltpu.CompilerParams(vmem_limit_bytes=8 * 1024 * 1024),
     )(meta, own, back, far, ahead)
-    return plan, unit
+    return plan, unit, b_held
 
 
 def gather_and_contract(plan, chol, unit, a_tiles, b_own, b_other, sizes):
@@ -352,8 +358,9 @@
     place = jnp.stack([lax.axis_index("alpha"), lax.axis_index("beta"), chol]).astype(jnp.int32)
     pairs = jnp.concatenate([b_source.reshape(-1), b_sign.reshape(-1)])
     meta = jnp.concatenate([place, a_source.reshape(-1), a_sign.reshape(-1), pairs, core_other(pairs)])
-    plan, unit = gather_sources(meta, quarter, sizes)
-    mine, other = gather_and_contract(plan, chol[None], unit, a_tiles, b_tiles, core_other(b_tiles), sizes)
+    plan, unit, b_held = gather_sources(meta, quarter, b_tiles, sizes)
+    b_other = core_other(b_held)
+    mine, other = gather_and_contract(plan, chol[None], unit, a_tiles, b_tiles, b_other, sizes)
     own, *pieces = merge(mine, core_other(other))
     for shift, piece in enumerate(pieces, 1):
         own = own + shifted(piece, "chol", chols, lambda i: (i + shift) % chols).astype(jnp.float32)

time: 92.7 us -> 87.8 us (0.947); the launches traced: 94.6 us -> 86.6 us
  starting transfers between devices: 36.6 us -> 30.4 us
  waiting for transfers between devices: 23.6 us -> 19.2 us
  Pallas kernels: 28.2 us -> 30.8 us
    ppermute x19, starting transfers between devices: 36.6 us -> 30.4 us  [shifted(): return lax.ppermute(value, axis, [(i, moves_to(i)) for i in range(size)])]
    ppermute x19, waiting for transfers between devices: 23.6 us -> 19.2 us  [shifted(): return lax.ppermute(value, axis, [(i, moves_to(i)) for i in range(size)])]
    pallas_call x4, Pallas kernels: 22.5 us -> 25.1 us  [contract(): pl.pallas_call(functools.partial(contract_kernel, index, last), out_shape...]
  transfers between devices with their start and end apart: 19 -> 19, of which waited for: 9 -> 11; matrix products, arithmetic and copies ran while one was open for 3% -> 4% of each run, Pallas kernels for 25% -> 31%
where the time goes in v5:
time: 87.8 us; the launch traced here: 86.6 us
  Pallas kernels  30.8 us (35%)
  starting transfers between devices  30.4 us (35%)
  waiting for transfers between devices  19.2 us (22%)
  local copies, waits for them, and re-layouts  5.25 us (6%)
    ppermute x19, starting transfers between devices, shifted(): return lax.ppermute(value, axis, [(i, moves_to(i)) for i in range(size)])  30.4 us
    pallas_call x4, Pallas kernels, contract(): pl.pallas_call(functools.partial(contract_kernel, index, last), out_shape...  25.1 us
    ppermute x19, waiting for transfers between devices, shifted(): return lax.ppermute(value, axis, [(i, moves_to(i)) for i in range(size)])  19.2 us
    unnamed x8, local copies, waits for them, and re-layouts  3.77 us
    pallas_call x1, Pallas kernels, flip(): pl.pallas_call(flip_kernel, out_shape=jax.ShapeDtypeStruct((A_SLOTS * BLK...  2.33 us
    pallas_call x1, Pallas kernels, make_plan(): pl.pallas_call(plan_kernel, out_shape=jax.ShapeDtypeStruct((KERNELS * PLA...  2.27 us
  transfers between devices with their start and end apart: 19, of which 11 were waited for; matrix products, arithmetic and copies ran while one was open for 4% of the time, Pallas kernels for 31%

profile of v5, /device:TPU:6, one launch (start us, length us, event | category | flops | bytes accessed | tf_op | source)
XLA Modules:
  0.0 86.6 jit_solution(15377618645027796875)
XLA Ops:
  0.0 0.9 %copy-done = bf16[128,1024]{1,0:T(8,128)(2,1)S(1)} copy-done((bf16[128,1024]{1,0:T(8,128)(2,1)S(1)}, bf16[128,1024]{1,0:T(8,128)(2,1)}, u32[]{:S(2)}) %copy-start) | copy-done | bytes 262168
  1.0 7.3 %collective-permute-start.1 = (bf16[128,256]{1,0:T(8,128)(2,1)S(1)}, bf16[128,256]{1,0:T(8,128)(2,1)S(1)}, u32[]{:S(2)}, u32[]{:S(2)}) collective-permute-start(bf16[128,256]{1,0:T(8,128)(2,1)S(1)} %constant_dynamic-slice_fusion), channel_id=1, source_target_pairs={{0,128},{16,144},{32,160},{48,176},{64,192},{80,208},{96,224},{112... | collective-permute-start | bytes 196616 | tf_op jit(solution)/shard_map/ppermute | solution.py:31
  8.2 2.9 %collective-permute-start.2 = (bf16[128,256]{1,0:T(8,128)(2,1)S(1)}, bf16[128,256]{1,0:T(8,128)(2,1)S(1)}, u32[]{:S(2)}, u32[]{:S(2)}) collective-permute-start(bf16[128,256]{1,0:T(8,128)(2,1)S(1)} %constant_dynamic-slice_fusion), channel_id=1, source_target_pairs={{0,64},{16,80},{32,96},{48,112},{64,128},{80,144},{96,160},{112,17... | collective-permute-start | bytes 196616 | tf_op jit(solution)/shard_map/ppermute | solution.py:31
  11.2 0.8 copy.10
  12.0 0.8 copy.11
  13.0 1.1 %collective-permute-done.3 = s32[48]{0:T(128)S(1)} collective-permute-done((s32[48]{0:T(128)S(1)}, s32[48]{0:T(128)S(1)}, u32[]{:S(2)}, u32[]{:S(2)}) %collective-permute-start.3) | collective-permute-done | bytes 224 | tf_op jit(solution)/shard_map/ppermute | solution.py:31
  14.1 1.3 %concatenate.8.meta_ref = s32[111]{0:T(128)} concatenate(s32[1]{0:T(128)} %bitcast.1, s32[1]{0:T(128)} %bitcast.2, s32[1]{0:T(128)} %bitcast.3.rest_2_, s32[6]{0:T(128)} %bitcast.13, s32[6]{0:T(128)} %bitcast.14, s32[24]{0:T(128)S(1)} %reshape.14, s32[24]{0:T(128)S(1)} %reshape.15, s32[48]{0:T(128)S(1)} %collective-permute-done.3), dimensions={0} | concatenate | bytes 888 | tf_op jit(solution)/shard_map/concatenate | solution.py:360
  16.3 1.5 %collective-permute-start.6 = (bf16[4,128,256]{2,1,0:T(8,128)(2,1)S(1)}, bf16[4,128,256]{2,1,0:T(8,128)(2,1)S(1)}, u32[]{:S(2)}, u32[]{:S(2)}) collective-permute-start(bf16[4,128,256]{2,1,0:T(8,128)(2,1)S(1)} %pad_maximum_fusion.own_ref), channel_id=1, source_target_pairs={{0,48},{4,20},{8,56},{12,28},{16,0},{20,36},{24,8},{28,44},{32,16}... | collective-permute-start | bytes 786440 | tf_op jit(solution)/shard_map/ppermute | solution.py:31
  17.8 2.3 %shard_map.73.plan_ref = s32[256]{0:T(256)} custom-call(s32[111]{0:T(128)} %concatenate.8.meta_ref), custom_call_target="tpu_custom_call" | custom-call | tf_op jit(solution)/shard_map/pallas_call | solution.py:284
  20.1 4.8 %collective-permute-done.4.ahead_ref = bf16[4,128,256]{2,1,0:T(8,128)(2,1)S(1)} collective-permute-done((bf16[4,128,256]{2,1,0:T(8,128)(2,1)S(1)}, bf16[4,128,256]{2,1,0:T(8,128)(2,1)S(1)}, u32[]{:S(2)}, u32[]{:S(2)}) %collective-permute-start.4) | collective-permute-done | bytes 262176 | tf_op jit(solution)/shard_map/ppermute | solution.py:31
  24.9 0.7 collective-permute-done.6.back_ref
  25.5 5.7 %collective-permute-done.7.far_ref = bf16[4,128,256]{2,1,0:T(8,128)(2,1)S(1)} collective-permute-done((bf16[4,128,256]{2,1,0:T(8,128)(2,1)S(1)}, bf16[4,128,256]{2,1,0:T(8,128)(2,1)S(1)}, u32[]{:S(2)}, u32[]{:S(2)}) %collective-permute-start.7) | collective-permute-done | bytes 262176 | tf_op jit(solution)/shard_map/ppermute | solution.py:31
  31.2 0.6 copy-done.2
  31.9 1.1 %shard_map.75.rest_0_ = bf16[2,128,768]{2,1,0:T(8,128)(2,1)S(1)} custom-call(s32[111]{0:T(128)S(1)} %copy-done.2, bf16[4,128,256]{2,1,0:T(8,128)(2,1)S(1)} %pad_maximum_fusion.own_ref, bf16[4,128,256]{2,1,0:T(8,128)(2,1)S(1)} %collective-permute-done.6.back_ref, bf16[4,128,256]{2,1,0:T(8,128)(2,1)S(1)} %collective-permute-done.7.far_ref, ...), custom_call_target="tpu_custom_call" | custom-call | tf_op jit(solution)/shard_map/pallas_call | solution.py:313
  33.0 3.1 %collective-permute-start.10 = (bf16[2,128,768]{2,1,0:T(8,128)(2,1)S(1)}, bf16[2,128,768]{2,1,0:T(8,128)(2,1)S(1)}, u32[]{:S(2)}, u32[]{:S(2)}) collective-permute-start(bf16[2,128,768]{2,1,0:T(8,128)(2,1)S(1)} %shard_map.75.rest_0_), channel_id=1, source_target_pairs={{0,3},{1,0},{2,1},{3,2},{4,5},{5,6},{6,7},{7,4},{8,11},{9,8},{10,9... | collective-permute-start | bytes 1179656 | tf_op jit(solution)/shard_map/ppermute | solution.py:31
  36.0 1.2 %collective-permute-start.9 = (bf16[2,128,768]{2,1,0:T(8,128)(2,1)S(1)}, bf16[2,128,768]{2,1,0:T(8,128)(2,1)S(1)}, u32[]{:S(2)}, u32[]{:S(2)}) collective-permute-start(bf16[2,128,768]{2,1,0:T(8,128)(2,1)S(1)} %shard_map.75.rest_0_), channel_id=1, source_target_pairs={{0,8},{4,12},{8,0},{12,4},{1,9},{5,13},{9,1},{13,5},{2,10},{6,14},... | collective-permute-start | bytes 1179656 | tf_op jit(solution)/shard_map/ppermute | solution.py:31
  37.2 2.3 %shard_map.74.a_ref = bf16[768,2048]{1,0:T(8,128)(2,1)S(1)} custom-call(bf16[16,1,6,128,128]{4,3,2,1,0:T(8,128)(2,1)} %a_hbm.1), custom_call_target="tpu_custom_call" | custom-call | bytes 6291456 | tf_op jit(solution)/shard_map/pallas_call | solution.py:272
  39.6 0.7 copy-done.1
  40.2 4.9 %shard_map.76.rest_3_ = f32[16,128,128]{2,1,0:T(8,128)S(1)} custom-call(s32[256]{0:T(256)S(1)} %copy-done.1, bf16[768,2048]{1,0:T(8,128)(2,1)S(1)} %shard_map.74.a_ref, bf16[16,8,3,128,128]{4,3,2,1,0:T(8,128)(2,1)} %b_own.7, bf16[16,8,3,128,128]{4,3,2,1,0:T(8,128)(2,1)} %collective-permute-done.5.b_other, bf16[2,128,768]{2,1,0:T(8,128)(2,1)S(1)} %shard_map.75.rest_0_), custom_call_target="tpu_custom_call" | custom-call | flops 1409286144 | bytes 4718592 | tf_op jit(solution)/shard_map/pallas_call | solution.py:236
  45.5 0.7 collective-permute-done.8.rest_0_
  46.2 2.2 %collective-permute-start.13 = (bf16[2,128,768]{2,1,0:T(8,128)(2,1)S(1)}, bf16[2,128,768]{2,1,0:T(8,128)(2,1)S(1)}, u32[]{:S(2)}, u32[]{:S(2)}) collective-permute-start(bf16[2,128,768]{2,1,0:T(8,128)(2,1)S(1)} %collective-permute-done.8.rest_0_), channel_id=1, source_target_pairs={{0,8},{4,12},{8,0},{12,4},{1,9},{5,13},{9,1},{13,5},{2,10},{6,14},... | collective-permute-start | bytes 1179656 | tf_op jit(solution)/shard_map/ppermute | solution.py:31
  48.4 3.2 %collective-permute-start.12 = (bf16[2,128,768]{2,1,0:T(8,128)(2,1)S(1)}, bf16[2,128,768]{2,1,0:T(8,128)(2,1)S(1)}, u32[]{:S(2)}, u32[]{:S(2)}) collective-permute-start(bf16[2,128,768]{2,1,0:T(8,128)(2,1)S(1)} %collective-permute-done.9.rest_1_), channel_id=1, source_target_pairs={{0,3},{1,0},{2,1},{3,2},{4,5},{5,6},{6,7},{7,4},{8,11},{9,8},{10,9... | collective-permute-start | bytes 1179656 | tf_op jit(solution)/shard_map/ppermute | solution.py:31
  51.6 9.3 %shard_map.77.rest_3_ = f32[16,128,128]{2,1,0:T(8,128)S(1)} custom-call(s32[256]{0:T(256)S(1)} %copy-done.1, bf16[768,2048]{1,0:T(8,128)(2,1)S(1)} %shard_map.74.a_ref, bf16[16,8,3,128,128]{4,3,2,1,0:T(8,128)(2,1)} %b_own.7, bf16[16,8,3,128,128]{4,3,2,1,0:T(8,128)(2,1)} %collective-permute-done.5.b_other, ...), custom_call_target="tpu_custom_call" | custom-call | flops 4227858432 | bytes 7864320 | tf_op jit(solution)/shard_map/pallas_call | solution.py:236
  61.2 7.3 %shard_map.78.rest_1_ = f32[16,128,128]{2,1,0:T(8,128)S(1)} custom-call(s32[256]{0:T(256)S(1)} %copy-done.1, bf16[768,2048]{1,0:T(8,128)(2,1)S(1)} %shard_map.74.a_ref, bf16[16,8,3,128,128]{4,3,2,1,0:T(8,128)(2,1)} %b_own.7, bf16[16,8,3,128,128]{4,3,2,1,0:T(8,128)(2,1)} %collective-permute-done.5.b_other, ...), custom_call_target="tpu_custom_call" | custom-call | flops 4227858432 | bytes 7864320 | tf_op jit(solution)/shard_map/pallas_call | solution.py:236
  68.5 1.7 %collective-permute-done.14.rest_0_ = bf16[2,128,768]{2,1,0:T(8,128)(2,1)S(1)} collective-permute-done((bf16[2,128,768]{2,1,0:T(8,128)(2,1)S(1)}, bf16[2,128,768]{2,1,0:T(8,128)(2,1)S(1)}, u32[]{:S(2)}, u32[]{:S(2)}) %collective-permute-start.14) | collective-permute-done | bytes 393248 | tf_op jit(solution)/shard_map/ppermute | solution.py:31
  70.2 3.7 %shard_map.79 = (f32[4,128,256]{2,1,0:T(8,128)S(1)}, f32[4,128,256]{2,1,0:T(8,128)S(1)}) custom-call(s32[256]{0:T(256)S(1)} %copy-done.1, bf16[768,2048]{1,0:T(8,128)(2,1)S(1)} %shard_map.74.a_ref, bf16[16,8,3,128,128]{4,3,2,1,0:T(8,128)(2,1)} %b_own.7, bf16[16,8,3,128,128]{4,3,2,1,0:T(8,128)(2,1)} %collective-permute-done.5.b_other, ...), custom_call_target="tpu_custom_call" | custom-call | flops 1409286144 | bytes 4718592 | tf_op jit(solution)/shard_map/pallas_call | solution.py:236
  74.0 1.9 %collective-permute-done.15.arrived_ref = f32[4,128,256]{2,1,0:T(8,128)S(1)} collective-permute-done((f32[4,128,256]{2,1,0:T(8,128)S(1)}, f32[4,128,256]{2,1,0:T(8,128)S(1)}, u32[]{:S(2)}, u32[]{:S(2)}) %collective-permute-start.15) | collective-permute-done | bytes 524320 | tf_op jit(solution)/shard_map/ppermute | solution.py:31
  76.1 5.4 %collective-permute-start.17 = (bf16[128,256]{1,0:T(8,128)(2,1)S(1)}, bf16[128,256]{1,0:T(8,128)(2,1)S(1)}, u32[]{:S(2)}, u32[]{:S(2)}) collective-permute-start(bf16[128,256]{1,0:T(8,128)(2,1)S(1)} %get-tuple-element.49), channel_id=1, source_target_pairs={{0,2},{1,3},{2,0},{3,1},{4,6},{5,7},{6,4},{7,5},{8,10},{9,11},{10,... | collective-permute-start | bytes 196616 | tf_op jit(solution)/shard_map/ppermute | solution.py:31
  81.5 2.5 %collective-permute-start.18 = (bf16[128,256]{1,0:T(8,128)(2,1)S(1)}, bf16[128,256]{1,0:T(8,128)(2,1)S(1)}, u32[]{:S(2)}, u32[]{:S(2)}) collective-permute-start(bf16[128,256]{1,0:T(8,128)(2,1)S(1)} %get-tuple-element.50), channel_id=1, source_target_pairs={{0,3},{1,0},{2,1},{3,2},{4,7},{5,4},{6,5},{7,6},{8,11},{9,8},{10,9... | collective-permute-start | bytes 196616 | tf_op jit(solution)/shard_map/ppermute | solution.py:31
  84.0 1.2 %collective-permute-done.17 = bf16[128,256]{1,0:T(8,128)(2,1)S(1)} collective-permute-done((bf16[128,256]{1,0:T(8,128)(2,1)S(1)}, bf16[128,256]{1,0:T(8,128)(2,1)S(1)}, u32[]{:S(2)}, u32[]{:S(2)}) %collective-permute-start.17) | collective-permute-done | bytes 65568 | tf_op jit(solution)/shard_map/ppermute | solution.py:31
  85.2 0.7 collective-permute-done.18
  85.9 0.7 add_convert_fusion
  (30 shorter events, 2.1 us)
Async XLA Ops:
  0.0 1.0 %copy-start = (bf16[128,1024]{1,0:T(8,128)(2,1)S(1)}, bf16[128,1024]{1,0:T(8,128)(2,1)}, u32[]{:S(2)}) copy-start(bf16[128,1024]{1,0:T(8,128)(2,1)} %param.7) | copy-start | bytes 786436
  1.0 14.4 %collective-permute-start.1 = (bf16[128,256]{1,0:T(8,128)(2,1)S(1)}, bf16[128,256]{1,0:T(8,128)(2,1)S(1)}, u32[]{:S(2)}, u32[]{:S(2)}) collective-permute-start(bf16[128,256]{1,0:T(8,128)(2,1)S(1)} %constant_dynamic-slice_fusion), channel_id=1, source_target_pairs={{0,128},{16,144},{32,160},{48,176},{64,192},{80,208},{96,224},{112... | collective-permute-start | bytes 196616 | tf_op jit(solution)/shard_map/ppermute | solution.py:31
  8.2 7.1 %collective-permute-start = (bf16[128,256]{1,0:T(8,128)(2,1)S(1)}, bf16[128,256]{1,0:T(8,128)(2,1)S(1)}, u32[]{:S(2)}, u32[]{:S(2)}) collective-permute-start(bf16[128,256]{1,0:T(8,128)(2,1)S(1)} %constant_dynamic-slice_fusion), channel_id=1, source_target_pairs={{0,192},{16,208},{32,224},{48,240},{64,0},{80,16},{96,32},{112,48}... | collective-permute-start | bytes 196616 | tf_op jit(solution)/shard_map/ppermute | solution.py:31
  8.2 7.1 %collective-permute-start.2 = (bf16[128,256]{1,0:T(8,128)(2,1)S(1)}, bf16[128,256]{1,0:T(8,128)(2,1)S(1)}, u32[]{:S(2)}, u32[]{:S(2)}) collective-permute-start(bf16[128,256]{1,0:T(8,128)(2,1)S(1)} %constant_dynamic-slice_fusion), channel_id=1, source_target_pairs={{0,64},{16,80},{32,96},{48,112},{64,128},{80,144},{96,160},{112,17... | collective-permute-start | bytes 196616 | tf_op jit(solution)/shard_map/ppermute | solution.py:31
  12.9 1.1 %collective-permute-start.3 = (s32[48]{0:T(128)S(1)}, s32[48]{0:T(128)S(1)}, u32[]{:S(2)}, u32[]{:S(2)}) collective-permute-start(s32[48]{0:T(128)S(1)} %pad_add_fusion), channel_id=1, source_target_pairs={{0,4},{4,0},{8,12},{12,8},{1,5},{5,1},{9,13},{13,9},{2,6},{6,2},{1... | collective-permute-start | bytes 584 | tf_op jit(solution)/shard_map/ppermute | solution.py:31
  15.4 24.2 %collective-permute-start.5 = (bf16[16,8,3,128,128]{4,3,2,1,0:T(8,128)(2,1)}, bf16[16,8,3,128,128]{4,3,2,1,0:T(8,128)(2,1)}, u32[]{:S(2)}, u32[]{:S(2)}) collective-permute-start(bf16[16,8,3,128,128]{4,3,2,1,0:T(8,128)(2,1)} %b_own.7), channel_id=1, source_target_pairs={{0,4},{4,0},{8,12},{12,8},{1,5},{5,1},{9,13},{13,9},{2,6},{6,2},{1... | collective-permute-start | bytes 37748744 | tf_op jit(solution)/shard_map/ppermute | solution.py:31
  15.7 9.1 %collective-permute-start.4 = (bf16[4,128,256]{2,1,0:T(8,128)(2,1)S(1)}, bf16[4,128,256]{2,1,0:T(8,128)(2,1)S(1)}, u32[]{:S(2)}, u32[]{:S(2)}) collective-permute-start(bf16[4,128,256]{2,1,0:T(8,128)(2,1)S(1)} %pad_maximum_fusion.own_ref), channel_id=1, source_target_pairs={{0,16},{4,52},{8,24},{12,60},{16,32},{20,4},{24,40},{28,12},{32,48... | collective-permute-start | bytes 786440 | tf_op jit(solution)/shard_map/ppermute | solution.py:31
  16.3 9.2 %collective-permute-start.6 = (bf16[4,128,256]{2,1,0:T(8,128)(2,1)S(1)}, bf16[4,128,256]{2,1,0:T(8,128)(2,1)S(1)}, u32[]{:S(2)}, u32[]{:S(2)}) collective-permute-start(bf16[4,128,256]{2,1,0:T(8,128)(2,1)S(1)} %pad_maximum_fusion.own_ref), channel_id=1, source_target_pairs={{0,48},{4,20},{8,56},{12,28},{16,0},{20,36},{24,8},{28,44},{32,16}... | collective-permute-start | bytes 786440 | tf_op jit(solution)/shard_map/ppermute | solution.py:31
  24.9 6.4 %collective-permute-start.7 = (bf16[4,128,256]{2,1,0:T(8,128)(2,1)S(1)}, bf16[4,128,256]{2,1,0:T(8,128)(2,1)S(1)}, u32[]{:S(2)}, u32[]{:S(2)}) collective-permute-start(bf16[4,128,256]{2,1,0:T(8,128)(2,1)S(1)} %collective-permute-done.4.ahead_ref), channel_id=1, source_target_pairs={{0,16},{4,52},{8,24},{12,60},{16,32},{20,4},{24,40},{28,12},{32,48... | collective-permute-start | bytes 786440 | tf_op jit(solution)/shard_map/ppermute | solution.py:31
  31.2 0.6 copy-start.2
  33.0 12.5 %collective-permute-start.10 = (bf16[2,128,768]{2,1,0:T(8,128)(2,1)S(1)}, bf16[2,128,768]{2,1,0:T(8,128)(2,1)S(1)}, u32[]{:S(2)}, u32[]{:S(2)}) collective-permute-start(bf16[2,128,768]{2,1,0:T(8,128)(2,1)S(1)} %shard_map.75.rest_0_), channel_id=1, source_target_pairs={{0,3},{1,0},{2,1},{3,2},{4,5},{5,6},{6,7},{7,4},{8,11},{9,8},{10,9... | collective-permute-start | bytes 1179656 | tf_op jit(solution)/shard_map/ppermute | solution.py:31
  36.0 9.4 %collective-permute-start.9 = (bf16[2,128,768]{2,1,0:T(8,128)(2,1)S(1)}, bf16[2,128,768]{2,1,0:T(8,128)(2,1)S(1)}, u32[]{:S(2)}, u32[]{:S(2)}) collective-permute-start(bf16[2,128,768]{2,1,0:T(8,128)(2,1)S(1)} %shard_map.75.rest_0_), channel_id=1, source_target_pairs={{0,8},{4,12},{8,0},{12,4},{1,9},{5,13},{9,1},{13,5},{2,10},{6,14},... | collective-permute-start | bytes 1179656 | tf_op jit(solution)/shard_map/ppermute | solution.py:31
  37.2 9.0 %collective-permute-start.8 = (bf16[2,128,768]{2,1,0:T(8,128)(2,1)S(1)}, bf16[2,128,768]{2,1,0:T(8,128)(2,1)S(1)}, u32[]{:S(2)}, u32[]{:S(2)}) collective-permute-start(bf16[2,128,768]{2,1,0:T(8,128)(2,1)S(1)} %shard_map.75.rest_0_), channel_id=1, source_target_pairs={{0,1},{1,2},{2,3},{3,0},{4,7},{5,4},{6,5},{7,6},{8,9},{9,10},{10,1... | collective-permute-start | bytes 1179656 | tf_op jit(solution)/shard_map/ppermute | solution.py:31
  39.6 0.7 copy-start.1
  46.2 14.7 %collective-permute-start.13 = (bf16[2,128,768]{2,1,0:T(8,128)(2,1)S(1)}, bf16[2,128,768]{2,1,0:T(8,128)(2,1)S(1)}, u32[]{:S(2)}, u32[]{:S(2)}) collective-permute-start(bf16[2,128,768]{2,1,0:T(8,128)(2,1)S(1)} %collective-permute-done.8.rest_0_), channel_id=1, source_target_pairs={{0,8},{4,12},{8,0},{12,4},{1,9},{5,13},{9,1},{13,5},{2,10},{6,14},... | collective-permute-start | bytes 1179656 | tf_op jit(solution)/shard_map/ppermute | solution.py:31
  48.4 12.9 %collective-permute-start.11 = (bf16[2,128,768]{2,1,0:T(8,128)(2,1)S(1)}, bf16[2,128,768]{2,1,0:T(8,128)(2,1)S(1)}, u32[]{:S(2)}, u32[]{:S(2)}) collective-permute-start(bf16[2,128,768]{2,1,0:T(8,128)(2,1)S(1)} %collective-permute-done.8.rest_0_), channel_id=1, source_target_pairs={{0,1},{1,2},{2,3},{3,0},{4,7},{5,4},{6,5},{7,6},{8,9},{9,10},{10,1... | collective-permute-start | bytes 1179656 | tf_op jit(solution)/shard_map/ppermute | solution.py:31
  48.4 12.5 %collective-permute-start.12 = (bf16[2,128,768]{2,1,0:T(8,128)(2,1)S(1)}, bf16[2,128,768]{2,1,0:T(8,128)(2,1)S(1)}, u32[]{:S(2)}, u32[]{:S(2)}) collective-permute-start(bf16[2,128,768]{2,1,0:T(8,128)(2,1)S(1)} %collective-permute-done.9.rest_1_), channel_id=1, source_target_pairs={{0,3},{1,0},{2,1},{3,2},{4,5},{5,6},{6,7},{7,4},{8,11},{9,8},{10,9... | collective-permute-start | bytes 1179656 | tf_op jit(solution)/shard_map/ppermute | solution.py:31
  61.2 9.0 %collective-permute-start.14 = (bf16[2,128,768]{2,1,0:T(8,128)(2,1)S(1)}, bf16[2,128,768]{2,1,0:T(8,128)(2,1)S(1)}, u32[]{:S(2)}, u32[]{:S(2)}) collective-permute-start(bf16[2,128,768]{2,1,0:T(8,128)(2,1)S(1)} %collective-permute-done.13.rest_2_), channel_id=1, source_target_pairs={{0,1},{1,2},{2,3},{3,0},{4,7},{5,4},{6,5},{7,6},{8,9},{9,10},{10,1... | collective-permute-start | bytes 1179656 | tf_op jit(solution)/shard_map/ppermute | solution.py:31
  73.9 2.0 %collective-permute-start.15 = (f32[4,128,256]{2,1,0:T(8,128)S(1)}, f32[4,128,256]{2,1,0:T(8,128)S(1)}, u32[]{:S(2)}, u32[]{:S(2)}) collective-permute-start(f32[4,128,256]{2,1,0:T(8,128)S(1)} %get-tuple-element.46), channel_id=1, source_target_pairs={{0,4},{4,0},{8,12},{12,8},{1,5},{5,1},{9,13},{13,9},{2,6},{6,2},{1... | collective-permute-start | bytes 1572872 | tf_op jit(solution)/shard_map/ppermute | solution.py:31
  76.0 8.0 %collective-permute-start.16 = (bf16[128,256]{1,0:T(8,128)(2,1)S(1)}, bf16[128,256]{1,0:T(8,128)(2,1)S(1)}, u32[]{:S(2)}, u32[]{:S(2)}) collective-permute-start(bf16[128,256]{1,0:T(8,128)(2,1)S(1)} %get-tuple-element.48), channel_id=1, source_target_pairs={{0,1},{1,2},{2,3},{3,0},{4,5},{5,6},{6,7},{7,4},{8,9},{9,10},{10,1... | collective-permute-start | bytes 196616 | tf_op jit(solution)/shard_map/ppermute | solution.py:31
  76.1 9.1 %collective-permute-start.17 = (bf16[128,256]{1,0:T(8,128)(2,1)S(1)}, bf16[128,256]{1,0:T(8,128)(2,1)S(1)}, u32[]{:S(2)}, u32[]{:S(2)}) collective-permute-start(bf16[128,256]{1,0:T(8,128)(2,1)S(1)} %get-tuple-element.49), channel_id=1, source_target_pairs={{0,2},{1,3},{2,0},{3,1},{4,6},{5,7},{6,4},{7,5},{8,10},{9,11},{10,... | collective-permute-start | bytes 196616 | tf_op jit(solution)/shard_map/ppermute | solution.py:31
  81.5 4.4 %collective-permute-start.18 = (bf16[128,256]{1,0:T(8,128)(2,1)S(1)}, bf16[128,256]{1,0:T(8,128)(2,1)S(1)}, u32[]{:S(2)}, u32[]{:S(2)}) collective-permute-start(bf16[128,256]{1,0:T(8,128)(2,1)S(1)} %get-tuple-element.50), channel_id=1, source_target_pairs={{0,3},{1,0},{2,1},{3,2},{4,7},{5,4},{6,5},{7,6},{8,11},{9,8},{10,9... | collective-permute-start | bytes 196616 | tf_op jit(solution)/shard_map/ppermute | solution.py:31

commit v6 on v5

--- a/solution.py
+++ b/solution.py
@@ -8,7 +8,7 @@
 from jax.sharding import PartitionSpec as P
 
 BLK = 128
-VECTORS_PER_GROUP = 4
+VECTORS_PER_GROUP = 8
 WIDE, NARROW = 4, 2
 X_SIZE = 4
 A_SLOTS, B_SLOTS, B_BLOCKS = 6, 3, 8
@@ -19,8 +19,10 @@
 B_SIGN = B_SOURCE + PAIRS
 OTHER = 2 * PAIRS
 ARRIVAL = 0x67521430
-FIRST_UNITS = (0, 1, 4, 7, 8)
-KERNELS = len(FIRST_UNITS) - 1
+UNITS = (range(0, 1), range(1, 4), range(4, 7), range(7, 8), range(6, 8))
+OWN_UNITS = (UNITS[0], UNITS[1], range(4, 6), range(0), UNITS[4])
+OTHER_UNITS = (UNITS[0], UNITS[1], UNITS[2], UNITS[3], range(0))
+KERNELS, FOR_OTHER = len(UNITS), 3
 PLAN = 64
 SMEM = pl.BlockSpec(memory_space=pltpu.SMEM)
 VMEM = pl.BlockSpec(memory_space=pltpu.VMEM)
@@ -76,10 +78,13 @@
         unit = (jnp.int32(ARRIVAL) >> (4 * (((owner ^ beta) & 2) * 2 + dy))) & 7
         live = (sign != 0) & ((owner & 1) == core)
         for index in range(KERNELS):
-            low, high = FIRST_UNITS[index], FIRST_UNITS[index + 1]
-            entry = pair + ((unit - low) << 6) + ((m & 1) << 9) + ((sign + 1) << 10)
+            used = (OTHER_UNITS if pair >= PAIRS else OWN_UNITS)[index]
+            if not used:
+                continue
+            entry = pair + ((unit - UNITS[index].start) << 6) + ((m & 1) << 9) + ((sign + 1) << 10)
             plan_ref[index * PLAN + 1 + counts[index]] = entry
-            counts[index] = counts[index] + jnp.where(live & (unit >= low) & (unit < high), 1, 0)
+            here = live & (unit >= used.start) & (unit < used.stop)
+            counts[index] = counts[index] + jnp.where(here, 1, 0)
     for index in range(KERNELS):
         plan_ref[index * PLAN] = counts[index]
 
@@ -102,15 +107,17 @@
         choose(dx, 0, X_SIZE, put)
 
 
-def contract_kernel(index, last, plan_ref, a_ref, b_own, b_other, *rest):
-    count_units = FIRST_UNITS[index + 1] - FIRST_UNITS[index]
+def contract_kernel(index, plan_ref, a_ref, b_own, b_other, *rest):
+    count_units = len(UNITS[index])
     units, rest = rest[:count_units], rest[count_units:]
     if index:
         sum_ref, rest = rest[0], rest[1:]
+    last = index >= FOR_OTHER
     if last:
-        chol_ref, mine_ref, other_ref, acc, c_buf, b_buf, c_sem, b_sem = rest
+        chol_ref, share_ref, acc, c_buf, b_buf, b_sem = rest
     else:
-        acc, c_buf, b_buf, c_sem, b_sem = rest
+        acc, c_buf, b_buf, b_sem = rest
+    first_block = B_BLOCKS if index == FOR_OTHER else 0
     vectors = b_own.shape[0]
     count = plan_ref[index * PLAN]
     wide_steps = count >> 2
@@ -123,22 +130,11 @@
     def entry_of(at):
         return plan_ref[index * PLAN + 1 + jnp.minimum(at, count - 1)]
 
-    def c_copy(unit, half, slot, lane):
-        return pltpu.make_async_copy(
-            unit.at[half], c_buf.at[slot, pl.ds(lane * BLK, BLK)], c_sem.at[slot, lane]
-        )
-
     def b_copy(ref, u, l, slot, lane, part):
         vectors_of = (pl.ds(0, VECTORS_PER_GROUP), pl.ds(VECTORS_PER_GROUP, vectors - VECTORS_PER_GROUP))[part]
         return pltpu.make_async_copy(
             ref.at[vectors_of, u, l], b_buf.at[slot, lane, vectors_of], b_sem.at[slot, lane, part]
         )
-
-    def start_c(step, slot, lanes):
-        for lane in lanes:
-            entry = entry_of(first_of(step) + lane)
-            half = (entry >> 9) & 1
-            choose((entry >> 6) & 7, 0, count_units, lambda i: c_copy(units[i], half, slot, lane).start())
 
     def start_b(step, slot, lanes, part):
         for lane in lanes:
@@ -159,7 +155,6 @@
 
     def start_step(step, slot):
         def start(lanes):
-            start_c(step, slot, lanes)
             for part in range(2):
                 start_b(step, slot, lanes, part)
 
@@ -172,19 +167,25 @@
             start(range(NARROW))
 
     start_step(0, 0)
-    acc[...] = sum_ref[...] if index else jnp.zeros_like(acc)
+    acc[...] = sum_ref[first_block : first_block + acc.shape[0]] if index else jnp.zeros_like(acc)
 
     def body(width, step, carry):
         slot = step & 1
         start_step(step + 1, 1 - slot)
         for lane in range(width):
-            c_copy(units[0], 0, slot, lane).wait()
+            entry = entry_of(first_of(step) + lane)
+            half = (entry >> 9) & 1
+
+            def fill(i, lane=lane, half=half):
+                c_buf[lane * BLK : (lane + 1) * BLK] = units[i][half]
+
+            choose((entry >> 6) & 7, 0, count_units, fill)
         sums = [jnp.zeros((BLK, BLK), jnp.float32) for _ in range(width)]
 
         def panel_of(group):
             columns = slice(group * BLK, (group + VECTORS_PER_GROUP) * BLK)
             return jnp.dot(
-                c_buf[slot, : width * BLK], a_ref[:, columns], preferred_element_type=jnp.float32
+                c_buf[: width * BLK], a_ref[:, columns], preferred_element_type=jnp.float32
             ).astype(jnp.bfloat16)
 
         panel = panel_of(0)
@@ -209,7 +210,7 @@
             at = first_of(step) + lane
             entry = entry_of(at)
             factor = jnp.where(at < count, (entry >> 10) - 1, 0).astype(jnp.float32)
-            acc[(entry & 63) // B_SLOTS] += factor * sums[lane]
+            acc[(entry & 63) // B_SLOTS - first_block] += factor * sums[lane]
         return carry
 
     lax.fori_loop(0, wide_steps, functools.partial(body, WIDE), 0)
@@ -218,15 +219,13 @@
         for shift in range(4):
             for half in range(2):
                 u = ((chol_ref[0] + shift) & 3) * 2 + half
-                lanes = slice(half * BLK, (half + 1) * BLK)
-                mine_ref[shift, :, lanes] = acc[u].T
-                other_ref[shift, :, lanes] = acc[B_BLOCKS + u].T
+                share_ref[shift, :, half * BLK : (half + 1) * BLK] = acc[u].T
 
 
 def contract(index, plan, a_flipped, b_own, b_other, units, running=None, chol=None):
     vectors, blocks = b_own.shape[:2]
-    last = chol is not None
-    part = len(units) / 8
+    last = index >= FOR_OTHER
+    part = (len(OWN_UNITS[index]) + len(OTHER_UNITS[index])) / 16
     flops = int(part * 2 * (a_flipped.size * blocks * B_SLOTS * BLK + b_own.size * BLK))
     moved = int(part * 2 * b_own.size) + 2 * a_flipped.size
     whole = jax.ShapeDtypeStruct((2 * blocks, BLK, BLK), jnp.float32)
@@ -234,15 +233,14 @@
     sums = [] if running is None else [running]
     chols = [chol] if last else []
     return pl.pallas_call(
-        functools.partial(contract_kernel, index, last),
-        out_shape=[shares, shares] if last else whole,
-        in_specs=[SMEM, VMEM, HBM, HBM] + [HBM] * len(units) + [VMEM] * len(sums) + [SMEM] * len(chols),
-        out_specs=[VMEM, VMEM] if last else VMEM,
-        scratch_shapes=[pltpu.VMEM(whole.shape, jnp.float32)] * last
+        functools.partial(contract_kernel, index),
+        out_shape=shares if last else whole,
+        in_specs=[SMEM, VMEM, HBM, HBM] + [VMEM] * (len(units) + len(sums)) + [SMEM] * len(chols),
+        out_specs=VMEM,
+        scratch_shapes=[pltpu.VMEM((blocks, BLK, BLK), jnp.float32)] * last
         + [
-            pltpu.VMEM((2, WIDE * BLK, A_SLOTS * BLK), jnp.bfloat16),
+            pltpu.VMEM((WIDE * BLK, A_SLOTS * BLK), jnp.bfloat16),
             pltpu.VMEM((2, WIDE, vectors, BLK, BLK), jnp.bfloat16),
-            pltpu.SemaphoreType.DMA((2, WIDE)),
             pltpu.SemaphoreType.DMA((2, WIDE, 2)),
         ],
         compiler_params=pltpu.CompilerParams(vmem_limit_bytes=47 * 1024 * 1024),
@@ -343,7 +341,8 @@
     far_middle = by_core(far_ahead, 1)
     running = contract(2, *tiles, [middle, far_back, far_ahead], running)
     running, far_middle = lax.optimization_barrier((running, far_middle))
-    return contract(3, *tiles, [far_middle], running, chol=chol)
+    other = contract(FOR_OTHER, *tiles, [far_middle], running, chol)
+    return contract(4, *tiles, [far_ahead, far_middle], running, chol), other
 
 
 def per_device(sizes, ci_vector, a_tiles, a_source, a_sign, b_tiles, b_source, b_sign):

time: 87.8 us -> 82.9 us (0.944); the launches traced: 86.6 us -> 83 us
  waiting for transfers between devices: 19.2 us -> 26.1 us
  starting transfers between devices: 30.4 us -> 25 us
  Pallas kernels: 30.8 us -> 25.6 us
    ppermute x19, waiting for transfers between devices: 19.2 us -> 26.1 us  [shifted(): return lax.ppermute(value, axis, [(i, moves_to(i)) for i in range(size)])]
    ppermute x19, starting transfers between devices: 30.4 us -> 25 us  [shifted(): return lax.ppermute(value, axis, [(i, moves_to(i)) for i in range(size)])]
    pallas_call x4 -> x5, Pallas kernels: 25.1 us -> 19.8 us  [contract(): pl.pallas_call(functools.partial(contract_kernel, index), out_shape=share...]
  transfers between devices with their start and end apart: 19 -> 19, of which waited for: 11 -> 11; matrix products, arithmetic and copies ran while one was open for 4% -> 4% of each run, Pallas kernels for 31% -> 28%
where the time goes in v6:
time: 82.9 us; the launch traced here: 83 us
  waiting for transfers between devices  26.1 us (31%)
  Pallas kernels  25.6 us (31%)
  starting transfers between devices  25 us (30%)
  local copies, waits for them, and re-layouts  5.31 us (6%)
    ppermute x19, waiting for transfers between devices, shifted(): return lax.ppermute(value, axis, [(i, moves_to(i)) for i in range(size)])  26.1 us
    ppermute x19, starting transfers between devices, shifted(): return lax.ppermute(value, axis, [(i, moves_to(i)) for i in range(size)])  25 us
    pallas_call x5, Pallas kernels, contract(): pl.pallas_call(functools.partial(contract_kernel, index), out_shape=share...  19.8 us
    unnamed x8, local copies, waits for them, and re-layouts  3.8 us
    pallas_call x1, Pallas kernels, flip(): pl.pallas_call(flip_kernel, out_shape=jax.ShapeDtypeStruct((A_SLOTS * BLK...  2.33 us
    pallas_call x1, Pallas kernels, make_plan(): pl.pallas_call(plan_kernel, out_shape=jax.ShapeDtypeStruct((KERNELS * PLA...  2.27 us
  transfers between devices with their start and end apart: 19, of which 11 were waited for; matrix products, arithmetic and copies ran while one was open for 4% of the time, Pallas kernels for 28%

profile of v6, /device:TPU:6, one launch (start us, length us, event | category | flops | bytes accessed | tf_op | source)
XLA Modules:
  0.0 83.0 jit_solution(11216072442992143828)
XLA Ops:
  0.0 0.9 %copy-done = bf16[128,1024]{1,0:T(8,128)(2,1)S(1)} copy-done((bf16[128,1024]{1,0:T(8,128)(2,1)S(1)}, bf16[128,1024]{1,0:T(8,128)(2,1)}, u32[]{:S(2)}) %copy-start) | copy-done | bytes 262168
  1.0 7.3 %collective-permute-start.1 = (bf16[128,256]{1,0:T(8,128)(2,1)S(1)}, bf16[128,256]{1,0:T(8,128)(2,1)S(1)}, u32[]{:S(2)}, u32[]{:S(2)}) collective-permute-start(bf16[128,256]{1,0:T(8,128)(2,1)S(1)} %constant_dynamic-slice_fusion), channel_id=1, source_target_pairs={{0,128},{16,144},{32,160},{48,176},{64,192},{80,208},{96,224},{112... | collective-permute-start | bytes 196616 | tf_op jit(solution)/shard_map/ppermute | solution.py:33
  8.2 2.9 %collective-permute-start.2 = (bf16[128,256]{1,0:T(8,128)(2,1)S(1)}, bf16[128,256]{1,0:T(8,128)(2,1)S(1)}, u32[]{:S(2)}, u32[]{:S(2)}) collective-permute-start(bf16[128,256]{1,0:T(8,128)(2,1)S(1)} %constant_dynamic-slice_fusion), channel_id=1, source_target_pairs={{0,64},{16,80},{32,96},{48,112},{64,128},{80,144},{96,160},{112,17... | collective-permute-start | bytes 196616 | tf_op jit(solution)/shard_map/ppermute | solution.py:33
  11.2 0.8 copy.10
  12.0 0.8 copy.11
  13.0 1.1 %collective-permute-done.3 = s32[48]{0:T(128)S(1)} collective-permute-done((s32[48]{0:T(128)S(1)}, s32[48]{0:T(128)S(1)}, u32[]{:S(2)}, u32[]{:S(2)}) %collective-permute-start.3) | collective-permute-done | bytes 224 | tf_op jit(solution)/shard_map/ppermute | solution.py:33
  14.1 1.3 %concatenate.8.meta_ref = s32[111]{0:T(128)} concatenate(s32[1]{0:T(128)} %bitcast.1, s32[1]{0:T(128)} %bitcast.2, s32[1]{0:T(128)} %bitcast.3.rest_3_.rest_2_, s32[6]{0:T(128)} %bitcast.13, s32[6]{0:T(128)} %bitcast.14, s32[24]{0:T(128)S(1)} %reshape.14, s32[24]{0:T(128)S(1)} %reshape.15, s32[48]{0:T(128)S(1)} %collective-permute-done.3), dimensions={0} | concatenate | bytes 888 | tf_op jit(solution)/shard_map/concatenate | solution.py:359
  16.3 1.5 %collective-permute-start.6 = (bf16[4,128,256]{2,1,0:T(8,128)(2,1)S(1)}, bf16[4,128,256]{2,1,0:T(8,128)(2,1)S(1)}, u32[]{:S(2)}, u32[]{:S(2)}) collective-permute-start(bf16[4,128,256]{2,1,0:T(8,128)(2,1)S(1)} %pad_maximum_fusion.own_ref), channel_id=1, source_target_pairs={{0,48},{4,20},{8,56},{12,28},{16,0},{20,36},{24,8},{28,44},{32,16}... | collective-permute-start | bytes 786440 | tf_op jit(solution)/shard_map/ppermute | solution.py:33
  17.9 2.3 %shard_map.73.plan_ref = s32[320]{0:T(512)} custom-call(s32[111]{0:T(128)} %concatenate.8.meta_ref), custom_call_target="tpu_custom_call" | custom-call | tf_op jit(solution)/shard_map/pallas_call | solution.py:282
  20.1 4.8 %collective-permute-done.4.ahead_ref = bf16[4,128,256]{2,1,0:T(8,128)(2,1)S(1)} collective-permute-done((bf16[4,128,256]{2,1,0:T(8,128)(2,1)S(1)}, bf16[4,128,256]{2,1,0:T(8,128)(2,1)S(1)}, u32[]{:S(2)}, u32[]{:S(2)}) %collective-permute-start.4) | collective-permute-done | bytes 262176 | tf_op jit(solution)/shard_map/ppermute | solution.py:33
  25.6 5.7 %collective-permute-done.7.far_ref = bf16[4,128,256]{2,1,0:T(8,128)(2,1)S(1)} collective-permute-done((bf16[4,128,256]{2,1,0:T(8,128)(2,1)S(1)}, bf16[4,128,256]{2,1,0:T(8,128)(2,1)S(1)}, u32[]{:S(2)}, u32[]{:S(2)}) %collective-permute-start.7) | collective-permute-done | bytes 262176 | tf_op jit(solution)/shard_map/ppermute | solution.py:33
  31.9 1.1 %shard_map.75.rest_0_ = bf16[2,128,768]{2,1,0:T(8,128)(2,1)S(1)} custom-call(s32[111]{0:T(128)S(1)} %copy-done.2, bf16[4,128,256]{2,1,0:T(8,128)(2,1)S(1)} %pad_maximum_fusion.own_ref, bf16[4,128,256]{2,1,0:T(8,128)(2,1)S(1)} %collective-permute-done.6.back_ref, bf16[4,128,256]{2,1,0:T(8,128)(2,1)S(1)} %collective-permute-done.7.far_ref, ...), custom_call_target="tpu_custom_call" | custom-call | tf_op jit(solution)/shard_map/pallas_call | solution.py:311
  33.0 3.1 %collective-permute-start.10 = (bf16[2,128,768]{2,1,0:T(8,128)(2,1)S(1)}, bf16[2,128,768]{2,1,0:T(8,128)(2,1)S(1)}, u32[]{:S(2)}, u32[]{:S(2)}) collective-permute-start(bf16[2,128,768]{2,1,0:T(8,128)(2,1)S(1)} %shard_map.75.rest_0_), channel_id=1, source_target_pairs={{0,3},{1,0},{2,1},{3,2},{4,5},{5,6},{6,7},{7,4},{8,11},{9,8},{10,9... | collective-permute-start | bytes 1179656 | tf_op jit(solution)/shard_map/ppermute | solution.py:33
  36.1 1.1 %collective-permute-start.9 = (bf16[2,128,768]{2,1,0:T(8,128)(2,1)S(1)}, bf16[2,128,768]{2,1,0:T(8,128)(2,1)S(1)}, u32[]{:S(2)}, u32[]{:S(2)}) collective-permute-start(bf16[2,128,768]{2,1,0:T(8,128)(2,1)S(1)} %shard_map.75.rest_0_), channel_id=1, source_target_pairs={{0,8},{4,12},{8,0},{12,4},{1,9},{5,13},{9,1},{13,5},{2,10},{6,14},... | collective-permute-start | bytes 1179656 | tf_op jit(solution)/shard_map/ppermute | solution.py:33
  37.2 2.3 %shard_map.74.a_ref = bf16[768,2048]{1,0:T(8,128)(2,1)S(1)} custom-call(bf16[16,1,6,128,128]{4,3,2,1,0:T(8,128)(2,1)} %a_hbm.1), custom_call_target="tpu_custom_call" | custom-call | bytes 6291456 | tf_op jit(solution)/shard_map/pallas_call | solution.py:270
  39.6 0.7 copy-done.1
  40.3 2.5 %shard_map.76.rest_3_ = f32[16,128,128]{2,1,0:T(8,128)S(1)} custom-call(s32[320]{0:T(512)S(1)} %copy-done.1, bf16[768,2048]{1,0:T(8,128)(2,1)S(1)} %shard_map.74.a_ref, bf16[16,8,3,128,128]{4,3,2,1,0:T(8,128)(2,1)} %b_own.9, bf16[16,8,3,128,128]{4,3,2,1,0:T(8,128)(2,1)} %collective-permute-done.5.b_other, bf16[2,128,768]{2,1,0:T(8,128)(2,1)S(1)} %shard_map.75.rest_0_), custom_call_target="tpu_custom_call" | custom-call | flops 1409286144 | bytes 4718592 | tf_op jit(solution)/shard_map/pallas_call | solution.py:235
  42.8 2.8 %collective-permute-done.10.rest_2_ = bf16[2,128,768]{2,1,0:T(8,128)(2,1)S(1)} collective-permute-done((bf16[2,128,768]{2,1,0:T(8,128)(2,1)S(1)}, bf16[2,128,768]{2,1,0:T(8,128)(2,1)S(1)}, u32[]{:S(2)}, u32[]{:S(2)}) %collective-permute-start.10) | collective-permute-done | bytes 393248 | tf_op jit(solution)/shard_map/ppermute | solution.py:33
  46.2 0.9 %collective-permute-start.13 = (bf16[2,128,768]{2,1,0:T(8,128)(2,1)S(1)}, bf16[2,128,768]{2,1,0:T(8,128)(2,1)S(1)}, u32[]{:S(2)}, u32[]{:S(2)}) collective-permute-start(bf16[2,128,768]{2,1,0:T(8,128)(2,1)S(1)} %collective-permute-done.8.rest_0_), channel_id=1, source_target_pairs={{0,8},{4,12},{8,0},{12,4},{1,9},{5,13},{9,1},{13,5},{2,10},{6,14},... | collective-permute-start | bytes 1179656 | tf_op jit(solution)/shard_map/ppermute | solution.py:33
  47.1 1.1 %collective-permute-start.11 = (bf16[2,128,768]{2,1,0:T(8,128)(2,1)S(1)}, bf16[2,128,768]{2,1,0:T(8,128)(2,1)S(1)}, u32[]{:S(2)}, u32[]{:S(2)}) collective-permute-start(bf16[2,128,768]{2,1,0:T(8,128)(2,1)S(1)} %collective-permute-done.8.rest_0_), channel_id=1, source_target_pairs={{0,1},{1,2},{2,3},{3,0},{4,7},{5,4},{6,5},{7,6},{8,9},{9,10},{10,1... | collective-permute-start | bytes 1179656 | tf_op jit(solution)/shard_map/ppermute | solution.py:33
  48.2 2.2 %collective-permute-start.12 = (bf16[2,128,768]{2,1,0:T(8,128)(2,1)S(1)}, bf16[2,128,768]{2,1,0:T(8,128)(2,1)S(1)}, u32[]{:S(2)}, u32[]{:S(2)}) collective-permute-start(bf16[2,128,768]{2,1,0:T(8,128)(2,1)S(1)} %collective-permute-done.9.rest_1_), channel_id=1, source_target_pairs={{0,3},{1,0},{2,1},{3,2},{4,5},{5,6},{6,7},{7,4},{8,11},{9,8},{10,9... | collective-permute-start | bytes 1179656 | tf_op jit(solution)/shard_map/ppermute | solution.py:33
  50.4 5.2 %shard_map.77.rest_3_ = f32[16,128,128]{2,1,0:T(8,128)S(1)} custom-call(s32[320]{0:T(512)S(1)} %copy-done.1, bf16[768,2048]{1,0:T(8,128)(2,1)S(1)} %shard_map.74.a_ref, bf16[16,8,3,128,128]{4,3,2,1,0:T(8,128)(2,1)} %b_own.9, bf16[16,8,3,128,128]{4,3,2,1,0:T(8,128)(2,1)} %collective-permute-done.5.b_other, ...), custom_call_target="tpu_custom_call" | custom-call | flops 4227858432 | bytes 7864320 | tf_op jit(solution)/shard_map/pallas_call | solution.py:235
  55.6 2.3 %collective-permute-done.12.rest_1_ = bf16[2,128,768]{2,1,0:T(8,128)(2,1)S(1)} collective-permute-done((bf16[2,128,768]{2,1,0:T(8,128)(2,1)S(1)}, bf16[2,128,768]{2,1,0:T(8,128)(2,1)S(1)}, u32[]{:S(2)}, u32[]{:S(2)}) %collective-permute-start.12) | collective-permute-done | bytes 393248 | tf_op jit(solution)/shard_map/ppermute | solution.py:33
  57.9 1.4 %collective-permute-done.11.rest_0_ = bf16[2,128,768]{2,1,0:T(8,128)(2,1)S(1)} collective-permute-done((bf16[2,128,768]{2,1,0:T(8,128)(2,1)S(1)}, bf16[2,128,768]{2,1,0:T(8,128)(2,1)S(1)}, u32[]{:S(2)}, u32[]{:S(2)}) %collective-permute-start.11) | collective-permute-done | bytes 393248 | tf_op jit(solution)/shard_map/ppermute | solution.py:33
  60.0 5.4 %shard_map.78.rest_2_.rest_1_ = f32[16,128,128]{2,1,0:T(8,128)S(1)} custom-call(s32[320]{0:T(512)S(1)} %copy-done.1, bf16[768,2048]{1,0:T(8,128)(2,1)S(1)} %shard_map.74.a_ref, bf16[16,8,3,128,128]{4,3,2,1,0:T(8,128)(2,1)} %b_own.9, bf16[16,8,3,128,128]{4,3,2,1,0:T(8,128)(2,1)} %collective-permute-done.5.b_other, ...), custom_call_target="tpu_custom_call" | custom-call | flops 3523215360 | bytes 7077888 | tf_op jit(solution)/shard_map/pallas_call | solution.py:235
  65.4 2.9 %collective-permute-done.14.rest_1_.rest_0_ = bf16[2,128,768]{2,1,0:T(8,128)(2,1)S(1)} collective-permute-done((bf16[2,128,768]{2,1,0:T(8,128)(2,1)S(1)}, bf16[2,128,768]{2,1,0:T(8,128)(2,1)S(1)}, u32[]{:S(2)}, u32[]{:S(2)}) %collective-permute-start.14) | collective-permute-done | bytes 393248 | tf_op jit(solution)/shard_map/ppermute | solution.py:33
  68.3 2.6 %shard_map.80 = f32[4,128,256]{2,1,0:T(8,128)S(1)} custom-call(s32[320]{0:T(512)S(1)} %copy-done.1, bf16[768,2048]{1,0:T(8,128)(2,1)S(1)} %shard_map.74.a_ref, bf16[16,8,3,128,128]{4,3,2,1,0:T(8,128)(2,1)} %b_own.9, bf16[16,8,3,128,128]{4,3,2,1,0:T(8,128)(2,1)} %collective-permute-done.5.b_other, ...), custom_call_target="tpu_custom_call" | custom-call | flops 704643072 | bytes 3932160 | tf_op jit(solution)/shard_map/pallas_call | solution.py:235
  71.0 4.1 %shard_map.79.mine_ref = f32[4,128,256]{2,1,0:T(8,128)S(1)} custom-call(s32[320]{0:T(512)S(1)} %copy-done.1, bf16[768,2048]{1,0:T(8,128)(2,1)S(1)} %shard_map.74.a_ref, bf16[16,8,3,128,128]{4,3,2,1,0:T(8,128)(2,1)} %b_own.9, bf16[16,8,3,128,128]{4,3,2,1,0:T(8,128)(2,1)} %collective-permute-done.5.b_other, ...), custom_call_target="tpu_custom_call" | custom-call | flops 1409286144 | bytes 4718592 | tf_op jit(solution)/shard_map/pallas_call | solution.py:235
  75.3 1.0 %collective-permute-start.17 = (bf16[128,256]{1,0:T(8,128)(2,1)S(1)}, bf16[128,256]{1,0:T(8,128)(2,1)S(1)}, u32[]{:S(2)}, u32[]{:S(2)}) collective-permute-start(bf16[128,256]{1,0:T(8,128)(2,1)S(1)} %get-tuple-element.45), channel_id=1, source_target_pairs={{0,2},{1,3},{2,0},{3,1},{4,6},{5,7},{6,4},{7,5},{8,10},{9,11},{10,... | collective-permute-start | bytes 196616 | tf_op jit(solution)/shard_map/ppermute | solution.py:33
  76.3 2.3 %collective-permute-start.18 = (bf16[128,256]{1,0:T(8,128)(2,1)S(1)}, bf16[128,256]{1,0:T(8,128)(2,1)S(1)}, u32[]{:S(2)}, u32[]{:S(2)}) collective-permute-start(bf16[128,256]{1,0:T(8,128)(2,1)S(1)} %get-tuple-element.46), channel_id=1, source_target_pairs={{0,3},{1,0},{2,1},{3,2},{4,7},{5,4},{6,5},{7,6},{8,11},{9,8},{10,9... | collective-permute-start | bytes 196616 | tf_op jit(solution)/shard_map/ppermute | solution.py:33
  78.5 2.9 %collective-permute-done.16 = bf16[128,256]{1,0:T(8,128)(2,1)S(1)} collective-permute-done((bf16[128,256]{1,0:T(8,128)(2,1)S(1)}, bf16[128,256]{1,0:T(8,128)(2,1)S(1)}, u32[]{:S(2)}, u32[]{:S(2)}) %collective-permute-start.16) | collective-permute-done | bytes 65568 | tf_op jit(solution)/shard_map/ppermute | solution.py:33
  81.5 0.9 %collective-permute-done.18 = bf16[128,256]{1,0:T(8,128)(2,1)S(1)} collective-permute-done((bf16[128,256]{1,0:T(8,128)(2,1)S(1)}, bf16[128,256]{1,0:T(8,128)(2,1)S(1)}, u32[]{:S(2)}, u32[]{:S(2)}) %collective-permute-start.18) | collective-permute-done | bytes 65568 | tf_op jit(solution)/shard_map/ppermute | solution.py:33
  (31 shorter events, 4.7 us)
Async XLA Ops:
  0.0 1.0 %copy-start = (bf16[128,1024]{1,0:T(8,128)(2,1)S(1)}, bf16[128,1024]{1,0:T(8,128)(2,1)}, u32[]{:S(2)}) copy-start(bf16[128,1024]{1,0:T(8,128)(2,1)} %param.7) | copy-start | bytes 786436
  1.0 14.4 %collective-permute-start.1 = (bf16[128,256]{1,0:T(8,128)(2,1)S(1)}, bf16[128,256]{1,0:T(8,128)(2,1)S(1)}, u32[]{:S(2)}, u32[]{:S(2)}) collective-permute-start(bf16[128,256]{1,0:T(8,128)(2,1)S(1)} %constant_dynamic-slice_fusion), channel_id=1, source_target_pairs={{0,128},{16,144},{32,160},{48,176},{64,192},{80,208},{96,224},{112... | collective-permute-start | bytes 196616 | tf_op jit(solution)/shard_map/ppermute | solution.py:33
  8.2 7.2 %collective-permute-start = (bf16[128,256]{1,0:T(8,128)(2,1)S(1)}, bf16[128,256]{1,0:T(8,128)(2,1)S(1)}, u32[]{:S(2)}, u32[]{:S(2)}) collective-permute-start(bf16[128,256]{1,0:T(8,128)(2,1)S(1)} %constant_dynamic-slice_fusion), channel_id=1, source_target_pairs={{0,192},{16,208},{32,224},{48,240},{64,0},{80,16},{96,32},{112,48}... | collective-permute-start | bytes 196616 | tf_op jit(solution)/shard_map/ppermute | solution.py:33
  8.2 7.2 %collective-permute-start.2 = (bf16[128,256]{1,0:T(8,128)(2,1)S(1)}, bf16[128,256]{1,0:T(8,128)(2,1)S(1)}, u32[]{:S(2)}, u32[]{:S(2)}) collective-permute-start(bf16[128,256]{1,0:T(8,128)(2,1)S(1)} %constant_dynamic-slice_fusion), channel_id=1, source_target_pairs={{0,64},{16,80},{32,96},{48,112},{64,128},{80,144},{96,160},{112,17... | collective-permute-start | bytes 196616 | tf_op jit(solution)/shard_map/ppermute | solution.py:33
  12.9 1.1 %collective-permute-start.3 = (s32[48]{0:T(128)S(1)}, s32[48]{0:T(128)S(1)}, u32[]{:S(2)}, u32[]{:S(2)}) collective-permute-start(s32[48]{0:T(128)S(1)} %pad_add_fusion), channel_id=1, source_target_pairs={{0,4},{4,0},{8,12},{12,8},{1,5},{5,1},{9,13},{13,9},{2,6},{6,2},{1... | collective-permute-start | bytes 584 | tf_op jit(solution)/shard_map/ppermute | solution.py:33
  15.4 24.2 %collective-permute-start.5 = (bf16[16,8,3,128,128]{4,3,2,1,0:T(8,128)(2,1)}, bf16[16,8,3,128,128]{4,3,2,1,0:T(8,128)(2,1)}, u32[]{:S(2)}, u32[]{:S(2)}) collective-permute-start(bf16[16,8,3,128,128]{4,3,2,1,0:T(8,128)(2,1)} %b_own.9), channel_id=1, source_target_pairs={{0,4},{4,0},{8,12},{12,8},{1,5},{5,1},{9,13},{13,9},{2,6},{6,2},{1... | collective-permute-start | bytes 37748744 | tf_op jit(solution)/shard_map/ppermute | solution.py:33
  15.8 9.1 %collective-permute-start.4 = (bf16[4,128,256]{2,1,0:T(8,128)(2,1)S(1)}, bf16[4,128,256]{2,1,0:T(8,128)(2,1)S(1)}, u32[]{:S(2)}, u32[]{:S(2)}) collective-permute-start(bf16[4,128,256]{2,1,0:T(8,128)(2,1)S(1)} %pad_maximum_fusion.own_ref), channel_id=1, source_target_pairs={{0,16},{4,52},{8,24},{12,60},{16,32},{20,4},{24,40},{28,12},{32,48... | collective-permute-start | bytes 786440 | tf_op jit(solution)/shard_map/ppermute | solution.py:33
  16.3 9.2 %collective-permute-start.6 = (bf16[4,128,256]{2,1,0:T(8,128)(2,1)S(1)}, bf16[4,128,256]{2,1,0:T(8,128)(2,1)S(1)}, u32[]{:S(2)}, u32[]{:S(2)}) collective-permute-start(bf16[4,128,256]{2,1,0:T(8,128)(2,1)S(1)} %pad_maximum_fusion.own_ref), channel_id=1, source_target_pairs={{0,48},{4,20},{8,56},{12,28},{16,0},{20,36},{24,8},{28,44},{32,16}... | collective-permute-start | bytes 786440 | tf_op jit(solution)/shard_map/ppermute | solution.py:33
  24.9 6.4 %collective-permute-start.7 = (bf16[4,128,256]{2,1,0:T(8,128)(2,1)S(1)}, bf16[4,128,256]{2,1,0:T(8,128)(2,1)S(1)}, u32[]{:S(2)}, u32[]{:S(2)}) collective-permute-start(bf16[4,128,256]{2,1,0:T(8,128)(2,1)S(1)} %collective-permute-done.4.ahead_ref), channel_id=1, source_target_pairs={{0,16},{4,52},{8,24},{12,60},{16,32},{20,4},{24,40},{28,12},{32,48... | collective-permute-start | bytes 786440 | tf_op jit(solution)/shard_map/ppermute | solution.py:33
  31.3 0.7 copy-start.2
  33.0 12.6 %collective-permute-start.10 = (bf16[2,128,768]{2,1,0:T(8,128)(2,1)S(1)}, bf16[2,128,768]{2,1,0:T(8,128)(2,1)S(1)}, u32[]{:S(2)}, u32[]{:S(2)}) collective-permute-start(bf16[2,128,768]{2,1,0:T(8,128)(2,1)S(1)} %shard_map.75.rest_0_), channel_id=1, source_target_pairs={{0,3},{1,0},{2,1},{3,2},{4,5},{5,6},{6,7},{7,4},{8,11},{9,8},{10,9... | collective-permute-start | bytes 1179656 | tf_op jit(solution)/shard_map/ppermute | solution.py:33
  36.1 9.5 %collective-permute-start.9 = (bf16[2,128,768]{2,1,0:T(8,128)(2,1)S(1)}, bf16[2,128,768]{2,1,0:T(8,128)(2,1)S(1)}, u32[]{:S(2)}, u32[]{:S(2)}) collective-permute-start(bf16[2,128,768]{2,1,0:T(8,128)(2,1)S(1)} %shard_map.75.rest_0_), channel_id=1, source_target_pairs={{0,8},{4,12},{8,0},{12,4},{1,9},{5,13},{9,1},{13,5},{2,10},{6,14},... | collective-permute-start | bytes 1179656 | tf_op jit(solution)/shard_map/ppermute | solution.py:33
  37.2 9.0 %collective-permute-start.8 = (bf16[2,128,768]{2,1,0:T(8,128)(2,1)S(1)}, bf16[2,128,768]{2,1,0:T(8,128)(2,1)S(1)}, u32[]{:S(2)}, u32[]{:S(2)}) collective-permute-start(bf16[2,128,768]{2,1,0:T(8,128)(2,1)S(1)} %shard_map.75.rest_0_), channel_id=1, source_target_pairs={{0,1},{1,2},{2,3},{3,0},{4,7},{5,4},{6,5},{7,6},{8,9},{9,10},{10,1... | collective-permute-start | bytes 1179656 | tf_op jit(solution)/shard_map/ppermute | solution.py:33
  39.6 0.7 copy-start.1
  46.2 11.7 %collective-permute-start.13 = (bf16[2,128,768]{2,1,0:T(8,128)(2,1)S(1)}, bf16[2,128,768]{2,1,0:T(8,128)(2,1)S(1)}, u32[]{:S(2)}, u32[]{:S(2)}) collective-permute-start(bf16[2,128,768]{2,1,0:T(8,128)(2,1)S(1)} %collective-permute-done.8.rest_0_), channel_id=1, source_target_pairs={{0,8},{4,12},{8,0},{12,4},{1,9},{5,13},{9,1},{13,5},{2,10},{6,14},... | collective-permute-start | bytes 1179656 | tf_op jit(solution)/shard_map/ppermute | solution.py:33
  47.1 12.2 %collective-permute-start.11 = (bf16[2,128,768]{2,1,0:T(8,128)(2,1)S(1)}, bf16[2,128,768]{2,1,0:T(8,128)(2,1)S(1)}, u32[]{:S(2)}, u32[]{:S(2)}) collective-permute-start(bf16[2,128,768]{2,1,0:T(8,128)(2,1)S(1)} %collective-permute-done.8.rest_0_), channel_id=1, source_target_pairs={{0,1},{1,2},{2,3},{3,0},{4,7},{5,4},{6,5},{7,6},{8,9},{9,10},{10,1... | collective-permute-start | bytes 1179656 | tf_op jit(solution)/shard_map/ppermute | solution.py:33
  48.2 9.7 %collective-permute-start.12 = (bf16[2,128,768]{2,1,0:T(8,128)(2,1)S(1)}, bf16[2,128,768]{2,1,0:T(8,128)(2,1)S(1)}, u32[]{:S(2)}, u32[]{:S(2)}) collective-permute-start(bf16[2,128,768]{2,1,0:T(8,128)(2,1)S(1)} %collective-permute-done.9.rest_1_), channel_id=1, source_target_pairs={{0,3},{1,0},{2,1},{3,2},{4,5},{5,6},{6,7},{7,4},{8,11},{9,8},{10,9... | collective-permute-start | bytes 1179656 | tf_op jit(solution)/shard_map/ppermute | solution.py:33
  59.3 9.0 %collective-permute-start.14 = (bf16[2,128,768]{2,1,0:T(8,128)(2,1)S(1)}, bf16[2,128,768]{2,1,0:T(8,128)(2,1)S(1)}, u32[]{:S(2)}, u32[]{:S(2)}) collective-permute-start(bf16[2,128,768]{2,1,0:T(8,128)(2,1)S(1)} %collective-permute-done.13.rest_2_.rest_0_), channel_id=1, source_target_pairs={{0,1},{1,2},{2,3},{3,0},{4,7},{5,4},{6,5},{7,6},{8,9},{9,10},{10,1... | collective-permute-start | bytes 1179656 | tf_op jit(solution)/shard_map/ppermute | solution.py:33
  70.9 4.2 %collective-permute-start.15 = (f32[4,128,256]{2,1,0:T(8,128)S(1)}, f32[4,128,256]{2,1,0:T(8,128)S(1)}, u32[]{:S(2)}, u32[]{:S(2)}) collective-permute-start(f32[4,128,256]{2,1,0:T(8,128)S(1)} %shard_map.80), channel_id=1, source_target_pairs={{0,4},{4,0},{8,12},{12,8},{1,5},{5,1},{9,13},{13,9},{2,6},{6,2},{1... | collective-permute-start | bytes 1572872 | tf_op jit(solution)/shard_map/ppermute | solution.py:33
  75.2 6.3 %collective-permute-start.16 = (bf16[128,256]{1,0:T(8,128)(2,1)S(1)}, bf16[128,256]{1,0:T(8,128)(2,1)S(1)}, u32[]{:S(2)}, u32[]{:S(2)}) collective-permute-start(bf16[128,256]{1,0:T(8,128)(2,1)S(1)} %get-tuple-element.44), channel_id=1, source_target_pairs={{0,1},{1,2},{2,3},{3,0},{4,5},{5,6},{6,7},{7,4},{8,9},{9,10},{10,1... | collective-permute-start | bytes 196616 | tf_op jit(solution)/shard_map/ppermute | solution.py:33
  75.3 6.2 %collective-permute-start.17 = (bf16[128,256]{1,0:T(8,128)(2,1)S(1)}, bf16[128,256]{1,0:T(8,128)(2,1)S(1)}, u32[]{:S(2)}, u32[]{:S(2)}) collective-permute-start(bf16[128,256]{1,0:T(8,128)(2,1)S(1)} %get-tuple-element.45), channel_id=1, source_target_pairs={{0,2},{1,3},{2,0},{3,1},{4,6},{5,7},{6,4},{7,5},{8,10},{9,11},{10,... | collective-permute-start | bytes 196616 | tf_op jit(solution)/shard_map/ppermute | solution.py:33
  76.3 6.0 %collective-permute-start.18 = (bf16[128,256]{1,0:T(8,128)(2,1)S(1)}, bf16[128,256]{1,0:T(8,128)(2,1)S(1)}, u32[]{:S(2)}, u32[]{:S(2)}) collective-permute-start(bf16[128,256]{1,0:T(8,128)(2,1)S(1)} %get-tuple-element.46), channel_id=1, source_target_pairs={{0,3},{1,0},{2,1},{3,2},{4,7},{5,4},{6,5},{7,6},{8,11},{9,8},{10,9... | collective-permute-start | bytes 196616 | tf_op jit(solution)/shard_map/ppermute | solution.py:33

commit v7 on v6

--- a/solution.py
+++ b/solution.py
@@ -19,10 +19,9 @@
 B_SIGN = B_SOURCE + PAIRS
 OTHER = 2 * PAIRS
 ARRIVAL = 0x67521430
-UNITS = (range(0, 1), range(1, 4), range(4, 7), range(7, 8), range(6, 8))
-OWN_UNITS = (UNITS[0], UNITS[1], range(4, 6), range(0), UNITS[4])
-OTHER_UNITS = (UNITS[0], UNITS[1], UNITS[2], UNITS[3], range(0))
-KERNELS, FOR_OTHER = len(UNITS), 3
+FIRST_UNITS = (0, 1, 4, 7, 8)
+KERNELS = len(FIRST_UNITS) - 1
+LAST = KERNELS - 1
 PLAN = 64
 SMEM = pl.BlockSpec(memory_space=pltpu.SMEM)
 VMEM = pl.BlockSpec(memory_space=pltpu.VMEM)
@@ -78,18 +77,16 @@
         unit = (jnp.int32(ARRIVAL) >> (4 * (((owner ^ beta) & 2) * 2 + dy))) & 7
         live = (sign != 0) & ((owner & 1) == core)
         for index in range(KERNELS):
-            used = (OTHER_UNITS if pair >= PAIRS else OWN_UNITS)[index]
-            if not used:
-                continue
-            entry = pair + ((unit - UNITS[index].start) << 6) + ((m & 1) << 9) + ((sign + 1) << 10)
-            plan_ref[index * PLAN + 1 + counts[index]] = entry
-            here = live & (unit >= used.start) & (unit < used.stop)
-            counts[index] = counts[index] + jnp.where(here, 1, 0)
+            low, high = FIRST_UNITS[index], FIRST_UNITS[index + 1]
+            where = (m & 1) << 6 if index == LAST else ((unit - low) << 6) + ((m & 1) << 9)
+            plan_ref[index * PLAN + 1 + counts[index]] = pair + where + ((sign + 1) << 10)
+            counts[index] = counts[index] + jnp.where(live & (unit >= low) & (unit < high), 1, 0)
     for index in range(KERNELS):
         plan_ref[index * PLAN] = counts[index]
 
 
-def pick_kernel(meta_ref, own_ref, back_ref, far_ref, ahead_ref, out_ref):
+def pick_kernel(meta_ref, *refs):
+    stacks, out_ref = refs[:-1], refs[-1]
     alpha = meta_ref[ALPHA]
     core = meta_ref[BETA] & 1
     for k in range(A_SLOTS):
@@ -98,26 +95,26 @@
         dz = ((source >> 2) - (alpha >> 2)) & 3
         dx = (source - alpha) & 3
         dx = jnp.where(core != 0, (4 - dx) & 3, dx)
-
-        def put(i, k=k, sign=sign, dz=dz):
+        which = jnp.where(dx == 2, 2 + (dz >> 1), dx + (dx >> 1 & dx))
+        place = jnp.where(dx == 2, dz & 1, dz)
+
+        def put(i, k=k, sign=sign, place=place):
             for half in range(2):
-                block = (own_ref, back_ref, far_ref, ahead_ref)[i][dz, :, half * BLK : (half + 1) * BLK]
+                block = stacks[i][place, :, half * BLK : (half + 1) * BLK]
                 out_ref[half, :, k * BLK : (k + 1) * BLK] = block.T * sign
 
-        choose(dx, 0, X_SIZE, put)
+        choose(which, 0, len(stacks), put)
 
 
 def contract_kernel(index, plan_ref, a_ref, b_own, b_other, *rest):
-    count_units = len(UNITS[index])
+    count_units = 2 if index == LAST else FIRST_UNITS[index + 1] - FIRST_UNITS[index]
     units, rest = rest[:count_units], rest[count_units:]
     if index:
         sum_ref, rest = rest[0], rest[1:]
-    last = index >= FOR_OTHER
-    if last:
-        chol_ref, share_ref, acc, c_buf, b_buf, b_sem = rest
+    if index == LAST:
+        chol_ref, mine_ref, other_ref, acc, c_buf, b_buf, b_sem = rest
     else:
         acc, c_buf, b_buf, b_sem = rest
-    first_block = B_BLOCKS if index == FOR_OTHER else 0
     vectors = b_own.shape[0]
     count = plan_ref[index * PLAN]
     wide_steps = count >> 2
@@ -167,7 +164,7 @@
             start(range(NARROW))
 
     start_step(0, 0)
-    acc[...] = sum_ref[first_block : first_block + acc.shape[0]] if index else jnp.zeros_like(acc)
+    acc[...] = sum_ref[...] if index else jnp.zeros_like(acc)
 
     def body(width, step, carry):
         slot = step & 1
@@ -210,22 +207,24 @@
             at = first_of(step) + lane
             entry = entry_of(at)
             factor = jnp.where(at < count, (entry >> 10) - 1, 0).astype(jnp.float32)
-            acc[(entry & 63) // B_SLOTS - first_block] += factor * sums[lane]
+            acc[(entry & 63) // B_SLOTS] += factor * sums[lane]
         return carry
 
     lax.fori_loop(0, wide_steps, functools.partial(body, WIDE), 0)
     lax.fori_loop(wide_steps, steps, functools.partial(body, NARROW), 0)
-    if last:
+    if index == LAST:
         for shift in range(4):
             for half in range(2):
                 u = ((chol_ref[0] + shift) & 3) * 2 + half
-                share_ref[shift, :, half * BLK : (half + 1) * BLK] = acc[u].T
+                lanes = slice(half * BLK, (half + 1) * BLK)
+                mine_ref[shift, :, lanes] = acc[u].T
+                other_ref[shift, :, lanes] = acc[B_BLOCKS + u].T
 
 
 def contract(index, plan, a_flipped, b_own, b_other, units, running=None, chol=None):
     vectors, blocks = b_own.shape[:2]
-    last = index >= FOR_OTHER
-    part = (len(OWN_UNITS[index]) + len(OTHER_UNITS[index])) / 16
+    last = index == LAST
+    part = (FIRST_UNITS[index + 1] - FIRST_UNITS[index]) / 8
     flops = int(part * 2 * (a_flipped.size * blocks * B_SLOTS * BLK + b_own.size * BLK))
     moved = int(part * 2 * b_own.size) + 2 * a_flipped.size
     whole = jax.ShapeDtypeStruct((2 * blocks, BLK, BLK), jnp.float32)
@@ -234,10 +233,10 @@
     chols = [chol] if last else []
     return pl.pallas_call(
         functools.partial(contract_kernel, index),
-        out_shape=shares if last else whole,
+        out_shape=[shares, shares] if last else whole,
         in_specs=[SMEM, VMEM, HBM, HBM] + [VMEM] * (len(units) + len(sums)) + [SMEM] * len(chols),
-        out_specs=VMEM,
-        scratch_shapes=[pltpu.VMEM((blocks, BLK, BLK), jnp.float32)] * last
+        out_specs=[VMEM, VMEM] if last else VMEM,
+        scratch_shapes=[pltpu.VMEM(whole.shape, jnp.float32)] * last
         + [
             pltpu.VMEM((WIDE * BLK, A_SLOTS * BLK), jnp.bfloat16),
             pltpu.VMEM((2, WIDE, vectors, BLK, BLK), jnp.bfloat16),
@@ -287,7 +286,7 @@
     )(meta)
 
 
-def gather_sources(meta, quarter, b_tiles, sizes):
+def gather_sources(meta, other_pairs, quarter, b_tiles, sizes):
     alphas, betas = sizes["alpha"], sizes["beta"]
     zs = alphas // X_SIZE
 
@@ -303,18 +302,19 @@
         return shifted(value, ("alpha", "beta"), alphas * betas, moved)
 
     others = [z_from(quarter, distance) for distance in (1, 2, 3)]
-    others, meta, b_held = lax.optimization_barrier((others, meta, b_tiles))
+    others, other_pairs, b_held = lax.optimization_barrier((others, other_pairs, b_tiles))
+    meta = jnp.concatenate([meta, other_pairs])
     own = jnp.stack([quarter] + others)
     ahead, back = by_core(own, 1), by_core(own, -1)
     ahead, plan = lax.optimization_barrier((ahead, make_plan(meta)))
-    far = by_core(ahead, 1)
+    far_low, far_high = by_core(ahead[:2], 1), by_core(back[2:], -1)
     unit = pl.pallas_call(
         pick_kernel,
         out_shape=jax.ShapeDtypeStruct((2, BLK, A_SLOTS * BLK), quarter.dtype),
-        in_specs=[SMEM] + [VMEM] * 4,
+        in_specs=[SMEM] + [VMEM] * 5,
         out_specs=VMEM,
         compiler_params=pltpu.CompilerParams(vmem_limit_bytes=8 * 1024 * 1024),
-    )(meta, own, back, far, ahead)
+    )(meta, own, back, far_low, far_high, ahead)
     return plan, unit, b_held
 
 
@@ -338,11 +338,10 @@
     middle, far_ahead, far_back = by_core(ahead, 1), z_other(ahead), by_core(across, -1)
     running = contract(1, *tiles, [ahead, across, back], running)
     running, middle, far_back, far_ahead = lax.optimization_barrier((running, middle, far_back, far_ahead))
-    far_middle = by_core(far_ahead, 1)
+    far_middle = [by_core(far_ahead[:1], 1), by_core(far_back[1:], -1)]
     running = contract(2, *tiles, [middle, far_back, far_ahead], running)
     running, far_middle = lax.optimization_barrier((running, far_middle))
-    other = contract(FOR_OTHER, *tiles, [far_middle], running, chol)
-    return contract(4, *tiles, [far_ahead, far_middle], running, chol), other
+    return contract(LAST, *tiles, far_middle, running, chol)
 
 
 def per_device(sizes, ci_vector, a_tiles, a_source, a_sign, b_tiles, b_source, b_sign):
@@ -356,8 +355,8 @@
     quarter = lax.dynamic_slice_in_dim(ci_vector, chol * width, width, axis=1)
     place = jnp.stack([lax.axis_index("alpha"), lax.axis_index("beta"), chol]).astype(jnp.int32)
     pairs = jnp.concatenate([b_source.reshape(-1), b_sign.reshape(-1)])
-    meta = jnp.concatenate([place, a_source.reshape(-1), a_sign.reshape(-1), pairs, core_other(pairs)])
-    plan, unit, b_held = gather_sources(meta, quarter, b_tiles, sizes)
+    meta = jnp.concatenate([place, a_source.reshape(-1), a_sign.reshape(-1), pairs])
+    plan, unit, b_held = gather_sources(meta, core_other(pairs), quarter, b_tiles, sizes)
     b_other = core_other(b_held)
     mine, other = gather_and_contract(plan, chol[None], unit, a_tiles, b_tiles, b_other, sizes)
     own, *pieces = merge(mine, core_other(other))

time: 82.9 us -> 86.5 us (1.043)
  starting transfers between devices: 25 us -> 35 us
  Pallas kernels: 25.6 us -> 21.5 us
  waiting for transfers between devices: 26.1 us -> 23.4 us
    ppermute x19 -> x21, starting transfers between devices: 25 us -> 35 us  [shifted(): return lax.ppermute(value, axis, [(i, moves_to(i)) for i in range(size)])]
    pallas_call x5 -> x4, Pallas kernels: 19.8 us -> 15.7 us  [contract(): pl.pallas_call(functools.partial(contract_kernel, index), out_shape=[shar...]
    ppermute x19 -> x21, waiting for transfers between devices: 26.1 us -> 23.4 us  [shifted(): return lax.ppermute(value, axis, [(i, moves_to(i)) for i in range(size)])]
  transfers between devices with their start and end apart: 19 -> 21, of which waited for: 11 -> 13; matrix products, arithmetic and copies ran while one was open for 4% -> 4% of each run, Pallas kernels for 28% -> 22%
where the time goes in v7:
time: 86.5 us; the launch traced here: 86.1 us
  starting transfers between devices  35 us (40%)
  waiting for transfers between devices  23.4 us (27%)
  Pallas kernels  21.5 us (25%)
  local copies, waits for them, and re-layouts  5.24 us (6%)
    ppermute x21, starting transfers between devices, shifted(): return lax.ppermute(value, axis, [(i, moves_to(i)) for i in range(size)])  35 us
    ppermute x21, waiting for transfers between devices, shifted(): return lax.ppermute(value, axis, [(i, moves_to(i)) for i in range(size)])  23.4 us
    pallas_call x4, Pallas kernels, contract(): pl.pallas_call(functools.partial(contract_kernel, index), out_shape=[shar...  15.7 us
    unnamed x8, local copies, waits for them, and re-layouts  3.74 us
    pallas_call x1, Pallas kernels, flip(): pl.pallas_call(flip_kernel, out_shape=jax.ShapeDtypeStruct((A_SLOTS * BLK...  2.33 us
    pallas_call x1, Pallas kernels, make_plan(): pl.pallas_call(plan_kernel, out_shape=jax.ShapeDtypeStruct((KERNELS * PLA...  2.25 us
  transfers between devices with their start and end apart: 21, of which 13 were waited for; matrix products, arithmetic and copies ran while one was open for 4% of the time, Pallas kernels for 22%

profile of v7, /device:TPU:6, one launch (start us, length us, event | category | flops | bytes accessed | tf_op | source)
XLA Modules:
  0.0 86.1 jit_solution(14099406838424749256)
XLA Ops:
  0.0 0.9 %copy-done = bf16[128,1024]{1,0:T(8,128)(2,1)S(1)} copy-done((bf16[128,1024]{1,0:T(8,128)(2,1)S(1)}, bf16[128,1024]{1,0:T(8,128)(2,1)}, u32[]{:S(2)}) %copy-start) | copy-done | bytes 262168
  1.0 7.3 %collective-permute-start.1 = (bf16[128,256]{1,0:T(8,128)(2,1)S(1)}, bf16[128,256]{1,0:T(8,128)(2,1)S(1)}, u32[]{:S(2)}, u32[]{:S(2)}) collective-permute-start(bf16[128,256]{1,0:T(8,128)(2,1)S(1)} %constant_dynamic-slice_fusion), channel_id=1, source_target_pairs={{0,128},{16,144},{32,160},{48,176},{64,192},{80,208},{96,224},{112... | collective-permute-start | bytes 196616 | tf_op jit(solution)/shard_map/ppermute | solution.py:32
  8.2 2.9 %collective-permute-start.2 = (bf16[128,256]{1,0:T(8,128)(2,1)S(1)}, bf16[128,256]{1,0:T(8,128)(2,1)S(1)}, u32[]{:S(2)}, u32[]{:S(2)}) collective-permute-start(bf16[128,256]{1,0:T(8,128)(2,1)S(1)} %constant_dynamic-slice_fusion), channel_id=1, source_target_pairs={{0,64},{16,80},{32,96},{48,112},{64,128},{80,144},{96,160},{112,17... | collective-permute-start | bytes 196616 | tf_op jit(solution)/shard_map/ppermute | solution.py:32
  12.0 0.8 copy.11
  13.0 1.1 %collective-permute-done.3 = s32[48]{0:T(128)S(1)} collective-permute-done((s32[48]{0:T(128)S(1)}, s32[48]{0:T(128)S(1)}, u32[]{:S(2)}, u32[]{:S(2)}) %collective-permute-start.3) | collective-permute-done | bytes 224 | tf_op jit(solution)/shard_map/ppermute | solution.py:32
  14.1 1.1 %collective-permute-done = bf16[128,256]{1,0:T(8,128)(2,1)S(1)} collective-permute-done((bf16[128,256]{1,0:T(8,128)(2,1)S(1)}, bf16[128,256]{1,0:T(8,128)(2,1)S(1)}, u32[]{:S(2)}, u32[]{:S(2)}) %collective-permute-start) | collective-permute-done | bytes 65568 | tf_op jit(solution)/shard_map/ppermute | solution.py:32
  15.2 0.9 %collective-permute-start.6 = (bf16[4,128,256]{2,1,0:T(8,128)(2,1)S(1)}, bf16[4,128,256]{2,1,0:T(8,128)(2,1)S(1)}, u32[]{:S(2)}, u32[]{:S(2)}) collective-permute-start(bf16[4,128,256]{2,1,0:T(8,128)(2,1)S(1)} %pad_maximum_fusion.refs_0_), channel_id=1, source_target_pairs={{0,48},{4,20},{8,56},{12,28},{16,0},{20,36},{24,8},{28,44},{32,16}... | collective-permute-start | bytes 786440 | tf_op jit(solution)/shard_map/ppermute | solution.py:32
  16.1 2.4 %collective-permute-start.4 = (bf16[4,128,256]{2,1,0:T(8,128)(2,1)S(1)}, bf16[4,128,256]{2,1,0:T(8,128)(2,1)S(1)}, u32[]{:S(2)}, u32[]{:S(2)}) collective-permute-start(bf16[4,128,256]{2,1,0:T(8,128)(2,1)S(1)} %pad_maximum_fusion.refs_0_), channel_id=1, source_target_pairs={{0,16},{4,52},{8,24},{12,60},{16,32},{20,4},{24,40},{28,12},{32,48... | collective-permute-start | bytes 786440 | tf_op jit(solution)/shard_map/ppermute | solution.py:32
  18.5 1.3 %concatenate.8.meta_ref = s32[111]{0:T(128)} concatenate(s32[1]{0:T(128)} %bitcast.4, s32[1]{0:T(128)} %bitcast.5, s32[1]{0:T(128)} %bitcast.6.rest_3_, s32[6]{0:T(128)} %bitcast.13, s32[6]{0:T(128)} %bitcast.14, s32[24]{0:T(128)S(1)} %reshape.12, s32[24]{0:T(128)S(1)} %reshape.13, s32[48]{0:T(128)S(1)} %collective-permute-done.3), dimensions={0} | concatenate | bytes 888 | tf_op jit(solution)/shard_map/concatenate | solution.py:306
  19.8 2.3 %shard_map.73.plan_ref = s32[256]{0:T(256)} custom-call(s32[111]{0:T(128)} %concatenate.8.meta_ref), custom_call_target="tpu_custom_call" | custom-call | tf_op jit(solution)/shard_map/pallas_call | solution.py:281
  22.1 3.4 %collective-permute-done.6.refs_1_ = bf16[4,128,256]{2,1,0:T(8,128)(2,1)S(1)} collective-permute-done((bf16[4,128,256]{2,1,0:T(8,128)(2,1)S(1)}, bf16[4,128,256]{2,1,0:T(8,128)(2,1)S(1)}, u32[]{:S(2)}, u32[]{:S(2)}) %collective-permute-start.6) | collective-permute-done | bytes 262176 | tf_op jit(solution)/shard_map/ppermute | solution.py:32
  25.6 3.3 %collective-permute-start.7 = (bf16[2,128,256]{2,1,0:T(8,128)(2,1)S(1)}, bf16[2,128,256]{2,1,0:T(8,128)(2,1)S(1)}, u32[]{:S(2)}, u32[]{:S(2)}) collective-permute-start(bf16[2,128,256]{2,1,0:T(8,128)(2,1)S(1)} %slice.12), channel_id=1, source_target_pairs={{0,16},{4,52},{8,24},{12,60},{16,32},{20,4},{24,40},{28,12},{32,48... | collective-permute-start | bytes 393224 | tf_op jit(solution)/shard_map/ppermute | solution.py:32
  28.8 3.1 %collective-permute-done.8.refs_3_ = bf16[2,128,256]{2,1,0:T(8,128)(2,1)S(1)} collective-permute-done((bf16[2,128,256]{2,1,0:T(8,128)(2,1)S(1)}, bf16[2,128,256]{2,1,0:T(8,128)(2,1)S(1)}, u32[]{:S(2)}, u32[]{:S(2)}) %collective-permute-start.8) | collective-permute-done | bytes 131104 | tf_op jit(solution)/shard_map/ppermute | solution.py:32
  32.6 1.1 %shard_map.75.rest_0_ = bf16[2,128,768]{2,1,0:T(8,128)(2,1)S(1)} custom-call(s32[111]{0:T(128)S(1)} %copy-done.2, bf16[4,128,256]{2,1,0:T(8,128)(2,1)S(1)} %pad_maximum_fusion.refs_0_, bf16[4,128,256]{2,1,0:T(8,128)(2,1)S(1)} %collective-permute-done.6.refs_1_, bf16[2,128,256]{2,1,0:T(8,128)(2,1)S(1)} %collective-permute-done.7.refs_2_, ...), custom_call_target="tpu_custom_call" | custom-call | tf_op jit(solution)/shard_map/pallas_call | solution.py:311
  33.7 3.1 %collective-permute-start.11 = (bf16[2,128,768]{2,1,0:T(8,128)(2,1)S(1)}, bf16[2,128,768]{2,1,0:T(8,128)(2,1)S(1)}, u32[]{:S(2)}, u32[]{:S(2)}) collective-permute-start(bf16[2,128,768]{2,1,0:T(8,128)(2,1)S(1)} %shard_map.75.rest_0_), channel_id=1, source_target_pairs={{0,3},{1,0},{2,1},{3,2},{4,5},{5,6},{6,7},{7,4},{8,11},{9,8},{10,9... | collective-permute-start | bytes 1179656 | tf_op jit(solution)/shard_map/ppermute | solution.py:32
  36.8 1.6 %collective-permute-start.10 = (bf16[2,128,768]{2,1,0:T(8,128)(2,1)S(1)}, bf16[2,128,768]{2,1,0:T(8,128)(2,1)S(1)}, u32[]{:S(2)}, u32[]{:S(2)}) collective-permute-start(bf16[2,128,768]{2,1,0:T(8,128)(2,1)S(1)} %shard_map.75.rest_0_), channel_id=1, source_target_pairs={{0,8},{4,12},{8,0},{12,4},{1,9},{5,13},{9,1},{13,5},{2,10},{6,14},... | collective-permute-start | bytes 1179656 | tf_op jit(solution)/shard_map/ppermute | solution.py:32
  38.4 2.3 %shard_map.74.a_ref = bf16[768,2048]{1,0:T(8,128)(2,1)S(1)} custom-call(bf16[16,1,6,128,128]{4,3,2,1,0:T(8,128)(2,1)} %a_hbm.1), custom_call_target="tpu_custom_call" | custom-call | bytes 6291456 | tf_op jit(solution)/shard_map/pallas_call | solution.py:269
  41.4 3.6 %shard_map.76.rest_3_ = f32[16,128,128]{2,1,0:T(8,128)S(1)} custom-call(s32[256]{0:T(256)S(1)} %copy-done.1, bf16[768,2048]{1,0:T(8,128)(2,1)S(1)} %shard_map.74.a_ref, bf16[16,8,3,128,128]{4,3,2,1,0:T(8,128)(2,1)} %b_own.7, bf16[16,8,3,128,128]{4,3,2,1,0:T(8,128)(2,1)} %collective-permute-done.5.b_other, bf16[2,128,768]{2,1,0:T(8,128)(2,1)S(1)} %shard_map.75.rest_0_), custom_call_target="tpu_custom_call" | custom-call | flops 1409286144 | bytes 4718592 | tf_op jit(solution)/shard_map/pallas_call | solution.py:234
  45.7 1.6 %collective-permute-done.9.rest_0_ = bf16[2,128,768]{2,1,0:T(8,128)(2,1)S(1)} collective-permute-done((bf16[2,128,768]{2,1,0:T(8,128)(2,1)S(1)}, bf16[2,128,768]{2,1,0:T(8,128)(2,1)S(1)}, u32[]{:S(2)}, u32[]{:S(2)}) %collective-permute-start.9) | collective-permute-done | bytes 393248 | tf_op jit(solution)/shard_map/ppermute | solution.py:32
  48.4 2.7 %collective-permute-start.13 = (bf16[2,128,768]{2,1,0:T(8,128)(2,1)S(1)}, bf16[2,128,768]{2,1,0:T(8,128)(2,1)S(1)}, u32[]{:S(2)}, u32[]{:S(2)}) collective-permute-start(bf16[2,128,768]{2,1,0:T(8,128)(2,1)S(1)} %collective-permute-done.10.rest_1_), channel_id=1, source_target_pairs={{0,3},{1,0},{2,1},{3,2},{4,5},{5,6},{6,7},{7,4},{8,11},{9,8},{10,9... | collective-permute-start | bytes 1179656 | tf_op jit(solution)/shard_map/ppermute | solution.py:32
  51.0 5.2 %shard_map.77.rest_3_ = f32[16,128,128]{2,1,0:T(8,128)S(1)} custom-call(s32[256]{0:T(256)S(1)} %copy-done.1, bf16[768,2048]{1,0:T(8,128)(2,1)S(1)} %shard_map.74.a_ref, bf16[16,8,3,128,128]{4,3,2,1,0:T(8,128)(2,1)} %b_own.7, bf16[16,8,3,128,128]{4,3,2,1,0:T(8,128)(2,1)} %collective-permute-done.5.b_other, ...), custom_call_target="tpu_custom_call" | custom-call | flops 4227858432 | bytes 7864320 | tf_op jit(solution)/shard_map/pallas_call | solution.py:234
  56.2 1.4 %collective-permute-done.13.rest_1_ = bf16[2,128,768]{2,1,0:T(8,128)(2,1)S(1)} collective-permute-done((bf16[2,128,768]{2,1,0:T(8,128)(2,1)S(1)}, bf16[2,128,768]{2,1,0:T(8,128)(2,1)S(1)}, u32[]{:S(2)}, u32[]{:S(2)}) %collective-permute-start.13) | collective-permute-done | bytes 393248 | tf_op jit(solution)/shard_map/ppermute | solution.py:32
  57.6 3.3 %collective-permute-done.12.rest_0_ = bf16[2,128,768]{2,1,0:T(8,128)(2,1)S(1)} collective-permute-done((bf16[2,128,768]{2,1,0:T(8,128)(2,1)S(1)}, bf16[2,128,768]{2,1,0:T(8,128)(2,1)S(1)}, u32[]{:S(2)}, u32[]{:S(2)}) %collective-permute-start.12) | collective-permute-done | bytes 393248 | tf_op jit(solution)/shard_map/ppermute | solution.py:32
  61.4 1.7 %collective-permute-start.15 = (bf16[1,128,768]{2,1,0:T(8,128)(2,1)S(1)}, bf16[1,128,768]{2,1,0:T(8,128)(2,1)S(1)}, u32[]{:S(2)}, u32[]{:S(2)}) collective-permute-start(bf16[1,128,768]{2,1,0:T(8,128)(2,1)S(1)} %slice.14), channel_id=1, source_target_pairs={{0,1},{1,2},{2,3},{3,0},{4,7},{5,4},{6,5},{7,6},{8,9},{9,10},{10,1... | collective-permute-start | bytes 589832 | tf_op jit(solution)/shard_map/ppermute | solution.py:32
  63.1 4.2 %shard_map.78.rest_2_ = f32[16,128,128]{2,1,0:T(8,128)S(1)} custom-call(s32[256]{0:T(256)S(1)} %copy-done.1, bf16[768,2048]{1,0:T(8,128)(2,1)S(1)} %shard_map.74.a_ref, bf16[16,8,3,128,128]{4,3,2,1,0:T(8,128)(2,1)} %b_own.7, bf16[16,8,3,128,128]{4,3,2,1,0:T(8,128)(2,1)} %collective-permute-done.5.b_other, ...), custom_call_target="tpu_custom_call" | custom-call | flops 4227858432 | bytes 7864320 | tf_op jit(solution)/shard_map/pallas_call | solution.py:234
  67.3 0.8 collective-permute-done.16.rest_1_
  68.1 1.1 %collective-permute-done.15.rest_0_ = bf16[1,128,768]{2,1,0:T(8,128)(2,1)S(1)} collective-permute-done((bf16[1,128,768]{2,1,0:T(8,128)(2,1)S(1)}, bf16[1,128,768]{2,1,0:T(8,128)(2,1)S(1)}, u32[]{:S(2)}, u32[]{:S(2)}) %collective-permute-start.15) | collective-permute-done | bytes 196640 | tf_op jit(solution)/shard_map/ppermute | solution.py:32
  69.2 2.7 %shard_map.79 = (f32[4,128,256]{2,1,0:T(8,128)S(1)}, f32[4,128,256]{2,1,0:T(8,128)S(1)}) custom-call(s32[256]{0:T(256)S(1)} %copy-done.1, bf16[768,2048]{1,0:T(8,128)(2,1)S(1)} %shard_map.74.a_ref, bf16[16,8,3,128,128]{4,3,2,1,0:T(8,128)(2,1)} %b_own.7, bf16[16,8,3,128,128]{4,3,2,1,0:T(8,128)(2,1)} %collective-permute-done.5.b_other, ...), custom_call_target="tpu_custom_call" | custom-call | flops 1409286144 | bytes 4718592 | tf_op jit(solution)/shard_map/pallas_call | solution.py:234
  71.9 4.3 %collective-permute-start.17 = (f32[4,128,256]{2,1,0:T(8,128)S(1)}, f32[4,128,256]{2,1,0:T(8,128)S(1)}, u32[]{:S(2)}, u32[]{:S(2)}) collective-permute-start(f32[4,128,256]{2,1,0:T(8,128)S(1)} %get-tuple-element.48), channel_id=1, source_target_pairs={{0,4},{4,0},{8,12},{12,8},{1,5},{5,1},{9,13},{13,9},{2,6},{6,2},{1... | collective-permute-start | bytes 1572872 | tf_op jit(solution)/shard_map/ppermute | solution.py:32
  76.2 1.5 %collective-permute-done.17.arrived_ref = f32[4,128,256]{2,1,0:T(8,128)S(1)} collective-permute-done((f32[4,128,256]{2,1,0:T(8,128)S(1)}, f32[4,128,256]{2,1,0:T(8,128)S(1)}, u32[]{:S(2)}, u32[]{:S(2)}) %collective-permute-start.17) | collective-permute-done | bytes 524320 | tf_op jit(solution)/shard_map/ppermute | solution.py:32
  78.4 2.7 %collective-permute-start.20 = (bf16[128,256]{1,0:T(8,128)(2,1)S(1)}, bf16[128,256]{1,0:T(8,128)(2,1)S(1)}, u32[]{:S(2)}, u32[]{:S(2)}) collective-permute-start(bf16[128,256]{1,0:T(8,128)(2,1)S(1)} %get-tuple-element.52), channel_id=1, source_target_pairs={{0,3},{1,0},{2,1},{3,2},{4,7},{5,4},{6,5},{7,6},{8,11},{9,8},{10,9... | collective-permute-start | bytes 196616 | tf_op jit(solution)/shard_map/ppermute | solution.py:32
  81.1 3.7 %collective-permute-done.18 = bf16[128,256]{1,0:T(8,128)(2,1)S(1)} collective-permute-done((bf16[128,256]{1,0:T(8,128)(2,1)S(1)}, bf16[128,256]{1,0:T(8,128)(2,1)S(1)}, u32[]{:S(2)}, u32[]{:S(2)}) %collective-permute-start.18) | collective-permute-done | bytes 65568 | tf_op jit(solution)/shard_map/ppermute | solution.py:32
  (38 shorter events, 6.5 us)
Async XLA Ops:
  0.0 1.0 %copy-start = (bf16[128,1024]{1,0:T(8,128)(2,1)S(1)}, bf16[128,1024]{1,0:T(8,128)(2,1)}, u32[]{:S(2)}) copy-start(bf16[128,1024]{1,0:T(8,128)(2,1)} %param.7) | copy-start | bytes 786436
  1.0 13.1 %collective-permute-start.1 = (bf16[128,256]{1,0:T(8,128)(2,1)S(1)}, bf16[128,256]{1,0:T(8,128)(2,1)S(1)}, u32[]{:S(2)}, u32[]{:S(2)}) collective-permute-start(bf16[128,256]{1,0:T(8,128)(2,1)S(1)} %constant_dynamic-slice_fusion), channel_id=1, source_target_pairs={{0,128},{16,144},{32,160},{48,176},{64,192},{80,208},{96,224},{112... | collective-permute-start | bytes 196616 | tf_op jit(solution)/shard_map/ppermute | solution.py:32
  8.2 6.9 %collective-permute-start = (bf16[128,256]{1,0:T(8,128)(2,1)S(1)}, bf16[128,256]{1,0:T(8,128)(2,1)S(1)}, u32[]{:S(2)}, u32[]{:S(2)}) collective-permute-start(bf16[128,256]{1,0:T(8,128)(2,1)S(1)} %constant_dynamic-slice_fusion), channel_id=1, source_target_pairs={{0,192},{16,208},{32,224},{48,240},{64,0},{80,16},{96,32},{112,48}... | collective-permute-start | bytes 196616 | tf_op jit(solution)/shard_map/ppermute | solution.py:32
  8.2 6.9 %collective-permute-start.2 = (bf16[128,256]{1,0:T(8,128)(2,1)S(1)}, bf16[128,256]{1,0:T(8,128)(2,1)S(1)}, u32[]{:S(2)}, u32[]{:S(2)}) collective-permute-start(bf16[128,256]{1,0:T(8,128)(2,1)S(1)} %constant_dynamic-slice_fusion), channel_id=1, source_target_pairs={{0,64},{16,80},{32,96},{48,112},{64,128},{80,144},{96,160},{112,17... | collective-permute-start | bytes 196616 | tf_op jit(solution)/shard_map/ppermute | solution.py:32
  12.9 1.1 %collective-permute-start.3 = (s32[48]{0:T(128)S(1)}, s32[48]{0:T(128)S(1)}, u32[]{:S(2)}, u32[]{:S(2)}) collective-permute-start(s32[48]{0:T(128)S(1)} %pad_add_fusion), channel_id=1, source_target_pairs={{0,4},{4,0},{8,12},{12,8},{1,5},{5,1},{9,13},{13,9},{2,6},{6,2},{1... | collective-permute-start | bytes 584 | tf_op jit(solution)/shard_map/ppermute | solution.py:32
  15.2 25.6 %collective-permute-start.5 = (bf16[16,8,3,128,128]{4,3,2,1,0:T(8,128)(2,1)}, bf16[16,8,3,128,128]{4,3,2,1,0:T(8,128)(2,1)}, u32[]{:S(2)}, u32[]{:S(2)}) collective-permute-start(bf16[16,8,3,128,128]{4,3,2,1,0:T(8,128)(2,1)} %b_own.7), channel_id=1, source_target_pairs={{0,4},{4,0},{8,12},{12,8},{1,5},{5,1},{9,13},{13,9},{2,6},{6,2},{1... | collective-permute-start | bytes 37748744 | tf_op jit(solution)/shard_map/ppermute | solution.py:32
  15.2 10.2 %collective-permute-start.6 = (bf16[4,128,256]{2,1,0:T(8,128)(2,1)S(1)}, bf16[4,128,256]{2,1,0:T(8,128)(2,1)S(1)}, u32[]{:S(2)}, u32[]{:S(2)}) collective-permute-start(bf16[4,128,256]{2,1,0:T(8,128)(2,1)S(1)} %pad_maximum_fusion.refs_0_), channel_id=1, source_target_pairs={{0,48},{4,20},{8,56},{12,28},{16,0},{20,36},{24,8},{28,44},{32,16}... | collective-permute-start | bytes 786440 | tf_op jit(solution)/shard_map/ppermute | solution.py:32
  16.1 9.4 %collective-permute-start.4 = (bf16[4,128,256]{2,1,0:T(8,128)(2,1)S(1)}, bf16[4,128,256]{2,1,0:T(8,128)(2,1)S(1)}, u32[]{:S(2)}, u32[]{:S(2)}) collective-permute-start(bf16[4,128,256]{2,1,0:T(8,128)(2,1)S(1)} %pad_maximum_fusion.refs_0_), channel_id=1, source_target_pairs={{0,16},{4,52},{8,24},{12,60},{16,32},{20,4},{24,40},{28,12},{32,48... | collective-permute-start | bytes 786440 | tf_op jit(solution)/shard_map/ppermute | solution.py:32
  25.4 6.5 %collective-permute-start.8 = (bf16[2,128,256]{2,1,0:T(8,128)(2,1)S(1)}, bf16[2,128,256]{2,1,0:T(8,128)(2,1)S(1)}, u32[]{:S(2)}, u32[]{:S(2)}) collective-permute-start(bf16[2,128,256]{2,1,0:T(8,128)(2,1)S(1)} %slice.16), channel_id=1, source_target_pairs={{0,48},{4,20},{8,56},{12,28},{16,0},{20,36},{24,8},{28,44},{32,16}... | collective-permute-start | bytes 393224 | tf_op jit(solution)/shard_map/ppermute | solution.py:32
  25.6 6.4 %collective-permute-start.7 = (bf16[2,128,256]{2,1,0:T(8,128)(2,1)S(1)}, bf16[2,128,256]{2,1,0:T(8,128)(2,1)S(1)}, u32[]{:S(2)}, u32[]{:S(2)}) collective-permute-start(bf16[2,128,256]{2,1,0:T(8,128)(2,1)S(1)} %slice.12), channel_id=1, source_target_pairs={{0,16},{4,52},{8,24},{12,60},{16,32},{20,4},{24,40},{28,12},{32,48... | collective-permute-start | bytes 393224 | tf_op jit(solution)/shard_map/ppermute | solution.py:32
  32.0 0.6 copy-start.2
  33.7 12.1 %collective-permute-start.11 = (bf16[2,128,768]{2,1,0:T(8,128)(2,1)S(1)}, bf16[2,128,768]{2,1,0:T(8,128)(2,1)S(1)}, u32[]{:S(2)}, u32[]{:S(2)}) collective-permute-start(bf16[2,128,768]{2,1,0:T(8,128)(2,1)S(1)} %shard_map.75.rest_0_), channel_id=1, source_target_pairs={{0,3},{1,0},{2,1},{3,2},{4,5},{5,6},{6,7},{7,4},{8,11},{9,8},{10,9... | collective-permute-start | bytes 1179656 | tf_op jit(solution)/shard_map/ppermute | solution.py:32
  36.8 9.0 %collective-permute-start.10 = (bf16[2,128,768]{2,1,0:T(8,128)(2,1)S(1)}, bf16[2,128,768]{2,1,0:T(8,128)(2,1)S(1)}, u32[]{:S(2)}, u32[]{:S(2)}) collective-permute-start(bf16[2,128,768]{2,1,0:T(8,128)(2,1)S(1)} %shard_map.75.rest_0_), channel_id=1, source_target_pairs={{0,8},{4,12},{8,0},{12,4},{1,9},{5,13},{9,1},{13,5},{2,10},{6,14},... | collective-permute-start | bytes 1179656 | tf_op jit(solution)/shard_map/ppermute | solution.py:32
  38.4 9.0 %collective-permute-start.9 = (bf16[2,128,768]{2,1,0:T(8,128)(2,1)S(1)}, bf16[2,128,768]{2,1,0:T(8,128)(2,1)S(1)}, u32[]{:S(2)}, u32[]{:S(2)}) collective-permute-start(bf16[2,128,768]{2,1,0:T(8,128)(2,1)S(1)} %shard_map.75.rest_0_), channel_id=1, source_target_pairs={{0,1},{1,2},{2,3},{3,0},{4,7},{5,4},{6,5},{7,6},{8,9},{9,10},{10,1... | collective-permute-start | bytes 1179656 | tf_op jit(solution)/shard_map/ppermute | solution.py:32
  40.8 0.7 copy-start.1
  47.4 10.2 %collective-permute-start.14 = (bf16[2,128,768]{2,1,0:T(8,128)(2,1)S(1)}, bf16[2,128,768]{2,1,0:T(8,128)(2,1)S(1)}, u32[]{:S(2)}, u32[]{:S(2)}) collective-permute-start(bf16[2,128,768]{2,1,0:T(8,128)(2,1)S(1)} %collective-permute-done.9.rest_0_), channel_id=1, source_target_pairs={{0,8},{4,12},{8,0},{12,4},{1,9},{5,13},{9,1},{13,5},{2,10},{6,14},... | collective-permute-start | bytes 1179656 | tf_op jit(solution)/shard_map/ppermute | solution.py:32
  47.8 13.2 %collective-permute-start.12 = (bf16[2,128,768]{2,1,0:T(8,128)(2,1)S(1)}, bf16[2,128,768]{2,1,0:T(8,128)(2,1)S(1)}, u32[]{:S(2)}, u32[]{:S(2)}) collective-permute-start(bf16[2,128,768]{2,1,0:T(8,128)(2,1)S(1)} %collective-permute-done.9.rest_0_), channel_id=1, source_target_pairs={{0,1},{1,2},{2,3},{3,0},{4,7},{5,4},{6,5},{7,6},{8,9},{9,10},{10,1... | collective-permute-start | bytes 1179656 | tf_op jit(solution)/shard_map/ppermute | solution.py:32
  48.4 9.3 %collective-permute-start.13 = (bf16[2,128,768]{2,1,0:T(8,128)(2,1)S(1)}, bf16[2,128,768]{2,1,0:T(8,128)(2,1)S(1)}, u32[]{:S(2)}, u32[]{:S(2)}) collective-permute-start(bf16[2,128,768]{2,1,0:T(8,128)(2,1)S(1)} %collective-permute-done.10.rest_1_), channel_id=1, source_target_pairs={{0,3},{1,0},{2,1},{3,2},{4,5},{5,6},{6,7},{7,4},{8,11},{9,8},{10,9... | collective-permute-start | bytes 1179656 | tf_op jit(solution)/shard_map/ppermute | solution.py:32
  61.0 7.1 %collective-permute-start.16 = (bf16[1,128,768]{2,1,0:T(8,128)(2,1)S(1)}, bf16[1,128,768]{2,1,0:T(8,128)(2,1)S(1)}, u32[]{:S(2)}, u32[]{:S(2)}) collective-permute-start(bf16[1,128,768]{2,1,0:T(8,128)(2,1)S(1)} %slice.15), channel_id=1, source_target_pairs={{0,3},{1,0},{2,1},{3,2},{4,5},{5,6},{6,7},{7,4},{8,11},{9,8},{10,9... | collective-permute-start | bytes 589832 | tf_op jit(solution)/shard_map/ppermute | solution.py:32
  61.4 7.8 %collective-permute-start.15 = (bf16[1,128,768]{2,1,0:T(8,128)(2,1)S(1)}, bf16[1,128,768]{2,1,0:T(8,128)(2,1)S(1)}, u32[]{:S(2)}, u32[]{:S(2)}) collective-permute-start(bf16[1,128,768]{2,1,0:T(8,128)(2,1)S(1)} %slice.14), channel_id=1, source_target_pairs={{0,1},{1,2},{2,3},{3,0},{4,7},{5,4},{6,5},{7,6},{8,9},{9,10},{10,1... | collective-permute-start | bytes 589832 | tf_op jit(solution)/shard_map/ppermute | solution.py:32
  71.9 5.8 %collective-permute-start.17 = (f32[4,128,256]{2,1,0:T(8,128)S(1)}, f32[4,128,256]{2,1,0:T(8,128)S(1)}, u32[]{:S(2)}, u32[]{:S(2)}) collective-permute-start(f32[4,128,256]{2,1,0:T(8,128)S(1)} %get-tuple-element.48), channel_id=1, source_target_pairs={{0,4},{4,0},{8,12},{12,8},{1,5},{5,1},{9,13},{13,9},{2,6},{6,2},{1... | collective-permute-start | bytes 1572872 | tf_op jit(solution)/shard_map/ppermute | solution.py:32
  77.8 7.1 %collective-permute-start.18 = (bf16[128,256]{1,0:T(8,128)(2,1)S(1)}, bf16[128,256]{1,0:T(8,128)(2,1)S(1)}, u32[]{:S(2)}, u32[]{:S(2)}) collective-permute-start(bf16[128,256]{1,0:T(8,128)(2,1)S(1)} %get-tuple-element.50), channel_id=1, source_target_pairs={{0,1},{1,2},{2,3},{3,0},{4,5},{5,6},{6,7},{7,4},{8,9},{9,10},{10,1... | collective-permute-start | bytes 196616 | tf_op jit(solution)/shard_map/ppermute | solution.py:32
  77.9 7.0 %collective-permute-start.19 = (bf16[128,256]{1,0:T(8,128)(2,1)S(1)}, bf16[128,256]{1,0:T(8,128)(2,1)S(1)}, u32[]{:S(2)}, u32[]{:S(2)}) collective-permute-start(bf16[128,256]{1,0:T(8,128)(2,1)S(1)} %get-tuple-element.51), channel_id=1, source_target_pairs={{0,2},{1,3},{2,0},{3,1},{4,6},{5,7},{6,4},{7,5},{8,10},{9,11},{10,... | collective-permute-start | bytes 196616 | tf_op jit(solution)/shard_map/ppermute | solution.py:32
  78.4 7.0 %collective-permute-start.20 = (bf16[128,256]{1,0:T(8,128)(2,1)S(1)}, bf16[128,256]{1,0:T(8,128)(2,1)S(1)}, u32[]{:S(2)}, u32[]{:S(2)}) collective-permute-start(bf16[128,256]{1,0:T(8,128)(2,1)S(1)} %get-tuple-element.52), channel_id=1, source_target_pairs={{0,3},{1,0},{2,1},{3,2},{4,7},{5,4},{6,5},{7,6},{8,11},{9,8},{10,9... | collective-permute-start | bytes 196616 | tf_op jit(solution)/shard_map/ppermute | solution.py:32

commit v8 on v7

--- a/solution.py
+++ b/solution.py
@@ -9,7 +9,7 @@
 
 BLK = 128
 VECTORS_PER_GROUP = 8
-WIDE, NARROW = 4, 2
+ALL_WIDTHS = ((2,), (4, 2), (4, 2), (2,))
 X_SIZE = 4
 A_SLOTS, B_SLOTS, B_BLOCKS = 6, 3, 8
 PAIRS = B_SLOTS * B_BLOCKS
@@ -78,36 +78,38 @@
         live = (sign != 0) & ((owner & 1) == core)
         for index in range(KERNELS):
             low, high = FIRST_UNITS[index], FIRST_UNITS[index + 1]
-            where = (m & 1) << 6 if index == LAST else ((unit - low) << 6) + ((m & 1) << 9)
-            plan_ref[index * PLAN + 1 + counts[index]] = pair + where + ((sign + 1) << 10)
+            entry = pair + ((unit - low) << 6) + ((m & 1) << 9) + ((sign + 1) << 10)
+            plan_ref[index * PLAN + 1 + counts[index]] = entry
             counts[index] = counts[index] + jnp.where(live & (unit >= low) & (unit < high), 1, 0)
     for index in range(KERNELS):
         plan_ref[index * PLAN] = counts[index]
 
 
-def pick_kernel(meta_ref, *refs):
-    stacks, out_ref = refs[:-1], refs[-1]
+def pick_kernel(meta_ref, own_ref, back_ref, far_ref, ahead_ref, out_ref):
     alpha = meta_ref[ALPHA]
     core = meta_ref[BETA] & 1
-    for k in range(A_SLOTS):
+
+    def place(k, carry):
         source = meta_ref[A_SOURCE + k]
         sign = meta_ref[A_SIGN + k].astype(jnp.float32).astype(out_ref.dtype)
         dz = ((source >> 2) - (alpha >> 2)) & 3
         dx = (source - alpha) & 3
         dx = jnp.where(core != 0, (4 - dx) & 3, dx)
-        which = jnp.where(dx == 2, 2 + (dz >> 1), dx + (dx >> 1 & dx))
-        place = jnp.where(dx == 2, dz & 1, dz)
-
-        def put(i, k=k, sign=sign, place=place):
+        lanes = pl.ds(pl.multiple_of(k * BLK, BLK), BLK)
+
+        def put(i):
             for half in range(2):
-                block = stacks[i][place, :, half * BLK : (half + 1) * BLK]
-                out_ref[half, :, k * BLK : (k + 1) * BLK] = block.T * sign
-
-        choose(which, 0, len(stacks), put)
+                block = (own_ref, back_ref, far_ref, ahead_ref)[i][dz, :, half * BLK : (half + 1) * BLK]
+                out_ref[half, :, lanes] = block.T * sign
+
+        choose(dx, 0, X_SIZE, put)
+        return carry
+
+    lax.fori_loop(0, A_SLOTS, place, 0)
 
 
 def contract_kernel(index, plan_ref, a_ref, b_own, b_other, *rest):
-    count_units = 2 if index == LAST else FIRST_UNITS[index + 1] - FIRST_UNITS[index]
+    count_units = FIRST_UNITS[index + 1] - FIRST_UNITS[index]
     units, rest = rest[:count_units], rest[count_units:]
     if index:
         sum_ref, rest = rest[0], rest[1:]
@@ -115,14 +117,21 @@
         chol_ref, mine_ref, other_ref, acc, c_buf, b_buf, b_sem = rest
     else:
         acc, c_buf, b_buf, b_sem = rest
+    widths = ALL_WIDTHS[index]
     vectors = b_own.shape[0]
     count = plan_ref[index * PLAN]
-    wide_steps = count >> 2
-    narrow_steps = (count - WIDE * wide_steps + 1) >> 1
-    steps = wide_steps + narrow_steps
+    ends, firsts, taken, steps = [], [], jnp.int32(0), jnp.int32(0)
+    for width in widths:
+        firsts.append(taken - width * steps)
+        more = jnp.maximum(count - taken + 1, 0) // width
+        taken, steps = taken + width * more, steps + more
+        ends.append(steps)
 
     def first_of(step):
-        return jnp.where(step < wide_steps, WIDE * step, NARROW * step + (WIDE - NARROW) * wide_steps)
+        first = firsts[-1] + widths[-1] * step
+        for width, base, end in reversed(tuple(zip(widths[:-1], firsts, ends))):
+            first = jnp.where(step < end, base + width * step, first)
+        return first
 
     def entry_of(at):
         return plan_ref[index * PLAN + 1 + jnp.minimum(at, count - 1)]
@@ -155,13 +164,14 @@
             for part in range(2):
                 start_b(step, slot, lanes, part)
 
-        @pl.when(step < wide_steps)
-        def _():
-            start(range(WIDE))
-
-        @pl.when((step >= wide_steps) & (step < steps))
-        def _():
-            start(range(NARROW))
+        begin = 0
+        for width, end in zip(widths, ends):
+
+            @pl.when((step >= begin) & (step < end))
+            def _(width=width):
+                start(range(width))
+
+            begin = end
 
     start_step(0, 0)
     acc[...] = sum_ref[...] if index else jnp.zeros_like(acc)
@@ -210,8 +220,10 @@
             acc[(entry & 63) // B_SLOTS] += factor * sums[lane]
         return carry
 
-    lax.fori_loop(0, wide_steps, functools.partial(body, WIDE), 0)
-    lax.fori_loop(wide_steps, steps, functools.partial(body, NARROW), 0)
+    begin = 0
+    for width, end in zip(widths, ends):
+        lax.fori_loop(begin, end, functools.partial(body, width), 0)
+        begin = end
     if index == LAST:
         for shift in range(4):
             for half in range(2):
@@ -224,6 +236,7 @@
 def contract(index, plan, a_flipped, b_own, b_other, units, running=None, chol=None):
     vectors, blocks = b_own.shape[:2]
     last = index == LAST
+    widest = ALL_WIDTHS[index][0]
     part = (FIRST_UNITS[index + 1] - FIRST_UNITS[index]) / 8
     flops = int(part * 2 * (a_flipped.size * blocks * B_SLOTS * BLK + b_own.size * BLK))
     moved = int(part * 2 * b_own.size) + 2 * a_flipped.size
@@ -238,9 +251,9 @@
         out_specs=[VMEM, VMEM] if last else VMEM,
         scratch_shapes=[pltpu.VMEM(whole.shape, jnp.float32)] * last
         + [
-            pltpu.VMEM((WIDE * BLK, A_SLOTS * BLK), jnp.bfloat16),
-            pltpu.VMEM((2, WIDE, vectors, BLK, BLK), jnp.bfloat16),
-            pltpu.SemaphoreType.DMA((2, WIDE, 2)),
+            pltpu.VMEM((widest * BLK, A_SLOTS * BLK), jnp.bfloat16),
+            pltpu.VMEM((2, widest, vectors, BLK, BLK), jnp.bfloat16),
+            pltpu.SemaphoreType.DMA((2, widest, 2)),
         ],
         compiler_params=pltpu.CompilerParams(vmem_limit_bytes=47 * 1024 * 1024),
         cost_estimate=pl.CostEstimate(flops=flops, bytes_accessed=moved, transcendentals=0),
@@ -307,14 +320,14 @@
     own = jnp.stack([quarter] + others)
     ahead, back = by_core(own, 1), by_core(own, -1)
     ahead, plan = lax.optimization_barrier((ahead, make_plan(meta)))
-    far_low, far_high = by_core(ahead[:2], 1), by_core(back[2:], -1)
+    far = by_core(ahead, 1)
     unit = pl.pallas_call(
         pick_kernel,
         out_shape=jax.ShapeDtypeStruct((2, BLK, A_SLOTS * BLK), quarter.dtype),
-        in_specs=[SMEM] + [VMEM] * 5,
+        in_specs=[SMEM] + [VMEM] * X_SIZE,
         out_specs=VMEM,
         compiler_params=pltpu.CompilerParams(vmem_limit_bytes=8 * 1024 * 1024),
-    )(meta, own, back, far_low, far_high, ahead)
+    )(meta, own, back, far, ahead)
     return plan, unit, b_held
 
 
@@ -338,10 +351,10 @@
     middle, far_ahead, far_back = by_core(ahead, 1), z_other(ahead), by_core(across, -1)
     running = contract(1, *tiles, [ahead, across, back], running)
     running, middle, far_back, far_ahead = lax.optimization_barrier((running, middle, far_back, far_ahead))
-    far_middle = [by_core(far_ahead[:1], 1), by_core(far_back[1:], -1)]
+    far_middle = by_core(far_ahead, 1)
     running = contract(2, *tiles, [middle, far_back, far_ahead], running)
     running, far_middle = lax.optimization_barrier((running, far_middle))
-    return contract(LAST, *tiles, far_middle, running, chol)
+    return contract(LAST, *tiles, [far_middle], running, chol)
 
 
 def per_device(sizes, ci_vector, a_tiles, a_source, a_sign, b_tiles, b_source, b_sign):

time: 86.5 us -> 82.6 us (0.955)
  starting transfers between devices: 35 us -> 26.6 us
  waiting for transfers between devices: 23.4 us -> 29.2 us
  Pallas kernels: 21.5 us -> 19.7 us
    ppermute x21 -> x19, starting transfers between devices: 35 us -> 26.6 us  [shifted(): return lax.ppermute(value, axis, [(i, moves_to(i)) for i in range(size)])]
    ppermute x21 -> x19, waiting for transfers between devices: 23.4 us -> 29.2 us  [shifted(): return lax.ppermute(value, axis, [(i, moves_to(i)) for i in range(size)])]
    pallas_call x4, Pallas kernels: 15.7 us -> 13.9 us  [contract(): pl.pallas_call(functools.partial(contract_kernel, index), out_shape=[shar...]
  transfers between devices with their start and end apart: 21 -> 19, of which waited for: 13 -> 14; matrix products, arithmetic and copies ran while one was open for 4% -> 4% of each run, Pallas kernels for 22% -> 21%
where the time goes in v8:
time: 82.6 us; the launch traced here: 81.6 us
  waiting for transfers between devices  29.2 us (35%)
  starting transfers between devices  26.6 us (32%)
  Pallas kernels  19.7 us (24%)
  local copies, waits for them, and re-layouts  5.18 us (6%)
    ppermute x19, waiting for transfers between devices, shifted(): return lax.ppermute(value, axis, [(i, moves_to(i)) for i in range(size)])  29.2 us
    ppermute x19, starting transfers between devices, shifted(): return lax.ppermute(value, axis, [(i, moves_to(i)) for i in range(size)])  26.6 us
    pallas_call x4, Pallas kernels, contract(): pl.pallas_call(functools.partial(contract_kernel, index), out_shape=[shar...  13.9 us
    unnamed x8, local copies, waits for them, and re-layouts  3.74 us
    pallas_call x1, Pallas kernels, flip(): pl.pallas_call(flip_kernel, out_shape=jax.ShapeDtypeStruct((A_SLOTS * BLK...  2.33 us
    pallas_call x1, Pallas kernels, make_plan(): pl.pallas_call(plan_kernel, out_shape=jax.ShapeDtypeStruct((KERNELS * PLA...  2.27 us
  transfers between devices with their start and end apart: 19, of which 14 were waited for; matrix products, arithmetic and copies ran while one was open for 4% of the time, Pallas kernels for 21%

profile of v8, /device:TPU:6, one launch (start us, length us, event | category | flops | bytes accessed | tf_op | source)
XLA Modules:
  0.0 81.6 jit_solution(16413929318568402103)
XLA Ops:
  0.0 0.9 %copy-done = bf16[128,1024]{1,0:T(8,128)(2,1)S(1)} copy-done((bf16[128,1024]{1,0:T(8,128)(2,1)S(1)}, bf16[128,1024]{1,0:T(8,128)(2,1)}, u32[]{:S(2)}) %copy-start) | copy-done | bytes 262168
  1.0 7.3 %collective-permute-start.1 = (bf16[128,256]{1,0:T(8,128)(2,1)S(1)}, bf16[128,256]{1,0:T(8,128)(2,1)S(1)}, u32[]{:S(2)}, u32[]{:S(2)}) collective-permute-start(bf16[128,256]{1,0:T(8,128)(2,1)S(1)} %constant_dynamic-slice_fusion), channel_id=1, source_target_pairs={{0,128},{16,144},{32,160},{48,176},{64,192},{80,208},{96,224},{112... | collective-permute-start | bytes 196616 | tf_op jit(solution)/shard_map/ppermute | solution.py:32
  8.2 2.9 %collective-permute-start.2 = (bf16[128,256]{1,0:T(8,128)(2,1)S(1)}, bf16[128,256]{1,0:T(8,128)(2,1)S(1)}, u32[]{:S(2)}, u32[]{:S(2)}) collective-permute-start(bf16[128,256]{1,0:T(8,128)(2,1)S(1)} %constant_dynamic-slice_fusion), channel_id=1, source_target_pairs={{0,64},{16,80},{32,96},{48,112},{64,128},{80,144},{96,160},{112,17... | collective-permute-start | bytes 196616 | tf_op jit(solution)/shard_map/ppermute | solution.py:32
  12.0 0.8 copy.11
  13.0 1.1 %collective-permute-done.3 = s32[48]{0:T(128)S(1)} collective-permute-done((s32[48]{0:T(128)S(1)}, s32[48]{0:T(128)S(1)}, u32[]{:S(2)}, u32[]{:S(2)}) %collective-permute-start.3) | collective-permute-done | bytes 224 | tf_op jit(solution)/shard_map/ppermute | solution.py:32
  14.1 1.1 %collective-permute-done = bf16[128,256]{1,0:T(8,128)(2,1)S(1)} collective-permute-done((bf16[128,256]{1,0:T(8,128)(2,1)S(1)}, bf16[128,256]{1,0:T(8,128)(2,1)S(1)}, u32[]{:S(2)}, u32[]{:S(2)}) %collective-permute-start) | collective-permute-done | bytes 65568 | tf_op jit(solution)/shard_map/ppermute | solution.py:32
  15.8 1.5 %collective-permute-start.6 = (bf16[4,128,256]{2,1,0:T(8,128)(2,1)S(1)}, bf16[4,128,256]{2,1,0:T(8,128)(2,1)S(1)}, u32[]{:S(2)}, u32[]{:S(2)}) collective-permute-start(bf16[4,128,256]{2,1,0:T(8,128)(2,1)S(1)} %pad_maximum_fusion.own_ref), channel_id=1, source_target_pairs={{0,48},{4,20},{8,56},{12,28},{16,0},{20,36},{24,8},{28,44},{32,16}... | collective-permute-start | bytes 786440 | tf_op jit(solution)/shard_map/ppermute | solution.py:32
  17.3 1.3 %concatenate.8.meta_ref = s32[111]{0:T(128)} concatenate(s32[1]{0:T(128)} %bitcast.4, s32[1]{0:T(128)} %bitcast.5, s32[1]{0:T(128)} %bitcast.6.rest_2_, s32[6]{0:T(128)} %bitcast.13, s32[6]{0:T(128)} %bitcast.14, s32[24]{0:T(128)S(1)} %reshape.12, s32[24]{0:T(128)S(1)} %reshape.13, s32[48]{0:T(128)S(1)} %collective-permute-done.3), dimensions={0} | concatenate | bytes 888 | tf_op jit(solution)/shard_map/concatenate | solution.py:319
  18.6 2.3 %shard_map.73.plan_ref = s32[256]{0:T(256)} custom-call(s32[111]{0:T(128)} %concatenate.8.meta_ref), custom_call_target="tpu_custom_call" | custom-call | tf_op jit(solution)/shard_map/pallas_call | solution.py:294
  20.9 3.5 %collective-permute-done.4.ahead_ref = bf16[4,128,256]{2,1,0:T(8,128)(2,1)S(1)} collective-permute-done((bf16[4,128,256]{2,1,0:T(8,128)(2,1)S(1)}, bf16[4,128,256]{2,1,0:T(8,128)(2,1)S(1)}, u32[]{:S(2)}, u32[]{:S(2)}) %collective-permute-start.4) | collective-permute-done | bytes 262176 | tf_op jit(solution)/shard_map/ppermute | solution.py:32
  24.4 0.8 collective-permute-done.6.back_ref
  25.2 5.6 %collective-permute-done.7.far_ref = bf16[4,128,256]{2,1,0:T(8,128)(2,1)S(1)} collective-permute-done((bf16[4,128,256]{2,1,0:T(8,128)(2,1)S(1)}, bf16[4,128,256]{2,1,0:T(8,128)(2,1)S(1)}, u32[]{:S(2)}, u32[]{:S(2)}) %collective-permute-start.7) | collective-permute-done | bytes 262176 | tf_op jit(solution)/shard_map/ppermute | solution.py:32
  31.4 1.1 %shard_map.75.rest_0_ = bf16[2,128,768]{2,1,0:T(8,128)(2,1)S(1)} custom-call(s32[111]{0:T(128)S(1)} %copy-done.2, bf16[4,128,256]{2,1,0:T(8,128)(2,1)S(1)} %pad_maximum_fusion.own_ref, bf16[4,128,256]{2,1,0:T(8,128)(2,1)S(1)} %collective-permute-done.6.back_ref, bf16[4,128,256]{2,1,0:T(8,128)(2,1)S(1)} %collective-permute-done.7.far_ref, ...), custom_call_target="tpu_custom_call" | custom-call | tf_op jit(solution)/shard_map/pallas_call | solution.py:324
  32.5 3.1 %collective-permute-start.10 = (bf16[2,128,768]{2,1,0:T(8,128)(2,1)S(1)}, bf16[2,128,768]{2,1,0:T(8,128)(2,1)S(1)}, u32[]{:S(2)}, u32[]{:S(2)}) collective-permute-start(bf16[2,128,768]{2,1,0:T(8,128)(2,1)S(1)} %shard_map.75.rest_0_), channel_id=1, source_target_pairs={{0,3},{1,0},{2,1},{3,2},{4,5},{5,6},{6,7},{7,4},{8,11},{9,8},{10,9... | collective-permute-start | bytes 1179656 | tf_op jit(solution)/shard_map/ppermute | solution.py:32
  35.6 1.6 %collective-permute-start.9 = (bf16[2,128,768]{2,1,0:T(8,128)(2,1)S(1)}, bf16[2,128,768]{2,1,0:T(8,128)(2,1)S(1)}, u32[]{:S(2)}, u32[]{:S(2)}) collective-permute-start(bf16[2,128,768]{2,1,0:T(8,128)(2,1)S(1)} %shard_map.75.rest_0_), channel_id=1, source_target_pairs={{0,8},{4,12},{8,0},{12,4},{1,9},{5,13},{9,1},{13,5},{2,10},{6,14},... | collective-permute-start | bytes 1179656 | tf_op jit(solution)/shard_map/ppermute | solution.py:32
  37.2 2.3 %shard_map.74.a_ref = bf16[768,2048]{1,0:T(8,128)(2,1)S(1)} custom-call(bf16[16,1,6,128,128]{4,3,2,1,0:T(8,128)(2,1)} %a_hbm.1), custom_call_target="tpu_custom_call" | custom-call | bytes 6291456 | tf_op jit(solution)/shard_map/pallas_call | solution.py:282
  40.2 3.7 %shard_map.76.rest_3_ = f32[16,128,128]{2,1,0:T(8,128)S(1)} custom-call(s32[256]{0:T(256)S(1)} %copy-done.1, bf16[768,2048]{1,0:T(8,128)(2,1)S(1)} %shard_map.74.a_ref, bf16[16,8,3,128,128]{4,3,2,1,0:T(8,128)(2,1)} %b_own.7, bf16[16,8,3,128,128]{4,3,2,1,0:T(8,128)(2,1)} %collective-permute-done.5.b_other, bf16[2,128,768]{2,1,0:T(8,128)(2,1)S(1)} %shard_map.75.rest_0_), custom_call_target="tpu_custom_call" | custom-call | flops 1409286144 | bytes 4718592 | tf_op jit(solution)/shard_map/pallas_call | solution.py:247
  44.9 1.2 %collective-permute-done.8.rest_0_ = bf16[2,128,768]{2,1,0:T(8,128)(2,1)S(1)} collective-permute-done((bf16[2,128,768]{2,1,0:T(8,128)(2,1)S(1)}, bf16[2,128,768]{2,1,0:T(8,128)(2,1)S(1)}, u32[]{:S(2)}, u32[]{:S(2)}) %collective-permute-start.8) | collective-permute-done | bytes 393248 | tf_op jit(solution)/shard_map/ppermute | solution.py:32
  46.6 1.5 %collective-permute-start.11 = (bf16[2,128,768]{2,1,0:T(8,128)(2,1)S(1)}, bf16[2,128,768]{2,1,0:T(8,128)(2,1)S(1)}, u32[]{:S(2)}, u32[]{:S(2)}) collective-permute-start(bf16[2,128,768]{2,1,0:T(8,128)(2,1)S(1)} %collective-permute-done.8.rest_0_), channel_id=1, source_target_pairs={{0,1},{1,2},{2,3},{3,0},{4,7},{5,4},{6,5},{7,6},{8,9},{9,10},{10,1... | collective-permute-start | bytes 1179656 | tf_op jit(solution)/shard_map/ppermute | solution.py:32
  48.2 1.7 %collective-permute-start.12 = (bf16[2,128,768]{2,1,0:T(8,128)(2,1)S(1)}, bf16[2,128,768]{2,1,0:T(8,128)(2,1)S(1)}, u32[]{:S(2)}, u32[]{:S(2)}) collective-permute-start(bf16[2,128,768]{2,1,0:T(8,128)(2,1)S(1)} %collective-permute-done.9.rest_1_), channel_id=1, source_target_pairs={{0,3},{1,0},{2,1},{3,2},{4,5},{5,6},{6,7},{7,4},{8,11},{9,8},{10,9... | collective-permute-start | bytes 1179656 | tf_op jit(solution)/shard_map/ppermute | solution.py:32
  49.8 2.4 %shard_map.77.rest_3_ = f32[16,128,128]{2,1,0:T(8,128)S(1)} custom-call(s32[256]{0:T(256)S(1)} %copy-done.1, bf16[768,2048]{1,0:T(8,128)(2,1)S(1)} %shard_map.74.a_ref, bf16[16,8,3,128,128]{4,3,2,1,0:T(8,128)(2,1)} %b_own.7, bf16[16,8,3,128,128]{4,3,2,1,0:T(8,128)(2,1)} %collective-permute-done.5.b_other, ...), custom_call_target="tpu_custom_call" | custom-call | flops 4227858432 | bytes 7864320 | tf_op jit(solution)/shard_map/pallas_call | solution.py:247
  52.2 5.2 %collective-permute-done.12.rest_1_ = bf16[2,128,768]{2,1,0:T(8,128)(2,1)S(1)} collective-permute-done((bf16[2,128,768]{2,1,0:T(8,128)(2,1)S(1)}, bf16[2,128,768]{2,1,0:T(8,128)(2,1)S(1)}, u32[]{:S(2)}, u32[]{:S(2)}) %collective-permute-start.12) | collective-permute-done | bytes 393248 | tf_op jit(solution)/shard_map/ppermute | solution.py:32
  57.5 1.3 %collective-permute-done.11.rest_0_ = bf16[2,128,768]{2,1,0:T(8,128)(2,1)S(1)} collective-permute-done((bf16[2,128,768]{2,1,0:T(8,128)(2,1)S(1)}, bf16[2,128,768]{2,1,0:T(8,128)(2,1)S(1)}, u32[]{:S(2)}, u32[]{:S(2)}) %collective-permute-start.11) | collective-permute-done | bytes 393248 | tf_op jit(solution)/shard_map/ppermute | solution.py:32
  58.7 1.2 %collective-permute-start.14 = (bf16[2,128,768]{2,1,0:T(8,128)(2,1)S(1)}, bf16[2,128,768]{2,1,0:T(8,128)(2,1)S(1)}, u32[]{:S(2)}, u32[]{:S(2)}) collective-permute-start(bf16[2,128,768]{2,1,0:T(8,128)(2,1)S(1)} %collective-permute-done.13.rest_2_), channel_id=1, source_target_pairs={{0,1},{1,2},{2,3},{3,0},{4,7},{5,4},{6,5},{7,6},{8,9},{9,10},{10,1... | collective-permute-start | bytes 1179656 | tf_op jit(solution)/shard_map/ppermute | solution.py:32
  59.9 5.2 %shard_map.78.rest_1_ = f32[16,128,128]{2,1,0:T(8,128)S(1)} custom-call(s32[256]{0:T(256)S(1)} %copy-done.1, bf16[768,2048]{1,0:T(8,128)(2,1)S(1)} %shard_map.74.a_ref, bf16[16,8,3,128,128]{4,3,2,1,0:T(8,128)(2,1)} %b_own.7, bf16[16,8,3,128,128]{4,3,2,1,0:T(8,128)(2,1)} %collective-permute-done.5.b_other, ...), custom_call_target="tpu_custom_call" | custom-call | flops 4227858432 | bytes 7864320 | tf_op jit(solution)/shard_map/pallas_call | solution.py:247
  65.2 2.6 %collective-permute-done.14.rest_0_ = bf16[2,128,768]{2,1,0:T(8,128)(2,1)S(1)} collective-permute-done((bf16[2,128,768]{2,1,0:T(8,128)(2,1)S(1)}, bf16[2,128,768]{2,1,0:T(8,128)(2,1)S(1)}, u32[]{:S(2)}, u32[]{:S(2)}) %collective-permute-start.14) | collective-permute-done | bytes 393248 | tf_op jit(solution)/shard_map/ppermute | solution.py:32
  67.7 2.6 %shard_map.79 = (f32[4,128,256]{2,1,0:T(8,128)S(1)}, f32[4,128,256]{2,1,0:T(8,128)S(1)}) custom-call(s32[256]{0:T(256)S(1)} %copy-done.1, bf16[768,2048]{1,0:T(8,128)(2,1)S(1)} %shard_map.74.a_ref, bf16[16,8,3,128,128]{4,3,2,1,0:T(8,128)(2,1)} %b_own.7, bf16[16,8,3,128,128]{4,3,2,1,0:T(8,128)(2,1)} %collective-permute-done.5.b_other, ...), custom_call_target="tpu_custom_call" | custom-call | flops 1409286144 | bytes 4718592 | tf_op jit(solution)/shard_map/pallas_call | solution.py:247
  70.3 1.3 %collective-permute-start.15 = (f32[4,128,256]{2,1,0:T(8,128)S(1)}, f32[4,128,256]{2,1,0:T(8,128)S(1)}, u32[]{:S(2)}, u32[]{:S(2)}) collective-permute-start(f32[4,128,256]{2,1,0:T(8,128)S(1)} %get-tuple-element.46), channel_id=1, source_target_pairs={{0,4},{4,0},{8,12},{12,8},{1,5},{5,1},{9,13},{13,9},{2,6},{6,2},{1... | collective-permute-start | bytes 1572872 | tf_op jit(solution)/shard_map/ppermute | solution.py:32
  71.7 1.5 %collective-permute-done.15.arrived_ref = f32[4,128,256]{2,1,0:T(8,128)S(1)} collective-permute-done((f32[4,128,256]{2,1,0:T(8,128)S(1)}, f32[4,128,256]{2,1,0:T(8,128)S(1)}, u32[]{:S(2)}, u32[]{:S(2)}) %collective-permute-start.15) | collective-permute-done | bytes 524320 | tf_op jit(solution)/shard_map/ppermute | solution.py:32
  73.4 1.8 %collective-permute-start.17 = (bf16[128,256]{1,0:T(8,128)(2,1)S(1)}, bf16[128,256]{1,0:T(8,128)(2,1)S(1)}, u32[]{:S(2)}, u32[]{:S(2)}) collective-permute-start(bf16[128,256]{1,0:T(8,128)(2,1)S(1)} %get-tuple-element.49), channel_id=1, source_target_pairs={{0,2},{1,3},{2,0},{3,1},{4,6},{5,7},{6,4},{7,5},{8,10},{9,11},{10,... | collective-permute-start | bytes 196616 | tf_op jit(solution)/shard_map/ppermute | solution.py:32
  75.1 1.5 %collective-permute-start.18 = (bf16[128,256]{1,0:T(8,128)(2,1)S(1)}, bf16[128,256]{1,0:T(8,128)(2,1)S(1)}, u32[]{:S(2)}, u32[]{:S(2)}) collective-permute-start(bf16[128,256]{1,0:T(8,128)(2,1)S(1)} %get-tuple-element.50), channel_id=1, source_target_pairs={{0,3},{1,0},{2,1},{3,2},{4,7},{5,4},{6,5},{7,6},{8,11},{9,8},{10,9... | collective-permute-start | bytes 196616 | tf_op jit(solution)/shard_map/ppermute | solution.py:32
  76.6 3.7 %collective-permute-done.16 = bf16[128,256]{1,0:T(8,128)(2,1)S(1)} collective-permute-done((bf16[128,256]{1,0:T(8,128)(2,1)S(1)}, bf16[128,256]{1,0:T(8,128)(2,1)S(1)}, u32[]{:S(2)}, u32[]{:S(2)}) %collective-permute-start.16) | collective-permute-done | bytes 65568 | tf_op jit(solution)/shard_map/ppermute | solution.py:32
  (30 shorter events, 5.7 us)
Async XLA Ops:
  0.0 1.0 %copy-start = (bf16[128,1024]{1,0:T(8,128)(2,1)S(1)}, bf16[128,1024]{1,0:T(8,128)(2,1)}, u32[]{:S(2)}) copy-start(bf16[128,1024]{1,0:T(8,128)(2,1)} %param.7) | copy-start | bytes 786436
  1.0 13.1 %collective-permute-start.1 = (bf16[128,256]{1,0:T(8,128)(2,1)S(1)}, bf16[128,256]{1,0:T(8,128)(2,1)S(1)}, u32[]{:S(2)}, u32[]{:S(2)}) collective-permute-start(bf16[128,256]{1,0:T(8,128)(2,1)S(1)} %constant_dynamic-slice_fusion), channel_id=1, source_target_pairs={{0,128},{16,144},{32,160},{48,176},{64,192},{80,208},{96,224},{112... | collective-permute-start | bytes 196616 | tf_op jit(solution)/shard_map/ppermute | solution.py:32
  8.2 6.9 %collective-permute-start = (bf16[128,256]{1,0:T(8,128)(2,1)S(1)}, bf16[128,256]{1,0:T(8,128)(2,1)S(1)}, u32[]{:S(2)}, u32[]{:S(2)}) collective-permute-start(bf16[128,256]{1,0:T(8,128)(2,1)S(1)} %constant_dynamic-slice_fusion), channel_id=1, source_target_pairs={{0,192},{16,208},{32,224},{48,240},{64,0},{80,16},{96,32},{112,48}... | collective-permute-start | bytes 196616 | tf_op jit(solution)/shard_map/ppermute | solution.py:32
  8.2 6.9 %collective-permute-start.2 = (bf16[128,256]{1,0:T(8,128)(2,1)S(1)}, bf16[128,256]{1,0:T(8,128)(2,1)S(1)}, u32[]{:S(2)}, u32[]{:S(2)}) collective-permute-start(bf16[128,256]{1,0:T(8,128)(2,1)S(1)} %constant_dynamic-slice_fusion), channel_id=1, source_target_pairs={{0,64},{16,80},{32,96},{48,112},{64,128},{80,144},{96,160},{112,17... | collective-permute-start | bytes 196616 | tf_op jit(solution)/shard_map/ppermute | solution.py:32
  12.9 1.1 %collective-permute-start.3 = (s32[48]{0:T(128)S(1)}, s32[48]{0:T(128)S(1)}, u32[]{:S(2)}, u32[]{:S(2)}) collective-permute-start(s32[48]{0:T(128)S(1)} %pad_add_fusion), channel_id=1, source_target_pairs={{0,4},{4,0},{8,12},{12,8},{1,5},{5,1},{9,13},{13,9},{2,6},{6,2},{1... | collective-permute-start | bytes 584 | tf_op jit(solution)/shard_map/ppermute | solution.py:32
  15.2 24.4 %collective-permute-start.5 = (bf16[16,8,3,128,128]{4,3,2,1,0:T(8,128)(2,1)}, bf16[16,8,3,128,128]{4,3,2,1,0:T(8,128)(2,1)}, u32[]{:S(2)}, u32[]{:S(2)}) collective-permute-start(bf16[16,8,3,128,128]{4,3,2,1,0:T(8,128)(2,1)} %b_own.7), channel_id=1, source_target_pairs={{0,4},{4,0},{8,12},{12,8},{1,5},{5,1},{9,13},{13,9},{2,6},{6,2},{1... | collective-permute-start | bytes 37748744 | tf_op jit(solution)/shard_map/ppermute | solution.py:32
  15.2 9.2 %collective-permute-start.4 = (bf16[4,128,256]{2,1,0:T(8,128)(2,1)S(1)}, bf16[4,128,256]{2,1,0:T(8,128)(2,1)S(1)}, u32[]{:S(2)}, u32[]{:S(2)}) collective-permute-start(bf16[4,128,256]{2,1,0:T(8,128)(2,1)S(1)} %pad_maximum_fusion.own_ref), channel_id=1, source_target_pairs={{0,16},{4,52},{8,24},{12,60},{16,32},{20,4},{24,40},{28,12},{32,48... | collective-permute-start | bytes 786440 | tf_op jit(solution)/shard_map/ppermute | solution.py:32
  15.8 9.4 %collective-permute-start.6 = (bf16[4,128,256]{2,1,0:T(8,128)(2,1)S(1)}, bf16[4,128,256]{2,1,0:T(8,128)(2,1)S(1)}, u32[]{:S(2)}, u32[]{:S(2)}) collective-permute-start(bf16[4,128,256]{2,1,0:T(8,128)(2,1)S(1)} %pad_maximum_fusion.own_ref), channel_id=1, source_target_pairs={{0,48},{4,20},{8,56},{12,28},{16,0},{20,36},{24,8},{28,44},{32,16}... | collective-permute-start | bytes 786440 | tf_op jit(solution)/shard_map/ppermute | solution.py:32
  24.4 6.4 %collective-permute-start.7 = (bf16[4,128,256]{2,1,0:T(8,128)(2,1)S(1)}, bf16[4,128,256]{2,1,0:T(8,128)(2,1)S(1)}, u32[]{:S(2)}, u32[]{:S(2)}) collective-permute-start(bf16[4,128,256]{2,1,0:T(8,128)(2,1)S(1)} %collective-permute-done.4.ahead_ref), channel_id=1, source_target_pairs={{0,16},{4,52},{8,24},{12,60},{16,32},{20,4},{24,40},{28,12},{32,48... | collective-permute-start | bytes 786440 | tf_op jit(solution)/shard_map/ppermute | solution.py:32
  30.8 0.6 copy-start.2
  32.5 12.1 %collective-permute-start.10 = (bf16[2,128,768]{2,1,0:T(8,128)(2,1)S(1)}, bf16[2,128,768]{2,1,0:T(8,128)(2,1)S(1)}, u32[]{:S(2)}, u32[]{:S(2)}) collective-permute-start(bf16[2,128,768]{2,1,0:T(8,128)(2,1)S(1)} %shard_map.75.rest_0_), channel_id=1, source_target_pairs={{0,3},{1,0},{2,1},{3,2},{4,5},{5,6},{6,7},{7,4},{8,11},{9,8},{10,9... | collective-permute-start | bytes 1179656 | tf_op jit(solution)/shard_map/ppermute | solution.py:32
  35.6 9.3 %collective-permute-start.9 = (bf16[2,128,768]{2,1,0:T(8,128)(2,1)S(1)}, bf16[2,128,768]{2,1,0:T(8,128)(2,1)S(1)}, u32[]{:S(2)}, u32[]{:S(2)}) collective-permute-start(bf16[2,128,768]{2,1,0:T(8,128)(2,1)S(1)} %shard_map.75.rest_0_), channel_id=1, source_target_pairs={{0,8},{4,12},{8,0},{12,4},{1,9},{5,13},{9,1},{13,5},{2,10},{6,14},... | collective-permute-start | bytes 1179656 | tf_op jit(solution)/shard_map/ppermute | solution.py:32
  37.2 9.0 %collective-permute-start.8 = (bf16[2,128,768]{2,1,0:T(8,128)(2,1)S(1)}, bf16[2,128,768]{2,1,0:T(8,128)(2,1)S(1)}, u32[]{:S(2)}, u32[]{:S(2)}) collective-permute-start(bf16[2,128,768]{2,1,0:T(8,128)(2,1)S(1)} %shard_map.75.rest_0_), channel_id=1, source_target_pairs={{0,1},{1,2},{2,3},{3,0},{4,7},{5,4},{6,5},{7,6},{8,9},{9,10},{10,1... | collective-permute-start | bytes 1179656 | tf_op jit(solution)/shard_map/ppermute | solution.py:32
  39.5 0.7 copy-start.1
  46.2 11.3 %collective-permute-start.13 = (bf16[2,128,768]{2,1,0:T(8,128)(2,1)S(1)}, bf16[2,128,768]{2,1,0:T(8,128)(2,1)S(1)}, u32[]{:S(2)}, u32[]{:S(2)}) collective-permute-start(bf16[2,128,768]{2,1,0:T(8,128)(2,1)S(1)} %collective-permute-done.8.rest_0_), channel_id=1, source_target_pairs={{0,8},{4,12},{8,0},{12,4},{1,9},{5,13},{9,1},{13,5},{2,10},{6,14},... | collective-permute-start | bytes 1179656 | tf_op jit(solution)/shard_map/ppermute | solution.py:32
  46.6 12.1 %collective-permute-start.11 = (bf16[2,128,768]{2,1,0:T(8,128)(2,1)S(1)}, bf16[2,128,768]{2,1,0:T(8,128)(2,1)S(1)}, u32[]{:S(2)}, u32[]{:S(2)}) collective-permute-start(bf16[2,128,768]{2,1,0:T(8,128)(2,1)S(1)} %collective-permute-done.8.rest_0_), channel_id=1, source_target_pairs={{0,1},{1,2},{2,3},{3,0},{4,7},{5,4},{6,5},{7,6},{8,9},{9,10},{10,1... | collective-permute-start | bytes 1179656 | tf_op jit(solution)/shard_map/ppermute | solution.py:32
  48.2 9.3 %collective-permute-start.12 = (bf16[2,128,768]{2,1,0:T(8,128)(2,1)S(1)}, bf16[2,128,768]{2,1,0:T(8,128)(2,1)S(1)}, u32[]{:S(2)}, u32[]{:S(2)}) collective-permute-start(bf16[2,128,768]{2,1,0:T(8,128)(2,1)S(1)} %collective-permute-done.9.rest_1_), channel_id=1, source_target_pairs={{0,3},{1,0},{2,1},{3,2},{4,5},{5,6},{6,7},{7,4},{8,11},{9,8},{10,9... | collective-permute-start | bytes 1179656 | tf_op jit(solution)/shard_map/ppermute | solution.py:32
  58.7 9.0 %collective-permute-start.14 = (bf16[2,128,768]{2,1,0:T(8,128)(2,1)S(1)}, bf16[2,128,768]{2,1,0:T(8,128)(2,1)S(1)}, u32[]{:S(2)}, u32[]{:S(2)}) collective-permute-start(bf16[2,128,768]{2,1,0:T(8,128)(2,1)S(1)} %collective-permute-done.13.rest_2_), channel_id=1, source_target_pairs={{0,1},{1,2},{2,3},{3,0},{4,7},{5,4},{6,5},{7,6},{8,9},{9,10},{10,1... | collective-permute-start | bytes 1179656 | tf_op jit(solution)/shard_map/ppermute | solution.py:32
  70.3 2.9 %collective-permute-start.15 = (f32[4,128,256]{2,1,0:T(8,128)S(1)}, f32[4,128,256]{2,1,0:T(8,128)S(1)}, u32[]{:S(2)}, u32[]{:S(2)}) collective-permute-start(f32[4,128,256]{2,1,0:T(8,128)S(1)} %get-tuple-element.46), channel_id=1, source_target_pairs={{0,4},{4,0},{8,12},{12,8},{1,5},{5,1},{9,13},{13,9},{2,6},{6,2},{1... | collective-permute-start | bytes 1572872 | tf_op jit(solution)/shard_map/ppermute | solution.py:32
  73.3 7.1 %collective-permute-start.16 = (bf16[128,256]{1,0:T(8,128)(2,1)S(1)}, bf16[128,256]{1,0:T(8,128)(2,1)S(1)}, u32[]{:S(2)}, u32[]{:S(2)}) collective-permute-start(bf16[128,256]{1,0:T(8,128)(2,1)S(1)} %get-tuple-element.48), channel_id=1, source_target_pairs={{0,1},{1,2},{2,3},{3,0},{4,5},{5,6},{6,7},{7,4},{8,9},{9,10},{10,1... | collective-permute-start | bytes 196616 | tf_op jit(solution)/shard_map/ppermute | solution.py:32
  73.4 7.0 %collective-permute-start.17 = (bf16[128,256]{1,0:T(8,128)(2,1)S(1)}, bf16[128,256]{1,0:T(8,128)(2,1)S(1)}, u32[]{:S(2)}, u32[]{:S(2)}) collective-permute-start(bf16[128,256]{1,0:T(8,128)(2,1)S(1)} %get-tuple-element.49), channel_id=1, source_target_pairs={{0,2},{1,3},{2,0},{3,1},{4,6},{5,7},{6,4},{7,5},{8,10},{9,11},{10,... | collective-permute-start | bytes 196616 | tf_op jit(solution)/shard_map/ppermute | solution.py:32
  75.1 5.8 %collective-permute-start.18 = (bf16[128,256]{1,0:T(8,128)(2,1)S(1)}, bf16[128,256]{1,0:T(8,128)(2,1)S(1)}, u32[]{:S(2)}, u32[]{:S(2)}) collective-permute-start(bf16[128,256]{1,0:T(8,128)(2,1)S(1)} %get-tuple-element.50), channel_id=1, source_target_pairs={{0,3},{1,0},{2,1},{3,2},{4,7},{5,4},{6,5},{7,6},{8,11},{9,8},{10,9... | collective-permute-start | bytes 196616 | tf_op jit(solution)/shard_map/ppermute | solution.py:32

commit v9 on v8

--- a/solution.py
+++ b/solution.py
@@ -78,7 +78,8 @@
         live = (sign != 0) & ((owner & 1) == core)
         for index in range(KERNELS):
             low, high = FIRST_UNITS[index], FIRST_UNITS[index + 1]
-            entry = pair + ((unit - low) << 6) + ((m & 1) << 9) + ((sign + 1) << 10)
+            where = jnp.where(unit >= 6, (unit - low + (m & 1)) << 6, ((unit - low) << 6) + ((m & 1) << 9))
+            entry = pair + where + ((sign + 1) << 10)
             plan_ref[index * PLAN + 1 + counts[index]] = entry
             counts[index] = counts[index] + jnp.where(live & (unit >= low) & (unit < high), 1, 0)
     for index in range(KERNELS):
@@ -109,7 +110,7 @@
 
 
 def contract_kernel(index, plan_ref, a_ref, b_own, b_other, *rest):
-    count_units = FIRST_UNITS[index + 1] - FIRST_UNITS[index]
+    count_units = FIRST_UNITS[index + 1] - FIRST_UNITS[index] + (index >= 2)
     units, rest = rest[:count_units], rest[count_units:]
     if index:
         sum_ref, rest = rest[0], rest[1:]
@@ -348,13 +349,16 @@
     tiles = (plan, flip(a_tiles), b_own, b_other)
     running = contract(0, *tiles, [unit])
     running, ahead, across, back = lax.optimization_barrier((running, ahead, across, back))
-    middle, far_ahead, far_back = by_core(ahead, 1), z_other(ahead), by_core(across, -1)
+    middle, far_back = by_core(ahead, 1), by_core(across, -1)
+    far_low, far_high = z_other(ahead[:1]), z_other(ahead[1:])
     running = contract(1, *tiles, [ahead, across, back], running)
-    running, middle, far_back, far_ahead = lax.optimization_barrier((running, middle, far_back, far_ahead))
-    far_middle = by_core(far_ahead, 1)
-    running = contract(2, *tiles, [middle, far_back, far_ahead], running)
-    running, far_middle = lax.optimization_barrier((running, far_middle))
-    return contract(LAST, *tiles, [far_middle], running, chol)
+    running, far_low = lax.optimization_barrier((running, far_low))
+    last_low = by_core(far_low, 1)
+    running, middle, far_back, far_high = lax.optimization_barrier((running, middle, far_back, far_high))
+    last_high = by_core(far_high, 1)
+    running = contract(2, *tiles, [middle, far_back, far_low, far_high], running)
+    running, last_low, last_high = lax.optimization_barrier((running, last_low, last_high))
+    return contract(LAST, *tiles, [last_low, last_high], running, chol)
 
 
 def per_device(sizes, ci_vector, a_tiles, a_source, a_sign, b_tiles, b_source, b_sign):

time: 82.6 us -> 85.7 us (1.038)
  the two profiles are of different devices: /device:TPU:6 before, /device:TPU:38 now
where the time goes in v9:
time: 85.7 us; the launch traced here: 84.8 us
  waiting for transfers between devices  29.5 us (34%)
  starting transfers between devices  24.7 us (29%)
  Pallas kernels  24.2 us (28%)
  local copies, waits for them, and re-layouts  5.36 us (6%)
    ppermute x21, waiting for transfers between devices, shifted(): return lax.ppermute(value, axis, [(i, moves_to(i)) for i in range(size)])  29.5 us
    ppermute x21, starting transfers between devices, shifted(): return lax.ppermute(value, axis, [(i, moves_to(i)) for i in range(size)])  24.7 us
    pallas_call x4, Pallas kernels, contract(): pl.pallas_call(functools.partial(contract_kernel, index), out_shape=[shar...  18.3 us
    unnamed x8, local copies, waits for them, and re-layouts  3.81 us
    pallas_call x1, Pallas kernels, make_plan(): pl.pallas_call(plan_kernel, out_shape=jax.ShapeDtypeStruct((KERNELS * PLA...  2.43 us
    pallas_call x1, Pallas kernels, flip(): pl.pallas_call(flip_kernel, out_shape=jax.ShapeDtypeStruct((A_SLOTS * BLK...  2.33 us
  transfers between devices with their start and end apart: 21, of which 14 were waited for; matrix products, arithmetic and copies ran while one was open for 4% of the time, Pallas kernels for 23%

profile of v9, /device:TPU:38, one launch (start us, length us, event | category | flops | bytes accessed | tf_op | source)
XLA Modules:
  0.0 84.8 jit_solution(1591839106478368947)
XLA Ops:
  0.0 0.9 %copy-done = bf16[128,1024]{1,0:T(8,128)(2,1)S(1)} copy-done((bf16[128,1024]{1,0:T(8,128)(2,1)S(1)}, bf16[128,1024]{1,0:T(8,128)(2,1)}, u32[]{:S(2)}) %copy-start) | copy-done | bytes 262168
  1.0 5.5 %collective-permute-start = (bf16[128,256]{1,0:T(8,128)(2,1)S(1)}, bf16[128,256]{1,0:T(8,128)(2,1)S(1)}, u32[]{:S(2)}, u32[]{:S(2)}) collective-permute-start(bf16[128,256]{1,0:T(8,128)(2,1)S(1)} %constant_dynamic-slice_fusion), channel_id=1, source_target_pairs={{0,192},{16,208},{32,224},{48,240},{64,0},{80,16},{96,32},{112,48}... | collective-permute-start | bytes 196616 | tf_op jit(solution)/shard_map/ppermute | solution.py:32
  6.4 1.4 %collective-permute-start.1 = (bf16[128,256]{1,0:T(8,128)(2,1)S(1)}, bf16[128,256]{1,0:T(8,128)(2,1)S(1)}, u32[]{:S(2)}, u32[]{:S(2)}) collective-permute-start(bf16[128,256]{1,0:T(8,128)(2,1)S(1)} %constant_dynamic-slice_fusion), channel_id=1, source_target_pairs={{0,128},{16,144},{32,160},{48,176},{64,192},{80,208},{96,224},{112... | collective-permute-start | bytes 196616 | tf_op jit(solution)/shard_map/ppermute | solution.py:32
  7.9 2.4 %collective-permute-start.2 = (bf16[128,256]{1,0:T(8,128)(2,1)S(1)}, bf16[128,256]{1,0:T(8,128)(2,1)S(1)}, u32[]{:S(2)}, u32[]{:S(2)}) collective-permute-start(bf16[128,256]{1,0:T(8,128)(2,1)S(1)} %constant_dynamic-slice_fusion), channel_id=1, source_target_pairs={{0,64},{16,80},{32,96},{48,112},{64,128},{80,144},{96,160},{112,17... | collective-permute-start | bytes 196616 | tf_op jit(solution)/shard_map/ppermute | solution.py:32
  10.3 0.8 copy.10
  11.1 0.8 copy.11
  12.0 1.1 %collective-permute-done.3 = s32[48]{0:T(128)S(1)} collective-permute-done((s32[48]{0:T(128)S(1)}, s32[48]{0:T(128)S(1)}, u32[]{:S(2)}, u32[]{:S(2)}) %collective-permute-start.3) | collective-permute-done | bytes 224 | tf_op jit(solution)/shard_map/ppermute | solution.py:32
  13.2 1.7 %collective-permute-done.1 = bf16[128,256]{1,0:T(8,128)(2,1)S(1)} collective-permute-done((bf16[128,256]{1,0:T(8,128)(2,1)S(1)}, bf16[128,256]{1,0:T(8,128)(2,1)S(1)}, u32[]{:S(2)}, u32[]{:S(2)}) %collective-permute-start.1) | collective-permute-done | bytes 65568 | tf_op jit(solution)/shard_map/ppermute | solution.py:32
  14.9 1.3 %collective-permute-done.2 = bf16[128,256]{1,0:T(8,128)(2,1)S(1)} collective-permute-done((bf16[128,256]{1,0:T(8,128)(2,1)S(1)}, bf16[128,256]{1,0:T(8,128)(2,1)S(1)}, u32[]{:S(2)}, u32[]{:S(2)}) %collective-permute-start.2) | collective-permute-done | bytes 65568 | tf_op jit(solution)/shard_map/ppermute | solution.py:32
  16.7 1.7 %collective-permute-start.6 = (bf16[4,128,256]{2,1,0:T(8,128)(2,1)S(1)}, bf16[4,128,256]{2,1,0:T(8,128)(2,1)S(1)}, u32[]{:S(2)}, u32[]{:S(2)}) collective-permute-start(bf16[4,128,256]{2,1,0:T(8,128)(2,1)S(1)} %pad_maximum_fusion.own_ref), channel_id=1, source_target_pairs={{0,48},{4,20},{8,56},{12,28},{16,0},{20,36},{24,8},{28,44},{32,16}... | collective-permute-start | bytes 786440 | tf_op jit(solution)/shard_map/ppermute | solution.py:32
  18.4 1.3 %concatenate.8.meta_ref = s32[111]{0:T(128)} concatenate(s32[1]{0:T(128)} %bitcast.4, s32[1]{0:T(128)} %bitcast.5, s32[1]{0:T(128)} %bitcast.6.rest_3_, s32[6]{0:T(128)} %bitcast.13, s32[6]{0:T(128)} %bitcast.14, s32[24]{0:T(128)S(1)} %reshape.12, s32[24]{0:T(128)S(1)} %reshape.13, s32[48]{0:T(128)S(1)} %collective-permute-done.3), dimensions={0} | concatenate | bytes 888 | tf_op jit(solution)/shard_map/concatenate | solution.py:320
  19.7 2.4 %shard_map.73.plan_ref = s32[256]{0:T(256)} custom-call(s32[111]{0:T(128)} %concatenate.8.meta_ref), custom_call_target="tpu_custom_call" | custom-call | tf_op jit(solution)/shard_map/pallas_call | solution.py:295
  22.1 3.3 %collective-permute-done.4.ahead_ref = bf16[4,128,256]{2,1,0:T(8,128)(2,1)S(1)} collective-permute-done((bf16[4,128,256]{2,1,0:T(8,128)(2,1)S(1)}, bf16[4,128,256]{2,1,0:T(8,128)(2,1)S(1)}, u32[]{:S(2)}, u32[]{:S(2)}) %collective-permute-start.4) | collective-permute-done | bytes 262176 | tf_op jit(solution)/shard_map/ppermute | solution.py:32
  25.4 0.8 collective-permute-done.6.back_ref
  26.3 5.5 %collective-permute-done.7.far_ref = bf16[4,128,256]{2,1,0:T(8,128)(2,1)S(1)} collective-permute-done((bf16[4,128,256]{2,1,0:T(8,128)(2,1)S(1)}, bf16[4,128,256]{2,1,0:T(8,128)(2,1)S(1)}, u32[]{:S(2)}, u32[]{:S(2)}) %collective-permute-start.7) | collective-permute-done | bytes 262176 | tf_op jit(solution)/shard_map/ppermute | solution.py:32
  32.5 1.1 %shard_map.75.rest_0_ = bf16[2,128,768]{2,1,0:T(8,128)(2,1)S(1)} custom-call(s32[111]{0:T(128)S(1)} %copy-done.2, bf16[4,128,256]{2,1,0:T(8,128)(2,1)S(1)} %pad_maximum_fusion.own_ref, bf16[4,128,256]{2,1,0:T(8,128)(2,1)S(1)} %collective-permute-done.6.back_ref, bf16[4,128,256]{2,1,0:T(8,128)(2,1)S(1)} %collective-permute-done.7.far_ref, ...), custom_call_target="tpu_custom_call" | custom-call | tf_op jit(solution)/shard_map/pallas_call | solution.py:325
  33.6 3.1 %collective-permute-start.10 = (bf16[2,128,768]{2,1,0:T(8,128)(2,1)S(1)}, bf16[2,128,768]{2,1,0:T(8,128)(2,1)S(1)}, u32[]{:S(2)}, u32[]{:S(2)}) collective-permute-start(bf16[2,128,768]{2,1,0:T(8,128)(2,1)S(1)} %shard_map.75.rest_0_), channel_id=1, source_target_pairs={{0,3},{1,0},{2,1},{3,2},{4,5},{5,6},{6,7},{7,4},{8,11},{9,8},{10,9... | collective-permute-start | bytes 1179656 | tf_op jit(solution)/shard_map/ppermute | solution.py:32
  37.2 2.3 %shard_map.74.a_ref = bf16[768,2048]{1,0:T(8,128)(2,1)S(1)} custom-call(bf16[16,1,6,128,128]{4,3,2,1,0:T(8,128)(2,1)} %a_hbm.1), custom_call_target="tpu_custom_call" | custom-call | bytes 6291456 | tf_op jit(solution)/shard_map/pallas_call | solution.py:283
  40.2 2.3 %shard_map.76.rest_3_ = f32[16,128,128]{2,1,0:T(8,128)S(1)} custom-call(s32[256]{0:T(256)S(1)} %copy-done.1, bf16[768,2048]{1,0:T(8,128)(2,1)S(1)} %shard_map.74.a_ref, bf16[16,8,3,128,128]{4,3,2,1,0:T(8,128)(2,1)} %b_own.7, bf16[16,8,3,128,128]{4,3,2,1,0:T(8,128)(2,1)} %collective-permute-done.5.b_other, bf16[2,128,768]{2,1,0:T(8,128)(2,1)S(1)} %shard_map.75.rest_0_), custom_call_target="tpu_custom_call" | custom-call | flops 1409286144 | bytes 4718592 | tf_op jit(solution)/shard_map/pallas_call | solution.py:248
  42.5 2.9 %collective-permute-done.10.rest_2_ = bf16[2,128,768]{2,1,0:T(8,128)(2,1)S(1)} collective-permute-done((bf16[2,128,768]{2,1,0:T(8,128)(2,1)S(1)}, bf16[2,128,768]{2,1,0:T(8,128)(2,1)S(1)}, u32[]{:S(2)}, u32[]{:S(2)}) %collective-permute-start.10) | collective-permute-done | bytes 393248 | tf_op jit(solution)/shard_map/ppermute | solution.py:32
  46.1 1.5 %collective-permute-done.9.rest_1_ = bf16[2,128,768]{2,1,0:T(8,128)(2,1)S(1)} collective-permute-done((bf16[2,128,768]{2,1,0:T(8,128)(2,1)S(1)}, bf16[2,128,768]{2,1,0:T(8,128)(2,1)S(1)}, u32[]{:S(2)}, u32[]{:S(2)}) %collective-permute-start.9) | collective-permute-done | bytes 393248 | tf_op jit(solution)/shard_map/ppermute | solution.py:32
  48.6 1.5 %collective-permute-start.14 = (bf16[1,128,768]{2,1,0:T(8,128)(2,1)S(1)}, bf16[1,128,768]{2,1,0:T(8,128)(2,1)S(1)}, u32[]{:S(2)}, u32[]{:S(2)}) collective-permute-start(bf16[1,128,768]{2,1,0:T(8,128)(2,1)S(1)} %get-tuple-element.57), channel_id=1, source_target_pairs={{0,8},{4,12},{8,0},{12,4},{1,9},{5,13},{9,1},{13,5},{2,10},{6,14},... | collective-permute-start | bytes 589832 | tf_op jit(solution)/shard_map/ppermute | solution.py:32
  50.1 3.0 %collective-permute-start.13 = (bf16[2,128,768]{2,1,0:T(8,128)(2,1)S(1)}, bf16[2,128,768]{2,1,0:T(8,128)(2,1)S(1)}, u32[]{:S(2)}, u32[]{:S(2)}) collective-permute-start(bf16[2,128,768]{2,1,0:T(8,128)(2,1)S(1)} %collective-permute-done.9.rest_1_), channel_id=1, source_target_pairs={{0,3},{1,0},{2,1},{3,2},{4,5},{5,6},{6,7},{7,4},{8,11},{9,8},{10,9... | collective-permute-start | bytes 1179656 | tf_op jit(solution)/shard_map/ppermute | solution.py:32
  53.1 8.0 %shard_map.77.rest_4_ = f32[16,128,128]{2,1,0:T(8,128)S(1)} custom-call(s32[256]{0:T(256)S(1)} %copy-done.1, bf16[768,2048]{1,0:T(8,128)(2,1)S(1)} %shard_map.74.a_ref, bf16[16,8,3,128,128]{4,3,2,1,0:T(8,128)(2,1)} %b_own.7, bf16[16,8,3,128,128]{4,3,2,1,0:T(8,128)(2,1)} %collective-permute-done.5.b_other, ...), custom_call_target="tpu_custom_call" | custom-call | flops 4227858432 | bytes 7864320 | tf_op jit(solution)/shard_map/pallas_call | solution.py:248
  62.0 3.6 %shard_map.78.rest_2_ = f32[16,128,128]{2,1,0:T(8,128)S(1)} custom-call(s32[256]{0:T(256)S(1)} %copy-done.1, bf16[768,2048]{1,0:T(8,128)(2,1)S(1)} %shard_map.74.a_ref, bf16[16,8,3,128,128]{4,3,2,1,0:T(8,128)(2,1)} %b_own.7, bf16[16,8,3,128,128]{4,3,2,1,0:T(8,128)(2,1)} %collective-permute-done.5.b_other, ...), custom_call_target="tpu_custom_call" | custom-call | flops 4227858432 | bytes 7864320 | tf_op jit(solution)/shard_map/pallas_call | solution.py:248
  65.6 2.5 %collective-permute-done.15.rest_0_ = bf16[1,128,768]{2,1,0:T(8,128)(2,1)S(1)} collective-permute-done((bf16[1,128,768]{2,1,0:T(8,128)(2,1)S(1)}, bf16[1,128,768]{2,1,0:T(8,128)(2,1)S(1)}, u32[]{:S(2)}, u32[]{:S(2)}) %collective-permute-start.15) | collective-permute-done | bytes 196640 | tf_op jit(solution)/shard_map/ppermute | solution.py:32
  68.1 2.1 %collective-permute-done.16.rest_1_ = bf16[1,128,768]{2,1,0:T(8,128)(2,1)S(1)} collective-permute-done((bf16[1,128,768]{2,1,0:T(8,128)(2,1)S(1)}, bf16[1,128,768]{2,1,0:T(8,128)(2,1)S(1)}, u32[]{:S(2)}, u32[]{:S(2)}) %collective-permute-start.16) | collective-permute-done | bytes 196640 | tf_op jit(solution)/shard_map/ppermute | solution.py:32
  70.2 4.4 %shard_map.79 = (f32[4,128,256]{2,1,0:T(8,128)S(1)}, f32[4,128,256]{2,1,0:T(8,128)S(1)}) custom-call(s32[256]{0:T(256)S(1)} %copy-done.1, bf16[768,2048]{1,0:T(8,128)(2,1)S(1)} %shard_map.74.a_ref, bf16[16,8,3,128,128]{4,3,2,1,0:T(8,128)(2,1)} %b_own.7, bf16[16,8,3,128,128]{4,3,2,1,0:T(8,128)(2,1)} %collective-permute-done.5.b_other, ...), custom_call_target="tpu_custom_call" | custom-call | flops 1409286144 | bytes 4718592 | tf_op jit(solution)/shard_map/pallas_call | solution.py:248
  74.7 1.9 %collective-permute-done.17.arrived_ref = f32[4,128,256]{2,1,0:T(8,128)S(1)} collective-permute-done((f32[4,128,256]{2,1,0:T(8,128)S(1)}, f32[4,128,256]{2,1,0:T(8,128)S(1)}, u32[]{:S(2)}, u32[]{:S(2)}) %collective-permute-start.17) | collective-permute-done | bytes 524320 | tf_op jit(solution)/shard_map/ppermute | solution.py:32
  76.8 0.8 collective-permute-start.19
  77.6 2.5 %collective-permute-start.20 = (bf16[128,256]{1,0:T(8,128)(2,1)S(1)}, bf16[128,256]{1,0:T(8,128)(2,1)S(1)}, u32[]{:S(2)}, u32[]{:S(2)}) collective-permute-start(bf16[128,256]{1,0:T(8,128)(2,1)S(1)} %get-tuple-element.56), channel_id=1, source_target_pairs={{0,3},{1,0},{2,1},{3,2},{4,7},{5,4},{6,5},{7,6},{8,11},{9,8},{10,9... | collective-permute-start | bytes 196616 | tf_op jit(solution)/shard_map/ppermute | solution.py:32
  80.0 3.5 %collective-permute-done.18 = bf16[128,256]{1,0:T(8,128)(2,1)S(1)} collective-permute-done((bf16[128,256]{1,0:T(8,128)(2,1)S(1)}, bf16[128,256]{1,0:T(8,128)(2,1)S(1)}, u32[]{:S(2)}, u32[]{:S(2)}) %collective-permute-start.18) | collective-permute-done | bytes 65568 | tf_op jit(solution)/shard_map/ppermute | solution.py:32
  (35 shorter events, 6.6 us)
Async XLA Ops:
  0.0 1.0 %copy-start = (bf16[128,1024]{1,0:T(8,128)(2,1)S(1)}, bf16[128,1024]{1,0:T(8,128)(2,1)}, u32[]{:S(2)}) copy-start(bf16[128,1024]{1,0:T(8,128)(2,1)} %param.7) | copy-start | bytes 786436
  1.0 12.2 %collective-permute-start = (bf16[128,256]{1,0:T(8,128)(2,1)S(1)}, bf16[128,256]{1,0:T(8,128)(2,1)S(1)}, u32[]{:S(2)}, u32[]{:S(2)}) collective-permute-start(bf16[128,256]{1,0:T(8,128)(2,1)S(1)} %constant_dynamic-slice_fusion), channel_id=1, source_target_pairs={{0,192},{16,208},{32,224},{48,240},{64,0},{80,16},{96,32},{112,48}... | collective-permute-start | bytes 196616 | tf_op jit(solution)/shard_map/ppermute | solution.py:32
  6.4 8.4 %collective-permute-start.1 = (bf16[128,256]{1,0:T(8,128)(2,1)S(1)}, bf16[128,256]{1,0:T(8,128)(2,1)S(1)}, u32[]{:S(2)}, u32[]{:S(2)}) collective-permute-start(bf16[128,256]{1,0:T(8,128)(2,1)S(1)} %constant_dynamic-slice_fusion), channel_id=1, source_target_pairs={{0,128},{16,144},{32,160},{48,176},{64,192},{80,208},{96,224},{112... | collective-permute-start | bytes 196616 | tf_op jit(solution)/shard_map/ppermute | solution.py:32
  7.9 8.3 %collective-permute-start.2 = (bf16[128,256]{1,0:T(8,128)(2,1)S(1)}, bf16[128,256]{1,0:T(8,128)(2,1)S(1)}, u32[]{:S(2)}, u32[]{:S(2)}) collective-permute-start(bf16[128,256]{1,0:T(8,128)(2,1)S(1)} %constant_dynamic-slice_fusion), channel_id=1, source_target_pairs={{0,64},{16,80},{32,96},{48,112},{64,128},{80,144},{96,160},{112,17... | collective-permute-start | bytes 196616 | tf_op jit(solution)/shard_map/ppermute | solution.py:32
  12.0 1.1 %collective-permute-start.3 = (s32[48]{0:T(128)S(1)}, s32[48]{0:T(128)S(1)}, u32[]{:S(2)}, u32[]{:S(2)}) collective-permute-start(s32[48]{0:T(128)S(1)} %pad_add_fusion), channel_id=1, source_target_pairs={{0,4},{4,0},{8,12},{12,8},{1,5},{5,1},{9,13},{13,9},{2,6},{6,2},{1... | collective-permute-start | bytes 584 | tf_op jit(solution)/shard_map/ppermute | solution.py:32
  16.2 23.4 %collective-permute-start.5 = (bf16[16,8,3,128,128]{4,3,2,1,0:T(8,128)(2,1)}, bf16[16,8,3,128,128]{4,3,2,1,0:T(8,128)(2,1)}, u32[]{:S(2)}, u32[]{:S(2)}) collective-permute-start(bf16[16,8,3,128,128]{4,3,2,1,0:T(8,128)(2,1)} %b_own.7), channel_id=1, source_target_pairs={{0,4},{4,0},{8,12},{12,8},{1,5},{5,1},{9,13},{13,9},{2,6},{6,2},{1... | collective-permute-start | bytes 37748744 | tf_op jit(solution)/shard_map/ppermute | solution.py:32
  16.3 9.2 %collective-permute-start.4 = (bf16[4,128,256]{2,1,0:T(8,128)(2,1)S(1)}, bf16[4,128,256]{2,1,0:T(8,128)(2,1)S(1)}, u32[]{:S(2)}, u32[]{:S(2)}) collective-permute-start(bf16[4,128,256]{2,1,0:T(8,128)(2,1)S(1)} %pad_maximum_fusion.own_ref), channel_id=1, source_target_pairs={{0,16},{4,52},{8,24},{12,60},{16,32},{20,4},{24,40},{28,12},{32,48... | collective-permute-start | bytes 786440 | tf_op jit(solution)/shard_map/ppermute | solution.py:32
  16.7 9.6 %collective-permute-start.6 = (bf16[4,128,256]{2,1,0:T(8,128)(2,1)S(1)}, bf16[4,128,256]{2,1,0:T(8,128)(2,1)S(1)}, u32[]{:S(2)}, u32[]{:S(2)}) collective-permute-start(bf16[4,128,256]{2,1,0:T(8,128)(2,1)S(1)} %pad_maximum_fusion.own_ref), channel_id=1, source_target_pairs={{0,48},{4,20},{8,56},{12,28},{16,0},{20,36},{24,8},{28,44},{32,16}... | collective-permute-start | bytes 786440 | tf_op jit(solution)/shard_map/ppermute | solution.py:32
  25.4 6.4 %collective-permute-start.7 = (bf16[4,128,256]{2,1,0:T(8,128)(2,1)S(1)}, bf16[4,128,256]{2,1,0:T(8,128)(2,1)S(1)}, u32[]{:S(2)}, u32[]{:S(2)}) collective-permute-start(bf16[4,128,256]{2,1,0:T(8,128)(2,1)S(1)} %collective-permute-done.4.ahead_ref), channel_id=1, source_target_pairs={{0,16},{4,52},{8,24},{12,60},{16,32},{20,4},{24,40},{28,12},{32,48... | collective-permute-start | bytes 786440 | tf_op jit(solution)/shard_map/ppermute | solution.py:32
  31.8 0.7 copy-start.2
  33.6 11.8 %collective-permute-start.10 = (bf16[2,128,768]{2,1,0:T(8,128)(2,1)S(1)}, bf16[2,128,768]{2,1,0:T(8,128)(2,1)S(1)}, u32[]{:S(2)}, u32[]{:S(2)}) collective-permute-start(bf16[2,128,768]{2,1,0:T(8,128)(2,1)S(1)} %shard_map.75.rest_0_), channel_id=1, source_target_pairs={{0,3},{1,0},{2,1},{3,2},{4,5},{5,6},{6,7},{7,4},{8,11},{9,8},{10,9... | collective-permute-start | bytes 1179656 | tf_op jit(solution)/shard_map/ppermute | solution.py:32
  36.7 9.4 %collective-permute-start.8 = (bf16[2,128,768]{2,1,0:T(8,128)(2,1)S(1)}, bf16[2,128,768]{2,1,0:T(8,128)(2,1)S(1)}, u32[]{:S(2)}, u32[]{:S(2)}) collective-permute-start(bf16[2,128,768]{2,1,0:T(8,128)(2,1)S(1)} %shard_map.75.rest_0_), channel_id=1, source_target_pairs={{0,1},{1,2},{2,3},{3,0},{4,7},{5,4},{6,5},{7,6},{8,9},{9,10},{10,1... | collective-permute-start | bytes 1179656 | tf_op jit(solution)/shard_map/ppermute | solution.py:32
  36.7 10.9 %collective-permute-start.9 = (bf16[2,128,768]{2,1,0:T(8,128)(2,1)S(1)}, bf16[2,128,768]{2,1,0:T(8,128)(2,1)S(1)}, u32[]{:S(2)}, u32[]{:S(2)}) collective-permute-start(bf16[2,128,768]{2,1,0:T(8,128)(2,1)S(1)} %shard_map.75.rest_0_), channel_id=1, source_target_pairs={{0,8},{4,12},{8,0},{12,4},{1,9},{5,13},{9,1},{13,5},{2,10},{6,14},... | collective-permute-start | bytes 1179656 | tf_op jit(solution)/shard_map/ppermute | solution.py:32
  39.5 0.7 copy-start.1
  47.6 13.7 %collective-permute-start.12 = (bf16[2,128,768]{2,1,0:T(8,128)(2,1)S(1)}, bf16[2,128,768]{2,1,0:T(8,128)(2,1)S(1)}, u32[]{:S(2)}, u32[]{:S(2)}) collective-permute-start(bf16[2,128,768]{2,1,0:T(8,128)(2,1)S(1)} %collective-permute-done.8.rest_0_), channel_id=1, source_target_pairs={{0,1},{1,2},{2,3},{3,0},{4,7},{5,4},{6,5},{7,6},{8,9},{9,10},{10,1... | collective-permute-start | bytes 1179656 | tf_op jit(solution)/shard_map/ppermute | solution.py:32
  48.1 13.1 %collective-permute-start.11 = (bf16[1,128,768]{2,1,0:T(8,128)(2,1)S(1)}, bf16[1,128,768]{2,1,0:T(8,128)(2,1)S(1)}, u32[]{:S(2)}, u32[]{:S(2)}) collective-permute-start(bf16[1,128,768]{2,1,0:T(8,128)(2,1)S(1)} %get-tuple-element.58), channel_id=1, source_target_pairs={{0,8},{4,12},{8,0},{12,4},{1,9},{5,13},{9,1},{13,5},{2,10},{6,14},... | collective-permute-start | bytes 589832 | tf_op jit(solution)/shard_map/ppermute | solution.py:32
  48.6 12.7 %collective-permute-start.14 = (bf16[1,128,768]{2,1,0:T(8,128)(2,1)S(1)}, bf16[1,128,768]{2,1,0:T(8,128)(2,1)S(1)}, u32[]{:S(2)}, u32[]{:S(2)}) collective-permute-start(bf16[1,128,768]{2,1,0:T(8,128)(2,1)S(1)} %get-tuple-element.57), channel_id=1, source_target_pairs={{0,8},{4,12},{8,0},{12,4},{1,9},{5,13},{9,1},{13,5},{2,10},{6,14},... | collective-permute-start | bytes 589832 | tf_op jit(solution)/shard_map/ppermute | solution.py:32
  50.1 11.2 %collective-permute-start.13 = (bf16[2,128,768]{2,1,0:T(8,128)(2,1)S(1)}, bf16[2,128,768]{2,1,0:T(8,128)(2,1)S(1)}, u32[]{:S(2)}, u32[]{:S(2)}) collective-permute-start(bf16[2,128,768]{2,1,0:T(8,128)(2,1)S(1)} %collective-permute-done.9.rest_1_), channel_id=1, source_target_pairs={{0,3},{1,0},{2,1},{3,2},{4,5},{5,6},{6,7},{7,4},{8,11},{9,8},{10,9... | collective-permute-start | bytes 1179656 | tf_op jit(solution)/shard_map/ppermute | solution.py:32
  61.2 7.0 %collective-permute-start.15 = (bf16[1,128,768]{2,1,0:T(8,128)(2,1)S(1)}, bf16[1,128,768]{2,1,0:T(8,128)(2,1)S(1)}, u32[]{:S(2)}, u32[]{:S(2)}) collective-permute-start(bf16[1,128,768]{2,1,0:T(8,128)(2,1)S(1)} %collective-permute-done.11.rest_2_), channel_id=1, source_target_pairs={{0,1},{1,2},{2,3},{3,0},{4,7},{5,4},{6,5},{7,6},{8,9},{9,10},{10,1... | collective-permute-start | bytes 589832 | tf_op jit(solution)/shard_map/ppermute | solution.py:32
  61.3 8.9 %collective-permute-start.16 = (bf16[1,128,768]{2,1,0:T(8,128)(2,1)S(1)}, bf16[1,128,768]{2,1,0:T(8,128)(2,1)S(1)}, u32[]{:S(2)}, u32[]{:S(2)}) collective-permute-start(bf16[1,128,768]{2,1,0:T(8,128)(2,1)S(1)} %collective-permute-done.14.rest_3_), channel_id=1, source_target_pairs={{0,1},{1,2},{2,3},{3,0},{4,7},{5,4},{6,5},{7,6},{8,9},{9,10},{10,1... | collective-permute-start | bytes 589832 | tf_op jit(solution)/shard_map/ppermute | solution.py:32
  74.6 2.0 %collective-permute-start.17 = (f32[4,128,256]{2,1,0:T(8,128)S(1)}, f32[4,128,256]{2,1,0:T(8,128)S(1)}, u32[]{:S(2)}, u32[]{:S(2)}) collective-permute-start(f32[4,128,256]{2,1,0:T(8,128)S(1)} %get-tuple-element.52), channel_id=1, source_target_pairs={{0,4},{4,0},{8,12},{12,8},{1,5},{5,1},{9,13},{13,9},{2,6},{6,2},{1... | collective-permute-start | bytes 1572872 | tf_op jit(solution)/shard_map/ppermute | solution.py:32
  76.7 6.8 %collective-permute-start.18 = (bf16[128,256]{1,0:T(8,128)(2,1)S(1)}, bf16[128,256]{1,0:T(8,128)(2,1)S(1)}, u32[]{:S(2)}, u32[]{:S(2)}) collective-permute-start(bf16[128,256]{1,0:T(8,128)(2,1)S(1)} %get-tuple-element.54), channel_id=1, source_target_pairs={{0,1},{1,2},{2,3},{3,0},{4,5},{5,6},{6,7},{7,4},{8,9},{9,10},{10,1... | collective-permute-start | bytes 196616 | tf_op jit(solution)/shard_map/ppermute | solution.py:32
  76.8 6.7 %collective-permute-start.19 = (bf16[128,256]{1,0:T(8,128)(2,1)S(1)}, bf16[128,256]{1,0:T(8,128)(2,1)S(1)}, u32[]{:S(2)}, u32[]{:S(2)}) collective-permute-start(bf16[128,256]{1,0:T(8,128)(2,1)S(1)} %get-tuple-element.55), channel_id=1, source_target_pairs={{0,2},{1,3},{2,0},{3,1},{4,6},{5,7},{6,4},{7,5},{8,10},{9,11},{10,... | collective-permute-start | bytes 196616 | tf_op jit(solution)/shard_map/ppermute | solution.py:32
  77.6 6.5 %collective-permute-start.20 = (bf16[128,256]{1,0:T(8,128)(2,1)S(1)}, bf16[128,256]{1,0:T(8,128)(2,1)S(1)}, u32[]{:S(2)}, u32[]{:S(2)}) collective-permute-start(bf16[128,256]{1,0:T(8,128)(2,1)S(1)} %get-tuple-element.56), channel_id=1, source_target_pairs={{0,3},{1,0},{2,1},{3,2},{4,7},{5,4},{6,5},{7,6},{8,11},{9,8},{10,9... | collective-permute-start | bytes 196616 | tf_op jit(solution)/shard_map/ppermute | solution.py:32

commit v10 on v8

--- a/solution.py
+++ b/solution.py
@@ -373,8 +373,9 @@
     b_other = core_other(b_held)
     mine, other = gather_and_contract(plan, chol[None], unit, a_tiles, b_tiles, b_other, sizes)
     own, *pieces = merge(mine, core_other(other))
-    for shift, piece in enumerate(pieces, 1):
-        own = own + shifted(piece, "chol", chols, lambda i: (i + shift) % chols).astype(jnp.float32)
+    for shift in (2, 1, 3):
+        moved = shifted(pieces[shift - 1], "chol", chols, lambda i: (i + shift) % chols)
+        own = own + moved.astype(jnp.float32)
     return own.astype(jnp.bfloat16)
 
 

time: 82.6 us -> 83 us (level)
  the two profiles are of different devices: /device:TPU:6 before, /device:TPU:1 now
where the time goes in v10:
time: 83 us; the launch traced here: 82 us
  starting transfers between devices  29.2 us (35%)
  waiting for transfers between devices  24.1 us (29%)
  Pallas kernels  22.5 us (27%)
  local copies, waits for them, and re-layouts  5.18 us (6%)
    ppermute x19, starting transfers between devices, shifted(): return lax.ppermute(value, axis, [(i, moves_to(i)) for i in range(size)])  29.2 us
    ppermute x19, waiting for transfers between devices, shifted(): return lax.ppermute(value, axis, [(i, moves_to(i)) for i in range(size)])  24.1 us
    pallas_call x4, Pallas kernels, contract(): pl.pallas_call(functools.partial(contract_kernel, index), out_shape=[shar...  16.8 us
    unnamed x8, local copies, waits for them, and re-layouts  3.74 us
    pallas_call x1, Pallas kernels, flip(): pl.pallas_call(flip_kernel, out_shape=jax.ShapeDtypeStruct((A_SLOTS * BLK...  2.33 us
    pallas_call x1, Pallas kernels, make_plan(): pl.pallas_call(plan_kernel, out_shape=jax.ShapeDtypeStruct((KERNELS * PLA...  2.27 us
  transfers between devices with their start and end apart: 19, of which 10 were waited for; matrix products, arithmetic and copies ran while one was open for 4% of the time, Pallas kernels for 22%

profile of v10, /device:TPU:1, one launch (start us, length us, event | category | flops | bytes accessed | tf_op | source)
XLA Modules:
  0.0 82.0 jit_solution(1321228940386964249)
XLA Ops:
  0.0 0.9 %copy-done = bf16[128,1024]{1,0:T(8,128)(2,1)S(1)} copy-done((bf16[128,1024]{1,0:T(8,128)(2,1)S(1)}, bf16[128,1024]{1,0:T(8,128)(2,1)}, u32[]{:S(2)}) %copy-start) | copy-done | bytes 262168
  1.0 7.8 %collective-permute-start.1 = (bf16[128,256]{1,0:T(8,128)(2,1)S(1)}, bf16[128,256]{1,0:T(8,128)(2,1)S(1)}, u32[]{:S(2)}, u32[]{:S(2)}) collective-permute-start(bf16[128,256]{1,0:T(8,128)(2,1)S(1)} %constant_dynamic-slice_fusion), channel_id=1, source_target_pairs={{0,128},{16,144},{32,160},{48,176},{64,192},{80,208},{96,224},{112... | collective-permute-start | bytes 196616 | tf_op jit(solution)/shard_map/ppermute | solution.py:32
  8.8 2.4 %collective-permute-start.2 = (bf16[128,256]{1,0:T(8,128)(2,1)S(1)}, bf16[128,256]{1,0:T(8,128)(2,1)S(1)}, u32[]{:S(2)}, u32[]{:S(2)}) collective-permute-start(bf16[128,256]{1,0:T(8,128)(2,1)S(1)} %constant_dynamic-slice_fusion), channel_id=1, source_target_pairs={{0,64},{16,80},{32,96},{48,112},{64,128},{80,144},{96,160},{112,17... | collective-permute-start | bytes 196616 | tf_op jit(solution)/shard_map/ppermute | solution.py:32
  11.2 0.8 copy.10
  12.0 0.8 copy.11
  12.9 1.5 %collective-permute-start.3 = (s32[48]{0:T(128)S(1)}, s32[48]{0:T(128)S(1)}, u32[]{:S(2)}, u32[]{:S(2)}) collective-permute-start(s32[48]{0:T(128)S(1)} %pad_add_fusion), channel_id=1, source_target_pairs={{0,4},{4,0},{8,12},{12,8},{1,5},{5,1},{9,13},{13,9},{2,6},{6,2},{1... | collective-permute-start | bytes 584 | tf_op jit(solution)/shard_map/ppermute | solution.py:32
  14.4 0.8 collective-permute-done.3
  15.3 0.9 %collective-permute-done = bf16[128,256]{1,0:T(8,128)(2,1)S(1)} collective-permute-done((bf16[128,256]{1,0:T(8,128)(2,1)S(1)}, bf16[128,256]{1,0:T(8,128)(2,1)S(1)}, u32[]{:S(2)}, u32[]{:S(2)}) %collective-permute-start) | collective-permute-done | bytes 65568 | tf_op jit(solution)/shard_map/ppermute | solution.py:32
  16.7 2.6 %collective-permute-start.4 = (bf16[4,128,256]{2,1,0:T(8,128)(2,1)S(1)}, bf16[4,128,256]{2,1,0:T(8,128)(2,1)S(1)}, u32[]{:S(2)}, u32[]{:S(2)}) collective-permute-start(bf16[4,128,256]{2,1,0:T(8,128)(2,1)S(1)} %pad_maximum_fusion.own_ref), channel_id=1, source_target_pairs={{0,16},{4,52},{8,24},{12,60},{16,32},{20,4},{24,40},{28,12},{32,48... | collective-permute-start | bytes 786440 | tf_op jit(solution)/shard_map/ppermute | solution.py:32
  19.3 1.3 %concatenate.8.meta_ref = s32[111]{0:T(128)} concatenate(s32[1]{0:T(128)} %bitcast.4, s32[1]{0:T(128)} %bitcast.5, s32[1]{0:T(128)} %bitcast.6.rest_2_, s32[6]{0:T(128)} %bitcast.13, s32[6]{0:T(128)} %bitcast.14, s32[24]{0:T(128)S(1)} %reshape.12, s32[24]{0:T(128)S(1)} %reshape.13, s32[48]{0:T(128)S(1)} %collective-permute-done.3), dimensions={0} | concatenate | bytes 888 | tf_op jit(solution)/shard_map/concatenate | solution.py:319
  20.5 2.3 %shard_map.73.plan_ref = s32[256]{0:T(256)} custom-call(s32[111]{0:T(128)} %concatenate.8.meta_ref), custom_call_target="tpu_custom_call" | custom-call | tf_op jit(solution)/shard_map/pallas_call | solution.py:294
  22.8 1.6 %collective-permute-done.4.ahead_ref = bf16[4,128,256]{2,1,0:T(8,128)(2,1)S(1)} collective-permute-done((bf16[4,128,256]{2,1,0:T(8,128)(2,1)S(1)}, bf16[4,128,256]{2,1,0:T(8,128)(2,1)S(1)}, u32[]{:S(2)}, u32[]{:S(2)}) %collective-permute-start.4) | collective-permute-done | bytes 262176 | tf_op jit(solution)/shard_map/ppermute | solution.py:32
  24.5 3.4 %collective-permute-start.7 = (bf16[4,128,256]{2,1,0:T(8,128)(2,1)S(1)}, bf16[4,128,256]{2,1,0:T(8,128)(2,1)S(1)}, u32[]{:S(2)}, u32[]{:S(2)}) collective-permute-start(bf16[4,128,256]{2,1,0:T(8,128)(2,1)S(1)} %collective-permute-done.4.ahead_ref), channel_id=1, source_target_pairs={{0,16},{4,52},{8,24},{12,60},{16,32},{20,4},{24,40},{28,12},{32,48... | collective-permute-start | bytes 786440 | tf_op jit(solution)/shard_map/ppermute | solution.py:32
  27.9 3.3 %collective-permute-done.7.far_ref = bf16[4,128,256]{2,1,0:T(8,128)(2,1)S(1)} collective-permute-done((bf16[4,128,256]{2,1,0:T(8,128)(2,1)S(1)}, bf16[4,128,256]{2,1,0:T(8,128)(2,1)S(1)}, u32[]{:S(2)}, u32[]{:S(2)}) %collective-permute-start.7) | collective-permute-done | bytes 262176 | tf_op jit(solution)/shard_map/ppermute | solution.py:32
  31.8 1.1 %shard_map.75.rest_0_ = bf16[2,128,768]{2,1,0:T(8,128)(2,1)S(1)} custom-call(s32[111]{0:T(128)S(1)} %copy-done.2, bf16[4,128,256]{2,1,0:T(8,128)(2,1)S(1)} %pad_maximum_fusion.own_ref, bf16[4,128,256]{2,1,0:T(8,128)(2,1)S(1)} %collective-permute-done.6.back_ref, bf16[4,128,256]{2,1,0:T(8,128)(2,1)S(1)} %collective-permute-done.7.far_ref, ...), custom_call_target="tpu_custom_call" | custom-call | tf_op jit(solution)/shard_map/pallas_call | solution.py:324
  32.9 1.4 %collective-permute-start.10 = (bf16[2,128,768]{2,1,0:T(8,128)(2,1)S(1)}, bf16[2,128,768]{2,1,0:T(8,128)(2,1)S(1)}, u32[]{:S(2)}, u32[]{:S(2)}) collective-permute-start(bf16[2,128,768]{2,1,0:T(8,128)(2,1)S(1)} %shard_map.75.rest_0_), channel_id=1, source_target_pairs={{0,3},{1,0},{2,1},{3,2},{4,5},{5,6},{6,7},{7,4},{8,11},{9,8},{10,9... | collective-permute-start | bytes 1179656 | tf_op jit(solution)/shard_map/ppermute | solution.py:32
  34.3 1.4 %collective-permute-start.9 = (bf16[2,128,768]{2,1,0:T(8,128)(2,1)S(1)}, bf16[2,128,768]{2,1,0:T(8,128)(2,1)S(1)}, u32[]{:S(2)}, u32[]{:S(2)}) collective-permute-start(bf16[2,128,768]{2,1,0:T(8,128)(2,1)S(1)} %shard_map.75.rest_0_), channel_id=1, source_target_pairs={{0,8},{4,12},{8,0},{12,4},{1,9},{5,13},{9,1},{13,5},{2,10},{6,14},... | collective-permute-start | bytes 1179656 | tf_op jit(solution)/shard_map/ppermute | solution.py:32
  35.6 1.5 %collective-permute-start.8 = (bf16[2,128,768]{2,1,0:T(8,128)(2,1)S(1)}, bf16[2,128,768]{2,1,0:T(8,128)(2,1)S(1)}, u32[]{:S(2)}, u32[]{:S(2)}) collective-permute-start(bf16[2,128,768]{2,1,0:T(8,128)(2,1)S(1)} %shard_map.75.rest_0_), channel_id=1, source_target_pairs={{0,1},{1,2},{2,3},{3,0},{4,7},{5,4},{6,5},{7,6},{8,9},{9,10},{10,1... | collective-permute-start | bytes 1179656 | tf_op jit(solution)/shard_map/ppermute | solution.py:32
  37.2 2.3 %shard_map.74.a_ref = bf16[768,2048]{1,0:T(8,128)(2,1)S(1)} custom-call(bf16[16,1,6,128,128]{4,3,2,1,0:T(8,128)(2,1)} %a_hbm.1), custom_call_target="tpu_custom_call" | custom-call | bytes 6291456 | tf_op jit(solution)/shard_map/pallas_call | solution.py:282
  40.2 2.3 %shard_map.76.rest_3_ = f32[16,128,128]{2,1,0:T(8,128)S(1)} custom-call(s32[256]{0:T(256)S(1)} %copy-done.1, bf16[768,2048]{1,0:T(8,128)(2,1)S(1)} %shard_map.74.a_ref, bf16[16,8,3,128,128]{4,3,2,1,0:T(8,128)(2,1)} %b_own.7, bf16[16,8,3,128,128]{4,3,2,1,0:T(8,128)(2,1)} %collective-permute-done.5.b_other, bf16[2,128,768]{2,1,0:T(8,128)(2,1)S(1)} %shard_map.75.rest_0_), custom_call_target="tpu_custom_call" | custom-call | flops 1409286144 | bytes 4718592 | tf_op jit(solution)/shard_map/pallas_call | solution.py:247
  42.5 3.9 %collective-permute-done.8.rest_0_ = bf16[2,128,768]{2,1,0:T(8,128)(2,1)S(1)} collective-permute-done((bf16[2,128,768]{2,1,0:T(8,128)(2,1)S(1)}, bf16[2,128,768]{2,1,0:T(8,128)(2,1)S(1)}, u32[]{:S(2)}, u32[]{:S(2)}) %collective-permute-start.8) | collective-permute-done | bytes 393248 | tf_op jit(solution)/shard_map/ppermute | solution.py:32
  46.4 2.3 %collective-permute-start.11 = (bf16[2,128,768]{2,1,0:T(8,128)(2,1)S(1)}, bf16[2,128,768]{2,1,0:T(8,128)(2,1)S(1)}, u32[]{:S(2)}, u32[]{:S(2)}) collective-permute-start(bf16[2,128,768]{2,1,0:T(8,128)(2,1)S(1)} %collective-permute-done.8.rest_0_), channel_id=1, source_target_pairs={{0,1},{1,2},{2,3},{3,0},{4,7},{5,4},{6,5},{7,6},{8,9},{9,10},{10,1... | collective-permute-start | bytes 1179656 | tf_op jit(solution)/shard_map/ppermute | solution.py:32
  48.7 5.2 %shard_map.77.rest_3_ = f32[16,128,128]{2,1,0:T(8,128)S(1)} custom-call(s32[256]{0:T(256)S(1)} %copy-done.1, bf16[768,2048]{1,0:T(8,128)(2,1)S(1)} %shard_map.74.a_ref, bf16[16,8,3,128,128]{4,3,2,1,0:T(8,128)(2,1)} %b_own.7, bf16[16,8,3,128,128]{4,3,2,1,0:T(8,128)(2,1)} %collective-permute-done.5.b_other, ...), custom_call_target="tpu_custom_call" | custom-call | flops 4227858432 | bytes 7864320 | tf_op jit(solution)/shard_map/pallas_call | solution.py:247
  53.9 6.5 %collective-permute-done.12.rest_1_ = bf16[2,128,768]{2,1,0:T(8,128)(2,1)S(1)} collective-permute-done((bf16[2,128,768]{2,1,0:T(8,128)(2,1)S(1)}, bf16[2,128,768]{2,1,0:T(8,128)(2,1)S(1)}, u32[]{:S(2)}, u32[]{:S(2)}) %collective-permute-start.12) | collective-permute-done | bytes 393248 | tf_op jit(solution)/shard_map/ppermute | solution.py:32
  60.5 5.2 %shard_map.78.rest_1_ = f32[16,128,128]{2,1,0:T(8,128)S(1)} custom-call(s32[256]{0:T(256)S(1)} %copy-done.1, bf16[768,2048]{1,0:T(8,128)(2,1)S(1)} %shard_map.74.a_ref, bf16[16,8,3,128,128]{4,3,2,1,0:T(8,128)(2,1)} %b_own.7, bf16[16,8,3,128,128]{4,3,2,1,0:T(8,128)(2,1)} %collective-permute-done.5.b_other, ...), custom_call_target="tpu_custom_call" | custom-call | flops 4227858432 | bytes 7864320 | tf_op jit(solution)/shard_map/pallas_call | solution.py:247
  65.7 1.7 %collective-permute-done.14.rest_0_ = bf16[2,128,768]{2,1,0:T(8,128)(2,1)S(1)} collective-permute-done((bf16[2,128,768]{2,1,0:T(8,128)(2,1)S(1)}, bf16[2,128,768]{2,1,0:T(8,128)(2,1)S(1)}, u32[]{:S(2)}, u32[]{:S(2)}) %collective-permute-start.14) | collective-permute-done | bytes 393248 | tf_op jit(solution)/shard_map/ppermute | solution.py:32
  67.4 4.1 %shard_map.79 = (f32[4,128,256]{2,1,0:T(8,128)S(1)}, f32[4,128,256]{2,1,0:T(8,128)S(1)}) custom-call(s32[256]{0:T(256)S(1)} %copy-done.1, bf16[768,2048]{1,0:T(8,128)(2,1)S(1)} %shard_map.74.a_ref, bf16[16,8,3,128,128]{4,3,2,1,0:T(8,128)(2,1)} %b_own.7, bf16[16,8,3,128,128]{4,3,2,1,0:T(8,128)(2,1)} %collective-permute-done.5.b_other, ...), custom_call_target="tpu_custom_call" | custom-call | flops 1409286144 | bytes 4718592 | tf_op jit(solution)/shard_map/pallas_call | solution.py:247
  71.5 1.7 %collective-permute-start.15 = (f32[4,128,256]{2,1,0:T(8,128)S(1)}, f32[4,128,256]{2,1,0:T(8,128)S(1)}, u32[]{:S(2)}, u32[]{:S(2)}) collective-permute-start(f32[4,128,256]{2,1,0:T(8,128)S(1)} %get-tuple-element.46), channel_id=1, source_target_pairs={{0,4},{4,0},{8,12},{12,8},{1,5},{5,1},{9,13},{13,9},{2,6},{6,2},{1... | collective-permute-start | bytes 1572872 | tf_op jit(solution)/shard_map/ppermute | solution.py:32
  73.1 1.5 %collective-permute-done.15.arrived_ref = f32[4,128,256]{2,1,0:T(8,128)S(1)} collective-permute-done((f32[4,128,256]{2,1,0:T(8,128)S(1)}, f32[4,128,256]{2,1,0:T(8,128)S(1)}, u32[]{:S(2)}, u32[]{:S(2)}) %collective-permute-start.15) | collective-permute-done | bytes 524320 | tf_op jit(solution)/shard_map/ppermute | solution.py:32
  74.9 2.7 %collective-permute-start.18 = (bf16[128,256]{1,0:T(8,128)(2,1)S(1)}, bf16[128,256]{1,0:T(8,128)(2,1)S(1)}, u32[]{:S(2)}, u32[]{:S(2)}) collective-permute-start(bf16[128,256]{1,0:T(8,128)(2,1)S(1)} %get-tuple-element.50), channel_id=1, source_target_pairs={{0,3},{1,0},{2,1},{3,2},{4,7},{5,4},{6,5},{7,6},{8,11},{9,8},{10,9... | collective-permute-start | bytes 196616 | tf_op jit(solution)/shard_map/ppermute | solution.py:32
  77.6 2.0 %collective-permute-done.16 = bf16[128,256]{1,0:T(8,128)(2,1)S(1)} collective-permute-done((bf16[128,256]{1,0:T(8,128)(2,1)S(1)}, bf16[128,256]{1,0:T(8,128)(2,1)S(1)}, u32[]{:S(2)}, u32[]{:S(2)}) %collective-permute-start.16) | collective-permute-done | bytes 65568 | tf_op jit(solution)/shard_map/ppermute | solution.py:32
  79.5 1.8 %collective-permute-done.17 = bf16[128,256]{1,0:T(8,128)(2,1)S(1)} collective-permute-done((bf16[128,256]{1,0:T(8,128)(2,1)S(1)}, bf16[128,256]{1,0:T(8,128)(2,1)S(1)}, u32[]{:S(2)}, u32[]{:S(2)}) %collective-permute-start.17) | collective-permute-done | bytes 65568 | tf_op jit(solution)/shard_map/ppermute | solution.py:32
  (30 shorter events, 3.0 us)
Async XLA Ops:
  0.0 1.0 %copy-start = (bf16[128,1024]{1,0:T(8,128)(2,1)S(1)}, bf16[128,1024]{1,0:T(8,128)(2,1)}, u32[]{:S(2)}) copy-start(bf16[128,1024]{1,0:T(8,128)(2,1)} %param.7) | copy-start | bytes 786436
  1.0 14.3 %collective-permute-start.1 = (bf16[128,256]{1,0:T(8,128)(2,1)S(1)}, bf16[128,256]{1,0:T(8,128)(2,1)S(1)}, u32[]{:S(2)}, u32[]{:S(2)}) collective-permute-start(bf16[128,256]{1,0:T(8,128)(2,1)S(1)} %constant_dynamic-slice_fusion), channel_id=1, source_target_pairs={{0,128},{16,144},{32,160},{48,176},{64,192},{80,208},{96,224},{112... | collective-permute-start | bytes 196616 | tf_op jit(solution)/shard_map/ppermute | solution.py:32
  8.8 7.4 %collective-permute-start = (bf16[128,256]{1,0:T(8,128)(2,1)S(1)}, bf16[128,256]{1,0:T(8,128)(2,1)S(1)}, u32[]{:S(2)}, u32[]{:S(2)}) collective-permute-start(bf16[128,256]{1,0:T(8,128)(2,1)S(1)} %constant_dynamic-slice_fusion), channel_id=1, source_target_pairs={{0,192},{16,208},{32,224},{48,240},{64,0},{80,16},{96,32},{112,48}... | collective-permute-start | bytes 196616 | tf_op jit(solution)/shard_map/ppermute | solution.py:32
  8.8 7.4 %collective-permute-start.2 = (bf16[128,256]{1,0:T(8,128)(2,1)S(1)}, bf16[128,256]{1,0:T(8,128)(2,1)S(1)}, u32[]{:S(2)}, u32[]{:S(2)}) collective-permute-start(bf16[128,256]{1,0:T(8,128)(2,1)S(1)} %constant_dynamic-slice_fusion), channel_id=1, source_target_pairs={{0,64},{16,80},{32,96},{48,112},{64,128},{80,144},{96,160},{112,17... | collective-permute-start | bytes 196616 | tf_op jit(solution)/shard_map/ppermute | solution.py:32
  12.9 2.4 %collective-permute-start.3 = (s32[48]{0:T(128)S(1)}, s32[48]{0:T(128)S(1)}, u32[]{:S(2)}, u32[]{:S(2)}) collective-permute-start(s32[48]{0:T(128)S(1)} %pad_add_fusion), channel_id=1, source_target_pairs={{0,4},{4,0},{8,12},{12,8},{1,5},{5,1},{9,13},{13,9},{2,6},{6,2},{1... | collective-permute-start | bytes 584 | tf_op jit(solution)/shard_map/ppermute | solution.py:32
  16.2 23.3 %collective-permute-start.5 = (bf16[16,8,3,128,128]{4,3,2,1,0:T(8,128)(2,1)}, bf16[16,8,3,128,128]{4,3,2,1,0:T(8,128)(2,1)}, u32[]{:S(2)}, u32[]{:S(2)}) collective-permute-start(bf16[16,8,3,128,128]{4,3,2,1,0:T(8,128)(2,1)} %b_own.7), channel_id=1, source_target_pairs={{0,4},{4,0},{8,12},{12,8},{1,5},{5,1},{9,13},{13,9},{2,6},{6,2},{1... | collective-permute-start | bytes 37748744 | tf_op jit(solution)/shard_map/ppermute | solution.py:32
  16.7 7.7 %collective-permute-start.4 = (bf16[4,128,256]{2,1,0:T(8,128)(2,1)S(1)}, bf16[4,128,256]{2,1,0:T(8,128)(2,1)S(1)}, u32[]{:S(2)}, u32[]{:S(2)}) collective-permute-start(bf16[4,128,256]{2,1,0:T(8,128)(2,1)S(1)} %pad_maximum_fusion.own_ref), channel_id=1, source_target_pairs={{0,16},{4,52},{8,24},{12,60},{16,32},{20,4},{24,40},{28,12},{32,48... | collective-permute-start | bytes 786440 | tf_op jit(solution)/shard_map/ppermute | solution.py:32
  19.3 8.6 %collective-permute-start.6 = (bf16[4,128,256]{2,1,0:T(8,128)(2,1)S(1)}, bf16[4,128,256]{2,1,0:T(8,128)(2,1)S(1)}, u32[]{:S(2)}, u32[]{:S(2)}) collective-permute-start(bf16[4,128,256]{2,1,0:T(8,128)(2,1)S(1)} %pad_maximum_fusion.own_ref), channel_id=1, source_target_pairs={{0,48},{4,20},{8,56},{12,28},{16,0},{20,36},{24,8},{28,44},{32,16}... | collective-permute-start | bytes 786440 | tf_op jit(solution)/shard_map/ppermute | solution.py:32
  24.5 6.7 %collective-permute-start.7 = (bf16[4,128,256]{2,1,0:T(8,128)(2,1)S(1)}, bf16[4,128,256]{2,1,0:T(8,128)(2,1)S(1)}, u32[]{:S(2)}, u32[]{:S(2)}) collective-permute-start(bf16[4,128,256]{2,1,0:T(8,128)(2,1)S(1)} %collective-permute-done.4.ahead_ref), channel_id=1, source_target_pairs={{0,16},{4,52},{8,24},{12,60},{16,32},{20,4},{24,40},{28,12},{32,48... | collective-permute-start | bytes 786440 | tf_op jit(solution)/shard_map/ppermute | solution.py:32
  31.2 0.6 copy-start.2
  32.9 9.6 %collective-permute-start.10 = (bf16[2,128,768]{2,1,0:T(8,128)(2,1)S(1)}, bf16[2,128,768]{2,1,0:T(8,128)(2,1)S(1)}, u32[]{:S(2)}, u32[]{:S(2)}) collective-permute-start(bf16[2,128,768]{2,1,0:T(8,128)(2,1)S(1)} %shard_map.75.rest_0_), channel_id=1, source_target_pairs={{0,3},{1,0},{2,1},{3,2},{4,5},{5,6},{6,7},{7,4},{8,11},{9,8},{10,9... | collective-permute-start | bytes 1179656 | tf_op jit(solution)/shard_map/ppermute | solution.py:32
  34.3 8.2 %collective-permute-start.9 = (bf16[2,128,768]{2,1,0:T(8,128)(2,1)S(1)}, bf16[2,128,768]{2,1,0:T(8,128)(2,1)S(1)}, u32[]{:S(2)}, u32[]{:S(2)}) collective-permute-start(bf16[2,128,768]{2,1,0:T(8,128)(2,1)S(1)} %shard_map.75.rest_0_), channel_id=1, source_target_pairs={{0,8},{4,12},{8,0},{12,4},{1,9},{5,13},{9,1},{13,5},{2,10},{6,14},... | collective-permute-start | bytes 1179656 | tf_op jit(solution)/shard_map/ppermute | solution.py:32
  35.6 10.8 %collective-permute-start.8 = (bf16[2,128,768]{2,1,0:T(8,128)(2,1)S(1)}, bf16[2,128,768]{2,1,0:T(8,128)(2,1)S(1)}, u32[]{:S(2)}, u32[]{:S(2)}) collective-permute-start(bf16[2,128,768]{2,1,0:T(8,128)(2,1)S(1)} %shard_map.75.rest_0_), channel_id=1, source_target_pairs={{0,1},{1,2},{2,3},{3,0},{4,7},{5,4},{6,5},{7,6},{8,9},{9,10},{10,1... | collective-permute-start | bytes 1179656 | tf_op jit(solution)/shard_map/ppermute | solution.py:32
  39.5 0.7 copy-start.1
  46.4 14.1 %collective-permute-start.13 = (bf16[2,128,768]{2,1,0:T(8,128)(2,1)S(1)}, bf16[2,128,768]{2,1,0:T(8,128)(2,1)S(1)}, u32[]{:S(2)}, u32[]{:S(2)}) collective-permute-start(bf16[2,128,768]{2,1,0:T(8,128)(2,1)S(1)} %collective-permute-done.8.rest_0_), channel_id=1, source_target_pairs={{0,8},{4,12},{8,0},{12,4},{1,9},{5,13},{9,1},{13,5},{2,10},{6,14},... | collective-permute-start | bytes 1179656 | tf_op jit(solution)/shard_map/ppermute | solution.py:32
  46.4 14.1 %collective-permute-start.11 = (bf16[2,128,768]{2,1,0:T(8,128)(2,1)S(1)}, bf16[2,128,768]{2,1,0:T(8,128)(2,1)S(1)}, u32[]{:S(2)}, u32[]{:S(2)}) collective-permute-start(bf16[2,128,768]{2,1,0:T(8,128)(2,1)S(1)} %collective-permute-done.8.rest_0_), channel_id=1, source_target_pairs={{0,1},{1,2},{2,3},{3,0},{4,7},{5,4},{6,5},{7,6},{8,9},{9,10},{10,1... | collective-permute-start | bytes 1179656 | tf_op jit(solution)/shard_map/ppermute | solution.py:32
  48.7 11.8 %collective-permute-start.12 = (bf16[2,128,768]{2,1,0:T(8,128)(2,1)S(1)}, bf16[2,128,768]{2,1,0:T(8,128)(2,1)S(1)}, u32[]{:S(2)}, u32[]{:S(2)}) collective-permute-start(bf16[2,128,768]{2,1,0:T(8,128)(2,1)S(1)} %collective-permute-done.9.rest_1_), channel_id=1, source_target_pairs={{0,3},{1,0},{2,1},{3,2},{4,5},{5,6},{6,7},{7,4},{8,11},{9,8},{10,9... | collective-permute-start | bytes 1179656 | tf_op jit(solution)/shard_map/ppermute | solution.py:32
  60.5 6.9 %collective-permute-start.14 = (bf16[2,128,768]{2,1,0:T(8,128)(2,1)S(1)}, bf16[2,128,768]{2,1,0:T(8,128)(2,1)S(1)}, u32[]{:S(2)}, u32[]{:S(2)}) collective-permute-start(bf16[2,128,768]{2,1,0:T(8,128)(2,1)S(1)} %collective-permute-done.13.rest_2_), channel_id=1, source_target_pairs={{0,1},{1,2},{2,3},{3,0},{4,7},{5,4},{6,5},{7,6},{8,9},{9,10},{10,1... | collective-permute-start | bytes 1179656 | tf_op jit(solution)/shard_map/ppermute | solution.py:32
  71.5 3.2 %collective-permute-start.15 = (f32[4,128,256]{2,1,0:T(8,128)S(1)}, f32[4,128,256]{2,1,0:T(8,128)S(1)}, u32[]{:S(2)}, u32[]{:S(2)}) collective-permute-start(f32[4,128,256]{2,1,0:T(8,128)S(1)} %get-tuple-element.46), channel_id=1, source_target_pairs={{0,4},{4,0},{8,12},{12,8},{1,5},{5,1},{9,13},{13,9},{2,6},{6,2},{1... | collective-permute-start | bytes 1572872 | tf_op jit(solution)/shard_map/ppermute | solution.py:32
  74.7 4.8 %collective-permute-start.16 = (bf16[128,256]{1,0:T(8,128)(2,1)S(1)}, bf16[128,256]{1,0:T(8,128)(2,1)S(1)}, u32[]{:S(2)}, u32[]{:S(2)}) collective-permute-start(bf16[128,256]{1,0:T(8,128)(2,1)S(1)} %get-tuple-element.48), channel_id=1, source_target_pairs={{0,2},{1,3},{2,0},{3,1},{4,6},{5,7},{6,4},{7,5},{8,10},{9,11},{10,... | collective-permute-start | bytes 196616 | tf_op jit(solution)/shard_map/ppermute | solution.py:32
  74.8 6.5 %collective-permute-start.17 = (bf16[128,256]{1,0:T(8,128)(2,1)S(1)}, bf16[128,256]{1,0:T(8,128)(2,1)S(1)}, u32[]{:S(2)}, u32[]{:S(2)}) collective-permute-start(bf16[128,256]{1,0:T(8,128)(2,1)S(1)} %get-tuple-element.49), channel_id=1, source_target_pairs={{0,1},{1,2},{2,3},{3,0},{4,5},{5,6},{6,7},{7,4},{8,9},{9,10},{10,1... | collective-permute-start | bytes 196616 | tf_op jit(solution)/shard_map/ppermute | solution.py:32
  74.9 6.4 %collective-permute-start.18 = (bf16[128,256]{1,0:T(8,128)(2,1)S(1)}, bf16[128,256]{1,0:T(8,128)(2,1)S(1)}, u32[]{:S(2)}, u32[]{:S(2)}) collective-permute-start(bf16[128,256]{1,0:T(8,128)(2,1)S(1)} %get-tuple-element.50), channel_id=1, source_target_pairs={{0,3},{1,0},{2,1},{3,2},{4,7},{5,4},{6,5},{7,6},{8,11},{9,8},{10,9... | collective-permute-start | bytes 196616 | tf_op jit(solution)/shard_map/ppermute | solution.py:32

commit v11 on v8

--- a/solution.py
+++ b/solution.py
@@ -256,7 +256,7 @@
             pltpu.SemaphoreType.DMA((2, widest, 2)),
         ],
         compiler_params=pltpu.CompilerParams(vmem_limit_bytes=47 * 1024 * 1024),
-        cost_estimate=pl.CostEstimate(flops=flops, bytes_accessed=moved, transcendentals=0),
+        cost_estimate=pl.CostEstimate(flops=flops // (1000 if index == 2 else 1), bytes_accessed=moved // (1000 if index == 2 else 1), transcendentals=0),
     )(plan, a_flipped, b_own, b_other, *units, *sums, *chols)
 
 
@@ -350,8 +350,9 @@
     running, ahead, across, back = lax.optimization_barrier((running, ahead, across, back))
     middle, far_ahead, far_back = by_core(ahead, 1), z_other(ahead), by_core(across, -1)
     running = contract(1, *tiles, [ahead, across, back], running)
-    running, middle, far_back, far_ahead = lax.optimization_barrier((running, middle, far_back, far_ahead))
+    running, far_ahead = lax.optimization_barrier((running, far_ahead))
     far_middle = by_core(far_ahead, 1)
+    running, middle, far_back = lax.optimization_barrier((running, middle, far_back))
     running = contract(2, *tiles, [middle, far_back, far_ahead], running)
     running, far_middle = lax.optimization_barrier((running, far_middle))
     return contract(LAST, *tiles, [far_middle], running, chol)

time: 82.6 us -> 82.6 us (level)
  Pallas kernels: 19.7 us -> 25.2 us
  waiting for transfers between devices: 29.2 us -> 23.9 us
    pallas_call x4, Pallas kernels: 13.9 us -> 19.5 us  [contract(): pl.pallas_call(functools.partial(contract_kernel, index), out_shape=[shar...]
    ppermute x19, waiting for transfers between devices: 29.2 us -> 23.9 us  [shifted(): return lax.ppermute(value, axis, [(i, moves_to(i)) for i in range(size)])]
  transfers between devices with their start and end apart: 19 -> 19, of which waited for: 14 -> 14; matrix products, arithmetic and copies ran while one was open for 4% -> 4% of each run, Pallas kernels for 21% -> 26%
where the time goes in v11:
time: 82.6 us; the launch traced here: 81.6 us
  starting transfers between devices  26.4 us (32%)
  Pallas kernels  25.2 us (31%)
  waiting for transfers between devices  23.9 us (29%)
  local copies, waits for them, and re-layouts  5.18 us (6%)
    ppermute x19, starting transfers between devices, shifted(): return lax.ppermute(value, axis, [(i, moves_to(i)) for i in range(size)])  26.4 us
    ppermute x19, waiting for transfers between devices, shifted(): return lax.ppermute(value, axis, [(i, moves_to(i)) for i in range(size)])  23.9 us
    pallas_call x4, Pallas kernels, contract(): pl.pallas_call(functools.partial(contract_kernel, index), out_shape=[shar...  19.5 us
    unnamed x8, local copies, waits for them, and re-layouts  3.74 us
    pallas_call x1, Pallas kernels, flip(): pl.pallas_call(flip_kernel, out_shape=jax.ShapeDtypeStruct((A_SLOTS * BLK...  2.33 us
    pallas_call x1, Pallas kernels, make_plan(): pl.pallas_call(plan_kernel, out_shape=jax.ShapeDtypeStruct((KERNELS * PLA...  2.27 us
  transfers between devices with their start and end apart: 19, of which 14 were waited for; matrix products, arithmetic and copies ran while one was open for 4% of the time, Pallas kernels for 26%

profile of v11, /device:TPU:6, one launch (start us, length us, event | category | flops | bytes accessed | tf_op | source)
XLA Modules:
  0.0 81.6 jit_solution(1743237108945389042)
XLA Ops:
  0.0 0.9 %copy-done = bf16[128,1024]{1,0:T(8,128)(2,1)S(1)} copy-done((bf16[128,1024]{1,0:T(8,128)(2,1)S(1)}, bf16[128,1024]{1,0:T(8,128)(2,1)}, u32[]{:S(2)}) %copy-start) | copy-done | bytes 262168
  1.0 7.3 %collective-permute-start.1 = (bf16[128,256]{1,0:T(8,128)(2,1)S(1)}, bf16[128,256]{1,0:T(8,128)(2,1)S(1)}, u32[]{:S(2)}, u32[]{:S(2)}) collective-permute-start(bf16[128,256]{1,0:T(8,128)(2,1)S(1)} %constant_dynamic-slice_fusion), channel_id=1, source_target_pairs={{0,128},{16,144},{32,160},{48,176},{64,192},{80,208},{96,224},{112... | collective-permute-start | bytes 196616 | tf_op jit(solution)/shard_map/ppermute | solution.py:32
  8.2 2.9 %collective-permute-start.2 = (bf16[128,256]{1,0:T(8,128)(2,1)S(1)}, bf16[128,256]{1,0:T(8,128)(2,1)S(1)}, u32[]{:S(2)}, u32[]{:S(2)}) collective-permute-start(bf16[128,256]{1,0:T(8,128)(2,1)S(1)} %constant_dynamic-slice_fusion), channel_id=1, source_target_pairs={{0,64},{16,80},{32,96},{48,112},{64,128},{80,144},{96,160},{112,17... | collective-permute-start | bytes 196616 | tf_op jit(solution)/shard_map/ppermute | solution.py:32
  11.2 0.8 copy.10
  12.0 0.8 copy.11
  13.0 1.1 %collective-permute-done.3 = s32[48]{0:T(128)S(1)} collective-permute-done((s32[48]{0:T(128)S(1)}, s32[48]{0:T(128)S(1)}, u32[]{:S(2)}, u32[]{:S(2)}) %collective-permute-start.3) | collective-permute-done | bytes 224 | tf_op jit(solution)/shard_map/ppermute | solution.py:32
  14.1 1.1 %collective-permute-done = bf16[128,256]{1,0:T(8,128)(2,1)S(1)} collective-permute-done((bf16[128,256]{1,0:T(8,128)(2,1)S(1)}, bf16[128,256]{1,0:T(8,128)(2,1)S(1)}, u32[]{:S(2)}, u32[]{:S(2)}) %collective-permute-start) | collective-permute-done | bytes 65568 | tf_op jit(solution)/shard_map/ppermute | solution.py:32
  15.8 1.5 %collective-permute-start.6 = (bf16[4,128,256]{2,1,0:T(8,128)(2,1)S(1)}, bf16[4,128,256]{2,1,0:T(8,128)(2,1)S(1)}, u32[]{:S(2)}, u32[]{:S(2)}) collective-permute-start(bf16[4,128,256]{2,1,0:T(8,128)(2,1)S(1)} %pad_maximum_fusion.own_ref), channel_id=1, source_target_pairs={{0,48},{4,20},{8,56},{12,28},{16,0},{20,36},{24,8},{28,44},{32,16}... | collective-permute-start | bytes 786440 | tf_op jit(solution)/shard_map/ppermute | solution.py:32
  17.3 1.3 %concatenate.8.meta_ref = s32[111]{0:T(128)} concatenate(s32[1]{0:T(128)} %bitcast.4, s32[1]{0:T(128)} %bitcast.5, s32[1]{0:T(128)} %bitcast.6.rest_2_, s32[6]{0:T(128)} %bitcast.13, s32[6]{0:T(128)} %bitcast.14, s32[24]{0:T(128)S(1)} %reshape.12, s32[24]{0:T(128)S(1)} %reshape.13, s32[48]{0:T(128)S(1)} %collective-permute-done.3), dimensions={0} | concatenate | bytes 888 | tf_op jit(solution)/shard_map/concatenate | solution.py:319
  18.6 2.3 %shard_map.73.plan_ref = s32[256]{0:T(256)} custom-call(s32[111]{0:T(128)} %concatenate.8.meta_ref), custom_call_target="tpu_custom_call" | custom-call | tf_op jit(solution)/shard_map/pallas_call | solution.py:294
  20.9 3.5 %collective-permute-done.4.ahead_ref = bf16[4,128,256]{2,1,0:T(8,128)(2,1)S(1)} collective-permute-done((bf16[4,128,256]{2,1,0:T(8,128)(2,1)S(1)}, bf16[4,128,256]{2,1,0:T(8,128)(2,1)S(1)}, u32[]{:S(2)}, u32[]{:S(2)}) %collective-permute-start.4) | collective-permute-done | bytes 262176 | tf_op jit(solution)/shard_map/ppermute | solution.py:32
  24.4 0.8 collective-permute-done.6.back_ref
  25.2 5.6 %collective-permute-done.7.far_ref = bf16[4,128,256]{2,1,0:T(8,128)(2,1)S(1)} collective-permute-done((bf16[4,128,256]{2,1,0:T(8,128)(2,1)S(1)}, bf16[4,128,256]{2,1,0:T(8,128)(2,1)S(1)}, u32[]{:S(2)}, u32[]{:S(2)}) %collective-permute-start.7) | collective-permute-done | bytes 262176 | tf_op jit(solution)/shard_map/ppermute | solution.py:32
  31.4 1.1 %shard_map.75.rest_0_ = bf16[2,128,768]{2,1,0:T(8,128)(2,1)S(1)} custom-call(s32[111]{0:T(128)S(1)} %copy-done.2, bf16[4,128,256]{2,1,0:T(8,128)(2,1)S(1)} %pad_maximum_fusion.own_ref, bf16[4,128,256]{2,1,0:T(8,128)(2,1)S(1)} %collective-permute-done.6.back_ref, bf16[4,128,256]{2,1,0:T(8,128)(2,1)S(1)} %collective-permute-done.7.far_ref, ...), custom_call_target="tpu_custom_call" | custom-call | tf_op jit(solution)/shard_map/pallas_call | solution.py:324
  32.5 3.1 %collective-permute-start.10 = (bf16[2,128,768]{2,1,0:T(8,128)(2,1)S(1)}, bf16[2,128,768]{2,1,0:T(8,128)(2,1)S(1)}, u32[]{:S(2)}, u32[]{:S(2)}) collective-permute-start(bf16[2,128,768]{2,1,0:T(8,128)(2,1)S(1)} %shard_map.75.rest_0_), channel_id=1, source_target_pairs={{0,3},{1,0},{2,1},{3,2},{4,5},{5,6},{6,7},{7,4},{8,11},{9,8},{10,9... | collective-permute-start | bytes 1179656 | tf_op jit(solution)/shard_map/ppermute | solution.py:32
  35.6 1.6 %collective-permute-start.9 = (bf16[2,128,768]{2,1,0:T(8,128)(2,1)S(1)}, bf16[2,128,768]{2,1,0:T(8,128)(2,1)S(1)}, u32[]{:S(2)}, u32[]{:S(2)}) collective-permute-start(bf16[2,128,768]{2,1,0:T(8,128)(2,1)S(1)} %shard_map.75.rest_0_), channel_id=1, source_target_pairs={{0,8},{4,12},{8,0},{12,4},{1,9},{5,13},{9,1},{13,5},{2,10},{6,14},... | collective-permute-start | bytes 1179656 | tf_op jit(solution)/shard_map/ppermute | solution.py:32
  37.2 2.3 %shard_map.74.a_ref = bf16[768,2048]{1,0:T(8,128)(2,1)S(1)} custom-call(bf16[16,1,6,128,128]{4,3,2,1,0:T(8,128)(2,1)} %a_hbm.1), custom_call_target="tpu_custom_call" | custom-call | bytes 6291456 | tf_op jit(solution)/shard_map/pallas_call | solution.py:282
  40.2 3.7 %shard_map.76.rest_3_ = f32[16,128,128]{2,1,0:T(8,128)S(1)} custom-call(s32[256]{0:T(256)S(1)} %copy-done.1, bf16[768,2048]{1,0:T(8,128)(2,1)S(1)} %shard_map.74.a_ref, bf16[16,8,3,128,128]{4,3,2,1,0:T(8,128)(2,1)} %b_own.7, bf16[16,8,3,128,128]{4,3,2,1,0:T(8,128)(2,1)} %collective-permute-done.5.b_other, bf16[2,128,768]{2,1,0:T(8,128)(2,1)S(1)} %shard_map.75.rest_0_), custom_call_target="tpu_custom_call" | custom-call | flops 1409286144 | bytes 4718592 | tf_op jit(solution)/shard_map/pallas_call | solution.py:247
  44.9 1.2 %collective-permute-done.8.rest_0_ = bf16[2,128,768]{2,1,0:T(8,128)(2,1)S(1)} collective-permute-done((bf16[2,128,768]{2,1,0:T(8,128)(2,1)S(1)}, bf16[2,128,768]{2,1,0:T(8,128)(2,1)S(1)}, u32[]{:S(2)}, u32[]{:S(2)}) %collective-permute-start.8) | collective-permute-done | bytes 393248 | tf_op jit(solution)/shard_map/ppermute | solution.py:32
  46.5 1.6 %collective-permute-start.11 = (bf16[2,128,768]{2,1,0:T(8,128)(2,1)S(1)}, bf16[2,128,768]{2,1,0:T(8,128)(2,1)S(1)}, u32[]{:S(2)}, u32[]{:S(2)}) collective-permute-start(bf16[2,128,768]{2,1,0:T(8,128)(2,1)S(1)} %collective-permute-done.8.rest_0_), channel_id=1, source_target_pairs={{0,8},{4,12},{8,0},{12,4},{1,9},{5,13},{9,1},{13,5},{2,10},{6,14},... | collective-permute-start | bytes 1179656 | tf_op jit(solution)/shard_map/ppermute | solution.py:32
  48.2 1.8 %collective-permute-start.13 = (bf16[2,128,768]{2,1,0:T(8,128)(2,1)S(1)}, bf16[2,128,768]{2,1,0:T(8,128)(2,1)S(1)}, u32[]{:S(2)}, u32[]{:S(2)}) collective-permute-start(bf16[2,128,768]{2,1,0:T(8,128)(2,1)S(1)} %collective-permute-done.9.rest_1_), channel_id=1, source_target_pairs={{0,3},{1,0},{2,1},{3,2},{4,5},{5,6},{6,7},{7,4},{8,11},{9,8},{10,9... | collective-permute-start | bytes 1179656 | tf_op jit(solution)/shard_map/ppermute | solution.py:32
  50.0 6.5 %shard_map.77.rest_3_ = f32[16,128,128]{2,1,0:T(8,128)S(1)} custom-call(s32[256]{0:T(256)S(1)} %copy-done.1, bf16[768,2048]{1,0:T(8,128)(2,1)S(1)} %shard_map.74.a_ref, bf16[16,8,3,128,128]{4,3,2,1,0:T(8,128)(2,1)} %b_own.7, bf16[16,8,3,128,128]{4,3,2,1,0:T(8,128)(2,1)} %collective-permute-done.5.b_other, ...), custom_call_target="tpu_custom_call" | custom-call | flops 4227858432 | bytes 7864320 | tf_op jit(solution)/shard_map/pallas_call | solution.py:247
  56.5 1.2 %collective-permute-done.11.rest_2_ = bf16[2,128,768]{2,1,0:T(8,128)(2,1)S(1)} collective-permute-done((bf16[2,128,768]{2,1,0:T(8,128)(2,1)S(1)}, bf16[2,128,768]{2,1,0:T(8,128)(2,1)S(1)}, u32[]{:S(2)}, u32[]{:S(2)}) %collective-permute-start.11) | collective-permute-done | bytes 393248 | tf_op jit(solution)/shard_map/ppermute | solution.py:32
  58.0 5.2 %shard_map.78.rest_1_ = f32[16,128,128]{2,1,0:T(8,128)S(1)} custom-call(s32[256]{0:T(256)S(1)} %copy-done.1, bf16[768,2048]{1,0:T(8,128)(2,1)S(1)} %shard_map.74.a_ref, bf16[16,8,3,128,128]{4,3,2,1,0:T(8,128)(2,1)} %b_own.7, bf16[16,8,3,128,128]{4,3,2,1,0:T(8,128)(2,1)} %collective-permute-done.5.b_other, ...), custom_call_target="tpu_custom_call" | custom-call | flops 4227858 | bytes 7864 | tf_op jit(solution)/shard_map/pallas_call | solution.py:247
  63.2 3.4 %collective-permute-done.14.rest_0_ = bf16[2,128,768]{2,1,0:T(8,128)(2,1)S(1)} collective-permute-done((bf16[2,128,768]{2,1,0:T(8,128)(2,1)S(1)}, bf16[2,128,768]{2,1,0:T(8,128)(2,1)S(1)}, u32[]{:S(2)}, u32[]{:S(2)}) %collective-permute-start.14) | collective-permute-done | bytes 393248 | tf_op jit(solution)/shard_map/ppermute | solution.py:32
  66.7 4.1 %shard_map.79 = (f32[4,128,256]{2,1,0:T(8,128)S(1)}, f32[4,128,256]{2,1,0:T(8,128)S(1)}) custom-call(s32[256]{0:T(256)S(1)} %copy-done.1, bf16[768,2048]{1,0:T(8,128)(2,1)S(1)} %shard_map.74.a_ref, bf16[16,8,3,128,128]{4,3,2,1,0:T(8,128)(2,1)} %b_own.7, bf16[16,8,3,128,128]{4,3,2,1,0:T(8,128)(2,1)} %collective-permute-done.5.b_other, ...), custom_call_target="tpu_custom_call" | custom-call | flops 1409286144 | bytes 4718592 | tf_op jit(solution)/shard_map/pallas_call | solution.py:247
  70.8 1.9 %collective-permute-done.15.arrived_ref = f32[4,128,256]{2,1,0:T(8,128)S(1)} collective-permute-done((f32[4,128,256]{2,1,0:T(8,128)S(1)}, f32[4,128,256]{2,1,0:T(8,128)S(1)}, u32[]{:S(2)}, u32[]{:S(2)}) %collective-permute-start.15) | collective-permute-done | bytes 524320 | tf_op jit(solution)/shard_map/ppermute | solution.py:32
  72.9 3.8 %collective-permute-start.17 = (bf16[128,256]{1,0:T(8,128)(2,1)S(1)}, bf16[128,256]{1,0:T(8,128)(2,1)S(1)}, u32[]{:S(2)}, u32[]{:S(2)}) collective-permute-start(bf16[128,256]{1,0:T(8,128)(2,1)S(1)} %get-tuple-element.51), channel_id=1, source_target_pairs={{0,2},{1,3},{2,0},{3,1},{4,6},{5,7},{6,4},{7,5},{8,10},{9,11},{10,... | collective-permute-start | bytes 196616 | tf_op jit(solution)/shard_map/ppermute | solution.py:32
  76.7 1.2 %collective-permute-start.18 = (bf16[128,256]{1,0:T(8,128)(2,1)S(1)}, bf16[128,256]{1,0:T(8,128)(2,1)S(1)}, u32[]{:S(2)}, u32[]{:S(2)}) collective-permute-start(bf16[128,256]{1,0:T(8,128)(2,1)S(1)} %get-tuple-element.52), channel_id=1, source_target_pairs={{0,3},{1,0},{2,1},{3,2},{4,7},{5,4},{6,5},{7,6},{8,11},{9,8},{10,9... | collective-permute-start | bytes 196616 | tf_op jit(solution)/shard_map/ppermute | solution.py:32
  77.9 0.8 collective-permute-done.16
  78.7 1.5 %collective-permute-done.17 = bf16[128,256]{1,0:T(8,128)(2,1)S(1)} collective-permute-done((bf16[128,256]{1,0:T(8,128)(2,1)S(1)}, bf16[128,256]{1,0:T(8,128)(2,1)S(1)}, u32[]{:S(2)}, u32[]{:S(2)}) %collective-permute-start.17) | collective-permute-done | bytes 65568 | tf_op jit(solution)/shard_map/ppermute | solution.py:32
  80.2 0.8 collective-permute-done.18
  (30 shorter events, 4.7 us)
Async XLA Ops:
  0.0 1.0 %copy-start = (bf16[128,1024]{1,0:T(8,128)(2,1)S(1)}, bf16[128,1024]{1,0:T(8,128)(2,1)}, u32[]{:S(2)}) copy-start(bf16[128,1024]{1,0:T(8,128)(2,1)} %param.7) | copy-start | bytes 786436
  1.0 13.1 %collective-permute-start.1 = (bf16[128,256]{1,0:T(8,128)(2,1)S(1)}, bf16[128,256]{1,0:T(8,128)(2,1)S(1)}, u32[]{:S(2)}, u32[]{:S(2)}) collective-permute-start(bf16[128,256]{1,0:T(8,128)(2,1)S(1)} %constant_dynamic-slice_fusion), channel_id=1, source_target_pairs={{0,128},{16,144},{32,160},{48,176},{64,192},{80,208},{96,224},{112... | collective-permute-start | bytes 196616 | tf_op jit(solution)/shard_map/ppermute | solution.py:32
  8.2 6.9 %collective-permute-start = (bf16[128,256]{1,0:T(8,128)(2,1)S(1)}, bf16[128,256]{1,0:T(8,128)(2,1)S(1)}, u32[]{:S(2)}, u32[]{:S(2)}) collective-permute-start(bf16[128,256]{1,0:T(8,128)(2,1)S(1)} %constant_dynamic-slice_fusion), channel_id=1, source_target_pairs={{0,192},{16,208},{32,224},{48,240},{64,0},{80,16},{96,32},{112,48}... | collective-permute-start | bytes 196616 | tf_op jit(solution)/shard_map/ppermute | solution.py:32
  8.2 6.9 %collective-permute-start.2 = (bf16[128,256]{1,0:T(8,128)(2,1)S(1)}, bf16[128,256]{1,0:T(8,128)(2,1)S(1)}, u32[]{:S(2)}, u32[]{:S(2)}) collective-permute-start(bf16[128,256]{1,0:T(8,128)(2,1)S(1)} %constant_dynamic-slice_fusion), channel_id=1, source_target_pairs={{0,64},{16,80},{32,96},{48,112},{64,128},{80,144},{96,160},{112,17... | collective-permute-start | bytes 196616 | tf_op jit(solution)/shard_map/ppermute | solution.py:32
  12.9 1.1 %collective-permute-start.3 = (s32[48]{0:T(128)S(1)}, s32[48]{0:T(128)S(1)}, u32[]{:S(2)}, u32[]{:S(2)}) collective-permute-start(s32[48]{0:T(128)S(1)} %pad_add_fusion), channel_id=1, source_target_pairs={{0,4},{4,0},{8,12},{12,8},{1,5},{5,1},{9,13},{13,9},{2,6},{6,2},{1... | collective-permute-start | bytes 584 | tf_op jit(solution)/shard_map/ppermute | solution.py:32
  15.2 24.4 %collective-permute-start.5 = (bf16[16,8,3,128,128]{4,3,2,1,0:T(8,128)(2,1)}, bf16[16,8,3,128,128]{4,3,2,1,0:T(8,128)(2,1)}, u32[]{:S(2)}, u32[]{:S(2)}) collective-permute-start(bf16[16,8,3,128,128]{4,3,2,1,0:T(8,128)(2,1)} %b_own.7), channel_id=1, source_target_pairs={{0,4},{4,0},{8,12},{12,8},{1,5},{5,1},{9,13},{13,9},{2,6},{6,2},{1... | collective-permute-start | bytes 37748744 | tf_op jit(solution)/shard_map/ppermute | solution.py:32
  15.2 9.2 %collective-permute-start.4 = (bf16[4,128,256]{2,1,0:T(8,128)(2,1)S(1)}, bf16[4,128,256]{2,1,0:T(8,128)(2,1)S(1)}, u32[]{:S(2)}, u32[]{:S(2)}) collective-permute-start(bf16[4,128,256]{2,1,0:T(8,128)(2,1)S(1)} %pad_maximum_fusion.own_ref), channel_id=1, source_target_pairs={{0,16},{4,52},{8,24},{12,60},{16,32},{20,4},{24,40},{28,12},{32,48... | collective-permute-start | bytes 786440 | tf_op jit(solution)/shard_map/ppermute | solution.py:32
  15.8 9.4 %collective-permute-start.6 = (bf16[4,128,256]{2,1,0:T(8,128)(2,1)S(1)}, bf16[4,128,256]{2,1,0:T(8,128)(2,1)S(1)}, u32[]{:S(2)}, u32[]{:S(2)}) collective-permute-start(bf16[4,128,256]{2,1,0:T(8,128)(2,1)S(1)} %pad_maximum_fusion.own_ref), channel_id=1, source_target_pairs={{0,48},{4,20},{8,56},{12,28},{16,0},{20,36},{24,8},{28,44},{32,16}... | collective-permute-start | bytes 786440 | tf_op jit(solution)/shard_map/ppermute | solution.py:32
  24.4 6.4 %collective-permute-start.7 = (bf16[4,128,256]{2,1,0:T(8,128)(2,1)S(1)}, bf16[4,128,256]{2,1,0:T(8,128)(2,1)S(1)}, u32[]{:S(2)}, u32[]{:S(2)}) collective-permute-start(bf16[4,128,256]{2,1,0:T(8,128)(2,1)S(1)} %collective-permute-done.4.ahead_ref), channel_id=1, source_target_pairs={{0,16},{4,52},{8,24},{12,60},{16,32},{20,4},{24,40},{28,12},{32,48... | collective-permute-start | bytes 786440 | tf_op jit(solution)/shard_map/ppermute | solution.py:32
  30.8 0.6 copy-start.2
  32.5 12.1 %collective-permute-start.10 = (bf16[2,128,768]{2,1,0:T(8,128)(2,1)S(1)}, bf16[2,128,768]{2,1,0:T(8,128)(2,1)S(1)}, u32[]{:S(2)}, u32[]{:S(2)}) collective-permute-start(bf16[2,128,768]{2,1,0:T(8,128)(2,1)S(1)} %shard_map.75.rest_0_), channel_id=1, source_target_pairs={{0,3},{1,0},{2,1},{3,2},{4,5},{5,6},{6,7},{7,4},{8,11},{9,8},{10,9... | collective-permute-start | bytes 1179656 | tf_op jit(solution)/shard_map/ppermute | solution.py:32
  35.6 9.3 %collective-permute-start.9 = (bf16[2,128,768]{2,1,0:T(8,128)(2,1)S(1)}, bf16[2,128,768]{2,1,0:T(8,128)(2,1)S(1)}, u32[]{:S(2)}, u32[]{:S(2)}) collective-permute-start(bf16[2,128,768]{2,1,0:T(8,128)(2,1)S(1)} %shard_map.75.rest_0_), channel_id=1, source_target_pairs={{0,8},{4,12},{8,0},{12,4},{1,9},{5,13},{9,1},{13,5},{2,10},{6,14},... | collective-permute-start | bytes 1179656 | tf_op jit(solution)/shard_map/ppermute | solution.py:32
  37.2 9.0 %collective-permute-start.8 = (bf16[2,128,768]{2,1,0:T(8,128)(2,1)S(1)}, bf16[2,128,768]{2,1,0:T(8,128)(2,1)S(1)}, u32[]{:S(2)}, u32[]{:S(2)}) collective-permute-start(bf16[2,128,768]{2,1,0:T(8,128)(2,1)S(1)} %shard_map.75.rest_0_), channel_id=1, source_target_pairs={{0,1},{1,2},{2,3},{3,0},{4,7},{5,4},{6,5},{7,6},{8,9},{9,10},{10,1... | collective-permute-start | bytes 1179656 | tf_op jit(solution)/shard_map/ppermute | solution.py:32
  39.5 0.7 copy-start.1
  46.2 11.8 %collective-permute-start.12 = (bf16[2,128,768]{2,1,0:T(8,128)(2,1)S(1)}, bf16[2,128,768]{2,1,0:T(8,128)(2,1)S(1)}, u32[]{:S(2)}, u32[]{:S(2)}) collective-permute-start(bf16[2,128,768]{2,1,0:T(8,128)(2,1)S(1)} %collective-permute-done.8.rest_0_), channel_id=1, source_target_pairs={{0,1},{1,2},{2,3},{3,0},{4,7},{5,4},{6,5},{7,6},{8,9},{9,10},{10,1... | collective-permute-start | bytes 1179656 | tf_op jit(solution)/shard_map/ppermute | solution.py:32
  46.5 11.2 %collective-permute-start.11 = (bf16[2,128,768]{2,1,0:T(8,128)(2,1)S(1)}, bf16[2,128,768]{2,1,0:T(8,128)(2,1)S(1)}, u32[]{:S(2)}, u32[]{:S(2)}) collective-permute-start(bf16[2,128,768]{2,1,0:T(8,128)(2,1)S(1)} %collective-permute-done.8.rest_0_), channel_id=1, source_target_pairs={{0,8},{4,12},{8,0},{12,4},{1,9},{5,13},{9,1},{13,5},{2,10},{6,14},... | collective-permute-start | bytes 1179656 | tf_op jit(solution)/shard_map/ppermute | solution.py:32
  48.2 9.8 %collective-permute-start.13 = (bf16[2,128,768]{2,1,0:T(8,128)(2,1)S(1)}, bf16[2,128,768]{2,1,0:T(8,128)(2,1)S(1)}, u32[]{:S(2)}, u32[]{:S(2)}) collective-permute-start(bf16[2,128,768]{2,1,0:T(8,128)(2,1)S(1)} %collective-permute-done.9.rest_1_), channel_id=1, source_target_pairs={{0,3},{1,0},{2,1},{3,2},{4,5},{5,6},{6,7},{7,4},{8,11},{9,8},{10,9... | collective-permute-start | bytes 1179656 | tf_op jit(solution)/shard_map/ppermute | solution.py:32
  57.7 9.0 %collective-permute-start.14 = (bf16[2,128,768]{2,1,0:T(8,128)(2,1)S(1)}, bf16[2,128,768]{2,1,0:T(8,128)(2,1)S(1)}, u32[]{:S(2)}, u32[]{:S(2)}) collective-permute-start(bf16[2,128,768]{2,1,0:T(8,128)(2,1)S(1)} %collective-permute-done.11.rest_2_), channel_id=1, source_target_pairs={{0,1},{1,2},{2,3},{3,0},{4,7},{5,4},{6,5},{7,6},{8,9},{9,10},{10,1... | collective-permute-start | bytes 1179656 | tf_op jit(solution)/shard_map/ppermute | solution.py:32
  70.7 2.0 %collective-permute-start.15 = (f32[4,128,256]{2,1,0:T(8,128)S(1)}, f32[4,128,256]{2,1,0:T(8,128)S(1)}, u32[]{:S(2)}, u32[]{:S(2)}) collective-permute-start(f32[4,128,256]{2,1,0:T(8,128)S(1)} %get-tuple-element.48), channel_id=1, source_target_pairs={{0,4},{4,0},{8,12},{12,8},{1,5},{5,1},{9,13},{13,9},{2,6},{6,2},{1... | collective-permute-start | bytes 1572872 | tf_op jit(solution)/shard_map/ppermute | solution.py:32
  72.8 5.9 %collective-permute-start.16 = (bf16[128,256]{1,0:T(8,128)(2,1)S(1)}, bf16[128,256]{1,0:T(8,128)(2,1)S(1)}, u32[]{:S(2)}, u32[]{:S(2)}) collective-permute-start(bf16[128,256]{1,0:T(8,128)(2,1)S(1)} %get-tuple-element.50), channel_id=1, source_target_pairs={{0,1},{1,2},{2,3},{3,0},{4,5},{5,6},{6,7},{7,4},{8,9},{9,10},{10,1... | collective-permute-start | bytes 196616 | tf_op jit(solution)/shard_map/ppermute | solution.py:32
  72.9 7.3 %collective-permute-start.17 = (bf16[128,256]{1,0:T(8,128)(2,1)S(1)}, bf16[128,256]{1,0:T(8,128)(2,1)S(1)}, u32[]{:S(2)}, u32[]{:S(2)}) collective-permute-start(bf16[128,256]{1,0:T(8,128)(2,1)S(1)} %get-tuple-element.51), channel_id=1, source_target_pairs={{0,2},{1,3},{2,0},{3,1},{4,6},{5,7},{6,4},{7,5},{8,10},{9,11},{10,... | collective-permute-start | bytes 196616 | tf_op jit(solution)/shard_map/ppermute | solution.py:32
  76.7 4.3 %collective-permute-start.18 = (bf16[128,256]{1,0:T(8,128)(2,1)S(1)}, bf16[128,256]{1,0:T(8,128)(2,1)S(1)}, u32[]{:S(2)}, u32[]{:S(2)}) collective-permute-start(bf16[128,256]{1,0:T(8,128)(2,1)S(1)} %get-tuple-element.52), channel_id=1, source_target_pairs={{0,3},{1,0},{2,1},{3,2},{4,7},{5,4},{6,5},{7,6},{8,11},{9,8},{10,9... | collective-permute-start | bytes 196616 | tf_op jit(solution)/shard_map/ppermute | solution.py:32
